TPU v7x, 32 devices: a whole 2x2x4 slice. The times are simulated.
32 devices in a mesh: expert: 8 (over z, y), tensor: 4 (over x, core).
Axes of the slice: x: 2, y: 2, z: 4, core: 2. Of those that a mesh axis runs over, the one named last changes fastest.
Arguments:
- tokens: bfloat16 [1024, 5120], P('expert', 'tensor'), may hold values from -6 to 6
- out_grad: bfloat16 [1024, 5120], P('expert', 'tensor'), may hold values from -6 to 6
- expert_ids: int32 [1024, 6], P('expert'), may hold values from 0 to 15, as said below
- router_probs: float32 [1024, 16], P('expert'), may hold values from 0 to 1, as said below
- router_weight: bfloat16 [5120, 16], P('tensor'), may hold values from -0.29882812 to 0.29882812
- gate_weight: bfloat16 [16, 5120, 768], P('expert', 'tensor'), may hold values from -0.078125 to 0.078125
- up_weight: bfloat16 [16, 5120, 768], P('expert', 'tensor'), may hold values from -0.078125 to 0.078125
- down_weight: bfloat16 [16, 768, 5120], P('expert', None, 'tensor'), may hold values from -0.21875 to 0.21875
- gate_saved: bfloat16 [16, 512, 768], P('expert'), may hold values from -6 to 6
- up_saved: bfloat16 [16, 512, 768], P('expert'), may hold values from -6 to 6
- shared_gate: bfloat16 [5120, 2048], P(None, 'tensor'), may hold values from -0.078125 to 0.078125
- shared_up: bfloat16 [5120, 2048], P(None, 'tensor'), may hold values from -0.078125 to 0.078125
- shared_down: bfloat16 [2048, 5120], P('tensor'), may hold values from -0.125 to 0.125
Outputs:
- input_grad: bfloat16 [1024, 5120], P('expert', 'tensor')
Inputs may be any that keep to these rules, and one draw needn't show every extreme that they name: `expert_ids`: each row names 6 different experts. `router_probs`: each row is positive and sums to one.
All inputs are finite; a program needn't handle non-finite values.
Results may differ from a plain program's by a relative error of at most 0.014.
Values may be sent and summed in bfloat16 or wider, within the bound.
No kernel may reach another device: no remote copies, remote signals or barrier semaphores. Data moves between devices by JAX's collectives and lax.ppermute only.
A program may use at most 128 MiB of HBM per device.

v0:
```python
import jax
import jax.numpy as jnp
from jax import lax
from jax.sharding import PartitionSpec as P


def silu_parts(preact):
    sigmoid_value = jax.nn.sigmoid(preact)
    return (preact * sigmoid_value, sigmoid_value * (1.0 + preact * (1.0 - sigmoid_value)))


def per_device(
    tokens,
    out_grad,
    expert_ids,
    router_probs,
    router_weight,
    gate_weight,
    up_weight,
    down_weight,
    gate_saved,
    up_saved,
    shared_gate,
    shared_up,
    shared_down,
):
    groups = lax.axis_size("expert")
    local_count, slot_count, hidden_units = gate_saved.shape
    capacity = slot_count // groups
    token_rows, route_width = expert_ids.shape
    expert_total = router_probs.shape[1]
    feature_cols = tokens.shape[1]
    column_total = local_count * groups * capacity
    flat_ids = expert_ids.reshape(-1)
    onehot = (flat_ids[:, None] == jnp.arange(expert_total, dtype=jnp.int32)[None, :]).astype(
        jnp.int32
    )
    slot_index = jnp.sum((jnp.cumsum(onehot, axis=0) - onehot) * onehot, axis=1)
    kept_mask = slot_index < capacity
    owner_group = flat_ids // local_count
    local_expert = flat_ids % local_count
    column_id = jnp.where(
        kept_mask, local_expert * (groups * capacity) + owner_group * capacity + slot_index, -1
    )
    column_grid = column_id.reshape(token_rows, route_width)
    column_match = (
        column_grid[:, :, None] == jnp.arange(column_total, dtype=jnp.int32)[None, None, :]
    )
    placement = jnp.sum(column_match.astype(jnp.float32), axis=1).astype(jnp.bfloat16)
    sectioning = jnp.einsum(
        "tc,td->cd", placement, out_grad, preferred_element_type=jnp.float32
    ).astype(jnp.bfloat16)
    outgoing = sectioning.reshape(local_count, groups, capacity * feature_cols)
    token_piece = lax.all_gather(tokens, "tensor", axis=1, tiled=True)
    grad_piece = lax.all_gather(out_grad, "tensor", axis=1, tiled=True)
    gate_pre = jnp.dot(token_piece, shared_gate, preferred_element_type=jnp.float32)
    up_pre = jnp.dot(token_piece, shared_up, preferred_element_type=jnp.float32)
    hidden_pre = jnp.einsum(
        "tc,fc->tf", grad_piece, shared_down, preferred_element_type=jnp.float32
    )
    active, slope_term = silu_parts(gate_pre)
    shared_dgate = (hidden_pre * up_pre * slope_term).astype(jnp.bfloat16)
    shared_dup = (hidden_pre * active).astype(jnp.bfloat16)
    shared_term = jnp.einsum(
        "tf,df->td", shared_dgate, shared_gate, preferred_element_type=jnp.float32
    ) + jnp.einsum("tf,df->td", shared_dup, shared_up, preferred_element_type=jnp.float32)
    shared_part = lax.psum_scatter(
        shared_term.astype(jnp.bfloat16), "tensor", scatter_dimension=1, tiled=True
    ).astype(jnp.float32)
    arrived = lax.all_to_all(outgoing, "expert", split_axis=1, concat_axis=1, tiled=True)
    arrived = arrived.reshape(local_count, slot_count, feature_cols)
    partial_hidden = jnp.einsum(
        "esd,efd->esf", arrived, down_weight, preferred_element_type=jnp.float32
    )
    up_full = up_saved.astype(jnp.float32)
    hidden_grad = lax.psum(partial_hidden.astype(jnp.bfloat16), "tensor").astype(jnp.float32)
    active, slope_term = silu_parts(gate_saved.astype(jnp.float32))
    d_gate = (hidden_grad * up_full * slope_term).astype(jnp.bfloat16)
    d_up = (hidden_grad * active).astype(jnp.bfloat16)
    score_rows = jnp.sum(up_full * d_up.astype(jnp.float32), axis=2).astype(jnp.bfloat16)
    expert_grad = jnp.einsum(
        "esf,edf->esd", d_gate, gate_weight, preferred_element_type=jnp.float32
    ) + jnp.einsum("esf,edf->esd", d_up, up_weight, preferred_element_type=jnp.float32)
    expert_grad = expert_grad.astype(jnp.bfloat16)
    back_grad, back_score = (
        lax.all_to_all(
            expert_grad.reshape(local_count, groups, capacity * feature_cols),
            "expert",
            split_axis=1,
            concat_axis=1,
            tiled=True,
        ),
        lax.all_to_all(
            score_rows.reshape(local_count, groups, capacity),
            "expert",
            split_axis=1,
            concat_axis=1,
            tiled=True,
        ),
    )
    returned_rows = back_grad.reshape(column_total, feature_cols)
    returned_scores = back_score.reshape(column_total).astype(jnp.float32)
    kept_value = kept_mask.astype(jnp.float32)
    probs_rows = jnp.repeat(router_probs, route_width, axis=0)
    onehot_float = onehot.astype(jnp.float32)
    gate_value = jnp.sum(onehot_float * probs_rows, axis=1)
    route_weight = (gate_value * kept_value).reshape(token_rows, route_width)
    combine_weight = jnp.sum(jnp.where(column_match, route_weight[:, :, None], 0.0), axis=1)
    routed_part = jnp.dot(
        combine_weight,
        returned_rows.astype(jnp.float32),
        precision=lax.Precision.HIGHEST,
        preferred_element_type=jnp.float32,
    )
    safe_column = jnp.maximum(column_id, 0)
    route_score = returned_scores[safe_column] * kept_value
    prob_grad = jnp.sum(
        (onehot_float * route_score[:, None]).reshape(token_rows, route_width, expert_total), axis=1
    )
    gate_total = jnp.sum((gate_value * route_score).reshape(token_rows, route_width), axis=1)
    logit_grad = (router_probs * (prob_grad - gate_total[:, None])).astype(jnp.bfloat16)
    router_part = jnp.einsum(
        "te,de->td", logit_grad, router_weight, preferred_element_type=jnp.float32
    )
    return (shared_part + routed_part + router_part).astype(jnp.bfloat16)


def solution(mesh):
    return jax.shard_map(
        per_device,
        mesh=mesh,
        in_specs=(
            P("expert", "tensor"),
            P("expert", "tensor"),
            P("expert", None),
            P("expert", None),
            P("tensor", None),
            P("expert", "tensor", None),
            P("expert", "tensor", None),
            P("expert", None, "tensor"),
            P("expert", None, None),
            P("expert", None, None),
            P(None, "tensor"),
            P(None, "tensor"),
            P("tensor", None),
        ),
        out_specs=P("expert", "tensor"),
        check_vma=False,
    )
```

profile of v0, /device:TPU:0, one launch (start us, length us, event | category | flops | bytes accessed | tf_op | source)
XLA Modules:
  0.0 245.7 jit_solution(3710820803463782855)
XLA Ops:
  6.5 0.8 copy.71
  7.6 0.7 multiply_reduce_fusion.1
  8.4 1.7 reduce-window.6
  10.7 0.7 fusion.32
  11.4 1.5 select_reduce_fusion
  12.9 1.8 convolution_convert_fusion
  14.7 2.3 reshape.240
  17.0 4.4 %copy.76 = bf16[2,8,81920]{2,0,1:T(2,128)(2,1)S(1)} copy(bf16[2,8,81920]{2,1,0:T(8,128)(2,1)} %reshape.240) | data formatting | bytes 5242880 | tf_op jit(solution)/shard_map/reshape | solution.py:53
  21.4 66.6 %all_to_all.15 = bf16[2,8,81920]{2,0,1:T(2,128)(2,1)S(1)} all-to-all(bf16[2,8,81920]{2,0,1:T(2,128)(2,1)S(1)} %copy.76), channel_id=1, replica_groups=mesh['expert'=8,'tensor'=4] {'expert'}, dimensions={1} | all-to-all | bytes 5242880 | tf_op jit(solution)/shard_map/all_to_all | solution.py:70
  88.0 1.4 copy.77
  89.4 2.3 reshape.241
  91.8 6.4 %convolution_convert_fusion.1 = bf16[2,512,768]{2,1,0:T(8,128)(2,1)} fusion(bf16[2,512,1280]{2,1,0:T(8,128)(2,1)} %reshape.241, bf16[2,768,1280]{2,1,0:T(8,128)(2,1)} %param.20), kind=kOutput, calls=%fused_computation.26 | convolution fusion | flops 2014052352 | bytes 8126464 | tf_op jit(solution)/shard_map/esd,efd->esf/dot_general | solution.py:72
  98.2 0.7 all-gather.3.cloned.1.call-update
  99.0 0.7 all-gather.5.cloned.1.call-update
  99.7 40.5 %all-reduce.2.cloned.1.call-done = bf16[2,512,768]{2,1,0:T(8,128)(2,1)} async-done(((bf16[2,512,768]{2,1,0:T(8,128)(2,1)}), bf16[2,512,768]{2,1,0:T(8,128)(2,1)}) %all-reduce.2.cloned.1.call-update) | async-done | bytes 1572880 | tf_op jit(solution)/shard_map/psum | solution.py:76
  140.2 2.6 %fusion.4 = bf16[2,512]{1,0:T(2,128)(2,1)S(1)} fusion(bf16[2,512,768]{2,1,0:T(8,128)(2,1)S(1)} %copy-done.1, bf16[2,512,768]{2,1,0:T(8,128)(2,1)S(1)} %copy-done.2, bf16[2,512,768]{2,1,0:T(8,128)(2,1)} %all-reduce.2.cloned.1.call-done), kind=kLoop, calls=%fused_computation.14 | loop fusion | flops 9436160 | bytes 4720640 | tf_op jit(solution)/shard_map/reduce_sum | solution.py:80
  143.5 5.5 %all-to-all-start.2 = ((bf16[2,8,64]{2,0,1:T(2,128)(2,1)}), bf16[2,8,64]{2,0,1:T(2,128)(2,1)S(1)}, u32[]{:S(2)}, u32[]{:S(2)}) async-start(bf16[2,8,64]{2,0,1:T(2,128)(2,1)} %copy.80), calls=%async_computation.3 | async-start | bytes 8192 | tf_op jit(solution)/shard_map/all_to_all | solution.py:93
  149.1 5.6 %fusion.12 = f32[2,512,1280]{2,1,0:T(8,128)S(1)} fusion(bf16[2,1280,768]{2,1,0:T(8,128)(2,1)} %param.18, bf16[2,512,768]{2,1,0:T(8,128)(2,1)S(1)} %copy-done.1, bf16[2,512,768]{2,1,0:T(8,128)(2,1)} %all-reduce.2.cloned.1.call-done, bf16[2,512,768]{2,1,0:T(8,128)(2,1)S(1)} %copy-done.2), kind=kOutput, calls=%fused_computation.27 | convolution fusion | flops 2023489536 | bytes 13893632 | tf_op jit(solution)/shard_map/esf,edf->esd/dot_general | solution.py:81
  154.7 4.0 %add_convert_fusion = bf16[2,512,1280]{2,1,0:T(8,128)(2,1)} fusion(f32[2,512,1280]{2,1,0:T(8,128)S(1)} %fusion.12, bf16[2,1280,768]{2,1,0:T(8,128)(2,1)S(1)} %copy-done.6, bf16[2,512,768]{2,1,0:T(8,128)(2,1)S(1)} %copy-done.3, bf16[2,512,768]{2,1,0:T(8,128)(2,1)S(1)} %copy-done.2), kind=kOutput, calls=%fused_computation.3 | convolution fusion | flops 2022178816 | bytes 14942208 | tf_op jit(solution)/shard_map/esf,edf->esd/dot_general | solution.py:83
  158.7 2.5 %reshape.242 = bf16[2,8,81920]{2,1,0:T(8,128)(2,1)S(1)} reshape(bf16[2,512,1280]{2,1,0:T(8,128)(2,1)} %add_convert_fusion) | data formatting | bytes 5242880 | tf_op jit(solution)/shard_map/reshape | solution.py:87
  161.2 4.2 %copy.78 = bf16[2,8,81920]{2,0,1:T(2,128)(2,1)} copy(bf16[2,8,81920]{2,1,0:T(8,128)(2,1)S(1)} %reshape.242) | data formatting | bytes 5242880 | tf_op jit(solution)/shard_map/reshape | solution.py:87
  165.4 6.0 %all-to-all-start.1 = ((bf16[2,8,81920]{2,0,1:T(2,128)(2,1)}), bf16[2,8,81920]{2,0,1:T(2,128)(2,1)S(1)}, u32[]{:S(2)}, u32[]{:S(2)}) async-start(bf16[2,8,81920]{2,0,1:T(2,128)(2,1)} %copy.78), calls=%async_computation.2 | async-start | bytes 5242880 | tf_op jit(solution)/shard_map/all_to_all | solution.py:86
  171.7 4.8 %fusion.49 = f32[128,512]{1,0:T(8,128)S(1)} fusion(bf16[128,5120]{1,0:T(8,128)(2,1)} %all-gather.3.cloned.1.call-done, bf16[512,5120]{1,0:T(8,128)(2,1)} %param.25), kind=kOutput, calls=%fused_computation.92 | convolution fusion | flops 671088640 | bytes 6815744 | tf_op jit(solution)/shard_map/tc,fc->tf/dot_general | solution.py:58
  176.5 3.4 %all-gather.5.cloned.1.call-done = bf16[128,5120]{1,0:T(8,128)(2,1)} async-done(((bf16[128,1280]{1,0:T(8,128)(2,1)}), bf16[128,5120]{1,0:T(8,128)(2,1)}) %all-gather.5.cloned.1.call-update) | async-done | bytes 1310736 | tf_op jit(solution)/shard_map/all_gather | solution.py:54
  179.8 3.7 %fusion.50 = f32[128,512]{1,0:T(8,128)S(1)} fusion(bf16[128,5120]{1,0:T(8,128)(2,1)} %all-gather.5.cloned.1.call-done, bf16[5120,512]{1,0:T(8,128)(2,1)} %param.23), kind=kOutput, calls=%fused_computation.93 | convolution fusion | flops 671088640 | bytes 6815744 | tf_op jit(solution)/shard_map/dot_general | solution.py:56
  183.6 8.6 %fusion.17 = f32[128,5120]{1,0:T(8,128)} fusion(bf16[5120,512]{1,0:T(8,128)(2,1)} %param.23, f32[128,512]{1,0:T(8,128)S(1)} %fusion.49, bf16[128,5120]{1,0:T(8,128)(2,1)} %all-gather.5.cloned.1.call-done, bf16[5120,512]{1,0:T(8,128)(2,1)} %param.24, f32[128,512]{1,0:T(8,128)S(1)} %fusion.50), kind=kOutput, calls=%fused_computation.32 | convolution fusion | flops 1342832640 | bytes 14942208 | tf_op jit(solution)/shard_map/tf,df->td/dot_general | solution.py:64
  192.1 6.2 %fusion = bf16[128,5120]{1,0:T(8,128)(2,1)} fusion(f32[128,5120]{1,0:T(8,128)} %fusion.17, bf16[5120,512]{1,0:T(8,128)(2,1)} %param.24, f32[128,512]{1,0:T(8,128)S(1)} %fusion.49, f32[128,512]{1,0:T(8,128)S(1)} %fusion.50), kind=kOutput, calls=%fused_computation.2 | convolution fusion | flops 672792576 | bytes 9699328 | tf_op jit(solution)/shard_map/tf,df->td/dot_general | solution.py:66
  198.7 3.2 %gather_fusion = f32[768]{0:T(1024)S(1)} fusion(f32[1024]{0:T(1024)S(1)} %reshape.245, s32[1024]{0:T(1024)S(1)} %pad_clamp_fusion), kind=kCustom, calls=%fused_computation | custom fusion | bytes 9216 | tf_op jit(solution)/shard_map/gather | solution.py:116
  202.4 28.0 %all-to-all-done.1 = bf16[2,8,81920]{2,0,1:T(2,128)(2,1)S(1)} async-done(((bf16[2,8,81920]{2,0,1:T(2,128)(2,1)}), bf16[2,8,81920]{2,0,1:T(2,128)(2,1)S(1)}, u32[]{:S(2)}, u32[]{:S(2)}) %all-to-all-start.1) | async-done | bytes 2621472 | tf_op jit(solution)/shard_map/all_to_all | solution.py:86
  230.4 2.9 %copy.79 = bf16[2,8,81920]{2,1,0:T(8,128)(2,1)} copy(bf16[2,8,81920]{2,0,1:T(2,128)(2,1)S(1)} %all-to-all-done.1) | data formatting | bytes 5242880 | tf_op jit(solution)/shard_map/all_to_all | solution.py:86
  233.3 2.5 %reshape.243 = bf16[1024,1280]{1,0:T(8,128)(2,1)S(1)} reshape(bf16[2,8,81920]{2,1,0:T(8,128)(2,1)} %copy.79) | data formatting | bytes 5242880 | tf_op jit(solution)/shard_map/reshape | solution.py:101
  235.9 3.3 %fusion.11 = bf16[128,1280]{1,0:T(8,128)(2,1)} fusion(f32[128,1280]{1,0:T(8,128)S(1)} %fusion.34, f32[128,1024]{1,0:T(8,128)} %get-tuple-element.5, bf16[1024,1280]{1,0:T(8,128)(2,1)S(1)} %reshape.243, bf16[128,1280]{1,0:T(8,128)(2,1)} %reduce-scatter.2.cloned.1.call-done), kind=kOutput, calls=%fused_computation.25 | convolution fusion | flops 2013921280 | bytes 4456448 | tf_op jit(solution)/shard_map/dot_general | solution.py:109
  (44 shorter events, 2.7 us)
Async XLA Ops:
  6.5 195.6 %copy-start = (bf16[1280,16]{0,1:T(8,128)(2,1)S(1)}, bf16[1280,16]{0,1:T(8,128)(2,1)}, u32[]{:S(2)}) copy-start(bf16[1280,16]{0,1:T(8,128)(2,1)} %param.17) | copy-start | bytes 122884
  6.5 133.6 %all-reduce.2.cloned.1.call-start = ((), (), s32[]{:S(2)}) async-start(), calls=%async_computation.7 | async-start | bytes 3145728 | tf_op jit(solution)/shard_map/psum | solution.py:76
  91.8 48.4 %copy-start.2 = (bf16[2,512,768]{2,1,0:T(8,128)(2,1)S(1)}, bf16[2,512,768]{2,1,0:T(8,128)(2,1)}, u32[]{:S(2)}) copy-start(bf16[2,512,768]{2,1,0:T(8,128)(2,1)} %param.21) | copy-start | bytes 4718596
  98.1 42.0 %copy-start.1 = (bf16[2,512,768]{2,1,0:T(8,128)(2,1)S(1)}, bf16[2,512,768]{2,1,0:T(8,128)(2,1)}, u32[]{:S(2)}) copy-start(bf16[2,512,768]{2,1,0:T(8,128)(2,1)} %param.22) | copy-start | bytes 4718596
  98.2 73.5 %all-gather.3.cloned.1.call-start = ((), (), s32[]{:S(2)}) async-start(), calls=%async_computation.4 | async-start | bytes 1638400 | tf_op jit(solution)/shard_map/all_gather | solution.py:55
  98.9 80.9 %all-gather.5.cloned.1.call-start = ((), (), s32[]{:S(2)}) async-start(), calls=%async_computation.5 | async-start | bytes 1638400 | tf_op jit(solution)/shard_map/all_gather | solution.py:54
  143.5 21.9 %all-to-all-start.2 = ((bf16[2,8,64]{2,0,1:T(2,128)(2,1)}), bf16[2,8,64]{2,0,1:T(2,128)(2,1)S(1)}, u32[]{:S(2)}, u32[]{:S(2)}) async-start(bf16[2,8,64]{2,0,1:T(2,128)(2,1)} %copy.80), calls=%async_computation.3 | async-start | bytes 8192 | tf_op jit(solution)/shard_map/all_to_all | solution.py:93
  149.0 5.7 %copy-start.3 = (bf16[2,512,768]{2,1,0:T(8,128)(2,1)S(1)}, bf16[2,512,768]{2,1,0:T(8,128)(2,1)}, u32[]{:S(2)}) copy-start(bf16[2,512,768]{2,1,0:T(8,128)(2,1)} %all-reduce.2.cloned.1.call-done) | copy-start | bytes 4718596
  149.0 5.7 %copy-start.6 = (bf16[2,1280,768]{2,1,0:T(8,128)(2,1)S(1)}, bf16[2,1280,768]{2,1,0:T(8,128)(2,1)}, u32[]{:S(2)}) copy-start(bf16[2,1280,768]{2,1,0:T(8,128)(2,1)} %param.19) | copy-start | bytes 11796484
  165.4 65.0 %all-to-all-start.1 = ((bf16[2,8,81920]{2,0,1:T(2,128)(2,1)}), bf16[2,8,81920]{2,0,1:T(2,128)(2,1)S(1)}, u32[]{:S(2)}, u32[]{:S(2)}) async-start(bf16[2,8,81920]{2,0,1:T(2,128)(2,1)} %copy.78), calls=%async_computation.2 | async-start | bytes 5242880 | tf_op jit(solution)/shard_map/all_to_all | solution.py:86
  171.4 64.5 %reduce-scatter.2.cloned.1.call-start = ((), (), s32[]{:S(2)}) async-start(), calls=%async_computation.6 | async-start | bytes 1638400 | tf_op jit(solution)/shard_map/reduce_scatter | solution.py:67
  198.4 3.7 %copy-start.4 = (s32[128,6]{0,1:T(8,128)S(1)}, s32[128,6]{0,1:T(8,128)}, u32[]{:S(2)}) copy-start(s32[128,6]{0,1:T(8,128)} %param.15) | copy-start | bytes 9220
  198.4 3.8 %copy-start.5 = (f32[128,16]{0,1:T(8,128)S(1)}, f32[128,16]{0,1:T(8,128)}, u32[]{:S(2)}) copy-start(f32[128,16]{0,1:T(8,128)} %param.16) | copy-start | bytes 24580
Sparse Core Ops, SparseCore 0:
  98.3 41.8 all-reduce.1
  141.7 18.2 all-gather.2
  161.6 18.1 all-gather.4
  198.5 26.5 reduce-scatter.1
where the time goes:
time: 246 us
  waiting for transfers between devices  73.3 us (30%)
  blocking collectives  66.6 us (27%)
  matrix products  44.7 us (18%)
  local copies, waits for them, and re-layouts  28.5 us (12%)
  between operations  13.4 us (5%)
  starting transfers between devices  11.8 us (5%)
  other arithmetic  7.5 us (3%)
    all_to_all x1, blocking collectives, per_device(): lax.all_to_all(outgoing, 'expert', split_axis=1, concat_axis=1, tiled=True)  66.6 us
    psum x1, waiting for transfers between devices, per_device(): lax.psum(partial_hidden.astype(jnp.bfloat16), 'tensor').astype(jnp.float32)  40.5 us
    all_to_all x1, waiting for transfers between devices, per_device(): lax.all_to_all(expert_grad.reshape(local_count, groups, capacity * featur...  28 us
    dot_general x1, matrix products, per_device(): jnp.einsum('tf,df->td', shared_dgate, shared_gate, preferred_element_type...  8.55 us
    reshape x2, local copies, waits for them, and re-layouts, per_device(): expert_grad.reshape(local_count, groups, capacity * feature_cols)  6.72 us
    reshape x2, local copies, waits for them, and re-layouts, per_device(): outgoing = sectioning.reshape(local_count, groups, capacity * feature_cols)  6.72 us
    dot_general x1, matrix products, per_device(): jnp.einsum('esd,efd->esf', arrived, down_weight, preferred_element_type=j...  6.38 us
    dot_general x1, matrix products, per_device(): jnp.einsum('tf,df->td', shared_dup, shared_up, preferred_element_type=jnp...  6.22 us
  transfers between devices with their start and end apart: 6, of which 3 were waited for; matrix products, arithmetic and copies ran while one was open for 21% of the time, Pallas kernels for 0%

commit v1 on v0

--- a/solution.py
+++ b/solution.py
@@ -9,7 +9,7 @@
     return (preact * sigmoid_value, sigmoid_value * (1.0 + preact * (1.0 - sigmoid_value)))
 
 
-def per_device(
+def per_device_wide(
     tokens,
     out_grad,
     expert_ids,
@@ -125,6 +125,208 @@
     return (shared_part + routed_part + router_part).astype(jnp.bfloat16)
 
 
+def ring_place(position):
+    position = position % 8
+    return jnp.where(position < 4, 2 * position, 15 - 2 * position)
+
+
+def per_device_ring(
+    tokens,
+    out_grad,
+    expert_ids,
+    router_probs,
+    router_weight,
+    gate_weight,
+    up_weight,
+    down_weight,
+    gate_saved,
+    up_saved,
+    shared_gate,
+    shared_up,
+    shared_down,
+):
+    f32, bf16 = jnp.float32, jnp.bfloat16
+    local_count, slot_count, hidden_units = gate_saved.shape
+    groups = lax.axis_size("expert")
+    capacity = slot_count // groups
+    rows, cols = tokens.shape
+    expert_total = router_probs.shape[1]
+    tiles = expert_total // 8
+    order = [0, 2, 4, 6, 7, 5, 3, 1]
+    ahead = [(order[i], order[(i + 1) % 8]) for i in range(8)]
+    behind = [(order[i], order[(i - 1) % 8]) for i in range(8)]
+    x_pairs = [(i, i ^ 2) for i in range(4)]
+    core_pairs = [(i, i ^ 1) for i in range(4)]
+    me = lax.axis_index("expert")
+    place = jnp.where(me % 2 == 0, me // 2, 7 - me // 2)
+    t_index = lax.axis_index("tensor")
+    core = t_index % 2
+
+    def swap_x(a):
+        return lax.ppermute(a, "tensor", x_pairs)
+
+    def swap_core(a):
+        return lax.ppermute(a, "tensor", core_pairs)
+
+    tok_core, grad_core = swap_core(tokens), swap_core(out_grad)
+    tok_x, grad_x = swap_x(tokens), swap_x(out_grad)
+
+    ids_t = expert_ids.T
+    member = jnp.any(
+        ids_t[None, :, :] == jnp.arange(expert_total, dtype=jnp.int32)[:, None, None], axis=1
+    )
+    lower = (jnp.arange(rows)[:, None] < jnp.arange(rows)[None, :]).astype(bf16)
+    before = jnp.dot(member.astype(bf16), lower, preferred_element_type=f32)
+    slot_t = jnp.where(member & (before < capacity), before, -1.0).astype(bf16)
+    probs_t = router_probs.T
+    high = probs_t.astype(bf16)
+    low = (probs_t - high.astype(f32)).astype(bf16)
+    meta = jnp.concatenate(
+        [a[8 * i : 8 * i + 8] for a in (slot_t, high, low) for i in range(tiles)]
+        + [jnp.zeros((8, cols - 3 * tiles * rows), bf16)],
+        axis=1,
+    )
+    payload = jnp.concatenate([out_grad, meta], axis=0)
+    half = (rows + 8) // 2
+
+    fore, back = payload, payload
+    blocks = {0: payload}
+    for r in range(1, 4):
+        fore = lax.ppermute(fore, "expert", ahead)
+        back = lax.ppermute(back, "expert", behind)
+        blocks[-r], blocks[r] = fore, back
+    top = lax.ppermute(fore[:half], "expert", ahead)
+    bottom = lax.ppermute(back[half:], "expert", behind)
+    blocks[4] = jnp.concatenate([top, bottom], axis=0)
+
+    first = me * local_count
+    slot_iota = jnp.arange(capacity, dtype=jnp.int32).astype(bf16)
+    contribution = {}
+    for chunk in ((0, -1, 1), (-2, 2), (-3, 3), (4,)):
+        data = jnp.stack([blocks[d] for d in chunk])
+        count = len(chunk)
+        info = data[:, rows:].reshape(count, 8, cols // rows, rows).transpose(0, 2, 1, 3)
+        info = info[:, : 3 * tiles].reshape(count, 3, expert_total, rows)
+        info = lax.dynamic_slice_in_dim(info, first, local_count, 2)
+        match = info[:, 0, :, None, :] == slot_iota[None, None, :, None]
+        gates = info[:, 1].astype(f32) + info[:, 2].astype(f32)
+        placed = jnp.einsum(
+            "best,btd->ebsd", match.astype(bf16), data[:, :rows], preferred_element_type=f32
+        ).astype(bf16)
+        placed = placed.reshape(local_count, count * capacity, cols)
+        partial = jnp.einsum("esd,efd->esf", placed, down_weight, preferred_element_type=f32)
+        partial = partial.astype(bf16)
+        mine = lax.dynamic_index_in_dim(partial, core, 0, keepdims=False)
+        other = lax.dynamic_index_in_dim(partial, 1 - core, 0, keepdims=False)
+        chip = (mine.astype(f32) + swap_core(other).astype(f32)).astype(bf16)
+        full = (chip.astype(f32) + swap_x(chip).astype(f32)).astype(bf16)
+        pair = swap_core(full)
+        hidden = jnp.stack([jnp.where(core == 0, full, pair), jnp.where(core == 0, pair, full)])
+        hidden = hidden.astype(f32)
+        starts = [ring_place(place + d) * capacity for d in chunk]
+        gate_rows = jnp.concatenate(
+            [lax.dynamic_slice_in_dim(gate_saved, s, capacity, 1) for s in starts], axis=1
+        ).astype(f32)
+        up_rows = jnp.concatenate(
+            [lax.dynamic_slice_in_dim(up_saved, s, capacity, 1) for s in starts], axis=1
+        ).astype(f32)
+        active, slope_term = silu_parts(gate_rows)
+        d_gate = (hidden * up_rows * slope_term).astype(bf16)
+        d_up = (hidden * active).astype(bf16)
+        score = jnp.sum(up_rows * d_up.astype(f32), axis=2).astype(bf16)
+        grad = jnp.einsum("esf,edf->esd", d_gate, gate_weight, preferred_element_type=f32)
+        grad = grad + jnp.einsum("esf,edf->esd", d_up, up_weight, preferred_element_type=f32)
+        grad = grad.astype(bf16).reshape(local_count, count, capacity, cols)
+        weights = jnp.where(match, gates[:, :, None, :], 0.0)
+        w_high = weights.astype(bf16)
+        w_low = (weights - w_high.astype(f32)).astype(bf16)
+        grad_b = grad.transpose(1, 0, 2, 3).reshape(count, local_count * capacity, cols)
+        w_high = w_high.reshape(count, local_count * capacity, rows)
+        w_low = w_low.reshape(count, local_count * capacity, rows)
+        token_rows = jnp.einsum("bct,bcd->btd", w_high, grad_b, preferred_element_type=f32)
+        token_rows = token_rows + jnp.einsum(
+            "bct,bcd->btd", w_low, grad_b, preferred_element_type=f32
+        )
+        score = score.reshape(local_count, count, capacity).astype(f32)
+        token_score = jnp.sum(
+            jnp.where(match, score.transpose(1, 0, 2)[:, :, :, None], 0.0), axis=2
+        )
+        wide = jnp.zeros((count, expert_total, rows), f32)
+        wide = lax.dynamic_update_slice_in_dim(wide, token_score, first, 1)
+        wide = jnp.concatenate(
+            [wide[:, 8 * i : 8 * i + 8] for i in range(tiles)]
+            + [jnp.zeros((count, 8, cols - tiles * rows), f32)],
+            axis=2,
+        )
+        both = jnp.concatenate([token_rows, wide], axis=1)
+        for i, d in enumerate(chunk):
+            contribution[d] = both[i]
+
+    top = lax.ppermute(contribution[4][:half].astype(bf16), "expert", ahead).astype(f32)
+    bottom = lax.ppermute(contribution[4][half:].astype(bf16), "expert", behind).astype(f32)
+    fore = jnp.concatenate([contribution[3][:half] + top, contribution[3][half:]], axis=0)
+    back = jnp.concatenate([contribution[-3][:half], contribution[-3][half:] + bottom], axis=0)
+    for d in (2, 1, 0):
+        fore = lax.ppermute(fore.astype(bf16), "expert", ahead).astype(f32)
+        back = lax.ppermute(back.astype(bf16), "expert", behind).astype(f32)
+        if d:
+            fore = fore + contribution[d]
+            back = back + contribution[-d]
+    total = contribution[0] + fore + back
+    routed_part = total[:rows]
+
+    def assemble(own, by_core, by_x):
+        by_both = swap_core(by_x)
+        wide = jnp.zeros((rows, 4 * cols), bf16)
+        for piece, flip in ((own, 0), (by_core, 1), (by_x, 2), (by_both, 3)):
+            at = jnp.bitwise_xor(t_index, flip) * cols
+            wide = lax.dynamic_update_slice_in_dim(wide, piece, at, 1)
+        return wide
+
+    token_piece = assemble(tokens, tok_core, tok_x)
+    grad_piece = assemble(out_grad, grad_core, grad_x)
+    gate_pre = jnp.dot(token_piece, shared_gate, preferred_element_type=f32)
+    up_pre = jnp.dot(token_piece, shared_up, preferred_element_type=f32)
+    hidden_pre = jnp.einsum("tc,fc->tf", grad_piece, shared_down, preferred_element_type=f32)
+    active, slope_term = silu_parts(gate_pre)
+    shared_dgate = (hidden_pre * up_pre * slope_term).astype(bf16)
+    shared_dup = (hidden_pre * active).astype(bf16)
+    term = jnp.einsum("tf,df->td", shared_dgate, shared_gate, preferred_element_type=f32)
+    term = term + jnp.einsum("tf,df->td", shared_dup, shared_up, preferred_element_type=f32)
+    term = term.astype(bf16)
+
+    def part(flip):
+        at = jnp.bitwise_xor(t_index, flip) * cols
+        return lax.dynamic_slice_in_dim(term, at, cols, 1)
+
+    near = swap_core(part(1)).astype(f32) + part(0).astype(f32)
+    far = swap_core(part(3)).astype(f32) + part(2).astype(f32)
+    shared_part = near + swap_x(far.astype(bf16)).astype(f32)
+
+    prob_grad = jnp.concatenate(
+        [total[rows:, i * rows : (i + 1) * rows] for i in range(tiles)], axis=0
+    ).T
+    gate_total = jnp.sum(router_probs * prob_grad, axis=1, keepdims=True)
+    logit_grad = (router_probs * (prob_grad - gate_total)).astype(bf16)
+    router_part = jnp.einsum("te,de->td", logit_grad, router_weight, preferred_element_type=f32)
+    return (shared_part + routed_part + router_part).astype(bf16)
+
+
+def per_device(*args):
+    tokens, router_probs, gate_weight = args[0], args[3], args[5]
+    rows, cols = tokens.shape
+    expert_total = router_probs.shape[1]
+    ring = (
+        lax.axis_size("expert") == 8
+        and lax.axis_size("tensor") == 4
+        and gate_weight.shape[0] == 2
+        and expert_total % 8 == 0
+        and cols % rows == 0
+        and 3 * (expert_total // 8) * rows <= cols
+    )
+    return (per_device_ring if ring else per_device_wide)(*args)
+
+
 def solution(mesh):
     return jax.shard_map(
         per_device,

time: 246 us -> 165 us (0.67)
  blocking collectives: 66.6 us -> 0 us
  waiting for transfers between devices: 73.3 us -> 44.6 us
  starting transfers between devices: 11.8 us -> 28.6 us
  other arithmetic: 7.5 us -> 21.6 us
  between operations: 13.4 us -> 1.31 us
  local copies, waits for them, and re-layouts: 28.5 us -> 19.4 us
  matrix products: 44.7 us -> 49.1 us
    all_to_all x1 -> x0, blocking collectives: 66.6 us -> none  [per_device(): lax.all_to_all(outgoing, 'expert', split_axis=1, concat_axis=1, tiled=True)]
    ppermute x0 -> x37, waiting for transfers between devices: none -> 44.6 us  [the longest x7 17.8 us: swap_x(): return lax.ppermute(a, 'tensor', x_pairs)]
    psum x1 -> x0, waiting for transfers between devices: 40.5 us -> none  [per_device(): lax.psum(partial_hidden.astype(jnp.bfloat16), 'tensor').astype(jnp.float32)]
    ppermute x0 -> x37, starting transfers between devices: none -> 28.6 us  [the longest x7 8.26 us: swap_x(): return lax.ppermute(a, 'tensor', x_pairs)]
    all_to_all x2 -> x0, waiting for transfers between devices: 28 us -> none  [the longest x1 28 us: per_device(): lax.all_to_all(expert_grad.reshape(local_count, groups, capacity * featur...]
    reshape x7 -> x0, local copies, waits for them, and re-layouts: 18.4 us -> none  [the longest x2 6.72 us: per_device(): expert_grad.reshape(local_count, groups, capacity * feature_cols)]
    all_to_all x2 -> x0, starting transfers between devices: 11.5 us -> none  [the longest x1 5.96 us: per_device(): lax.all_to_all(expert_grad.reshape(local_count, groups, capacity * featur...]
    convert_element_type x2 -> x19, other arithmetic: 0.01 us -> 10.2 us  [the longest x4 3.13 us: per_device_ring(): chip = (mine.astype(f32) + swap_core(other).astype(f32)).astype(bf16)]
  transfers between devices with their start and end apart: 6 -> 37, of which waited for: 3 -> 12; matrix products, arithmetic and copies ran while one was open for 21% -> 49% of each run, Pallas kernels for 0% -> 0%
where the time goes in v1:
time: 165 us; the launch traced here: 164 us
  matrix products  49.1 us (30%)
  waiting for transfers between devices  44.6 us (27%)
  starting transfers between devices  28.6 us (17%)
  other arithmetic  21.6 us (13%)
  local copies, waits for them, and re-layouts  19.4 us (12%)
    ppermute x7, waiting for transfers between devices, swap_x(): return lax.ppermute(a, 'tensor', x_pairs)  17.8 us
    ppermute x3, waiting for transfers between devices, per_device_ring(): fore = lax.ppermute(fore.astype(bf16), 'expert', ahead).astype(f32)  12.3 us
    dot_general x4, matrix products, per_device_ring(): jnp.einsum('esf,edf->esd', d_gate, gate_weight, preferred_element_type=f32)  8.92 us
    ppermute x7, starting transfers between devices, swap_x(): return lax.ppermute(a, 'tensor', x_pairs)  8.26 us
    ppermute x3, waiting for transfers between devices, per_device_ring(): back = lax.ppermute(back.astype(bf16), 'expert', behind).astype(f32)  8.12 us
    dot_general x1, matrix products, per_device_ring(): jnp.einsum('tf,df->td', shared_dgate, shared_gate, preferred_element_type...  8.11 us
    dot_general x4, matrix products, per_device_ring(): jnp.einsum('esd,efd->esf', placed, down_weight, preferred_element_type=f32)  7.77 us
    dot_general x4, matrix products, per_device_ring(): jnp.einsum('esf,edf->esd', d_up, up_weight, preferred_element_type=f32)  6.49 us
  transfers between devices with their start and end apart: 37, of which 12 were waited for; matrix products, arithmetic and copies ran while one was open for 49% of the time, Pallas kernels for 0%

profile of v1, /device:TPU:0, one launch (start us, length us, event | category | flops | bytes accessed | tf_op | source)
XLA Modules:
  0.0 164.5 jit_solution(18118310348604497836)
XLA Ops:
  1.6 1.8 %fusion.174 = (bf16[1,136,1280]{2,1,0:T(8,128)(2,1)S(1)}, bf16[136,1280]{1,0:T(8,128)(2,1)}) fusion(bf16[8,1280]{1,0:T(8,128)(2,1)S(1)} %constant_dynamic-update-slice_fusion, bf16[128,1280]{1,0:T(8,128)(2,1)} %param.14), kind=kLoop, calls=%fused_computation.345 | loop fusion | flops 696320 | bytes 1044480 | tf_op jit(solution)/shard_map/stack | solution.py:206
  3.4 3.0 %collective-permute-start.9 = (bf16[136,1280]{1,0:T(8,128)(2,1)}, bf16[136,1280]{1,0:T(8,128)(2,1)}, u32[]{:S(2)}, u32[]{:S(2)}) collective-permute-start(bf16[136,1280]{1,0:T(8,128)(2,1)} %get-tuple-element.40), channel_id=1, source_target_pairs={{0,8},{8,16},{16,24},{24,28},{28,20},{20,12},{12,4},{4,0},{1,9},{9... | collective-permute-start | bytes 1044488 | tf_op jit(solution)/shard_map/ppermute | solution.py:195
  6.5 1.9 %collective-permute-start.4 = (bf16[128,1280]{1,0:T(8,128)(2,1)}, bf16[128,1280]{1,0:T(8,128)(2,1)}, u32[]{:S(2)}, u32[]{:S(2)}) collective-permute-start(bf16[128,1280]{1,0:T(8,128)(2,1)} %param.13), channel_id=1, source_target_pairs={{0,2},{1,3},{2,0},{3,1},{4,6},{5,7},{6,4},{7,5},{8,10},{9,11},{10,... | collective-permute-start | bytes 983048 | tf_op jit(solution)/shard_map/ppermute | solution.py:166
  9.7 3.4 %constant_dynamic-slice_fusion.9 = (bf16[2,64,768]{2,1,0:T(8,128)(2,1)}, bf16[2,64,768]{2,1,0:T(8,128)(2,1)}, bf16[2,64,768]{2,1,0:T(8,128)(2,1)}, bf16[2,64,768...) fusion(bf16[2,512,768]{2,1,0:T(8,128)(2,1)} %param.21, ...), kind=kLoop, calls=%fused_computation.271 | loop fusion | bytes 5505052 | tf_op jit(solution)/shard_map/dynamic_slice | solution.py:228
  15.1 2.3 %collective-permute-done.4 = bf16[128,1280]{1,0:T(8,128)(2,1)} collective-permute-done((bf16[128,1280]{1,0:T(8,128)(2,1)}, bf16[128,1280]{1,0:T(8,128)(2,1)}, u32[]{:S(2)}, u32[]{:S(2)}) %collective-permute-start.4) | collective-permute-done | bytes 327712 | tf_op jit(solution)/shard_map/ppermute | solution.py:166
  17.4 6.8 %collective-permute-done.1 = bf16[128,1280]{1,0:T(8,128)(2,1)} collective-permute-done((bf16[128,1280]{1,0:T(8,128)(2,1)}, bf16[128,1280]{1,0:T(8,128)(2,1)}, u32[]{:S(2)}, u32[]{:S(2)}) %collective-permute-start.1) | collective-permute-done | bytes 327712 | tf_op jit(solution)/shard_map/ppermute | solution.py:166
  27.0 1.7 %fusion.2 = bf16[2,3,64,1280]{3,2,0,1:T(8,128)(2,1)S(1)} fusion(bf16[1,136,1280]{2,1,0:T(8,128)(2,1)} %bitcast.4, bf16[1,136,1280]{2,1,0:T(8,128)(2,1)} %bitcast.3, bf16[1,136,1280]{2,1,0:T(8,128)(2,1)S(1)} %get-tuple-element.39, bf16[3,2,128]{2,1,0:T(2,128)(2,1)S(1)} %fusion.149, bf16[64]{0:T(256)(128)(2,1)S(1)} %iota_convert_fusion), kind=kOutput, calls=%fused_computation.10 | convolution fusion | flops 129417216 | bytes 2029184 | tf_op jit(solution)/shard_map/best,btd->ebsd/dot_general | solution.py:213
  33.8 1.8 %collective-permute-start.14 = (bf16[136,1280]{1,0:T(8,128)(2,1)}, bf16[136,1280]{1,0:T(8,128)(2,1)}, u32[]{:S(2)}, u32[]{:S(2)}) collective-permute-start(bf16[136,1280]{1,0:T(8,128)(2,1)} %collective-permute-done.9), channel_id=1, source_target_pairs={{0,8},{8,16},{16,24},{24,28},{28,20},{20,12},{12,4},{4,0},{1,9},{9... | collective-permute-start | bytes 1044488 | tf_op jit(solution)/shard_map/ppermute | solution.py:195
  36.0 1.8 %collective-permute-start.12 = (bf16[192,768]{1,0:T(8,128)(2,1)S(1)}, bf16[192,768]{1,0:T(8,128)(2,1)}, u32[]{:S(2)}, u32[]{:S(2)}) collective-permute-start(bf16[192,768]{1,0:T(8,128)(2,1)S(1)} %fusion.67), channel_id=1, source_target_pairs={{0,2},{1,3},{2,0},{3,1},{4,6},{5,7},{6,4},{7,5},{8,10},{9,11},{10,... | collective-permute-start | bytes 884744 | tf_op jit(solution)/shard_map/ppermute | solution.py:166
  38.9 1.9 %fusion.184 = f32[128,512]{1,0:T(8,128)S(1)} fusion(bf16[128,5120]{1,0:T(8,128)(2,1)S(1)} %constant_dynamic-update-slice_fusion.15, bf16[512,5120]{1,0:T(8,128)(2,1)S(1)} %bitcast.350), kind=kOutput, calls=%fused_computation.351 | convolution fusion | flops 671088640 | bytes 6815744 | tf_op jit(solution)/shard_map/tc,fc->tf/dot_general | solution.py:290
  40.7 8.1 %fusion.25 = f32[128,5120]{1,0:T(8,128)} fusion(bf16[5120,512]{1,0:T(8,128)(2,1)} %param.23, f32[128,512]{1,0:T(8,128)S(1)} %fusion.184, bf16[128,5120]{1,0:T(8,128)(2,1)S(1)} %constant_dynamic-update-slice_fusion.11, bf16[5120,512]{1,0:T(8,128)(2,1)} %param.24, f32[128,512]{1,0:T(8,128)S(1)} %fusion.185), kind=kOutput, calls=%fused_computation.58 | convolution fusion | flops 1342832640 | bytes 14942208 | tf_op jit(solution)/shard_map/tf,df->td/dot_general | solution.py:294
  48.8 5.1 %fusion = bf16[128,5120]{1,0:T(8,128)(2,1)S(1)} fusion(f32[128,5120]{1,0:T(8,128)} %fusion.25, bf16[5120,512]{1,0:T(8,128)(2,1)} %param.24, f32[128,512]{1,0:T(8,128)S(1)} %fusion.184, f32[128,512]{1,0:T(8,128)S(1)} %fusion.185), kind=kOutput, calls=%fused_computation.1 | convolution fusion | flops 672792576 | bytes 9699328 | tf_op jit(solution)/shard_map/tf,df->td/dot_general | solution.py:295
  55.5 1.6 collective-permute-start.15
  59.5 6.3 %collective-permute-done.15 = bf16[136,1280]{1,0:T(8,128)(2,1)S(1)} collective-permute-done((bf16[136,1280]{1,0:T(8,128)(2,1)}, bf16[136,1280]{1,0:T(8,128)(2,1)S(1)}, u32[]{:S(2)}, u32[]{:S(2)}) %collective-permute-start.15) | collective-permute-done | bytes 348192 | tf_op jit(solution)/shard_map/ppermute | solution.py:195
  65.8 1.6 collective-permute-start.21
  76.6 3.6 %fusion.22 = bf16[2,64,768]{2,1,0:T(8,128)(2,1)S(1)} fusion(bf16[2,768,1280]{2,1,0:T(8,128)(2,1)} %param.20, bf16[1,136,1280]{2,1,0:T(8,128)(2,1)S(1)} %maximum_bitcast_fusion, bf16[2,128]{1,0:T(2,128)(2,1)S(1)} %fusion.157, bf16[64]{0:T(256)(128)(2,1)S(1)} %iota_convert_fusion), kind=kOutput, calls=%fused_computation.54 | convolution fusion | flops 293912576 | bytes 4457472 | tf_op jit(solution)/shard_map/esd,efd->esf/dot_general | solution.py:217
  83.1 3.7 %fusion.65 = f32[2,192,1280]{2,1,0:T(8,128)S(1)} fusion(bf16[2,1280,768]{2,1,0:T(8,128)(2,1)} %param.18, bf16[1,192,768]{2,1,0:T(8,128)(2,1)S(1)} %get-tuple-element.34, bf16[1,192,768]{2,1,0:T(8,128)(2,1)S(1)} %get-tuple-element.33, bf16[2,64,768]{2,1,0:T(8,128)(2,1)S(1)} %copy-done.14, bf16[2,64,768]{2,1,0:T(8,128)(2,1)S(1)} %copy-done.15, ...), kind=kOutput, calls=%fused_computation.115 | convolution fusion | flops 762642432 | bytes 7667712 | tf_op jit(solution)/shard_map/esf,edf->esd/dot_general | solution.py:237
  86.8 1.5 fusion.1
  96.6 4.7 %collective-permute-done.24 = bf16[64,768]{1,0:T(8,128)(2,1)S(1)} collective-permute-done((bf16[64,768]{1,0:T(8,128)(2,1)S(1)}, bf16[64,768]{1,0:T(8,128)(2,1)S(1)}, u32[]{:S(2)}, u32[]{:S(2)}) %collective-permute-start.24) | collective-permute-done | bytes 98336 | tf_op jit(solution)/shard_map/ppermute | solution.py:166
  102.0 3.0 %collective-permute-done.19 = bf16[128,768]{1,0:T(8,128)(2,1)S(1)} collective-permute-done((bf16[128,768]{1,0:T(8,128)(2,1)S(1)}, bf16[128,768]{1,0:T(8,128)(2,1)S(1)}, u32[]{:S(2)}, u32[]{:S(2)}) %collective-permute-start.19) | collective-permute-done | bytes 196640 | tf_op jit(solution)/shard_map/ppermute | solution.py:166
  106.5 2.5 %fusion.95 = f32[2,64,1280]{2,1,0:T(8,128)S(1)} fusion(bf16[2,1280,768]{2,1,0:T(8,128)(2,1)S(1)} %copy-done.48, bf16[2,512,768]{2,1,0:T(8,128)(2,1)} %param.21, s32[]{:T(128)S(6)} %select_n.297, bf16[2,512,768]{2,1,0:T(8,128)(2,1)} %param.22, bf16[1,64,768]{2,1,0:T(8,128)(2,1)S(1)} %get-tuple-element.44, bf16[1,64,768]{2,1,0:T(8,128)(2,1)S(1)} %get-tuple-element.43), kind=kOutput, calls=%fused_computation.176 | convolution fusion | flops 253231104 | bytes 5177348 | tf_op jit(solution)/shard_map/esf,edf->esd/dot_general | solution.py:237
  109.2 2.2 %fusion.9 = bf16[2,64,1280]{2,1,0:T(8,128)(2,1)S(1)} fusion(f32[2,64,1280]{2,1,0:T(8,128)S(1)} %fusion.95, bf16[2,1280,768]{2,1,0:T(8,128)(2,1)S(1)} %copy-done.9, bf16[2,512,768]{2,1,0:T(8,128)(2,1)} %param.21, s32[]{:T(128)S(6)} %select_n.297, bf16[1,64,768]{2,1,0:T(8,128)(2,1)S(1)} %get-tuple-element.44, bf16[1,64,768]{2,1,0:T(8,128)(2,1)S(1)} %get-tuple-element.43), kind=kOutput, calls=%fused_computation.22 | convolution fusion | flops 253067264 | bytes 5308420 | tf_op jit(solution)/shard_map/esf,edf->esd/dot_general | solution.py:238
  113.3 1.5 collective-permute-start.33
  124.8 1.5 fusion.187
  130.3 1.6 collective-permute-start.34
  134.0 6.4 %collective-permute-done.34 = bf16[136,1280]{1,0:T(8,128)(2,1)S(1)} collective-permute-done((bf16[136,1280]{1,0:T(8,128)(2,1)S(1)}, bf16[136,1280]{1,0:T(8,128)(2,1)S(1)}, u32[]{:S(2)}, u32[]{:S(2)}) %collective-permute-start.34) | collective-permute-done | bytes 348192 | tf_op jit(solution)/shard_map/ppermute | solution.py:271
  140.4 2.3 %collective-permute-done.27 = bf16[136,1280]{1,0:T(8,128)(2,1)S(1)} collective-permute-done((bf16[136,1280]{1,0:T(8,128)(2,1)S(1)}, bf16[136,1280]{1,0:T(8,128)(2,1)S(1)}, u32[]{:S(2)}, u32[]{:S(2)}) %collective-permute-start.27) | collective-permute-done | bytes 348192 | tf_op jit(solution)/shard_map/ppermute | solution.py:270
  143.4 1.5 collective-permute-start.35
  145.1 6.6 %collective-permute-done.31 = bf16[136,1280]{1,0:T(8,128)(2,1)S(1)} collective-permute-done((bf16[136,1280]{1,0:T(8,128)(2,1)S(1)}, bf16[136,1280]{1,0:T(8,128)(2,1)S(1)}, u32[]{:S(2)}, u32[]{:S(2)}) %collective-permute-start.31) | collective-permute-done | bytes 348192 | tf_op jit(solution)/shard_map/ppermute | solution.py:270
  152.2 1.7 %collective-permute-start.32 = (bf16[136,1280]{1,0:T(8,128)(2,1)S(1)}, bf16[136,1280]{1,0:T(8,128)(2,1)S(1)}, u32[]{:S(2)}, u32[]{:S(2)}) collective-permute-start(bf16[136,1280]{1,0:T(8,128)(2,1)S(1)} %get-tuple-element.9), channel_id=1, source_target_pairs={{0,8},{8,16},{16,24},{24,28},{28,20},{20,12},{12,4},{4,0},{1,9},{9... | collective-permute-start | bytes 1044488 | tf_op jit(solution)/shard_map/ppermute | solution.py:270
  156.4 3.4 %collective-permute-done.32 = bf16[136,1280]{1,0:T(8,128)(2,1)S(1)} collective-permute-done((bf16[136,1280]{1,0:T(8,128)(2,1)S(1)}, bf16[136,1280]{1,0:T(8,128)(2,1)S(1)}, u32[]{:S(2)}, u32[]{:S(2)}) %collective-permute-start.32) | collective-permute-done | bytes 348192 | tf_op jit(solution)/shard_map/ppermute | solution.py:270
  162.5 2.0 %fusion.58 = bf16[128,1280]{1,0:T(8,128)(2,1)} fusion(f32[136,1280]{1,0:T(8,128)S(1)} %fusion.56, bf16[128,1280]{1,0:T(8,128)(2,1)S(1)} %collective-permute-done.8, bf16[128,1280]{1,0:T(8,128)(2,1)} %collective-permute-done.6, bf16[128,5120]{1,0:T(8,128)(2,1)S(1)} %copy-done.7, s32[]{:T(128)S(6)} %select_n.255, bf16[1280,16]{0,1:T(8,128)(2,1)S(1)} %copy-done, ...), kind=kOutput, calls=%fused_computation.104 | convolution fusion | flops 6561792 | bytes 2023940 | tf_op jit(solution)/shard_map/te,de->td/dot_general | solution.py:311
  (292 shorter events, 64.5 us)
Async XLA Ops:
  3.4 22.8 %collective-permute-start.9 = (bf16[136,1280]{1,0:T(8,128)(2,1)}, bf16[136,1280]{1,0:T(8,128)(2,1)}, u32[]{:S(2)}, u32[]{:S(2)}) collective-permute-start(bf16[136,1280]{1,0:T(8,128)(2,1)} %get-tuple-element.40), channel_id=1, source_target_pairs={{0,8},{8,16},{16,24},{24,28},{28,20},{20,12},{12,4},{4,0},{1,9},{9... | collective-permute-start | bytes 1044488 | tf_op jit(solution)/shard_map/ppermute | solution.py:195
  6.4 19.7 %collective-permute-start.10 = (bf16[136,1280]{1,0:T(8,128)(2,1)}, bf16[136,1280]{1,0:T(8,128)(2,1)}, u32[]{:S(2)}, u32[]{:S(2)}) collective-permute-start(bf16[136,1280]{1,0:T(8,128)(2,1)} %get-tuple-element.40), channel_id=1, source_target_pairs={{0,4},{8,0},{16,8},{24,16},{28,24},{20,28},{12,20},{4,12},{1,5},{9... | collective-permute-start | bytes 1044488 | tf_op jit(solution)/shard_map/ppermute | solution.py:196
  6.4 8.5 %collective-permute-start.3 = (bf16[128,1280]{1,0:T(8,128)(2,1)}, bf16[128,1280]{1,0:T(8,128)(2,1)}, u32[]{:S(2)}, u32[]{:S(2)}) collective-permute-start(bf16[128,1280]{1,0:T(8,128)(2,1)} %param.13), channel_id=1, source_target_pairs={{0,1},{1,0},{2,3},{3,2},{4,5},{5,4},{6,7},{7,6},{8,9},{9,8},{10,11... | collective-permute-start | bytes 983048 | tf_op jit(solution)/shard_map/ppermute | solution.py:169
  6.5 10.9 %collective-permute-start.4 = (bf16[128,1280]{1,0:T(8,128)(2,1)}, bf16[128,1280]{1,0:T(8,128)(2,1)}, u32[]{:S(2)}, u32[]{:S(2)}) collective-permute-start(bf16[128,1280]{1,0:T(8,128)(2,1)} %param.13), channel_id=1, source_target_pairs={{0,2},{1,3},{2,0},{3,1},{4,6},{5,7},{6,4},{7,5},{8,10},{9,11},{10,... | collective-permute-start | bytes 983048 | tf_op jit(solution)/shard_map/ppermute | solution.py:166
  8.4 15.7 %collective-permute-start.1 = (bf16[128,1280]{1,0:T(8,128)(2,1)}, bf16[128,1280]{1,0:T(8,128)(2,1)}, u32[]{:S(2)}, u32[]{:S(2)}) collective-permute-start(bf16[128,1280]{1,0:T(8,128)(2,1)} %param.14), channel_id=1, source_target_pairs={{0,2},{1,3},{2,0},{3,1},{4,6},{5,7},{6,4},{7,5},{8,10},{9,11},{10,... | collective-permute-start | bytes 983048 | tf_op jit(solution)/shard_map/ppermute | solution.py:166
  14.9 11.2 %collective-permute-start = (bf16[128,1280]{1,0:T(8,128)(2,1)S(1)}, bf16[128,1280]{1,0:T(8,128)(2,1)S(1)}, u32[]{:S(2)}, u32[]{:S(2)}) collective-permute-start(bf16[128,1280]{1,0:T(8,128)(2,1)S(1)} %copy-done.12), channel_id=1, source_target_pairs={{0,1},{1,0},{2,3},{3,2},{4,5},{5,4},{6,7},{7,6},{8,9},{9,8},{10,11... | collective-permute-start | bytes 983048 | tf_op jit(solution)/shard_map/ppermute | solution.py:169
  17.3 20.4 %collective-permute-start.5 = (bf16[128,1280]{1,0:T(8,128)(2,1)}, bf16[128,1280]{1,0:T(8,128)(2,1)S(1)}, u32[]{:S(2)}, u32[]{:S(2)}) collective-permute-start(bf16[128,1280]{1,0:T(8,128)(2,1)} %collective-permute-done.4), channel_id=1, source_target_pairs={{0,1},{1,0},{2,3},{3,2},{4,5},{5,4},{6,7},{7,6},{8,9},{9,8},{10,11... | collective-permute-start | bytes 983048 | tf_op jit(solution)/shard_map/ppermute | solution.py:169
  24.1 14.7 %collective-permute-start.2 = (bf16[128,1280]{1,0:T(8,128)(2,1)}, bf16[128,1280]{1,0:T(8,128)(2,1)S(1)}, u32[]{:S(2)}, u32[]{:S(2)}) collective-permute-start(bf16[128,1280]{1,0:T(8,128)(2,1)} %collective-permute-done.1), channel_id=1, source_target_pairs={{0,1},{1,0},{2,3},{3,2},{4,5},{5,4},{6,7},{7,6},{8,9},{9,8},{10,11... | collective-permute-start | bytes 983048 | tf_op jit(solution)/shard_map/ppermute | solution.py:169
  33.8 21.7 %collective-permute-start.14 = (bf16[136,1280]{1,0:T(8,128)(2,1)}, bf16[136,1280]{1,0:T(8,128)(2,1)}, u32[]{:S(2)}, u32[]{:S(2)}) collective-permute-start(bf16[136,1280]{1,0:T(8,128)(2,1)} %collective-permute-done.9), channel_id=1, source_target_pairs={{0,8},{8,16},{16,24},{24,28},{28,20},{20,12},{12,4},{4,0},{1,9},{9... | collective-permute-start | bytes 1044488 | tf_op jit(solution)/shard_map/ppermute | solution.py:195
  35.7 21.5 %collective-permute-start.16 = (bf16[136,1280]{1,0:T(8,128)(2,1)}, bf16[136,1280]{1,0:T(8,128)(2,1)}, u32[]{:S(2)}, u32[]{:S(2)}) collective-permute-start(bf16[136,1280]{1,0:T(8,128)(2,1)} %collective-permute-done.10), channel_id=1, source_target_pairs={{0,4},{8,0},{16,8},{24,16},{28,24},{20,28},{12,20},{4,12},{1,5},{9... | collective-permute-start | bytes 1044488 | tf_op jit(solution)/shard_map/ppermute | solution.py:196
  36.0 22.4 %collective-permute-start.12 = (bf16[192,768]{1,0:T(8,128)(2,1)S(1)}, bf16[192,768]{1,0:T(8,128)(2,1)}, u32[]{:S(2)}, u32[]{:S(2)}) collective-permute-start(bf16[192,768]{1,0:T(8,128)(2,1)S(1)} %fusion.67), channel_id=1, source_target_pairs={{0,2},{1,3},{2,0},{3,1},{4,6},{5,7},{6,4},{7,5},{8,10},{9,11},{10,... | collective-permute-start | bytes 884744 | tf_op jit(solution)/shard_map/ppermute | solution.py:166
  55.0 99.2 %collective-permute-start.7 = (bf16[128,1280]{1,0:T(8,128)(2,1)}, bf16[128,1280]{1,0:T(8,128)(2,1)}, u32[]{:S(2)}, u32[]{:S(2)}) collective-permute-start(bf16[128,1280]{1,0:T(8,128)(2,1)} %get-tuple-element.28), channel_id=1, source_target_pairs={{0,1},{1,0},{2,3},{3,2},{4,5},{5,4},{6,7},{7,6},{8,9},{9,8},{10,11... | collective-permute-start | bytes 983048 | tf_op jit(solution)/shard_map/ppermute | solution.py:169
  55.0 106.4 %collective-permute-start.6 = (bf16[128,1280]{1,0:T(8,128)(2,1)}, bf16[128,1280]{1,0:T(8,128)(2,1)}, u32[]{:S(2)}, u32[]{:S(2)}) collective-permute-start(bf16[128,1280]{1,0:T(8,128)(2,1)} %get-tuple-element.27), channel_id=1, source_target_pairs={{0,1},{1,0},{2,3},{3,2},{4,5},{5,4},{6,7},{7,6},{8,9},{9,8},{10,11... | collective-permute-start | bytes 983048 | tf_op jit(solution)/shard_map/ppermute | solution.py:169
  55.5 10.3 %collective-permute-start.15 = (bf16[136,1280]{1,0:T(8,128)(2,1)}, bf16[136,1280]{1,0:T(8,128)(2,1)S(1)}, u32[]{:S(2)}, u32[]{:S(2)}) collective-permute-start(bf16[136,1280]{1,0:T(8,128)(2,1)} %collective-permute-done.14), channel_id=1, source_target_pairs={{0,8},{8,16},{16,24},{24,28},{28,20},{20,12},{12,4},{4,0},{1,9},{9... | collective-permute-start | bytes 1044488 | tf_op jit(solution)/shard_map/ppermute | solution.py:195
  57.1 10.3 %collective-permute-start.17 = (bf16[136,1280]{1,0:T(8,128)(2,1)}, bf16[136,1280]{1,0:T(8,128)(2,1)S(1)}, u32[]{:S(2)}, u32[]{:S(2)}) collective-permute-start(bf16[136,1280]{1,0:T(8,128)(2,1)} %collective-permute-done.16), channel_id=1, source_target_pairs={{0,4},{8,0},{16,8},{24,16},{28,24},{20,28},{12,20},{4,12},{1,5},{9... | collective-permute-start | bytes 1044488 | tf_op jit(solution)/shard_map/ppermute | solution.py:196
  59.4 22.1 %collective-permute-start.13 = (bf16[192,768]{1,0:T(8,128)(2,1)S(1)}, bf16[192,768]{1,0:T(8,128)(2,1)}, u32[]{:S(2)}, u32[]{:S(2)}) collective-permute-start(bf16[192,768]{1,0:T(8,128)(2,1)S(1)} %add_convert_fusion.1), channel_id=1, source_target_pairs={{0,1},{1,0},{2,3},{3,2},{4,5},{5,4},{6,7},{7,6},{8,9},{9,8},{10,11... | collective-permute-start | bytes 884744 | tf_op jit(solution)/shard_map/ppermute | solution.py:169
  65.8 10.1 %collective-permute-start.21 = (bf16[68,1280]{1,0:T(8,128)(2,1)S(1)}, bf16[68,1280]{1,0:T(8,128)(2,1)S(1)}, u32[]{:S(2)}, u32[]{:S(2)}) collective-permute-start(bf16[68,1280]{1,0:T(8,128)(2,1)S(1)} %slice.261), channel_id=1, source_target_pairs={{0,8},{8,16},{16,24},{24,28},{28,20},{20,12},{12,4},{4,0},{1,9},{9... | collective-permute-start | bytes 522248 | tf_op jit(solution)/shard_map/ppermute | solution.py:198
  67.5 8.5 %collective-permute-start.22 = (bf16[68,1280]{1,0:T(8,128)(2,1)S(1)}, bf16[68,1280]{1,0:T(8,128)(2,1)S(1)}, u32[]{:S(2)}, u32[]{:S(2)}) collective-permute-start(bf16[68,1280]{1,0:T(8,128)(2,1)S(1)} %slice.262), channel_id=1, source_target_pairs={{0,4},{8,0},{16,8},{24,16},{28,24},{20,28},{12,20},{4,12},{1,5},{9... | collective-permute-start | bytes 522248 | tf_op jit(solution)/shard_map/ppermute | solution.py:199
  76.0 14.3 %collective-permute-start.28 = (bf16[128,768]{1,0:T(8,128)(2,1)}, bf16[128,768]{1,0:T(8,128)(2,1)}, u32[]{:S(2)}, u32[]{:S(2)}) collective-permute-start(bf16[128,768]{1,0:T(8,128)(2,1)} %dynamic-slice_bitcast_fusion.1), channel_id=1, source_target_pairs={{0,1},{1,0},{2,3},{3,2},{4,5},{5,4},{6,7},{7,6},{8,9},{9,8},{10,11... | collective-permute-start | bytes 589832 | tf_op jit(solution)/shard_map/ppermute | solution.py:169
  76.0 18.6 %collective-permute-start.18 = (bf16[128,768]{1,0:T(8,128)(2,1)}, bf16[128,768]{1,0:T(8,128)(2,1)}, u32[]{:S(2)}, u32[]{:S(2)}) collective-permute-start(bf16[128,768]{1,0:T(8,128)(2,1)} %dynamic-slice_bitcast_fusion.2), channel_id=1, source_target_pairs={{0,1},{1,0},{2,3},{3,2},{4,5},{5,4},{6,7},{7,6},{8,9},{9,8},{10,11... | collective-permute-start | bytes 589832 | tf_op jit(solution)/shard_map/ppermute | solution.py:169
  81.5 11.1 %collective-permute-start.23 = (bf16[64,768]{1,0:T(8,128)(2,1)}, bf16[64,768]{1,0:T(8,128)(2,1)}, u32[]{:S(2)}, u32[]{:S(2)}) collective-permute-start(bf16[64,768]{1,0:T(8,128)(2,1)} %dynamic-slice_bitcast_fusion.3), channel_id=1, source_target_pairs={{0,1},{1,0},{2,3},{3,2},{4,5},{5,4},{6,7},{7,6},{8,9},{9,8},{10,11... | collective-permute-start | bytes 294920 | tf_op jit(solution)/shard_map/ppermute | solution.py:169
  91.4 10.0 %collective-permute-start.29 = (bf16[128,768]{1,0:T(8,128)(2,1)S(1)}, bf16[128,768]{1,0:T(8,128)(2,1)S(1)}, u32[]{:S(2)}, u32[]{:S(2)}) collective-permute-start(bf16[128,768]{1,0:T(8,128)(2,1)S(1)} %fusion.82), channel_id=1, source_target_pairs={{0,2},{1,3},{2,0},{3,1},{4,6},{5,7},{6,4},{7,5},{8,10},{9,11},{10,... | collective-permute-start | bytes 589832 | tf_op jit(solution)/shard_map/ppermute | solution.py:166
  93.5 7.8 %collective-permute-start.24 = (bf16[64,768]{1,0:T(8,128)(2,1)S(1)}, bf16[64,768]{1,0:T(8,128)(2,1)S(1)}, u32[]{:S(2)}, u32[]{:S(2)}) collective-permute-start(bf16[64,768]{1,0:T(8,128)(2,1)S(1)} %fusion.98), channel_id=1, source_target_pairs={{0,2},{1,3},{2,0},{3,1},{4,6},{5,7},{6,4},{7,5},{8,10},{9,11},{10,... | collective-permute-start | bytes 294920 | tf_op jit(solution)/shard_map/ppermute | solution.py:166
  95.5 9.6 %collective-permute-start.19 = (bf16[128,768]{1,0:T(8,128)(2,1)S(1)}, bf16[128,768]{1,0:T(8,128)(2,1)S(1)}, u32[]{:S(2)}, u32[]{:S(2)}) collective-permute-start(bf16[128,768]{1,0:T(8,128)(2,1)S(1)} %fusion.83), channel_id=1, source_target_pairs={{0,2},{1,3},{2,0},{3,1},{4,6},{5,7},{6,4},{7,5},{8,10},{9,11},{10,... | collective-permute-start | bytes 589832 | tf_op jit(solution)/shard_map/ppermute | solution.py:166
  101.5 13.3 %collective-permute-start.30 = (bf16[128,768]{1,0:T(8,128)(2,1)S(1)}, bf16[128,768]{1,0:T(8,128)(2,1)S(1)}, u32[]{:S(2)}, u32[]{:S(2)}) collective-permute-start(bf16[128,768]{1,0:T(8,128)(2,1)S(1)} %add_convert_fusion.2), channel_id=1, source_target_pairs={{0,1},{1,0},{2,3},{3,2},{4,5},{5,4},{6,7},{7,6},{8,9},{9,8},{10,11... | collective-permute-start | bytes 589832 | tf_op jit(solution)/shard_map/ppermute | solution.py:169
  105.1 12.0 %collective-permute-start.20 = (bf16[128,768]{1,0:T(8,128)(2,1)S(1)}, bf16[128,768]{1,0:T(8,128)(2,1)S(1)}, u32[]{:S(2)}, u32[]{:S(2)}) collective-permute-start(bf16[128,768]{1,0:T(8,128)(2,1)S(1)} %add_convert_fusion.3), channel_id=1, source_target_pairs={{0,1},{1,0},{2,3},{3,2},{4,5},{5,4},{6,7},{7,6},{8,9},{9,8},{10,11... | collective-permute-start | bytes 589832 | tf_op jit(solution)/shard_map/ppermute | solution.py:169
  113.3 15.9 %collective-permute-start.33 = (bf16[68,1280]{1,0:T(8,128)(2,1)}, bf16[68,1280]{1,0:T(8,128)(2,1)}, u32[]{:S(2)}, u32[]{:S(2)}) collective-permute-start(bf16[68,1280]{1,0:T(8,128)(2,1)} %get-tuple-element.42), channel_id=1, source_target_pairs={{0,4},{8,0},{16,8},{24,16},{28,24},{20,28},{12,20},{4,12},{1,5},{9... | collective-permute-start | bytes 522248 | tf_op jit(solution)/shard_map/ppermute | solution.py:266
  114.8 17.1 %collective-permute-start.26 = (bf16[68,1280]{1,0:T(8,128)(2,1)}, bf16[68,1280]{1,0:T(8,128)(2,1)}, u32[]{:S(2)}, u32[]{:S(2)}) collective-permute-start(bf16[68,1280]{1,0:T(8,128)(2,1)} %get-tuple-element.41), channel_id=1, source_target_pairs={{0,8},{8,16},{16,24},{24,28},{28,20},{20,12},{12,4},{4,0},{1,9},{9... | collective-permute-start | bytes 522248 | tf_op jit(solution)/shard_map/ppermute | solution.py:265
  130.3 10.1 %collective-permute-start.34 = (bf16[136,1280]{1,0:T(8,128)(2,1)S(1)}, bf16[136,1280]{1,0:T(8,128)(2,1)S(1)}, u32[]{:S(2)}, u32[]{:S(2)}) collective-permute-start(bf16[136,1280]{1,0:T(8,128)(2,1)S(1)} %pad_maximum_fusion.17), channel_id=1, source_target_pairs={{0,4},{8,0},{16,8},{24,16},{28,24},{20,28},{12,20},{4,12},{1,5},{9... | collective-permute-start | bytes 1044488 | tf_op jit(solution)/shard_map/ppermute | solution.py:271
  132.9 9.7 %collective-permute-start.27 = (bf16[136,1280]{1,0:T(8,128)(2,1)S(1)}, bf16[136,1280]{1,0:T(8,128)(2,1)S(1)}, u32[]{:S(2)}, u32[]{:S(2)}) collective-permute-start(bf16[136,1280]{1,0:T(8,128)(2,1)S(1)} %pad_maximum_fusion.16), channel_id=1, source_target_pairs={{0,8},{8,16},{16,24},{24,28},{28,20},{20,12},{12,4},{4,0},{1,9},{9... | collective-permute-start | bytes 1044488 | tf_op jit(solution)/shard_map/ppermute | solution.py:270
  142.8 8.8 %collective-permute-start.31 = (bf16[136,1280]{1,0:T(8,128)(2,1)S(1)}, bf16[136,1280]{1,0:T(8,128)(2,1)S(1)}, u32[]{:S(2)}, u32[]{:S(2)}) collective-permute-start(bf16[136,1280]{1,0:T(8,128)(2,1)S(1)} %get-tuple-element.25), channel_id=1, source_target_pairs={{0,8},{8,16},{16,24},{24,28},{28,20},{20,12},{12,4},{4,0},{1,9},{9... | collective-permute-start | bytes 1044488 | tf_op jit(solution)/shard_map/ppermute | solution.py:270
  143.4 8.6 %collective-permute-start.35 = (bf16[136,1280]{1,0:T(8,128)(2,1)S(1)}, bf16[136,1280]{1,0:T(8,128)(2,1)S(1)}, u32[]{:S(2)}, u32[]{:S(2)}) collective-permute-start(bf16[136,1280]{1,0:T(8,128)(2,1)S(1)} %get-tuple-element.26), channel_id=1, source_target_pairs={{0,4},{8,0},{16,8},{24,16},{28,24},{20,28},{12,20},{4,12},{1,5},{9... | collective-permute-start | bytes 1044488 | tf_op jit(solution)/shard_map/ppermute | solution.py:271
  (58 other events, 387.3 us)

commit v2 on v0

--- a/solution.py
+++ b/solution.py
@@ -1,6 +1,10 @@
+import functools
+
 import jax
 import jax.numpy as jnp
 from jax import lax
+from jax.experimental import pallas as pl
+from jax.experimental.pallas import tpu as pltpu
 from jax.sharding import PartitionSpec as P
 
 
@@ -9,7 +13,7 @@
     return (preact * sigmoid_value, sigmoid_value * (1.0 + preact * (1.0 - sigmoid_value)))
 
 
-def per_device(
+def per_device_wide(
     tokens,
     out_grad,
     expert_ids,
@@ -125,7 +129,494 @@
     return (shared_part + routed_part + router_part).astype(jnp.bfloat16)
 
 
+F32, BF16 = jnp.float32, jnp.bfloat16
+LAST = (((1,), (1,)), ((), ()))
+FIRST = (((0,), (0,)), ((), ()))
+VMEM_BYTES = 48 * 1024 * 1024
+TOP_ROWS = 64
+
+
+def call(kernel, **settings):
+    return pl.pallas_call(
+        kernel,
+        compiler_params=pltpu.CompilerParams(vmem_limit_bytes=VMEM_BYTES),
+        cost_estimate=pl.CostEstimate(flops=1000, bytes_accessed=1000, transcendentals=0),
+        **settings,
+    )
+
+
+def whole(shape):
+    return pl.BlockSpec(shape, lambda *_: (0,) * len(shape))
+
+
+def payload_kernel(capacity, ids_ref, probs_ref, grad_ref, out_ref):
+    rows, expert_total = probs_ref.shape
+    cols = grad_ref.shape[1]
+    experts = lax.broadcasted_iota(jnp.int32, (rows, expert_total), 1)
+    ids = ids_ref[...]
+    member = jnp.zeros((rows, expert_total), F32)
+    for k in range(ids.shape[1]):
+        member = member + jnp.where(ids[:, k : k + 1] == experts, 1.0, 0.0)
+    member = member.astype(BF16)
+    row_at = lax.broadcasted_iota(jnp.int32, (rows, rows), 0)
+    col_at = lax.broadcasted_iota(jnp.int32, (rows, rows), 1)
+    lower = jnp.where(row_at < col_at, 1.0, 0.0).astype(BF16)
+    same = jnp.where(row_at == col_at, 1.0, 0.0).astype(BF16)
+    probs = probs_ref[...]
+    high = probs.astype(BF16)
+    low = (probs - high.astype(F32)).astype(BF16)
+
+    def turned(a, by):
+        return lax.dot_general(a, by, FIRST, preferred_element_type=F32)
+
+    before = turned(member, lower)
+    slot = jnp.where((turned(member, same) > 0.5) & (before < capacity), before, -1.0)
+    parts = [slot, turned(high, same), turned(low, same)]
+    pieces = [a[8 * i : 8 * i + 8] for a in parts for i in range(expert_total // 8)]
+    pieces.append(jnp.zeros((8, cols - len(pieces) * rows), F32))
+    out_ref[0:rows, :] = grad_ref[...]
+    out_ref[rows : rows + 8, :] = jnp.concatenate(pieces, axis=1).astype(BF16)
+
+
+def hidden_kernel(halves, tiles, capacity, info_ref, *refs):
+    block_refs = refs[: len(halves)]
+    weight_ref, other_ref, mine_ref, meta_ref, placed_ref = refs[len(halves) :]
+    step, part = pl.program_id(0), pl.program_id(1)
+    core, tile, row = info_ref[0], info_ref[1], info_ref[2]
+    blocks, at = [], 0
+    while at < len(halves):
+        if halves[at]:
+            blocks.append((block_refs[at], block_refs[at + 1]))
+            at += 2
+        else:
+            blocks.append((block_refs[at],))
+            at += 1
+    rows = 128
+
+    def meta_of(block):
+        last = block[-1]
+        return last[last.shape[0] - 8 :, :].astype(F32)
+
+    def pick(meta, kind, which):
+        value = meta[:, kind * tiles * rows : (kind * tiles + 1) * rows]
+        for i in range(1, tiles):
+            at_lane = (kind * tiles + i) * rows
+            value = jnp.where(tile == i, meta[:, at_lane : at_lane + rows], value)
+        line = lax.broadcasted_iota(jnp.int32, (8, rows), 0)
+        return jnp.sum(jnp.where(line == which, value, 0.0), axis=0, keepdims=True)
+
+    @pl.when(part == 0)
+    def _():
+        expert = jnp.where(step == 0, 1 - core, core)
+        for b, block in enumerate(blocks):
+            slot = pick(meta_of(block), 0, row + expert)
+            slot_at = lax.broadcasted_iota(jnp.int32, (capacity, rows), 0).astype(F32)
+            match = jnp.where(slot_at == slot, 1.0, 0.0).astype(BF16)
+            if len(block) == 1:
+                data = block[0][0:rows, :]
+            else:
+                data = jnp.concatenate([block[0][...], block[1][0 : rows - TOP_ROWS, :]], axis=0)
+            placed = jnp.dot(match, data, preferred_element_type=F32)
+            placed_ref[b * capacity : (b + 1) * capacity, :] = placed.astype(BF16)
+
+    @pl.when((part == 0) & (step == 0))
+    def _():
+        for b, block in enumerate(blocks):
+            meta = meta_of(block)
+            lines = [pick(meta, 0, row), pick(meta, 0, row + 1)]
+            lines += [pick(meta, 1, row) + pick(meta, 2, row)]
+            lines += [pick(meta, 1, row + 1) + pick(meta, 2, row + 1)]
+            lines += [jnp.zeros((4, rows), F32)]
+            meta_ref[8 * b : 8 * b + 8, :] = jnp.concatenate(lines, axis=0)
+
+    value = lax.dot_general(placed_ref[...], weight_ref[0], LAST, preferred_element_type=F32)
+    value = value.astype(BF16)
+    width = value.shape[1]
+    lanes = pl.ds(pl.multiple_of(part * width, width), width)
+
+    @pl.when(step == 0)
+    def _():
+        other_ref[:, lanes] = value
+
+    @pl.when(step == 1)
+    def _():
+        mine_ref[:, lanes] = value
+
+
+def hidden_part(info, blocks, down_weight, tiles, capacity):
+    local_count, hidden_units, cols = down_weight.shape
+    flat, halves = [], []
+    for block in blocks:
+        pair = isinstance(block, tuple)
+        flat += list(block) if pair else [block]
+        halves += [pair, pair] if pair else [False]
+    count = len(blocks)
+    width = hidden_units // 2
+    shape = (count * capacity, hidden_units)
+    spec = pltpu.PrefetchScalarGridSpec(
+        num_scalar_prefetch=1,
+        grid=(2, 2),
+        in_specs=[whole(a.shape) for a in flat]
+        + [
+            pl.BlockSpec(
+                (1, width, cols),
+                lambda s, p, info: (jnp.where(s == 0, 1 - info[0], info[0]), p, 0),
+            )
+        ],
+        out_specs=[whole(shape), whole(shape), whole((8 * count, 128))],
+        scratch_shapes=[pltpu.VMEM((count * capacity, cols), BF16)],
+    )
+    return call(
+        functools.partial(hidden_kernel, halves, tiles, capacity),
+        grid_spec=spec,
+        out_shape=[
+            jax.ShapeDtypeStruct(shape, BF16),
+            jax.ShapeDtypeStruct(shape, BF16),
+            jax.ShapeDtypeStruct((8 * count, 128), F32),
+        ],
+    )(info, *flat, down_weight)
+
+
+def grad_kernel(count, split, tiles, capacity, info_ref, *refs):
+    gate_refs, up_refs = refs[:count], refs[count : 2 * count]
+    full_ref, pair_ref, meta_ref, gate_w_ref, up_w_ref = refs[2 * count : 2 * count + 5]
+    out_refs = refs[2 * count + 5 : -4]
+    dgate_ref, dup_ref, combine_ref, score_ref = refs[-4:]
+    step = pl.program_id(0)
+    core, tile, row = info_ref[0], info_ref[1], info_ref[2]
+    rows = 128
+
+    @pl.when(step == 0)
+    def _():
+        line = lax.broadcasted_iota(jnp.int32, (8, rows), 0)
+        slot_at = lax.broadcasted_iota(jnp.int32, (capacity, rows), 0).astype(F32)
+        for b in range(count):
+            span = slice(b * capacity, (b + 1) * capacity)
+            lines = meta_ref[8 * b : 8 * b + 8, :]
+            score_rows = jnp.zeros((8, rows), F32)
+            stacked = []
+            for e in range(2):
+                hidden = jnp.where(core == e, full_ref[span, :], pair_ref[span, :]).astype(F32)
+                gate = gate_refs[b][e].astype(F32)
+                up = up_refs[b][e].astype(F32)
+                active, slope_term = silu_parts(gate)
+                dup = (hidden * active).astype(BF16)
+                dgate_ref[e, span, :] = (hidden * up * slope_term).astype(BF16)
+                dup_ref[e, span, :] = dup
+                score = jnp.sum(up * dup.astype(F32), axis=1, keepdims=True)
+                score = score.astype(BF16).astype(F32)
+                match = slot_at == lines[e : e + 1, :]
+                token_score = jnp.sum(jnp.where(match, score, 0.0), axis=0, keepdims=True)
+                score_rows = score_rows + jnp.where(line == row + e, token_score, 0.0)
+                weight = jnp.where(match, lines[2 + e : 3 + e, :], 0.0)
+                high = weight.astype(BF16)
+                stacked += [high, (weight - high.astype(F32)).astype(BF16)]
+            combine_ref[b] = jnp.concatenate(stacked, axis=0)
+            score_ref[b] = score_rows
+
+    grads = []
+    for e in range(2):
+        value = lax.dot_general(dgate_ref[e], gate_w_ref[e], LAST, preferred_element_type=F32)
+        value = value + lax.dot_general(dup_ref[e], up_w_ref[e], LAST, preferred_element_type=F32)
+        grads.append(value.astype(BF16))
+    width = grads[0].shape[1]
+    for b in range(count):
+        span = slice(b * capacity, (b + 1) * capacity)
+        pile = jnp.concatenate([g[span] for g in grads for _ in range(2)], axis=0)
+        value = lax.dot_general(combine_ref[b], pile, FIRST, preferred_element_type=F32)
+        lanes = [jnp.where((step == 0) & (tile == i), score_ref[b], 0.0) for i in range(tiles)]
+        if tiles * rows < width:
+            lanes.append(jnp.zeros((8, width - tiles * rows), F32))
+        lanes = jnp.concatenate(lanes, axis=1)
+        if split:
+            out_refs[2 * b][...] = value[:TOP_ROWS].astype(BF16)
+            out_refs[2 * b + 1][...] = jnp.concatenate([value[TOP_ROWS:], lanes], 0).astype(BF16)
+        else:
+            out_refs[b][...] = jnp.concatenate([value, lanes], axis=0).astype(BF16)
+
+
+def grad_part(info, full, pair, meta, saved, weights, count, split, tiles, capacity):
+    gate_saved, up_saved = saved
+    gate_weight, up_weight = weights
+    local_count, cols, hidden_units = gate_weight.shape
+    width = 256
+    heights = [TOP_ROWS, 136 - TOP_ROWS] * count if split else [136] * count
+
+    def saved_spec(b):
+        return pl.BlockSpec((2, capacity, hidden_units), lambda n, info: (0, info[3 + b], 0))
+
+    weight_spec = pl.BlockSpec((2, width, hidden_units), lambda n, info: (0, n, 0))
+    spec = pltpu.PrefetchScalarGridSpec(
+        num_scalar_prefetch=1,
+        grid=(cols // width,),
+        in_specs=[saved_spec(b) for b in range(count)] * 2
+        + [whole(full.shape), whole(pair.shape), whole(meta.shape)]
+        + [weight_spec, weight_spec],
+        out_specs=[pl.BlockSpec((h, width), lambda n, info: (0, n)) for h in heights],
+        scratch_shapes=[
+            pltpu.VMEM((2, count * capacity, hidden_units), BF16),
+            pltpu.VMEM((2, count * capacity, hidden_units), BF16),
+            pltpu.VMEM((count, 4 * capacity, 128), BF16),
+            pltpu.VMEM((count, 8, 128), F32),
+        ],
+    )
+    return call(
+        functools.partial(grad_kernel, count, split, tiles, capacity),
+        grid_spec=spec,
+        out_shape=[jax.ShapeDtypeStruct((h, cols), BF16) for h in heights],
+    )(
+        info,
+        *([gate_saved] * count),
+        *([up_saved] * count),
+        full,
+        pair,
+        meta,
+        gate_weight,
+        up_weight,
+    )
+
+
+def shared_kernel(info_ref, *refs):
+    token_refs, grad_refs = refs[0:4], refs[4:8]
+    gate_hbm, up_hbm, down_hbm = refs[8:11]
+    out_refs = refs[11:15]
+    gate_ref, up_ref, down_ref, sems = refs[15:]
+    here = info_ref[0]
+    rows, cols = token_refs[0].shape
+    units = gate_ref.shape[2]
+
+    def copies(q):
+        at = pl.multiple_of(jnp.bitwise_xor(here, q) * cols, cols)
+        return (
+            pltpu.make_async_copy(gate_hbm.at[pl.ds(at, cols), :], gate_ref.at[q], sems.at[q, 0]),
+            pltpu.make_async_copy(up_hbm.at[pl.ds(at, cols), :], up_ref.at[q], sems.at[q, 1]),
+            pltpu.make_async_copy(down_hbm.at[:, pl.ds(at, cols)], down_ref.at[q], sems.at[q, 2]),
+        )
+
+    for q in range(4):
+        for copy in copies(q):
+            copy.start()
+    gate_pre = jnp.zeros((rows, units), F32)
+    up_pre = jnp.zeros((rows, units), F32)
+    hidden_pre = jnp.zeros((rows, units), F32)
+    for q in range(4):
+        for copy in copies(q):
+            copy.wait()
+        token, grad = token_refs[q][...], grad_refs[q][...]
+        gate_pre = gate_pre + jnp.dot(token, gate_ref[q], preferred_element_type=F32)
+        up_pre = up_pre + jnp.dot(token, up_ref[q], preferred_element_type=F32)
+        hidden_pre = hidden_pre + lax.dot_general(
+            grad, down_ref[q], LAST, preferred_element_type=F32
+        )
+    active, slope_term = silu_parts(gate_pre)
+    dgate = (hidden_pre * up_pre * slope_term).astype(BF16)
+    dup = (hidden_pre * active).astype(BF16)
+    for q in range(4):
+        term = lax.dot_general(dgate, gate_ref[q], LAST, preferred_element_type=F32)
+        term = term + lax.dot_general(dup, up_ref[q], LAST, preferred_element_type=F32)
+        out_refs[q][...] = term.astype(BF16)
+
+
+def shared_part_terms(here, token_blocks, grad_blocks, shared_gate, shared_up, shared_down):
+    rows, cols = token_blocks[0].shape
+    units = shared_gate.shape[1]
+    spec = pltpu.PrefetchScalarGridSpec(
+        num_scalar_prefetch=1,
+        grid=(1,),
+        in_specs=[whole((rows, cols))] * 8 + [pl.BlockSpec(memory_space=pl.ANY)] * 3,
+        out_specs=[whole((rows, cols))] * 4,
+        scratch_shapes=[
+            pltpu.VMEM((4, cols, units), BF16),
+            pltpu.VMEM((4, cols, units), BF16),
+            pltpu.VMEM((4, units, cols), BF16),
+            pltpu.SemaphoreType.DMA((4, 3)),
+        ],
+    )
+    return call(
+        shared_kernel,
+        grid_spec=spec,
+        out_shape=[jax.ShapeDtypeStruct((rows, cols), BF16)] * 4,
+    )(here, *token_blocks, *grad_blocks, shared_gate, shared_up, shared_down)
+
+
+def ring_place(position):
+    position = position % 8
+    return jnp.where(position < 4, 2 * position, 15 - 2 * position)
+
+
+def per_device_ring(
+    tokens,
+    out_grad,
+    expert_ids,
+    router_probs,
+    router_weight,
+    gate_weight,
+    up_weight,
+    down_weight,
+    gate_saved,
+    up_saved,
+    shared_gate,
+    shared_up,
+    shared_down,
+):
+    slot_count = gate_saved.shape[1]
+    capacity = slot_count // 8
+    rows, cols = tokens.shape
+    expert_total = router_probs.shape[1]
+    tiles = expert_total // 8
+    order = [0, 2, 4, 6, 7, 5, 3, 1]
+    ahead = [(order[i], order[(i + 1) % 8]) for i in range(8)]
+    behind = [(order[i], order[(i - 1) % 8]) for i in range(8)]
+    x_pairs = [(i, i ^ 2) for i in range(4)]
+    core_pairs = [(i, i ^ 1) for i in range(4)]
+    me = lax.axis_index("expert")
+    place = jnp.where(me % 2 == 0, me // 2, 7 - me // 2)
+    here = lax.axis_index("tensor")
+    first = me * 2
+    base = [here % 2, first // 8, first % 8]
+    tie = lax.optimization_barrier
+
+    def swap_x(a):
+        return lax.ppermute(a, "tensor", x_pairs)
+
+    def swap_core(a):
+        return lax.ppermute(a, "tensor", core_pairs)
+
+    def ring(fore, back):
+        return lax.ppermute(fore, "expert", ahead), lax.ppermute(back, "expert", behind)
+
+    def info(chunk):
+        numbers = base + [ring_place(place + d) for d in chunk]
+        return jnp.stack([jnp.asarray(n, jnp.int32) for n in numbers])
+
+    def hidden(blocks):
+        return hidden_part(info(()), blocks, down_weight, tiles, capacity)
+
+    def grads(chunk, full, pair, meta):
+        split = chunk == (4,)
+        return grad_part(
+            info(chunk),
+            full,
+            pair,
+            meta,
+            (gate_saved, up_saved),
+            (gate_weight, up_weight),
+            len(chunk),
+            split,
+            tiles,
+            capacity,
+        )
+
+    def add(a, *others):
+        total = a.astype(F32)
+        for other in others:
+            total = total + other.astype(F32)
+        return total.astype(BF16)
+
+    tok_core, grad_core = swap_core(tokens), swap_core(out_grad)
+    tok_x, grad_x = swap_x(tokens), swap_x(out_grad)
+    payload = call(
+        functools.partial(payload_kernel, capacity),
+        out_shape=jax.ShapeDtypeStruct((rows + 8, cols), BF16),
+    )(expert_ids, router_probs, out_grad)
+
+    fore1, back1 = ring(payload, payload)
+    fore2, back2 = ring(fore1, back1)
+    other1, mine1, meta1 = hidden([payload, fore1, back1])
+    fore2, back2, other1, mine1 = tie((fore2, back2, other1, mine1))
+
+    fore3, back3 = ring(fore2, back2)
+    chip1 = add(mine1, swap_core(other1))
+    far1 = swap_x(chip1)
+    other2, mine2, meta2 = hidden([fore2, back2])
+    fore3, back3, chip1, other2, mine2 = tie((fore3, back3, chip1, other2, mine2))
+
+    top, bottom = ring(fore3[:TOP_ROWS], back3[TOP_ROWS:])
+    chip2 = add(mine2, swap_core(other2))
+    far2 = swap_x(chip2)
+    other3, mine3, meta3 = hidden([fore3, back3])
+    top, bottom, chip2, other3, mine3 = tie((top, bottom, chip2, other3, mine3))
+
+    other4, mine4, meta4 = hidden([(top, bottom)])
+    chip3 = add(mine3, swap_core(other3))
+    chip4 = add(mine4, swap_core(other4))
+    far4 = swap_x(chip4)
+    full1 = add(chip1, far1)
+    pair1 = swap_core(full1)
+    full2 = add(chip2, far2)
+    pair2 = swap_core(full2)
+    near0, near_b1, near_f1 = grads((0, -1, 1), full1, pair1, meta1)
+    far4, near0 = tie((far4, near0))
+    full4 = add(chip4, far4)
+    pair4 = swap_core(full4)
+    far3 = swap_x(chip3)
+    top, bottom = grads((4,), full4, pair4, meta4)
+
+    top, bottom, full2, pair2 = tie((top, bottom, full2, pair2))
+    fore, back = ring(top, bottom)
+    full3 = add(chip3, far3)
+    pair3 = swap_core(full3)
+    near_b3, near_f3 = grads((-3, 3), full3, pair3, meta3)
+    near_b2, near_f2 = grads((-2, 2), full2, pair2, meta2)
+    fore, back, near_f3, near_b3, near_f2, near_b2 = tie(
+        (fore, back, near_f3, near_b3, near_f2, near_b2)
+    )
+
+    fore = jnp.concatenate([add(near_f3[:TOP_ROWS], fore), near_f3[TOP_ROWS:]], axis=0)
+    back = jnp.concatenate([near_b3[:TOP_ROWS], add(near_b3[TOP_ROWS:], back)], axis=0)
+    tok_both, grad_both = swap_core(tok_x), swap_core(grad_x)
+    fore, back, tok_both, grad_both = tie((fore, back, tok_both, grad_both))
+    fore, back = ring(fore, back)
+    terms = shared_part_terms(
+        here.reshape(1).astype(jnp.int32),
+        [tokens, tok_core, tok_x, tok_both],
+        [out_grad, grad_core, grad_x, grad_both],
+        shared_gate,
+        shared_up,
+        shared_down,
+    )
+    fore, back, *terms = tie((fore, back, *terms))
+
+    fore, back = add(near_f2, fore), add(near_b2, back)
+    fore, back = ring(fore, back)
+    far = add(terms[2], swap_core(terms[3]))
+    near = swap_core(terms[1])
+    shared_far = swap_x(far)
+    fore, back, near = tie((fore, back, near))
+
+    fore, back = add(near_f1, fore), add(near_b1, back)
+    fore, back = ring(fore, back)
+    total = near0.astype(F32) + fore.astype(F32) + back.astype(F32)
+    shared_part = terms[0].astype(F32) + near.astype(F32) + shared_far.astype(F32)
+    prob_grad = jnp.concatenate(
+        [total[rows:, i * rows : (i + 1) * rows] for i in range(tiles)], axis=0
+    ).T
+    gate_total = jnp.sum(router_probs * prob_grad, axis=1, keepdims=True)
+    logit_grad = (router_probs * (prob_grad - gate_total)).astype(BF16)
+    router_part = jnp.einsum("te,de->td", logit_grad, router_weight, preferred_element_type=F32)
+    return (shared_part + total[:rows] + router_part).astype(BF16)
+
+
+def per_device(*args):
+    tokens, router_probs, gate_weight, gate_saved = args[0], args[3], args[5], args[8]
+    rows, cols = tokens.shape
+    expert_total = router_probs.shape[1]
+    ring = (
+        lax.axis_size("expert") == 8
+        and lax.axis_size("tensor") == 4
+        and gate_weight.shape[0] == 2
+        and gate_saved.shape[1] == 8 * 64
+        and gate_saved.shape[2] % 256 == 0
+        and rows == 128
+        and expert_total == 16
+        and cols % 256 == 0
+        and cols >= 6 * rows
+    )
+    return (per_device_ring if ring else per_device_wide)(*args)
+
+
 def solution(mesh):
+
     return jax.shard_map(
         per_device,
         mesh=mesh,

time: 246 us -> 148 us (0.60)
  blocking collectives: 66.6 us -> 0 us
  Pallas kernels: 0 us -> 56.9 us
  matrix products: 44.7 us -> 1.03 us
  waiting for transfers between devices: 73.3 us -> 41.2 us
  starting transfers between devices: 11.8 us -> 27 us
  local copies, waits for them, and re-layouts: 28.5 us -> 14.6 us
  between operations: 13.4 us -> 0.42 us
    all_to_all x1 -> x0, blocking collectives: 66.6 us -> none  [per_device(): lax.all_to_all(outgoing, 'expert', split_axis=1, concat_axis=1, tiled=True)]
    pallas_call x0 -> x10, Pallas kernels: none -> 56.9 us  [the longest x4 32.6 us: grad_part(): call(functools.partial(grad_kernel, count, split, tiles, capacity), grid_...]
    dot_general x10 -> x1, matrix products: 44.7 us -> 1.03 us  [per_device_ring(): jnp.einsum('te,de->td', logit_grad, router_weight, preferred_element_type...]
    ppermute x0 -> x37, waiting for transfers between devices: none -> 41.2 us  [the longest x8 20.6 us: ring(): lax.ppermute(fore, 'expert', ahead)]
    psum x1 -> x0, waiting for transfers between devices: 40.5 us -> none  [per_device(): lax.psum(partial_hidden.astype(jnp.bfloat16), 'tensor').astype(jnp.float32)]
    all_to_all x2 -> x0, waiting for transfers between devices: 28 us -> none  [the longest x1 28 us: per_device(): lax.all_to_all(expert_grad.reshape(local_count, groups, capacity * featur...]
    ppermute x0 -> x37, starting transfers between devices: none -> 27 us  [the longest x8 9.46 us: ring(): lax.ppermute(back, 'expert', behind)]
    reshape x7 -> x0, local copies, waits for them, and re-layouts: 18.4 us -> none  [the longest x2 6.72 us: per_device(): expert_grad.reshape(local_count, groups, capacity * feature_cols)]
  transfers between devices with their start and end apart: 6 -> 37, of which waited for: 3 -> 15; matrix products, arithmetic and copies ran while one was open for 21% -> 6% of each run, Pallas kernels for 0% -> 38%
where the time goes in v2:
time: 148 us
  Pallas kernels  56.9 us (38%)
  waiting for transfers between devices  41.2 us (28%)
  starting transfers between devices  27 us (18%)
  local copies, waits for them, and re-layouts  14.6 us (10%)
  other arithmetic  6.48 us (4%)
    pallas_call x4, Pallas kernels, grad_part(): call(functools.partial(grad_kernel, count, split, tiles, capacity), grid_...  32.6 us
    ppermute x8, waiting for transfers between devices, ring(): lax.ppermute(fore, 'expert', ahead)  20.6 us
    ppermute x8, waiting for transfers between devices, ring(): lax.ppermute(back, 'expert', behind)  14.3 us
    pallas_call x4, Pallas kernels, hidden_part(): call(functools.partial(hidden_kernel, halves, tiles, capacity), grid_spec...  12.6 us
    unnamed x50, local copies, waits for them, and re-layouts  12.3 us
    pallas_call x1, Pallas kernels, shared_part_terms(): call(shared_kernel, grid_spec=spec, out_shape=[jax.ShapeDtypeStruct((rows...  11.3 us
    ppermute x8, starting transfers between devices, ring(): lax.ppermute(back, 'expert', behind)  9.46 us
    ppermute x8, starting transfers between devices, ring(): lax.ppermute(fore, 'expert', ahead)  8.13 us
  transfers between devices with their start and end apart: 37, of which 15 were waited for; matrix products, arithmetic and copies ran while one was open for 6% of the time, Pallas kernels for 38%

profile of v2, /device:TPU:0, one launch (start us, length us, event | category | flops | bytes accessed | tf_op | source)
XLA Modules:
  0.0 147.6 jit_solution(10051752095743440880)
XLA Ops:
  2.9 3.0 %collective-permute-start.2 = (bf16[136,1280]{1,0:T(8,128)(2,1)S(1)}, bf16[136,1280]{1,0:T(8,128)(2,1)S(1)}, u32[]{:S(2)}, u32[]{:S(2)}) collective-permute-start(bf16[136,1280]{1,0:T(8,128)(2,1)S(1)} %shard_map.127.refs_0_), channel_id=1, source_target_pairs={{0,4},{8,0},{16,8},{24,16},{28,24},{20,28},{12,20},{4,12},{1,5},{9... | collective-permute-start | bytes 1044488 | tf_op jit(solution)/shard_map/ppermute | solution.py:486
  6.0 8.1 %collective-permute-done.2.refs_2_ = bf16[136,1280]{1,0:T(8,128)(2,1)S(1)} collective-permute-done((bf16[136,1280]{1,0:T(8,128)(2,1)S(1)}, bf16[136,1280]{1,0:T(8,128)(2,1)S(1)}, u32[]{:S(2)}, u32[]{:S(2)}) %collective-permute-start.2) | collective-permute-done | bytes 348192 | tf_op jit(solution)/shard_map/ppermute | solution.py:486
  14.1 1.7 %collective-permute-start.3 = (bf16[136,1280]{1,0:T(8,128)(2,1)S(1)}, bf16[136,1280]{1,0:T(8,128)(2,1)S(1)}, u32[]{:S(2)}, u32[]{:S(2)}) collective-permute-start(bf16[136,1280]{1,0:T(8,128)(2,1)S(1)} %collective-permute-done.2.refs_2_), channel_id=1, source_target_pairs={{0,4},{8,0},{16,8},{24,16},{28,24},{20,28},{12,20},{4,12},{1,5},{9... | collective-permute-start | bytes 1044488 | tf_op jit(solution)/shard_map/ppermute | solution.py:486
  16.2 2.1 %copy-done.3 = bf16[2,768,1280]{2,1,0:T(8,128)(2,1)S(1)} copy-done((bf16[2,768,1280]{2,1,0:T(8,128)(2,1)S(1)}, bf16[2,768,1280]{2,1,0:T(8,128)(2,1)}, u32[]{:S(2)}) %copy-start.3) | copy-done | bytes 3932184
  18.4 3.2 %shard_map.128 = (bf16[192,768]{1,0:T(8,128)(2,1)S(1)}, bf16[192,768]{1,0:T(8,128)(2,1)S(1)}, f32[24,128]{1,0:T(8,128)S(1)}) custom-call(s32[3]{0:T(128)S(1)} %pad_add_fusion.1.info_ref, bf16[136,1280]{1,0:T(8,128)(2,1)S(1)} %shard_map.127.refs_0_, bf16[136,1280]{1,0:T(8,128)(2,1)S(1)} %collective-permute-done.refs_1_, ...), custom_call_target="tpu_custom_call" | custom-call | flops 1000 | bytes 1000 | tf_op jit(solution)/shard_map/pallas_call | solution.py:269
  21.6 1.8 %collective-permute-done.3.refs_1_ = bf16[136,1280]{1,0:T(8,128)(2,1)S(1)} collective-permute-done((bf16[136,1280]{1,0:T(8,128)(2,1)S(1)}, bf16[136,1280]{1,0:T(8,128)(2,1)S(1)}, u32[]{:S(2)}, u32[]{:S(2)}) %collective-permute-start.3) | collective-permute-done | bytes 348192 | tf_op jit(solution)/shard_map/ppermute | solution.py:486
  25.2 1.4 collective-permute-start.5
  26.6 3.6 %shard_map.129 = (bf16[128,768]{1,0:T(8,128)(2,1)}, bf16[128,768]{1,0:T(8,128)(2,1)S(1)}, f32[16,128]{1,0:T(8,128)S(1)}) custom-call(s32[3]{0:T(128)S(1)} %pad_add_fusion.1.info_ref, bf16[136,1280]{1,0:T(8,128)(2,1)S(1)} %collective-permute-done.1.refs_0_, bf16[136,1280]{1,0:T(8,128)(2,1)S(1)} %collective-permute-done.3.refs_1_, ...), custom_call_target="tpu_custom_call" | custom-call | flops 1000 | bytes 1000 | tf_op jit(solution)/shard_map/pallas_call | solution.py:269
  31.0 4.1 %collective-permute-done.4.refs_0_ = bf16[136,1280]{1,0:T(8,128)(2,1)S(1)} collective-permute-done((bf16[136,1280]{1,0:T(8,128)(2,1)S(1)}, bf16[136,1280]{1,0:T(8,128)(2,1)S(1)}, u32[]{:S(2)}, u32[]{:S(2)}) %collective-permute-start.4) | collective-permute-done | bytes 348192 | tf_op jit(solution)/shard_map/ppermute | solution.py:486
  35.5 1.3 collective-permute-start.12
  37.5 1.3 collective-permute-start.22
  39.0 2.1 %copy-done.5 = bf16[2,768,1280]{2,1,0:T(8,128)(2,1)S(1)} copy-done((bf16[2,768,1280]{2,1,0:T(8,128)(2,1)S(1)}, bf16[2,768,1280]{2,1,0:T(8,128)(2,1)}, u32[]{:S(2)}) %copy-start.5) | copy-done | bytes 3932184
  41.1 2.9 %shard_map.130 = (bf16[128,768]{1,0:T(8,128)(2,1)S(1)}, bf16[128,768]{1,0:T(8,128)(2,1)S(1)}, f32[16,128]{1,0:T(8,128)S(1)}) custom-call(s32[3]{0:T(128)S(1)} %pad_add_fusion.1.info_ref, bf16[136,1280]{1,0:T(8,128)(2,1)S(1)} %collective-permute-done.4.refs_0_, bf16[136,1280]{1,0:T(8,128)(2,1)S(1)} %collective-permute-done.5.refs_1_, ...), custom_call_target="tpu_custom_call" | custom-call | flops 1000 | bytes 1000 | tf_op jit(solution)/shard_map/pallas_call | solution.py:269
  47.5 1.6 %collective-permute-start.7 = (bf16[64,1280]{1,0:T(8,128)(2,1)S(1)}, bf16[64,1280]{1,0:T(8,128)(2,1)S(1)}, u32[]{:S(2)}, u32[]{:S(2)}) collective-permute-start(bf16[64,1280]{1,0:T(8,128)(2,1)S(1)} %slice.27), channel_id=1, source_target_pairs={{0,8},{8,16},{16,24},{24,28},{28,20},{20,12},{12,4},{4,0},{1,9},{9... | collective-permute-start | bytes 491528 | tf_op jit(solution)/shard_map/ppermute | solution.py:486
  50.6 2.7 %collective-permute-done.7.refs_0_ = bf16[64,1280]{1,0:T(8,128)(2,1)S(1)} collective-permute-done((bf16[64,1280]{1,0:T(8,128)(2,1)S(1)}, bf16[64,1280]{1,0:T(8,128)(2,1)S(1)}, u32[]{:S(2)}, u32[]{:S(2)}) %collective-permute-start.7) | collective-permute-done | bytes 163872 | tf_op jit(solution)/shard_map/ppermute | solution.py:486
  55.1 2.8 %shard_map.131 = (bf16[64,768]{1,0:T(8,128)(2,1)S(1)}, bf16[64,768]{1,0:T(8,128)(2,1)S(1)}, f32[8,128]{1,0:T(8,128)S(1)}) custom-call(s32[3]{0:T(128)S(1)} %pad_add_fusion.1.info_ref, bf16[64,1280]{1,0:T(8,128)(2,1)S(1)} %collective-permute-done.7.refs_0_, bf16[72,1280]{1,0:T(8,128)(2,1)S(1)} %collective-permute-done.8.refs_1_, ...), custom_call_target="tpu_custom_call" | custom-call | flops 1000 | bytes 1000 | tf_op jit(solution)/shard_map/pallas_call | solution.py:269
  60.4 3.3 %collective-permute-done.15 = bf16[128,768]{1,0:T(8,128)(2,1)S(1)} collective-permute-done((bf16[128,768]{1,0:T(8,128)(2,1)S(1)}, bf16[128,768]{1,0:T(8,128)(2,1)S(1)}, u32[]{:S(2)}, u32[]{:S(2)}) %collective-permute-start.15) | collective-permute-done | bytes 196640 | tf_op jit(solution)/shard_map/ppermute | solution.py:480
  63.8 1.3 collective-permute-start.20
  65.3 8.5 %shard_map.132 = (bf16[136,1280]{1,0:T(8,128)(2,1)S(1)}, bf16[136,1280]{1,0:T(8,128)(2,1)S(1)}, bf16[136,1280]{1,0:T(8,128)(2,1)S(1)}) custom-call(s32[6]{0:T(128)S(1)} %stack.81.info_ref, bf16[2,512,768]{2,1,0:T(8,128)(2,1)S(1)} %copy-done.1, bf16[2,512,768]{2,1,0:T(8,128)(2,1)S(1)} %copy-done.1, bf16[2,512,768]{2,1,0:T(8,128)(2,1)S(1)} %copy-done.1, ...), custom_call_target="tpu_custom_call" | custom-call | flops 1000 | bytes 1000 | tf_op jit(solution)/shard_map/pallas_call | solution.py:363
  76.8 8.0 %shard_map.133 = (bf16[64,1280]{1,0:T(8,128)(2,1)}, bf16[72,1280]{1,0:T(8,128)(2,1)}) custom-call(s32[4]{0:T(128)S(1)} %pad_add_fusion.info_ref, bf16[2,512,768]{2,1,0:T(8,128)(2,1)S(1)} %copy-done.1, bf16[2,512,768]{2,1,0:T(8,128)(2,1)S(1)} %copy-done.2, bf16[64,768]{1,0:T(8,128)(2,1)S(1)} %add_convert_fusion.13.refs_2_, ...), custom_call_target="tpu_custom_call" | custom-call | flops 1000 | bytes 1000 | tf_op jit(solution)/shard_map/pallas_call | solution.py:363
  85.5 1.5 %collective-permute-start.18 = (bf16[72,1280]{1,0:T(8,128)(2,1)}, bf16[72,1280]{1,0:T(8,128)(2,1)}, u32[]{:S(2)}, u32[]{:S(2)}) collective-permute-start(bf16[72,1280]{1,0:T(8,128)(2,1)} %get-tuple-element.96), channel_id=1, source_target_pairs={{0,4},{8,0},{16,8},{24,16},{28,24},{20,28},{12,20},{4,12},{1,5},{9... | collective-permute-start | bytes 552968 | tf_op jit(solution)/shard_map/ppermute | solution.py:486
  90.1 8.0 %shard_map.135 = (bf16[136,1280]{1,0:T(8,128)(2,1)S(1)}, bf16[136,1280]{1,0:T(8,128)(2,1)S(1)}) custom-call(s32[5]{0:T(128)S(1)} %stack.87.info_ref, bf16[2,512,768]{2,1,0:T(8,128)(2,1)S(1)} %copy-done.1, bf16[2,512,768]{2,1,0:T(8,128)(2,1)S(1)} %copy-done.1, bf16[2,512,768]{2,1,0:T(8,128)(2,1)S(1)} %copy-done.2, bf16[2,512,768]{2,1,0:T(8,128)(2,1)S(1)} %copy-done.2, ...), custom_call_target="tpu_custom_call" | custom-call | flops 1000 | bytes 1000 | tf_op jit(solution)/shard_map/pallas_call | solution.py:363
  98.1 8.1 %shard_map.134 = (bf16[136,1280]{1,0:T(8,128)(2,1)S(1)}, bf16[136,1280]{1,0:T(8,128)(2,1)S(1)}) custom-call(s32[5]{0:T(128)S(1)} %stack.84.info_ref, bf16[2,512,768]{2,1,0:T(8,128)(2,1)S(1)} %copy-done.1, bf16[2,512,768]{2,1,0:T(8,128)(2,1)S(1)} %copy-done.1, bf16[2,512,768]{2,1,0:T(8,128)(2,1)S(1)} %copy-done.2, bf16[2,512,768]{2,1,0:T(8,128)(2,1)S(1)} %copy-done.2, ...), custom_call_target="tpu_custom_call" | custom-call | flops 1000 | bytes 1000 | tf_op jit(solution)/shard_map/pallas_call | solution.py:363
  108.3 1.6 %collective-permute-start.26 = (bf16[136,1280]{1,0:T(8,128)(2,1)S(1)}, bf16[136,1280]{1,0:T(8,128)(2,1)S(1)}, u32[]{:S(2)}, u32[]{:S(2)}) collective-permute-start(bf16[136,1280]{1,0:T(8,128)(2,1)S(1)} %get-tuple-element.111), channel_id=1, source_target_pairs={{0,8},{8,16},{16,24},{24,28},{28,20},{20,12},{12,4},{4,0},{1,9},{9... | collective-permute-start | bytes 1044488 | tf_op jit(solution)/shard_map/ppermute | solution.py:486
  110.9 1.8 %collective-permute-done.28.refs_1_ = bf16[128,1280]{1,0:T(8,128)(2,1)S(1)} collective-permute-done((bf16[128,1280]{1,0:T(8,128)(2,1)}, bf16[128,1280]{1,0:T(8,128)(2,1)S(1)}, u32[]{:S(2)}, u32[]{:S(2)}) %collective-permute-start.28) | collective-permute-done | bytes 327712 | tf_op jit(solution)/shard_map/ppermute | solution.py:483
  112.7 11.3 %shard_map.136 = (bf16[128,1280]{1,0:T(8,128)(2,1)S(1)}, bf16[128,1280]{1,0:T(8,128)(2,1)S(1)}, bf16[128,1280]{1,0:T(8,128)(2,1)S(1)}, bf16[128,1280]{1,0:T(8,128)(2,1)S(1)}) custom-call(s32[1]{0:T(128)} %bitcast.11.info_ref, bf16[128,1280]{1,0:T(8,128)(2,1)} %refs_0_.9, bf16[128,1280]{1,0:T(8,128)(2,1)S(1)} %collective-permute-done.28.refs_1_, ...), custom_call_target="tpu_custom_call" | custom-call | flops 1000 | bytes 1000 | tf_op jit(solution)/shard_map/pallas_call | solution.py:435
  124.1 1.6 %collective-permute-start.30 = (bf16[136,1280]{1,0:T(8,128)(2,1)S(1)}, bf16[136,1280]{1,0:T(8,128)(2,1)S(1)}, u32[]{:S(2)}, u32[]{:S(2)}) collective-permute-start(bf16[136,1280]{1,0:T(8,128)(2,1)S(1)} %add_convert_fusion.3), channel_id=1, source_target_pairs={{0,8},{8,16},{16,24},{24,28},{28,20},{20,12},{12,4},{4,0},{1,9},{9... | collective-permute-start | bytes 1044488 | tf_op jit(solution)/shard_map/ppermute | solution.py:486
  128.0 6.4 %collective-permute-done.30 = bf16[136,1280]{1,0:T(8,128)(2,1)S(1)} collective-permute-done((bf16[136,1280]{1,0:T(8,128)(2,1)S(1)}, bf16[136,1280]{1,0:T(8,128)(2,1)S(1)}, u32[]{:S(2)}, u32[]{:S(2)}) %collective-permute-start.30) | collective-permute-done | bytes 348192 | tf_op jit(solution)/shard_map/ppermute | solution.py:486
  134.4 1.4 collective-permute-done.31
  135.9 1.6 %collective-permute-start.35 = (bf16[136,1280]{1,0:T(8,128)(2,1)S(1)}, bf16[136,1280]{1,0:T(8,128)(2,1)S(1)}, u32[]{:S(2)}, u32[]{:S(2)}) collective-permute-start(bf16[136,1280]{1,0:T(8,128)(2,1)S(1)} %add_convert_fusion.1), channel_id=1, source_target_pairs={{0,8},{8,16},{16,24},{24,28},{28,20},{20,12},{12,4},{4,0},{1,9},{9... | collective-permute-start | bytes 1044488 | tf_op jit(solution)/shard_map/ppermute | solution.py:486
  138.7 6.2 %collective-permute-done.35 = bf16[136,1280]{1,0:T(8,128)(2,1)S(1)} collective-permute-done((bf16[136,1280]{1,0:T(8,128)(2,1)S(1)}, bf16[136,1280]{1,0:T(8,128)(2,1)S(1)}, u32[]{:S(2)}, u32[]{:S(2)}) %collective-permute-start.35) | collective-permute-done | bytes 348192 | tf_op jit(solution)/shard_map/ppermute | solution.py:486
  145.0 1.5 collective-permute-done.36
  (131 shorter events, 30.9 us)
Async XLA Ops:
  2.9 11.2 %collective-permute-start.2 = (bf16[136,1280]{1,0:T(8,128)(2,1)S(1)}, bf16[136,1280]{1,0:T(8,128)(2,1)S(1)}, u32[]{:S(2)}, u32[]{:S(2)}) collective-permute-start(bf16[136,1280]{1,0:T(8,128)(2,1)S(1)} %shard_map.127.refs_0_), channel_id=1, source_target_pairs={{0,4},{8,0},{16,8},{24,16},{28,24},{20,28},{12,20},{4,12},{1,5},{9... | collective-permute-start | bytes 1044488 | tf_op jit(solution)/shard_map/ppermute | solution.py:486
  5.9 9.9 %collective-permute-start = (bf16[136,1280]{1,0:T(8,128)(2,1)S(1)}, bf16[136,1280]{1,0:T(8,128)(2,1)S(1)}, u32[]{:S(2)}, u32[]{:S(2)}) collective-permute-start(bf16[136,1280]{1,0:T(8,128)(2,1)S(1)} %shard_map.127.refs_0_), channel_id=1, source_target_pairs={{0,8},{8,16},{16,24},{24,28},{28,20},{20,12},{12,4},{4,0},{1,9},{9... | collective-permute-start | bytes 1044488 | tf_op jit(solution)/shard_map/ppermute | solution.py:486
  14.1 9.3 %collective-permute-start.3 = (bf16[136,1280]{1,0:T(8,128)(2,1)S(1)}, bf16[136,1280]{1,0:T(8,128)(2,1)S(1)}, u32[]{:S(2)}, u32[]{:S(2)}) collective-permute-start(bf16[136,1280]{1,0:T(8,128)(2,1)S(1)} %collective-permute-done.2.refs_2_), channel_id=1, source_target_pairs={{0,4},{8,0},{16,8},{24,16},{28,24},{20,28},{12,20},{4,12},{1,5},{9... | collective-permute-start | bytes 1044488 | tf_op jit(solution)/shard_map/ppermute | solution.py:486
  15.8 8.7 %collective-permute-start.1 = (bf16[136,1280]{1,0:T(8,128)(2,1)S(1)}, bf16[136,1280]{1,0:T(8,128)(2,1)S(1)}, u32[]{:S(2)}, u32[]{:S(2)}) collective-permute-start(bf16[136,1280]{1,0:T(8,128)(2,1)S(1)} %collective-permute-done.refs_1_), channel_id=1, source_target_pairs={{0,8},{8,16},{16,24},{24,28},{28,20},{20,12},{12,4},{4,0},{1,9},{9... | collective-permute-start | bytes 1044488 | tf_op jit(solution)/shard_map/ppermute | solution.py:486
  24.6 5.7 %collective-permute-start.6 = (bf16[192,768]{1,0:T(8,128)(2,1)S(1)}, bf16[192,768]{1,0:T(8,128)(2,1)S(1)}, u32[]{:S(2)}, u32[]{:S(2)}) collective-permute-start(bf16[192,768]{1,0:T(8,128)(2,1)S(1)} %get-tuple-element.74), channel_id=1, source_target_pairs={{0,1},{1,0},{2,3},{3,2},{4,5},{5,4},{6,7},{7,6},{8,9},{9,8},{10,11... | collective-permute-start | bytes 884744 | tf_op jit(solution)/shard_map/ppermute | solution.py:483
  24.6 10.6 %collective-permute-start.4 = (bf16[136,1280]{1,0:T(8,128)(2,1)S(1)}, bf16[136,1280]{1,0:T(8,128)(2,1)S(1)}, u32[]{:S(2)}, u32[]{:S(2)}) collective-permute-start(bf16[136,1280]{1,0:T(8,128)(2,1)S(1)} %collective-permute-done.1.refs_0_), channel_id=1, source_target_pairs={{0,8},{8,16},{16,24},{24,28},{28,20},{20,12},{12,4},{4,0},{1,9},{9... | collective-permute-start | bytes 1044488 | tf_op jit(solution)/shard_map/ppermute | solution.py:486
  25.2 10.3 %collective-permute-start.5 = (bf16[136,1280]{1,0:T(8,128)(2,1)S(1)}, bf16[136,1280]{1,0:T(8,128)(2,1)S(1)}, u32[]{:S(2)}, u32[]{:S(2)}) collective-permute-start(bf16[136,1280]{1,0:T(8,128)(2,1)S(1)} %collective-permute-done.3.refs_1_), channel_id=1, source_target_pairs={{0,4},{8,0},{16,8},{24,16},{28,24},{20,28},{12,20},{4,12},{1,5},{9... | collective-permute-start | bytes 1044488 | tf_op jit(solution)/shard_map/ppermute | solution.py:486
  35.5 13.6 %collective-permute-start.9 = (bf16[128,768]{1,0:T(8,128)(2,1)}, bf16[128,768]{1,0:T(8,128)(2,1)}, u32[]{:S(2)}, u32[]{:S(2)}) collective-permute-start(bf16[128,768]{1,0:T(8,128)(2,1)} %get-tuple-element.80), channel_id=1, source_target_pairs={{0,1},{1,0},{2,3},{3,2},{4,5},{5,4},{6,7},{7,6},{8,9},{9,8},{10,11... | collective-permute-start | bytes 589832 | tf_op jit(solution)/shard_map/ppermute | solution.py:483
  35.5 22.5 %collective-permute-start.12 = (bf16[192,768]{1,0:T(8,128)(2,1)}, bf16[192,768]{1,0:T(8,128)(2,1)}, u32[]{:S(2)}, u32[]{:S(2)}) collective-permute-start(bf16[192,768]{1,0:T(8,128)(2,1)} %add_convert_fusion.6), channel_id=1, source_target_pairs={{0,2},{1,3},{2,0},{3,1},{4,6},{5,7},{6,4},{7,5},{8,10},{9,11},{10,... | collective-permute-start | bytes 884744 | tf_op jit(solution)/shard_map/ppermute | solution.py:480
  36.9 50.9 %collective-permute-start.24 = (bf16[128,1280]{1,0:T(8,128)(2,1)S(1)}, bf16[128,1280]{1,0:T(8,128)(2,1)}, u32[]{:S(2)}, u32[]{:S(2)}) collective-permute-start(bf16[128,1280]{1,0:T(8,128)(2,1)S(1)} %copy-done.8), channel_id=1, source_target_pairs={{0,2},{1,3},{2,0},{3,1},{4,6},{5,7},{6,4},{7,5},{8,10},{9,11},{10,... | collective-permute-start | bytes 983048 | tf_op jit(solution)/shard_map/ppermute | solution.py:480
  37.5 50.2 %collective-permute-start.22 = (bf16[128,1280]{1,0:T(8,128)(2,1)}, bf16[128,1280]{1,0:T(8,128)(2,1)}, u32[]{:S(2)}, u32[]{:S(2)}) collective-permute-start(bf16[128,1280]{1,0:T(8,128)(2,1)} %refs_0_.9), channel_id=1, source_target_pairs={{0,2},{1,3},{2,0},{3,1},{4,6},{5,7},{6,4},{7,5},{8,10},{9,11},{10,... | collective-permute-start | bytes 983048 | tf_op jit(solution)/shard_map/ppermute | solution.py:480
  47.5 5.8 %collective-permute-start.7 = (bf16[64,1280]{1,0:T(8,128)(2,1)S(1)}, bf16[64,1280]{1,0:T(8,128)(2,1)S(1)}, u32[]{:S(2)}, u32[]{:S(2)}) collective-permute-start(bf16[64,1280]{1,0:T(8,128)(2,1)S(1)} %slice.27), channel_id=1, source_target_pairs={{0,8},{8,16},{16,24},{24,28},{28,20},{20,12},{12,4},{4,0},{1,9},{9... | collective-permute-start | bytes 491528 | tf_op jit(solution)/shard_map/ppermute | solution.py:486
  49.1 5.9 %collective-permute-start.8 = (bf16[72,1280]{1,0:T(8,128)(2,1)S(1)}, bf16[72,1280]{1,0:T(8,128)(2,1)S(1)}, u32[]{:S(2)}, u32[]{:S(2)}) collective-permute-start(bf16[72,1280]{1,0:T(8,128)(2,1)S(1)} %slice.28), channel_id=1, source_target_pairs={{0,4},{8,0},{16,8},{24,16},{28,24},{20,28},{12,20},{4,12},{1,5},{9... | collective-permute-start | bytes 552968 | tf_op jit(solution)/shard_map/ppermute | solution.py:486
  53.3 10.5 %collective-permute-start.15 = (bf16[128,768]{1,0:T(8,128)(2,1)S(1)}, bf16[128,768]{1,0:T(8,128)(2,1)S(1)}, u32[]{:S(2)}, u32[]{:S(2)}) collective-permute-start(bf16[128,768]{1,0:T(8,128)(2,1)S(1)} %add_convert_fusion.10), channel_id=1, source_target_pairs={{0,2},{1,3},{2,0},{3,1},{4,6},{5,7},{6,4},{7,5},{8,10},{9,11},{10,... | collective-permute-start | bytes 589832 | tf_op jit(solution)/shard_map/ppermute | solution.py:480
  59.6 5.6 %collective-permute-start.13 = (bf16[192,768]{1,0:T(8,128)(2,1)S(1)}, bf16[192,768]{1,0:T(8,128)(2,1)S(1)}, u32[]{:S(2)}, u32[]{:S(2)}) collective-permute-start(bf16[192,768]{1,0:T(8,128)(2,1)S(1)} %add_convert_fusion.5.refs_6_), channel_id=1, source_target_pairs={{0,1},{1,0},{2,3},{3,2},{4,5},{5,4},{6,7},{7,6},{8,9},{9,8},{10,11... | collective-permute-start | bytes 884744 | tf_op jit(solution)/shard_map/ppermute | solution.py:483
  59.8 15.5 %collective-permute-start.11 = (bf16[64,768]{1,0:T(8,128)(2,1)S(1)}, bf16[64,768]{1,0:T(8,128)(2,1)S(1)}, u32[]{:S(2)}, u32[]{:S(2)}) collective-permute-start(bf16[64,768]{1,0:T(8,128)(2,1)S(1)} %add_convert_fusion.14), channel_id=1, source_target_pairs={{0,2},{1,3},{2,0},{3,1},{4,6},{5,7},{6,4},{7,5},{8,10},{9,11},{10,... | collective-permute-start | bytes 294920 | tf_op jit(solution)/shard_map/ppermute | solution.py:480
  63.8 12.1 %collective-permute-start.20 = (bf16[128,768]{1,0:T(8,128)(2,1)S(1)}, bf16[128,768]{1,0:T(8,128)(2,1)S(1)}, u32[]{:S(2)}, u32[]{:S(2)}) collective-permute-start(bf16[128,768]{1,0:T(8,128)(2,1)S(1)} %add_convert_fusion.8), channel_id=1, source_target_pairs={{0,2},{1,3},{2,0},{3,1},{4,6},{5,7},{6,4},{7,5},{8,10},{9,11},{10,... | collective-permute-start | bytes 589832 | tf_op jit(solution)/shard_map/ppermute | solution.py:480
  65.2 19.7 %collective-permute-start.16 = (bf16[128,768]{1,0:T(8,128)(2,1)S(1)}, bf16[128,768]{1,0:T(8,128)(2,1)S(1)}, u32[]{:S(2)}, u32[]{:S(2)}) collective-permute-start(bf16[128,768]{1,0:T(8,128)(2,1)S(1)} %add_convert_fusion.9.refs_4_), channel_id=1, source_target_pairs={{0,1},{1,0},{2,3},{3,2},{4,5},{5,4},{6,7},{7,6},{8,9},{9,8},{10,11... | collective-permute-start | bytes 589832 | tf_op jit(solution)/shard_map/ppermute | solution.py:483
  76.6 21.5 %collective-permute-start.21 = (bf16[128,768]{1,0:T(8,128)(2,1)}, bf16[128,768]{1,0:T(8,128)(2,1)}, u32[]{:S(2)}, u32[]{:S(2)}) collective-permute-start(bf16[128,768]{1,0:T(8,128)(2,1)} %add_convert_fusion.7.refs_4_), channel_id=1, source_target_pairs={{0,1},{1,0},{2,3},{3,2},{4,5},{5,4},{6,7},{7,6},{8,9},{9,8},{10,11... | collective-permute-start | bytes 589832 | tf_op jit(solution)/shard_map/ppermute | solution.py:483
  85.5 20.7 %collective-permute-start.18 = (bf16[72,1280]{1,0:T(8,128)(2,1)}, bf16[72,1280]{1,0:T(8,128)(2,1)}, u32[]{:S(2)}, u32[]{:S(2)}) collective-permute-start(bf16[72,1280]{1,0:T(8,128)(2,1)} %get-tuple-element.96), channel_id=1, source_target_pairs={{0,4},{8,0},{16,8},{24,16},{28,24},{20,28},{12,20},{4,12},{1,5},{9... | collective-permute-start | bytes 552968 | tf_op jit(solution)/shard_map/ppermute | solution.py:486
  87.1 19.2 %collective-permute-start.17 = (bf16[64,1280]{1,0:T(8,128)(2,1)}, bf16[64,1280]{1,0:T(8,128)(2,1)}, u32[]{:S(2)}, u32[]{:S(2)}) collective-permute-start(bf16[64,1280]{1,0:T(8,128)(2,1)} %get-tuple-element.95), channel_id=1, source_target_pairs={{0,8},{8,16},{16,24},{24,28},{28,20},{20,12},{12,4},{4,0},{1,9},{9... | collective-permute-start | bytes 491528 | tf_op jit(solution)/shard_map/ppermute | solution.py:486
  87.7 20.6 %collective-permute-start.23 = (bf16[128,1280]{1,0:T(8,128)(2,1)}, bf16[128,1280]{1,0:T(8,128)(2,1)S(1)}, u32[]{:S(2)}, u32[]{:S(2)}) collective-permute-start(bf16[128,1280]{1,0:T(8,128)(2,1)} %collective-permute-done.22.refs_2_), channel_id=1, source_target_pairs={{0,1},{1,0},{2,3},{3,2},{4,5},{5,4},{6,7},{7,6},{8,9},{9,8},{10,11... | collective-permute-start | bytes 983048 | tf_op jit(solution)/shard_map/ppermute | solution.py:483
  87.8 20.5 %collective-permute-start.25 = (bf16[128,1280]{1,0:T(8,128)(2,1)}, bf16[128,1280]{1,0:T(8,128)(2,1)S(1)}, u32[]{:S(2)}, u32[]{:S(2)}) collective-permute-start(bf16[128,1280]{1,0:T(8,128)(2,1)} %collective-permute-done.24.refs_6_), channel_id=1, source_target_pairs={{0,1},{1,0},{2,3},{3,2},{4,5},{5,4},{6,7},{7,6},{8,9},{9,8},{10,11... | collective-permute-start | bytes 983048 | tf_op jit(solution)/shard_map/ppermute | solution.py:483
  108.3 15.7 %collective-permute-start.26 = (bf16[136,1280]{1,0:T(8,128)(2,1)S(1)}, bf16[136,1280]{1,0:T(8,128)(2,1)S(1)}, u32[]{:S(2)}, u32[]{:S(2)}) collective-permute-start(bf16[136,1280]{1,0:T(8,128)(2,1)S(1)} %get-tuple-element.111), channel_id=1, source_target_pairs={{0,8},{8,16},{16,24},{24,28},{28,20},{20,12},{12,4},{4,0},{1,9},{9... | collective-permute-start | bytes 1044488 | tf_op jit(solution)/shard_map/ppermute | solution.py:486
  109.9 14.1 %collective-permute-start.27 = (bf16[136,1280]{1,0:T(8,128)(2,1)S(1)}, bf16[136,1280]{1,0:T(8,128)(2,1)S(1)}, u32[]{:S(2)}, u32[]{:S(2)}) collective-permute-start(bf16[136,1280]{1,0:T(8,128)(2,1)S(1)} %get-tuple-element.112), channel_id=1, source_target_pairs={{0,4},{8,0},{16,8},{24,16},{28,24},{20,28},{12,20},{4,12},{1,5},{9... | collective-permute-start | bytes 1044488 | tf_op jit(solution)/shard_map/ppermute | solution.py:486
  110.4 2.3 %collective-permute-start.28 = (bf16[128,1280]{1,0:T(8,128)(2,1)}, bf16[128,1280]{1,0:T(8,128)(2,1)S(1)}, u32[]{:S(2)}, u32[]{:S(2)}) collective-permute-start(bf16[128,1280]{1,0:T(8,128)(2,1)} %refs_0_.9), channel_id=1, source_target_pairs={{0,1},{1,0},{2,3},{3,2},{4,5},{5,4},{6,7},{7,6},{8,9},{9,8},{10,11... | collective-permute-start | bytes 983048 | tf_op jit(solution)/shard_map/ppermute | solution.py:483
  124.1 10.2 %collective-permute-start.30 = (bf16[136,1280]{1,0:T(8,128)(2,1)S(1)}, bf16[136,1280]{1,0:T(8,128)(2,1)S(1)}, u32[]{:S(2)}, u32[]{:S(2)}) collective-permute-start(bf16[136,1280]{1,0:T(8,128)(2,1)S(1)} %add_convert_fusion.3), channel_id=1, source_target_pairs={{0,8},{8,16},{16,24},{24,28},{28,20},{20,12},{12,4},{4,0},{1,9},{9... | collective-permute-start | bytes 1044488 | tf_op jit(solution)/shard_map/ppermute | solution.py:486
  125.9 9.9 %collective-permute-start.31 = (bf16[136,1280]{1,0:T(8,128)(2,1)S(1)}, bf16[136,1280]{1,0:T(8,128)(2,1)S(1)}, u32[]{:S(2)}, u32[]{:S(2)}) collective-permute-start(bf16[136,1280]{1,0:T(8,128)(2,1)S(1)} %add_convert_fusion.2), channel_id=1, source_target_pairs={{0,4},{8,0},{16,8},{24,16},{28,24},{20,28},{12,20},{4,12},{1,5},{9... | collective-permute-start | bytes 1044488 | tf_op jit(solution)/shard_map/ppermute | solution.py:486
  126.4 11.7 %collective-permute-start.33 = (bf16[128,1280]{1,0:T(8,128)(2,1)S(1)}, bf16[128,1280]{1,0:T(8,128)(2,1)S(1)}, u32[]{:S(2)}, u32[]{:S(2)}) collective-permute-start(bf16[128,1280]{1,0:T(8,128)(2,1)S(1)} %get-tuple-element.127), channel_id=1, source_target_pairs={{0,1},{1,0},{2,3},{3,2},{4,5},{5,4},{6,7},{7,6},{8,9},{9,8},{10,11... | collective-permute-start | bytes 983048 | tf_op jit(solution)/shard_map/ppermute | solution.py:483
  135.9 9.1 %collective-permute-start.35 = (bf16[136,1280]{1,0:T(8,128)(2,1)S(1)}, bf16[136,1280]{1,0:T(8,128)(2,1)S(1)}, u32[]{:S(2)}, u32[]{:S(2)}) collective-permute-start(bf16[136,1280]{1,0:T(8,128)(2,1)S(1)} %add_convert_fusion.1), channel_id=1, source_target_pairs={{0,8},{8,16},{16,24},{24,28},{28,20},{20,12},{12,4},{4,0},{1,9},{9... | collective-permute-start | bytes 1044488 | tf_op jit(solution)/shard_map/ppermute | solution.py:486
  137.6 8.8 %collective-permute-start.36 = (bf16[136,1280]{1,0:T(8,128)(2,1)S(1)}, bf16[136,1280]{1,0:T(8,128)(2,1)S(1)}, u32[]{:S(2)}, u32[]{:S(2)}) collective-permute-start(bf16[136,1280]{1,0:T(8,128)(2,1)S(1)} %add_convert_fusion), channel_id=1, source_target_pairs={{0,4},{8,0},{16,8},{24,16},{28,24},{20,28},{12,20},{4,12},{1,5},{9... | collective-permute-start | bytes 1044488 | tf_op jit(solution)/shard_map/ppermute | solution.py:486
  138.2 8.4 %collective-permute-start.34 = (bf16[128,1280]{1,0:T(8,128)(2,1)S(1)}, bf16[128,1280]{1,0:T(8,128)(2,1)S(1)}, u32[]{:S(2)}, u32[]{:S(2)}) collective-permute-start(bf16[128,1280]{1,0:T(8,128)(2,1)S(1)} %add_convert_fusion.4), channel_id=1, source_target_pairs={{0,2},{1,3},{2,0},{3,1},{4,6},{5,7},{6,4},{7,5},{8,10},{9,11},{10,... | collective-permute-start | bytes 983048 | tf_op jit(solution)/shard_map/ppermute | solution.py:480
  (29 other events, 368.2 us)

commit v3 on v0

--- a/solution.py
+++ b/solution.py
@@ -1,6 +1,10 @@
+import functools
+
 import jax
 import jax.numpy as jnp
 from jax import lax
+from jax.experimental import pallas as pl
+from jax.experimental.pallas import tpu as pltpu
 from jax.sharding import PartitionSpec as P
 
 
@@ -9,7 +13,7 @@
     return (preact * sigmoid_value, sigmoid_value * (1.0 + preact * (1.0 - sigmoid_value)))
 
 
-def per_device(
+def per_device_wide(
     tokens,
     out_grad,
     expert_ids,
@@ -125,7 +129,503 @@
     return (shared_part + routed_part + router_part).astype(jnp.bfloat16)
 
 
+F32, BF16 = jnp.float32, jnp.bfloat16
+LAST = (((1,), (1,)), ((), ()))
+FIRST = (((0,), (0,)), ((), ()))
+TOP_ROWS = 64
+INFO_BLOCKS = 7
+
+
+def call(kernel, megabytes, out_shape, scratch_shapes=(), scalars=0, far=0):
+    def run(*operands):
+        near = len(operands) - scalars - far
+        memory = [pltpu.SMEM] * scalars + [pltpu.VMEM] * near + [pl.ANY] * far
+        return pl.pallas_call(
+            kernel,
+            in_specs=[pl.BlockSpec(memory_space=m) for m in memory],
+            out_specs=jax.tree.map(lambda _: pl.BlockSpec(memory_space=pltpu.VMEM), out_shape),
+            out_shape=out_shape,
+            scratch_shapes=scratch_shapes,
+            compiler_params=pltpu.CompilerParams(vmem_limit_bytes=megabytes * 1024 * 1024),
+            cost_estimate=pl.CostEstimate(flops=1000, bytes_accessed=1000, transcendentals=0),
+        )(*operands)
+
+    return run
+
+
+def sum_kernel(groups, *refs):
+    count = sum(groups)
+    at = 0
+    for out_ref, size in zip(refs[count:], groups):
+        total = refs[at][...].astype(F32)
+        for ref in refs[at + 1 : at + size]:
+            total = total + ref[...].astype(F32)
+        out_ref[...] = total.astype(BF16)
+        at += size
+
+
+def sums(*groups):
+    return call(
+        functools.partial(sum_kernel, [len(g) for g in groups]),
+        2,
+        [jax.ShapeDtypeStruct(g[0].shape, BF16) for g in groups],
+    )(*[a for g in groups for a in g])
+
+
+def halves_kernel(fore_ref, back_ref, top_ref, bottom_ref):
+    top_ref[...] = fore_ref[0:TOP_ROWS, :]
+    bottom_ref[...] = back_ref[TOP_ROWS:, :]
+
+
+def halves_of(fore, back):
+    rows, cols = fore.shape
+    return call(
+        halves_kernel,
+        2,
+        [
+            jax.ShapeDtypeStruct((TOP_ROWS, cols), BF16),
+            jax.ShapeDtypeStruct((rows - TOP_ROWS, cols), BF16),
+        ],
+    )(fore, back)
+
+
+def join_kernel(near_f_ref, top_ref, near_b_ref, bottom_ref, fore_ref, back_ref):
+    top = near_f_ref[0:TOP_ROWS, :].astype(F32) + top_ref[...].astype(F32)
+    fore_ref[0:TOP_ROWS, :] = top.astype(BF16)
+    fore_ref[TOP_ROWS:, :] = near_f_ref[TOP_ROWS:, :]
+    back_ref[0:TOP_ROWS, :] = near_b_ref[0:TOP_ROWS, :]
+    bottom = near_b_ref[TOP_ROWS:, :].astype(F32) + bottom_ref[...].astype(F32)
+    back_ref[TOP_ROWS:, :] = bottom.astype(BF16)
+
+
+def join(near_f, top, near_b, bottom):
+    shape = jax.ShapeDtypeStruct(near_f.shape, BF16)
+    return call(join_kernel, 2, [shape, shape])(near_f, top, near_b, bottom)
+
+
+def payload_kernel(capacity, ids_hbm, probs_hbm, grad_hbm, out_ref, ids_ref, probs_ref, sems):
+    expert_total, rows = probs_ref.shape
+    cols = grad_hbm.shape[1]
+    copies = [
+        pltpu.make_async_copy(ids_hbm, ids_ref, sems.at[0]),
+        pltpu.make_async_copy(probs_hbm, probs_ref, sems.at[1]),
+        pltpu.make_async_copy(grad_hbm, out_ref.at[0:rows, :], sems.at[2]),
+    ]
+    for copy in copies:
+        copy.start()
+    experts = lax.broadcasted_iota(jnp.int32, (expert_total, rows), 0)
+    row_at = lax.broadcasted_iota(jnp.int32, (rows, rows), 0)
+    col_at = lax.broadcasted_iota(jnp.int32, (rows, rows), 1)
+    lower = jnp.where(row_at < col_at, 1.0, 0.0).astype(BF16)
+    copies[0].wait()
+    ids = ids_ref[...]
+    member = jnp.zeros((expert_total, rows), F32)
+    for k in range(ids.shape[0]):
+        member = member + jnp.where(ids[k : k + 1, :] == experts, 1.0, 0.0)
+    before = jnp.dot(member.astype(BF16), lower, preferred_element_type=F32)
+    slot = jnp.where((member > 0.5) & (before < capacity), before, -1.0)
+    copies[1].wait()
+    probs = probs_ref[...]
+    high = probs.astype(BF16).astype(F32)
+    parts = [slot, high, probs - high]
+    pieces = [a[8 * i : 8 * i + 8] for a in parts for i in range(expert_total // 8)]
+    pieces.append(jnp.zeros((8, cols - len(pieces) * rows), F32))
+    out_ref[rows : rows + 8, :] = jnp.concatenate(pieces, axis=1).astype(BF16)
+    copies[2].wait()
+
+
+def payload_of(ids_t, probs_t, grad, capacity):
+    rows, cols = grad.shape
+    return call(
+        functools.partial(payload_kernel, capacity),
+        60,
+        jax.ShapeDtypeStruct((rows + 8, cols), BF16),
+        [
+            pltpu.VMEM(ids_t.shape, jnp.int32),
+            pltpu.VMEM(probs_t.shape, F32),
+            pltpu.SemaphoreType.DMA((3,)),
+        ],
+        0,
+        3,
+    )(ids_t, probs_t, grad)
+
+
+def hidden_kernel(halves, tiles, capacity, info_ref, *refs):
+    block_refs = refs[: len(halves)]
+    weight_ref, other_ref, mine_ref, meta_ref, placed_ref = refs[len(halves) :]
+    core, tile, row = info_ref[0], info_ref[1], info_ref[2]
+    blocks, at = [], 0
+    while at < len(halves):
+        size = 2 if halves[at] else 1
+        blocks.append(block_refs[at : at + size])
+        at += size
+    rows = 128
+    units = weight_ref.shape[1]
+
+    def pick(meta, kind, which):
+        value = meta[:, kind * tiles * rows : (kind * tiles + 1) * rows]
+        for i in range(1, tiles):
+            at_lane = (kind * tiles + i) * rows
+            value = jnp.where(tile == i, meta[:, at_lane : at_lane + rows], value)
+        line = lax.broadcasted_iota(jnp.int32, (8, rows), 0)
+        return jnp.sum(jnp.where(line == which, value, 0.0), axis=0, keepdims=True)
+
+    slot_at = lax.broadcasted_iota(jnp.int32, (capacity, rows), 0).astype(F32)
+    for step in range(2):
+        expert = 1 - core if step == 0 else core
+        for b, block in enumerate(blocks):
+            last = block[-1]
+            meta = last[last.shape[0] - 8 :, :].astype(F32)
+            match = jnp.where(slot_at == pick(meta, 0, row + expert), 1.0, 0.0).astype(BF16)
+            if len(block) == 1:
+                data = block[0][0:rows, :]
+            else:
+                data = jnp.concatenate([block[0][...], block[1][0 : rows - TOP_ROWS, :]], axis=0)
+            placed = jnp.dot(match, data, preferred_element_type=F32)
+            placed_ref[step, b * capacity : (b + 1) * capacity, :] = placed.astype(BF16)
+            if step == 1:
+                lines = [pick(meta, 0, row), pick(meta, 0, row + 1)]
+                lines += [pick(meta, 1, row) + pick(meta, 2, row)]
+                lines += [pick(meta, 1, row + 1) + pick(meta, 2, row + 1)]
+                lines += [jnp.zeros((4, rows), F32)]
+                meta_ref[8 * b : 8 * b + 8, :] = jnp.concatenate(lines, axis=0)
+        out_ref = other_ref if step == 0 else mine_ref
+        for n in range(0, units, 256):
+            value = lax.dot_general(
+                placed_ref[step],
+                weight_ref[expert, n : n + 256, :],
+                LAST,
+                preferred_element_type=F32,
+            )
+            out_ref[:, n : n + 256] = value.astype(BF16)
+
+
+def hidden_part(info, blocks, down_weight, tiles, capacity):
+    local_count, hidden_units, cols = down_weight.shape
+    flat, halves = [], []
+    for block in blocks:
+        pair = isinstance(block, tuple)
+        flat += list(block) if pair else [block]
+        halves += [pair, pair] if pair else [False]
+    count = len(blocks)
+    shape = (count * capacity, hidden_units)
+    return call(
+        functools.partial(hidden_kernel, halves, tiles, capacity),
+        10,
+        [
+            jax.ShapeDtypeStruct(shape, BF16),
+            jax.ShapeDtypeStruct(shape, BF16),
+            jax.ShapeDtypeStruct((8 * count, 128), F32),
+        ],
+        [pltpu.VMEM((2, count * capacity, cols), BF16)],
+        1,
+    )(info, *flat, down_weight)
+
+
+def grad_kernel(counts, chunk, split, tiles, capacity, info_ref, *refs):
+    groups = len(counts)
+    total = sum(counts)
+    hidden_refs = refs[: 3 * groups]
+    gate_ref, up_ref, gate_w_ref, up_w_ref = refs[3 * groups : 3 * groups + 4]
+    out_refs = refs[3 * groups + 4 : -2]
+    dgate_ref, dup_ref = refs[-2:]
+    core, tile, row = info_ref[0], info_ref[1], info_ref[2]
+    rows = 128
+    cols = gate_w_ref.shape[1]
+    line = lax.broadcasted_iota(jnp.int32, (8, rows), 0)
+    slot_at = lax.broadcasted_iota(jnp.int32, (capacity, rows), 0).astype(F32)
+    combine, scores = [], []
+    b = 0
+    for g in range(groups):
+        full_ref, pair_ref, meta_ref = hidden_refs[3 * g : 3 * g + 3]
+        for i in range(counts[g]):
+            span = slice(i * capacity, (i + 1) * capacity)
+            store = slice(b * capacity, (b + 1) * capacity)
+            saved = pl.ds(pl.multiple_of(info_ref[INFO_BLOCKS + chunk[b]] * capacity, capacity), capacity)
+            lines = meta_ref[8 * i : 8 * i + 8, :]
+            score_rows = jnp.zeros((8, rows), F32)
+            stacked = []
+            for e in range(2):
+                hidden = jnp.where(core == e, full_ref[span, :], pair_ref[span, :]).astype(F32)
+                gate = gate_ref[e, saved, :].astype(F32)
+                up = up_ref[e, saved, :].astype(F32)
+                active, slope_term = silu_parts(gate)
+                dup = hidden * active
+                match = slot_at == lines[e : e + 1, :]
+                weight = jnp.sum(
+                    jnp.where(match, lines[2 + e : 3 + e, :], 0.0), axis=1, keepdims=True
+                )
+                dgate_ref[e, store, :] = (hidden * up * slope_term * weight).astype(BF16)
+                dup_ref[e, store, :] = (dup * weight).astype(BF16)
+                score = jnp.sum(up * dup.astype(BF16).astype(F32), axis=1, keepdims=True)
+                score = score.astype(BF16).astype(F32)
+                token_score = jnp.sum(jnp.where(match, score, 0.0), axis=0, keepdims=True)
+                score_rows = score_rows + jnp.where(line == row + e, token_score, 0.0)
+                stacked.append(jnp.where(match, 1.0, 0.0).astype(BF16))
+            combine.append(jnp.concatenate(stacked, axis=0))
+            scores.append(score_rows)
+            b += 1
+    for n in range(0, cols, 256):
+        grads = []
+        for e in range(2):
+            value = lax.dot_general(
+                dgate_ref[e], gate_w_ref[e, n : n + 256, :], LAST, preferred_element_type=F32
+            )
+            value = value + lax.dot_general(
+                dup_ref[e], up_w_ref[e, n : n + 256, :], LAST, preferred_element_type=F32
+            )
+            grads.append(value.astype(BF16))
+        for b in range(total):
+            span = slice(b * capacity, (b + 1) * capacity)
+            pile = jnp.concatenate([g[span] for g in grads], axis=0)
+            value = lax.dot_general(combine[b], pile, FIRST, preferred_element_type=F32)
+            if n == 0:
+                lanes = [jnp.where(tile == i, scores[b], 0.0) for i in range(tiles)]
+                lanes = jnp.concatenate(lanes, axis=1)
+            else:
+                lanes = jnp.zeros((8, 256), F32)
+            if split:
+                out_refs[2 * b][:, n : n + 256] = value[:TOP_ROWS].astype(BF16)
+                low = jnp.concatenate([value[TOP_ROWS:], lanes], axis=0)
+                out_refs[2 * b + 1][:, n : n + 256] = low.astype(BF16)
+            else:
+                out_refs[b][:, n : n + 256] = jnp.concatenate([value, lanes], axis=0).astype(BF16)
+
+
+def grad_part(info, parts, saved, weights, counts, chunk, split, tiles, capacity):
+    local_count, cols, hidden_units = weights[0].shape
+    total = sum(counts)
+    heights = [TOP_ROWS, 136 - TOP_ROWS] * total if split else [136] * total
+    return call(
+        functools.partial(grad_kernel, counts, chunk, split, tiles, capacity),
+        14,
+        [jax.ShapeDtypeStruct((h, cols), BF16) for h in heights],
+        [
+            pltpu.VMEM((2, total * capacity, hidden_units), BF16),
+            pltpu.VMEM((2, total * capacity, hidden_units), BF16),
+        ],
+        1,
+    )(info, *parts, *saved, *weights)
+
+
+def shared_kernel(info_ref, *refs):
+    token_refs, grad_refs = refs[0:4], refs[4:8]
+    gate_ref, up_ref, down_ref = refs[8:11]
+    out_refs = refs[11:15]
+    here = info_ref[3]
+    rows, cols = token_refs[0].shape
+    units = gate_ref.shape[1]
+    spans = []
+    for q in range(4):
+        at = pl.multiple_of(jnp.bitwise_xor(here, q) * cols, cols)
+        spans.append(pl.ds(at, cols))
+    gate_pre = jnp.zeros((rows, units), F32)
+    up_pre = jnp.zeros((rows, units), F32)
+    hidden_pre = jnp.zeros((rows, units), F32)
+    for q in range(4):
+        token, grad = token_refs[q][...], grad_refs[q][...]
+        gate_pre = gate_pre + jnp.dot(token, gate_ref[spans[q], :], preferred_element_type=F32)
+        up_pre = up_pre + jnp.dot(token, up_ref[spans[q], :], preferred_element_type=F32)
+        hidden_pre = hidden_pre + lax.dot_general(
+            grad, down_ref[:, spans[q]], LAST, preferred_element_type=F32
+        )
+    active, slope_term = silu_parts(gate_pre)
+    dgate = (hidden_pre * up_pre * slope_term).astype(BF16)
+    dup = (hidden_pre * active).astype(BF16)
+    for q in range(4):
+        term = lax.dot_general(dgate, gate_ref[spans[q], :], LAST, preferred_element_type=F32)
+        term = term + lax.dot_general(dup, up_ref[spans[q], :], LAST, preferred_element_type=F32)
+        out_refs[q][...] = term.astype(BF16)
+
+
+def shared_part_terms(here, token_blocks, grad_blocks, shared_gate, shared_up, shared_down):
+    rows, cols = token_blocks[0].shape
+    return call(
+        shared_kernel,
+        10,
+        [jax.ShapeDtypeStruct((rows, cols), BF16)] * 4,
+        (),
+        1,
+    )(here, *token_blocks, *grad_blocks, shared_gate, shared_up, shared_down)
+
+
+def ring_place(position):
+    position = position % 8
+    return jnp.where(position < 4, 2 * position, 15 - 2 * position)
+
+
+def per_device_ring(
+    tokens,
+    out_grad,
+    expert_ids,
+    router_probs,
+    router_weight,
+    gate_weight,
+    up_weight,
+    down_weight,
+    gate_saved,
+    up_saved,
+    shared_gate,
+    shared_up,
+    shared_down,
+):
+    slot_count = gate_saved.shape[1]
+    capacity = slot_count // 8
+    rows, cols = tokens.shape
+    expert_total = router_probs.shape[1]
+    tiles = expert_total // 8
+    order = [0, 2, 4, 6, 7, 5, 3, 1]
+    ahead = [(order[i], order[(i + 1) % 8]) for i in range(8)]
+    behind = [(order[i], order[(i - 1) % 8]) for i in range(8)]
+    x_pairs = [(i, i ^ 2) for i in range(4)]
+    core_pairs = [(i, i ^ 1) for i in range(4)]
+    me = lax.axis_index("expert")
+    place = jnp.where(me % 2 == 0, me // 2, 7 - me // 2)
+    here = lax.axis_index("tensor")
+    first = me * 2
+    base = [here % 2, first // 8, first % 8]
+    tie = lax.optimization_barrier
+
+    def swap_x(a):
+        return lax.ppermute(a, "tensor", x_pairs)
+
+    def swap_core(a):
+        return lax.ppermute(a, "tensor", core_pairs)
+
+    def ring(fore, back):
+        return lax.ppermute(fore, "expert", ahead), lax.ppermute(back, "expert", behind)
+
+    def hidden(blocks):
+        return hidden_part(info, blocks, down_weight, tiles, capacity)
+
+    def grads(saved, weights, *parts):
+        chunk = sum((part[0] for part in parts), ())
+        return grad_part(
+            info,
+            [a for part in parts for a in part[1:]],
+            saved,
+            weights,
+            [len(part[0]) for part in parts],
+            chunk,
+            chunk == (4,),
+            tiles,
+            capacity,
+        )
+
+    numbers = base + [here] + [ring_place(place + d) for d in range(-3, 5)]
+    info = jnp.stack([jnp.asarray(n, jnp.int32) for n in numbers])
+    payload = payload_of(expert_ids.T, router_probs.T, out_grad, capacity)
+
+    payload, tokens, out_grad, info = tie((payload, tokens, out_grad, info))
+    fore, back = ring(payload, payload)
+    fore1, back1 = tie((fore, back))
+
+    fore, back = ring(fore1, back1)
+    other1, mine1, meta1 = hidden([payload, fore1, back1])
+    fore2, back2, other1, mine1 = tie((fore, back, other1, mine1))
+
+    fore, back = ring(fore2, back2)
+    (chip1,) = sums((mine1, swap_core(other1)))
+    far1 = swap_x(chip1)
+    other2, mine2, meta2 = hidden([fore2, back2])
+    fore3, back3, chip1, other2, mine2 = tie((fore, back, chip1, other2, mine2))
+
+    top, bottom = ring(*halves_of(fore3, back3))
+    (chip2,) = sums((mine2, swap_core(other2)))
+    far2 = swap_x(chip2)
+    other3, mine3, meta3 = hidden([fore3, back3])
+    top, bottom, chip2, other3, mine3, far1 = tie((top, bottom, chip2, other3, mine3, far1))
+
+    other4, mine4, meta4 = hidden([(top, bottom)])
+    swapped4, swapped3 = swap_core(other4), swap_core(other3)
+    (full1,) = sums((chip1, far1))
+    pair1 = swap_core(full1)
+    (chip4,) = sums((mine4, swapped4))
+    chip4, far2, swapped3, pair1 = tie((chip4, far2, swapped3, pair1))
+    far4 = swap_x(chip4)
+    chip3, full2 = sums((mine3, swapped3), (chip2, far2))
+    pair2 = swap_core(full2)
+    far4, chip3, full2, pair2 = tie((far4, chip3, full2, pair2))
+    (full4,) = sums((chip4, far4))
+    pair4 = swap_core(full4)
+    far3 = swap_x(chip3)
+    pair4, full4 = tie((pair4, full4))
+    saved = (gate_saved, up_saved)
+    weights = (gate_weight, up_weight)
+    top, bottom = grads(saved, weights, ((4,), full4, pair4, meta4))
+
+    top, bottom, far3, tokens, out_grad = tie((top, bottom, far3, tokens, out_grad))
+    fore, back = ring(top, bottom)
+    tok_x = swap_x(tokens)
+    tok_core, grad_core = swap_core(tokens), swap_core(out_grad)
+    (full3,) = sums((chip3, far3))
+    pair3 = swap_core(full3)
+    near_b3, near_f3, near_b2, near_f2 = grads(
+        saved, weights, ((-3, 3), full3, pair3, meta3), ((-2, 2), full2, pair2, meta2)
+    )
+    fore, back, near_f3, near_b3, near_f2, near_b2, full1, pair1, out_grad = tie(
+        (fore, back, near_f3, near_b3, near_f2, near_b2, full1, pair1, out_grad)
+    )
+
+    fore, back = join(near_f3, fore, near_b3, back)
+    fore, back = ring(fore, back)
+    grad_x = swap_x(out_grad)
+    tok_both = swap_core(tok_x)
+    near0, near_b1, near_f1 = grads(saved, weights, ((0, -1, 1), full1, pair1, meta1))
+    fore, back, near0, near_b1, near_f1, tok_x, tok_both, grad_x = tie(
+        (fore, back, near0, near_b1, near_f1, tok_x, tok_both, grad_x)
+    )
+
+    fore, back = sums((near_f2, fore), (near_b2, back))
+    fore, back = ring(fore, back)
+    grad_both = swap_core(grad_x)
+    terms = shared_part_terms(
+        info,
+        [tokens, tok_core, tok_x, tok_both],
+        [out_grad, grad_core, grad_x, grad_both],
+        shared_gate,
+        shared_up,
+        shared_down,
+    )
+    fore, back, *terms = tie((fore, back, *terms))
+
+    swapped = swap_core(terms[3])
+    near = swap_core(terms[1])
+    fore, back = sums((near_f1, fore), (near_b1, back))
+    fore, back = ring(fore, back)
+    (far,) = sums((terms[2], swapped))
+    shared_far = swap_x(far)
+    total = near0.astype(F32) + fore.astype(F32) + back.astype(F32)
+    shared_part = terms[0].astype(F32) + near.astype(F32) + shared_far.astype(F32)
+    prob_grad = jnp.concatenate(
+        [total[rows:, i * rows : (i + 1) * rows] for i in range(tiles)], axis=0
+    ).T
+    gate_total = jnp.sum(router_probs * prob_grad, axis=1, keepdims=True)
+    logit_grad = (router_probs * (prob_grad - gate_total)).astype(BF16)
+    router_part = jnp.einsum("te,de->td", logit_grad, router_weight, preferred_element_type=F32)
+    return (shared_part + total[:rows] + router_part).astype(BF16)
+
+
+def per_device(*args):
+    tokens, router_probs, gate_weight, gate_saved = args[0], args[3], args[5], args[8]
+    rows, cols = tokens.shape
+    expert_total = router_probs.shape[1]
+    ring = (
+        lax.axis_size("expert") == 8
+        and lax.axis_size("tensor") == 4
+        and gate_weight.shape[0] == 2
+        and gate_saved.shape[1] == 8 * 64
+        and gate_saved.shape[2] % 256 == 0
+        and rows == 128
+        and expert_total == 16
+        and cols % 256 == 0
+        and cols >= 6 * rows
+    )
+    return (per_device_ring if ring else per_device_wide)(*args)
+
+
 def solution(mesh):
+
     return jax.shard_map(
         per_device,
         mesh=mesh,

time: 246 us -> 109 us (0.44)
  blocking collectives: 66.6 us -> 0 us
  matrix products: 44.7 us -> 1.01 us
  Pallas kernels: 0 us -> 30.3 us
  waiting for transfers between devices: 73.3 us -> 45.2 us
  local copies, waits for them, and re-layouts: 28.5 us -> 3.26 us
  starting transfers between devices: 11.8 us -> 28.7 us
  between operations: 13.4 us -> 0.39 us
  other arithmetic: 7.5 us -> 0.15 us
    all_to_all x1 -> x0, blocking collectives: 66.6 us -> none  [per_device(): lax.all_to_all(outgoing, 'expert', split_axis=1, concat_axis=1, tiled=True)]
    ppermute x0 -> x37, waiting for transfers between devices: none -> 45.2 us  [the longest x8 16.9 us: ring(): lax.ppermute(fore, 'expert', ahead)]
    dot_general x10 -> x1, matrix products: 44.7 us -> 1.01 us  [per_device_ring(): jnp.einsum('te,de->td', logit_grad, router_weight, preferred_element_type...]
    psum x1 -> x0, waiting for transfers between devices: 40.5 us -> none  [per_device(): lax.psum(partial_hidden.astype(jnp.bfloat16), 'tensor').astype(jnp.float32)]
    pallas_call x0 -> x21, Pallas kernels: none -> 30.3 us  [run(): pl.pallas_call(kernel, in_specs=[pl.BlockSpec(memory_space=m) for m in me...]
    ppermute x0 -> x37, starting transfers between devices: none -> 28.7 us  [the longest x7 9.07 us: swap_x(): return lax.ppermute(a, 'tensor', x_pairs)]
    all_to_all x2 -> x0, waiting for transfers between devices: 28 us -> none  [the longest x1 28 us: per_device(): lax.all_to_all(expert_grad.reshape(local_count, groups, capacity * featur...]
    reshape x7 -> x0, local copies, waits for them, and re-layouts: 18.4 us -> none  [the longest x2 6.72 us: per_device(): expert_grad.reshape(local_count, groups, capacity * feature_cols)]
  transfers between devices with their start and end apart: 6 -> 37, of which waited for: 3 -> 22; matrix products, arithmetic and copies ran while one was open for 21% -> 0% of each run, Pallas kernels for 0% -> 26%
where the time goes in v3:
time: 109 us
  waiting for transfers between devices  45.2 us (41%)
  Pallas kernels  30.3 us (28%)
  starting transfers between devices  28.7 us (26%)
  local copies, waits for them, and re-layouts  3.26 us (3%)
    pallas_call x21, Pallas kernels, run(): pl.pallas_call(kernel, in_specs=[pl.BlockSpec(memory_space=m) for m in me...  30.3 us
    ppermute x8, waiting for transfers between devices, ring(): lax.ppermute(fore, 'expert', ahead)  16.9 us
    ppermute x8, waiting for transfers between devices, ring(): lax.ppermute(back, 'expert', behind)  11.6 us
    ppermute x7, waiting for transfers between devices, swap_x(): return lax.ppermute(a, 'tensor', x_pairs)  11.3 us
    ppermute x7, starting transfers between devices, swap_x(): return lax.ppermute(a, 'tensor', x_pairs)  9.07 us
    ppermute x8, starting transfers between devices, ring(): lax.ppermute(fore, 'expert', ahead)  9.05 us
    ppermute x8, starting transfers between devices, ring(): lax.ppermute(back, 'expert', behind)  8.71 us
    ppermute x14, waiting for transfers between devices, swap_core(): return lax.ppermute(a, 'tensor', core_pairs)  5.44 us
  transfers between devices with their start and end apart: 37, of which 22 were waited for; matrix products, arithmetic and copies ran while one was open for 0% of the time, Pallas kernels for 26%

profile of v3, /device:TPU:0, one launch (start us, length us, event | category | flops | bytes accessed | tf_op | source)
XLA Modules:
  0.0 109.0 jit_solution(7082186396756639224)
XLA Ops:
  0.0 1.8 %shard_map.127.refs_0_ = bf16[136,1280]{1,0:T(8,128)(2,1)} custom-call(s32[6,128]{1,0:T(8,128)} %bitcast.31, f32[16,128]{1,0:T(8,128)} %bitcast.30, bf16[128,1280]{1,0:T(8,128)(2,1)} %refs_4_.4), custom_call_target="tpu_custom_call" | custom-call | flops 1000 | bytes 1000 | tf_op jit(solution)/shard_map/pallas_call | solution.py:143
  1.9 3.0 %collective-permute-start.1 = (bf16[136,1280]{1,0:T(8,128)(2,1)}, bf16[136,1280]{1,0:T(8,128)(2,1)S(1)}, u32[]{:S(2)}, u32[]{:S(2)}) collective-permute-start(bf16[136,1280]{1,0:T(8,128)(2,1)} %shard_map.127.refs_0_), channel_id=1, source_target_pairs={{0,4},{8,0},{16,8},{24,16},{28,24},{20,28},{12,20},{4,12},{1,5},{9... | collective-permute-start | bytes 1044488 | tf_op jit(solution)/shard_map/ppermute | solution.py:496
  5.0 8.3 %collective-permute-done.1.refs_2_ = bf16[136,1280]{1,0:T(8,128)(2,1)S(1)} collective-permute-done((bf16[136,1280]{1,0:T(8,128)(2,1)}, bf16[136,1280]{1,0:T(8,128)(2,1)S(1)}, u32[]{:S(2)}, u32[]{:S(2)}) %collective-permute-start.1) | collective-permute-done | bytes 348192 | tf_op jit(solution)/shard_map/ppermute | solution.py:496
  13.3 1.4 %collective-permute-done.refs_1_ = bf16[136,1280]{1,0:T(8,128)(2,1)S(1)} collective-permute-done((bf16[136,1280]{1,0:T(8,128)(2,1)}, bf16[136,1280]{1,0:T(8,128)(2,1)S(1)}, u32[]{:S(2)}, u32[]{:S(2)}) %collective-permute-start) | collective-permute-done | bytes 348192 | tf_op jit(solution)/shard_map/ppermute | solution.py:496
  15.1 1.6 %collective-permute-start.3 = (bf16[136,1280]{1,0:T(8,128)(2,1)S(1)}, bf16[136,1280]{1,0:T(8,128)(2,1)S(1)}, u32[]{:S(2)}, u32[]{:S(2)}) collective-permute-start(bf16[136,1280]{1,0:T(8,128)(2,1)S(1)} %collective-permute-done.1.refs_2_), channel_id=1, source_target_pairs={{0,4},{8,0},{16,8},{24,16},{28,24},{20,28},{12,20},{4,12},{1,5},{9... | collective-permute-start | bytes 1044488 | tf_op jit(solution)/shard_map/ppermute | solution.py:496
  16.8 2.1 %copy-done.1 = bf16[2,768,1280]{2,1,0:T(8,128)(2,1)S(1)} copy-done((bf16[2,768,1280]{2,1,0:T(8,128)(2,1)S(1)}, bf16[2,768,1280]{2,1,0:T(8,128)(2,1)}, u32[]{:S(2)}) %copy-start.1) | copy-done | bytes 3932184
  19.9 2.2 %shard_map.128 = (bf16[192,768]{1,0:T(8,128)(2,1)S(1)}, bf16[192,768]{1,0:T(8,128)(2,1)S(1)}, f32[24,128]{1,0:T(8,128)S(1)}) custom-call(s32[12]{0:T(128)S(1)} %stack.51.info_ref, bf16[136,1280]{1,0:T(8,128)(2,1)S(1)} %copy-done.7, bf16[136,1280]{1,0:T(8,128)(2,1)S(1)} %collective-permute-done.refs_1_, bf16[136,1280]{1,0:T(8,128)(2,1)S(1)} %collective-permute-done.1.refs_2_, ...), custom_call_target="tpu_custom_call" | custom-call | flops 1000 | bytes 1000 | tf_op jit(solution)/shard_map/pallas_call | solution.py:143
  22.1 1.4 %collective-permute-done.2.refs_0_ = bf16[136,1280]{1,0:T(8,128)(2,1)S(1)} collective-permute-done((bf16[136,1280]{1,0:T(8,128)(2,1)S(1)}, bf16[136,1280]{1,0:T(8,128)(2,1)S(1)}, u32[]{:S(2)}, u32[]{:S(2)}) %collective-permute-start.2) | collective-permute-done | bytes 348192 | tf_op jit(solution)/shard_map/ppermute | solution.py:496
  23.9 1.5 %collective-permute-start.4 = (bf16[136,1280]{1,0:T(8,128)(2,1)S(1)}, bf16[136,1280]{1,0:T(8,128)(2,1)S(1)}, u32[]{:S(2)}, u32[]{:S(2)}) collective-permute-start(bf16[136,1280]{1,0:T(8,128)(2,1)S(1)} %collective-permute-done.2.refs_0_), channel_id=1, source_target_pairs={{0,8},{8,16},{16,24},{24,28},{28,20},{20,12},{12,4},{4,0},{1,9},{9... | collective-permute-start | bytes 1044488 | tf_op jit(solution)/shard_map/ppermute | solution.py:496
  26.0 1.5 %collective-permute-start.10 = (bf16[192,768]{1,0:T(8,128)(2,1)S(1)}, bf16[192,768]{1,0:T(8,128)(2,1)S(1)}, u32[]{:S(2)}, u32[]{:S(2)}) collective-permute-start(bf16[192,768]{1,0:T(8,128)(2,1)S(1)} %shard_map.129.refs_0_), channel_id=1, source_target_pairs={{0,2},{1,3},{2,0},{3,1},{4,6},{5,7},{6,4},{7,5},{8,10},{9,11},{10,... | collective-permute-start | bytes 884744 | tf_op jit(solution)/shard_map/ppermute | solution.py:490
  27.5 1.9 %shard_map.130 = (bf16[128,768]{1,0:T(8,128)(2,1)S(1)}, bf16[128,768]{1,0:T(8,128)(2,1)S(1)}, f32[16,128]{1,0:T(8,128)S(1)}) custom-call(s32[12]{0:T(128)S(1)} %stack.51.info_ref, bf16[136,1280]{1,0:T(8,128)(2,1)S(1)} %collective-permute-done.2.refs_0_, bf16[136,1280]{1,0:T(8,128)(2,1)S(1)} %collective-permute-done.3.refs_1_, bf16[2,768,1280]{2,1,0:T(8,128)(2,1)S(1)} %copy-done.2), custom_call_target="tpu_custom_call" | custom-call | flops 1000 | bytes 1000 | tf_op jit(solution)/shard_map/pallas_call | solution.py:143
  29.4 5.0 %collective-permute-done.4.fore_ref.refs_0_ = bf16[136,1280]{1,0:T(8,128)(2,1)S(1)} collective-permute-done((bf16[136,1280]{1,0:T(8,128)(2,1)S(1)}, bf16[136,1280]{1,0:T(8,128)(2,1)S(1)}, u32[]{:S(2)}, u32[]{:S(2)}) %collective-permute-start.4) | collective-permute-done | bytes 348192 | tf_op jit(solution)/shard_map/ppermute | solution.py:496
  36.3 1.5 %collective-permute-start.7 = (bf16[64,1280]{1,0:T(8,128)(2,1)S(1)}, bf16[64,1280]{1,0:T(8,128)(2,1)S(1)}, u32[]{:S(2)}, u32[]{:S(2)}) collective-permute-start(bf16[64,1280]{1,0:T(8,128)(2,1)S(1)} %get-tuple-element.113), channel_id=1, source_target_pairs={{0,8},{8,16},{16,24},{24,28},{28,20},{20,12},{12,4},{4,0},{1,9},{9... | collective-permute-start | bytes 491528 | tf_op jit(solution)/shard_map/ppermute | solution.py:496
  37.8 1.9 %shard_map.133 = (bf16[128,768]{1,0:T(8,128)(2,1)S(1)}, bf16[128,768]{1,0:T(8,128)(2,1)S(1)}, f32[16,128]{1,0:T(8,128)S(1)}) custom-call(s32[12]{0:T(128)S(1)} %stack.51.info_ref, bf16[136,1280]{1,0:T(8,128)(2,1)S(1)} %collective-permute-done.4.fore_ref.refs_0_, bf16[136,1280]{1,0:T(8,128)(2,1)S(1)} %collective-permute-done.5.back_ref.refs_1_, ...), custom_call_target="tpu_custom_call" | custom-call | flops 1000 | bytes 1000 | tf_op jit(solution)/shard_map/pallas_call | solution.py:143
  39.8 2.8 %collective-permute-done.7.refs_0_ = bf16[64,1280]{1,0:T(8,128)(2,1)S(1)} collective-permute-done((bf16[64,1280]{1,0:T(8,128)(2,1)S(1)}, bf16[64,1280]{1,0:T(8,128)(2,1)S(1)}, u32[]{:S(2)}, u32[]{:S(2)}) %collective-permute-start.7) | collective-permute-done | bytes 163872 | tf_op jit(solution)/shard_map/ppermute | solution.py:496
  43.0 1.6 %collective-permute-start.12 = (bf16[128,768]{1,0:T(8,128)(2,1)S(1)}, bf16[128,768]{1,0:T(8,128)(2,1)S(1)}, u32[]{:S(2)}, u32[]{:S(2)}) collective-permute-start(bf16[128,768]{1,0:T(8,128)(2,1)S(1)} %shard_map.132.refs_2_), channel_id=1, source_target_pairs={{0,2},{1,3},{2,0},{3,1},{4,6},{5,7},{6,4},{7,5},{8,10},{9,11},{10,... | collective-permute-start | bytes 589832 | tf_op jit(solution)/shard_map/ppermute | solution.py:490
  44.7 1.9 %shard_map.134 = (bf16[64,768]{1,0:T(8,128)(2,1)S(1)}, bf16[64,768]{1,0:T(8,128)(2,1)S(1)}, f32[8,128]{1,0:T(8,128)S(1)}) custom-call(s32[12]{0:T(128)S(1)} %stack.51.info_ref, bf16[64,1280]{1,0:T(8,128)(2,1)S(1)} %collective-permute-done.7.refs_0_, bf16[72,1280]{1,0:T(8,128)(2,1)S(1)} %collective-permute-done.8.refs_1_, bf16[2,768,1280]{2,1,0:T(8,128)(2,1)S(1)} %copy-done.2), custom_call_target="tpu_custom_call" | custom-call | flops 1000 | bytes 1000 | tf_op jit(solution)/shard_map/pallas_call | solution.py:143
  48.0 2.3 %collective-permute-done.12.refs_3_ = bf16[128,768]{1,0:T(8,128)(2,1)S(1)} collective-permute-done((bf16[128,768]{1,0:T(8,128)(2,1)S(1)}, bf16[128,768]{1,0:T(8,128)(2,1)S(1)}, u32[]{:S(2)}, u32[]{:S(2)}) %collective-permute-start.12) | collective-permute-done | bytes 196640 | tf_op jit(solution)/shard_map/ppermute | solution.py:490
  50.5 1.6 %collective-permute-start.15 = (bf16[64,768]{1,0:T(8,128)(2,1)S(1)}, bf16[64,768]{1,0:T(8,128)(2,1)S(1)}, u32[]{:S(2)}, u32[]{:S(2)}) collective-permute-start(bf16[64,768]{1,0:T(8,128)(2,1)S(1)} %shard_map.135.refs_0_), channel_id=1, source_target_pairs={{0,2},{1,3},{2,0},{3,1},{4,6},{5,7},{6,4},{7,5},{8,10},{9,11},{10,... | collective-permute-start | bytes 294920 | tf_op jit(solution)/shard_map/ppermute | solution.py:490
  52.0 3.7 %collective-permute-done.15.refs_1_ = bf16[64,768]{1,0:T(8,128)(2,1)S(1)} collective-permute-done((bf16[64,768]{1,0:T(8,128)(2,1)S(1)}, bf16[64,768]{1,0:T(8,128)(2,1)S(1)}, u32[]{:S(2)}, u32[]{:S(2)}) %collective-permute-start.15) | collective-permute-done | bytes 98336 | tf_op jit(solution)/shard_map/ppermute | solution.py:490
  55.7 1.5 %collective-permute-start.18 = (bf16[128,768]{1,0:T(8,128)(2,1)S(1)}, bf16[128,768]{1,0:T(8,128)(2,1)S(1)}, u32[]{:S(2)}, u32[]{:S(2)}) collective-permute-start(bf16[128,768]{1,0:T(8,128)(2,1)S(1)} %get-tuple-element.139.refs_0_), channel_id=1, source_target_pairs={{0,2},{1,3},{2,0},{3,1},{4,6},{5,7},{6,4},{7,5},{8,10},{9,11},{10,... | collective-permute-start | bytes 589832 | tf_op jit(solution)/shard_map/ppermute | solution.py:490
  57.3 1.3 %collective-permute-done.17.refs_1_ = bf16[64,768]{1,0:T(8,128)(2,1)S(1)} collective-permute-done((bf16[64,768]{1,0:T(8,128)(2,1)S(1)}, bf16[64,768]{1,0:T(8,128)(2,1)S(1)}, u32[]{:S(2)}, u32[]{:S(2)}) %collective-permute-start.17) | collective-permute-done | bytes 98336 | tf_op jit(solution)/shard_map/ppermute | solution.py:493
  58.6 3.7 %shard_map.139 = (bf16[64,1280]{1,0:T(8,128)(2,1)S(1)}, bf16[72,1280]{1,0:T(8,128)(2,1)S(1)}) custom-call(s32[12]{0:T(128)S(1)} %stack.51.info_ref, bf16[64,768]{1,0:T(8,128)(2,1)S(1)} %shard_map.138.refs_0_, bf16[64,768]{1,0:T(8,128)(2,1)S(1)} %collective-permute-done.17.refs_1_, f32[8,128]{1,0:T(8,128)S(1)} %get-tuple-element.136.refs_2_, ...), custom_call_target="tpu_custom_call" | custom-call | flops 1000 | bytes 1000 | tf_op jit(solution)/shard_map/pallas_call | solution.py:143
  65.9 4.6 %shard_map.141 = (bf16[136,1280]{1,0:T(8,128)(2,1)S(1)}, bf16[136,1280]{1,0:T(8,128)(2,1)S(1)}, bf16[136,1280]{1,0:T(8,128)(2,1)S(1)}, bf16[136,1280]{1,0:T(8,128)(2,1)S(1)}) custom-call(s32[12]{0:T(128)S(1)} %stack.51.info_ref, bf16[128,768]{1,0:T(8,128)(2,1)S(1)} %shard_map.140.refs_0_, bf16[128,768]{1,0:T(8,128)(2,1)S(1)} %collective-permute-done.21.refs_1_, ...), custom_call_target="tpu_custom_call" | custom-call | flops 1000 | bytes 1000 | tf_op jit(solution)/shard_map/pallas_call | solution.py:143
  71.3 1.4 %collective-permute-start.22 = (bf16[136,1280]{1,0:T(8,128)(2,1)S(1)}, bf16[136,1280]{1,0:T(8,128)(2,1)S(1)}, u32[]{:S(2)}, u32[]{:S(2)}) collective-permute-start(bf16[136,1280]{1,0:T(8,128)(2,1)S(1)} %get-tuple-element.160), channel_id=1, source_target_pairs={{0,8},{8,16},{16,24},{24,28},{28,20},{20,12},{12,4},{4,0},{1,9},{9... | collective-permute-start | bytes 1044488 | tf_op jit(solution)/shard_map/ppermute | solution.py:496
  74.4 4.2 %shard_map.143 = (bf16[136,1280]{1,0:T(8,128)(2,1)S(1)}, bf16[136,1280]{1,0:T(8,128)(2,1)S(1)}, bf16[136,1280]{1,0:T(8,128)(2,1)S(1)}) custom-call(s32[12]{0:T(128)S(1)} %stack.51.info_ref, bf16[192,768]{1,0:T(8,128)(2,1)S(1)} %shard_map.136.refs_0_, bf16[192,768]{1,0:T(8,128)(2,1)S(1)} %collective-permute-done.14.refs_1_, ...), custom_call_target="tpu_custom_call" | custom-call | flops 1000 | bytes 1000 | tf_op jit(solution)/shard_map/pallas_call | solution.py:143
  78.6 3.4 %collective-permute-done.26.refs_6_ = bf16[128,1280]{1,0:T(8,128)(2,1)S(1)} collective-permute-done((bf16[128,1280]{1,0:T(8,128)(2,1)S(1)}, bf16[128,1280]{1,0:T(8,128)(2,1)S(1)}, u32[]{:S(2)}, u32[]{:S(2)}) %collective-permute-start.26) | collective-permute-done | bytes 327712 | tf_op jit(solution)/shard_map/ppermute | solution.py:490
  82.3 1.6 %collective-permute-start.27 = (bf16[136,1280]{1,0:T(8,128)(2,1)S(1)}, bf16[136,1280]{1,0:T(8,128)(2,1)S(1)}, u32[]{:S(2)}, u32[]{:S(2)}) collective-permute-start(bf16[136,1280]{1,0:T(8,128)(2,1)S(1)} %get-tuple-element.173), channel_id=1, source_target_pairs={{0,8},{8,16},{16,24},{24,28},{28,20},{20,12},{12,4},{4,0},{1,9},{9... | collective-permute-start | bytes 1044488 | tf_op jit(solution)/shard_map/ppermute | solution.py:496
  87.1 7.2 %shard_map.145 = (bf16[128,1280]{1,0:T(8,128)(2,1)S(1)}, bf16[128,1280]{1,0:T(8,128)(2,1)S(1)}, bf16[128,1280]{1,0:T(8,128)(2,1)S(1)}, bf16[128,1280]{1,0:T(8,128)(2,1)S(1)}) custom-call(s32[12]{0:T(128)S(1)} %stack.51.info_ref, bf16[128,1280]{1,0:T(8,128)(2,1)S(1)} %copy-done.9, bf16[128,1280]{1,0:T(8,128)(2,1)S(1)} %collective-permute-done.29.refs_1_, ...), custom_call_target="tpu_custom_call" | custom-call | flops 1000 | bytes 1000 | tf_op jit(solution)/shard_map/pallas_call | solution.py:143
  94.4 1.6 %collective-permute-start.35 = (bf16[136,1280]{1,0:T(8,128)(2,1)S(1)}, bf16[136,1280]{1,0:T(8,128)(2,1)S(1)}, u32[]{:S(2)}, u32[]{:S(2)}) collective-permute-start(bf16[136,1280]{1,0:T(8,128)(2,1)S(1)} %get-tuple-element.191), channel_id=1, source_target_pairs={{0,8},{8,16},{16,24},{24,28},{28,20},{20,12},{12,4},{4,0},{1,9},{9... | collective-permute-start | bytes 1044488 | tf_op jit(solution)/shard_map/ppermute | solution.py:496
  99.1 5.6 %collective-permute-done.35 = bf16[136,1280]{1,0:T(8,128)(2,1)S(1)} collective-permute-done((bf16[136,1280]{1,0:T(8,128)(2,1)S(1)}, bf16[136,1280]{1,0:T(8,128)(2,1)S(1)}, u32[]{:S(2)}, u32[]{:S(2)}) %collective-permute-start.35) | collective-permute-done | bytes 348192 | tf_op jit(solution)/shard_map/ppermute | solution.py:496
  106.1 1.9 %collective-permute-done.34 = bf16[128,1280]{1,0:T(8,128)(2,1)S(1)} collective-permute-done((bf16[128,1280]{1,0:T(8,128)(2,1)S(1)}, bf16[128,1280]{1,0:T(8,128)(2,1)S(1)}, u32[]{:S(2)}, u32[]{:S(2)}) %collective-permute-start.34) | collective-permute-done | bytes 327712 | tf_op jit(solution)/shard_map/ppermute | solution.py:490
  (105 shorter events, 21.9 us)
Async XLA Ops:
  1.9 11.4 %collective-permute-start.1 = (bf16[136,1280]{1,0:T(8,128)(2,1)}, bf16[136,1280]{1,0:T(8,128)(2,1)S(1)}, u32[]{:S(2)}, u32[]{:S(2)}) collective-permute-start(bf16[136,1280]{1,0:T(8,128)(2,1)} %shard_map.127.refs_0_), channel_id=1, source_target_pairs={{0,4},{8,0},{16,8},{24,16},{28,24},{20,28},{12,20},{4,12},{1,5},{9... | collective-permute-start | bytes 1044488 | tf_op jit(solution)/shard_map/ppermute | solution.py:496
  4.9 9.8 %collective-permute-start = (bf16[136,1280]{1,0:T(8,128)(2,1)}, bf16[136,1280]{1,0:T(8,128)(2,1)S(1)}, u32[]{:S(2)}, u32[]{:S(2)}) collective-permute-start(bf16[136,1280]{1,0:T(8,128)(2,1)} %shard_map.127.refs_0_), channel_id=1, source_target_pairs={{0,8},{8,16},{16,24},{24,28},{28,20},{20,12},{12,4},{4,0},{1,9},{9... | collective-permute-start | bytes 1044488 | tf_op jit(solution)/shard_map/ppermute | solution.py:496
  14.7 8.7 %collective-permute-start.2 = (bf16[136,1280]{1,0:T(8,128)(2,1)S(1)}, bf16[136,1280]{1,0:T(8,128)(2,1)S(1)}, u32[]{:S(2)}, u32[]{:S(2)}) collective-permute-start(bf16[136,1280]{1,0:T(8,128)(2,1)S(1)} %collective-permute-done.refs_1_), channel_id=1, source_target_pairs={{0,8},{8,16},{16,24},{24,28},{28,20},{20,12},{12,4},{4,0},{1,9},{9... | collective-permute-start | bytes 1044488 | tf_op jit(solution)/shard_map/ppermute | solution.py:496
  15.1 8.7 %collective-permute-start.3 = (bf16[136,1280]{1,0:T(8,128)(2,1)S(1)}, bf16[136,1280]{1,0:T(8,128)(2,1)S(1)}, u32[]{:S(2)}, u32[]{:S(2)}) collective-permute-start(bf16[136,1280]{1,0:T(8,128)(2,1)S(1)} %collective-permute-done.1.refs_2_), channel_id=1, source_target_pairs={{0,4},{8,0},{16,8},{24,16},{28,24},{20,28},{12,20},{4,12},{1,5},{9... | collective-permute-start | bytes 1044488 | tf_op jit(solution)/shard_map/ppermute | solution.py:496
  23.9 10.6 %collective-permute-start.4 = (bf16[136,1280]{1,0:T(8,128)(2,1)S(1)}, bf16[136,1280]{1,0:T(8,128)(2,1)S(1)}, u32[]{:S(2)}, u32[]{:S(2)}) collective-permute-start(bf16[136,1280]{1,0:T(8,128)(2,1)S(1)} %collective-permute-done.2.refs_0_), channel_id=1, source_target_pairs={{0,8},{8,16},{16,24},{24,28},{28,20},{20,12},{12,4},{4,0},{1,9},{9... | collective-permute-start | bytes 1044488 | tf_op jit(solution)/shard_map/ppermute | solution.py:496
  25.4 10.3 %collective-permute-start.5 = (bf16[136,1280]{1,0:T(8,128)(2,1)S(1)}, bf16[136,1280]{1,0:T(8,128)(2,1)S(1)}, u32[]{:S(2)}, u32[]{:S(2)}) collective-permute-start(bf16[136,1280]{1,0:T(8,128)(2,1)S(1)} %collective-permute-done.3.refs_1_), channel_id=1, source_target_pairs={{0,4},{8,0},{16,8},{24,16},{28,24},{20,28},{12,20},{4,12},{1,5},{9... | collective-permute-start | bytes 1044488 | tf_op jit(solution)/shard_map/ppermute | solution.py:496
  26.0 16.8 %collective-permute-start.10 = (bf16[192,768]{1,0:T(8,128)(2,1)S(1)}, bf16[192,768]{1,0:T(8,128)(2,1)S(1)}, u32[]{:S(2)}, u32[]{:S(2)}) collective-permute-start(bf16[192,768]{1,0:T(8,128)(2,1)S(1)} %shard_map.129.refs_0_), channel_id=1, source_target_pairs={{0,2},{1,3},{2,0},{3,1},{4,6},{5,7},{6,4},{7,5},{8,10},{9,11},{10,... | collective-permute-start | bytes 884744 | tf_op jit(solution)/shard_map/ppermute | solution.py:490
  35.7 4.1 %collective-permute-start.9 = (bf16[128,768]{1,0:T(8,128)(2,1)S(1)}, bf16[128,768]{1,0:T(8,128)(2,1)S(1)}, u32[]{:S(2)}, u32[]{:S(2)}) collective-permute-start(bf16[128,768]{1,0:T(8,128)(2,1)S(1)} %get-tuple-element.116), channel_id=1, source_target_pairs={{0,1},{1,0},{2,3},{3,2},{4,5},{5,4},{6,7},{7,6},{8,9},{9,8},{10,11... | collective-permute-start | bytes 589832 | tf_op jit(solution)/shard_map/ppermute | solution.py:493
  35.7 7.1 %collective-permute-start.8 = (bf16[72,1280]{1,0:T(8,128)(2,1)S(1)}, bf16[72,1280]{1,0:T(8,128)(2,1)S(1)}, u32[]{:S(2)}, u32[]{:S(2)}) collective-permute-start(bf16[72,1280]{1,0:T(8,128)(2,1)S(1)} %get-tuple-element.114), channel_id=1, source_target_pairs={{0,4},{8,0},{16,8},{24,16},{28,24},{20,28},{12,20},{4,12},{1,5},{9... | collective-permute-start | bytes 552968 | tf_op jit(solution)/shard_map/ppermute | solution.py:496
  36.3 6.3 %collective-permute-start.7 = (bf16[64,1280]{1,0:T(8,128)(2,1)S(1)}, bf16[64,1280]{1,0:T(8,128)(2,1)S(1)}, u32[]{:S(2)}, u32[]{:S(2)}) collective-permute-start(bf16[64,1280]{1,0:T(8,128)(2,1)S(1)} %get-tuple-element.113), channel_id=1, source_target_pairs={{0,8},{8,16},{16,24},{24,28},{28,20},{20,12},{12,4},{4,0},{1,9},{9... | collective-permute-start | bytes 491528 | tf_op jit(solution)/shard_map/ppermute | solution.py:496
  42.9 7.4 %collective-permute-start.14 = (bf16[192,768]{1,0:T(8,128)(2,1)S(1)}, bf16[192,768]{1,0:T(8,128)(2,1)S(1)}, u32[]{:S(2)}, u32[]{:S(2)}) collective-permute-start(bf16[192,768]{1,0:T(8,128)(2,1)S(1)} %shard_map.136.refs_0_), channel_id=1, source_target_pairs={{0,1},{1,0},{2,3},{3,2},{4,5},{5,4},{6,7},{7,6},{8,9},{9,8},{10,11... | collective-permute-start | bytes 884744 | tf_op jit(solution)/shard_map/ppermute | solution.py:493
  43.0 7.3 %collective-permute-start.12 = (bf16[128,768]{1,0:T(8,128)(2,1)S(1)}, bf16[128,768]{1,0:T(8,128)(2,1)S(1)}, u32[]{:S(2)}, u32[]{:S(2)}) collective-permute-start(bf16[128,768]{1,0:T(8,128)(2,1)S(1)} %shard_map.132.refs_2_), channel_id=1, source_target_pairs={{0,2},{1,3},{2,0},{3,1},{4,6},{5,7},{6,4},{7,5},{8,10},{9,11},{10,... | collective-permute-start | bytes 589832 | tf_op jit(solution)/shard_map/ppermute | solution.py:490
  44.5 5.8 %collective-permute-start.13 = (bf16[128,768]{1,0:T(8,128)(2,1)S(1)}, bf16[128,768]{1,0:T(8,128)(2,1)S(1)}, u32[]{:S(2)}, u32[]{:S(2)}) collective-permute-start(bf16[128,768]{1,0:T(8,128)(2,1)S(1)} %get-tuple-element.123), channel_id=1, source_target_pairs={{0,1},{1,0},{2,3},{3,2},{4,5},{5,4},{6,7},{7,6},{8,9},{9,8},{10,11... | collective-permute-start | bytes 589832 | tf_op jit(solution)/shard_map/ppermute | solution.py:493
  50.4 5.3 %collective-permute-start.16 = (bf16[128,768]{1,0:T(8,128)(2,1)S(1)}, bf16[128,768]{1,0:T(8,128)(2,1)S(1)}, u32[]{:S(2)}, u32[]{:S(2)}) collective-permute-start(bf16[128,768]{1,0:T(8,128)(2,1)S(1)} %get-tuple-element.146.refs_3_), channel_id=1, source_target_pairs={{0,1},{1,0},{2,3},{3,2},{4,5},{5,4},{6,7},{7,6},{8,9},{9,8},{10,11... | collective-permute-start | bytes 589832 | tf_op jit(solution)/shard_map/ppermute | solution.py:493
  50.5 5.2 %collective-permute-start.15 = (bf16[64,768]{1,0:T(8,128)(2,1)S(1)}, bf16[64,768]{1,0:T(8,128)(2,1)S(1)}, u32[]{:S(2)}, u32[]{:S(2)}) collective-permute-start(bf16[64,768]{1,0:T(8,128)(2,1)S(1)} %shard_map.135.refs_0_), channel_id=1, source_target_pairs={{0,2},{1,3},{2,0},{3,1},{4,6},{5,7},{6,4},{7,5},{8,10},{9,11},{10,... | collective-permute-start | bytes 294920 | tf_op jit(solution)/shard_map/ppermute | solution.py:490
  55.7 6.7 %collective-permute-start.18 = (bf16[128,768]{1,0:T(8,128)(2,1)S(1)}, bf16[128,768]{1,0:T(8,128)(2,1)S(1)}, u32[]{:S(2)}, u32[]{:S(2)}) collective-permute-start(bf16[128,768]{1,0:T(8,128)(2,1)S(1)} %get-tuple-element.139.refs_0_), channel_id=1, source_target_pairs={{0,2},{1,3},{2,0},{3,1},{4,6},{5,7},{6,4},{7,5},{8,10},{9,11},{10,... | collective-permute-start | bytes 589832 | tf_op jit(solution)/shard_map/ppermute | solution.py:490
  62.4 12.0 %collective-permute-start.24 = (bf16[128,1280]{1,0:T(8,128)(2,1)S(1)}, bf16[128,1280]{1,0:T(8,128)(2,1)S(1)}, u32[]{:S(2)}, u32[]{:S(2)}) collective-permute-start(bf16[128,1280]{1,0:T(8,128)(2,1)S(1)} %copy-done.9), channel_id=1, source_target_pairs={{0,2},{1,3},{2,0},{3,1},{4,6},{5,7},{6,4},{7,5},{8,10},{9,11},{10,... | collective-permute-start | bytes 983048 | tf_op jit(solution)/shard_map/ppermute | solution.py:490
  63.7 2.2 %collective-permute-start.21 = (bf16[128,768]{1,0:T(8,128)(2,1)S(1)}, bf16[128,768]{1,0:T(8,128)(2,1)S(1)}, u32[]{:S(2)}, u32[]{:S(2)}) collective-permute-start(bf16[128,768]{1,0:T(8,128)(2,1)S(1)} %shard_map.140.refs_0_), channel_id=1, source_target_pairs={{0,1},{1,0},{2,3},{3,2},{4,5},{5,4},{6,7},{7,6},{8,9},{9,8},{10,11... | collective-permute-start | bytes 589832 | tf_op jit(solution)/shard_map/ppermute | solution.py:493
  63.8 7.4 %collective-permute-start.20 = (bf16[72,1280]{1,0:T(8,128)(2,1)S(1)}, bf16[72,1280]{1,0:T(8,128)(2,1)S(1)}, u32[]{:S(2)}, u32[]{:S(2)}) collective-permute-start(bf16[72,1280]{1,0:T(8,128)(2,1)S(1)} %get-tuple-element.143), channel_id=1, source_target_pairs={{0,4},{8,0},{16,8},{24,16},{28,24},{20,28},{12,20},{4,12},{1,5},{9... | collective-permute-start | bytes 552968 | tf_op jit(solution)/shard_map/ppermute | solution.py:496
  64.9 6.3 %collective-permute-start.19 = (bf16[64,1280]{1,0:T(8,128)(2,1)S(1)}, bf16[64,1280]{1,0:T(8,128)(2,1)S(1)}, u32[]{:S(2)}, u32[]{:S(2)}) collective-permute-start(bf16[64,1280]{1,0:T(8,128)(2,1)S(1)} %get-tuple-element.142), channel_id=1, source_target_pairs={{0,8},{8,16},{16,24},{24,28},{28,20},{20,12},{12,4},{4,0},{1,9},{9... | collective-permute-start | bytes 491528 | tf_op jit(solution)/shard_map/ppermute | solution.py:496
  71.3 10.7 %collective-permute-start.22 = (bf16[136,1280]{1,0:T(8,128)(2,1)S(1)}, bf16[136,1280]{1,0:T(8,128)(2,1)S(1)}, u32[]{:S(2)}, u32[]{:S(2)}) collective-permute-start(bf16[136,1280]{1,0:T(8,128)(2,1)S(1)} %get-tuple-element.160), channel_id=1, source_target_pairs={{0,8},{8,16},{16,24},{24,28},{28,20},{20,12},{12,4},{4,0},{1,9},{9... | collective-permute-start | bytes 1044488 | tf_op jit(solution)/shard_map/ppermute | solution.py:496
  72.7 9.4 %collective-permute-start.23 = (bf16[136,1280]{1,0:T(8,128)(2,1)S(1)}, bf16[136,1280]{1,0:T(8,128)(2,1)S(1)}, u32[]{:S(2)}, u32[]{:S(2)}) collective-permute-start(bf16[136,1280]{1,0:T(8,128)(2,1)S(1)} %get-tuple-element.161), channel_id=1, source_target_pairs={{0,4},{8,0},{16,8},{24,16},{28,24},{20,28},{12,20},{4,12},{1,5},{9... | collective-permute-start | bytes 1044488 | tf_op jit(solution)/shard_map/ppermute | solution.py:496
  73.6 8.4 %collective-permute-start.26 = (bf16[128,1280]{1,0:T(8,128)(2,1)S(1)}, bf16[128,1280]{1,0:T(8,128)(2,1)S(1)}, u32[]{:S(2)}, u32[]{:S(2)}) collective-permute-start(bf16[128,1280]{1,0:T(8,128)(2,1)S(1)} %copy-done.8), channel_id=1, source_target_pairs={{0,2},{1,3},{2,0},{3,1},{4,6},{5,7},{6,4},{7,5},{8,10},{9,11},{10,... | collective-permute-start | bytes 983048 | tf_op jit(solution)/shard_map/ppermute | solution.py:490
  74.4 7.8 %collective-permute-start.25 = (bf16[128,1280]{1,0:T(8,128)(2,1)S(1)}, bf16[128,1280]{1,0:T(8,128)(2,1)S(1)}, u32[]{:S(2)}, u32[]{:S(2)}) collective-permute-start(bf16[128,1280]{1,0:T(8,128)(2,1)S(1)} %collective-permute-done.24.refs_2_), channel_id=1, source_target_pairs={{0,1},{1,0},{2,3},{3,2},{4,5},{5,4},{6,7},{7,6},{8,9},{9,8},{10,11... | collective-permute-start | bytes 983048 | tf_op jit(solution)/shard_map/ppermute | solution.py:493
  82.3 11.9 %collective-permute-start.27 = (bf16[136,1280]{1,0:T(8,128)(2,1)S(1)}, bf16[136,1280]{1,0:T(8,128)(2,1)S(1)}, u32[]{:S(2)}, u32[]{:S(2)}) collective-permute-start(bf16[136,1280]{1,0:T(8,128)(2,1)S(1)} %get-tuple-element.173), channel_id=1, source_target_pairs={{0,8},{8,16},{16,24},{24,28},{28,20},{20,12},{12,4},{4,0},{1,9},{9... | collective-permute-start | bytes 1044488 | tf_op jit(solution)/shard_map/ppermute | solution.py:496
  83.9 10.3 %collective-permute-start.28 = (bf16[136,1280]{1,0:T(8,128)(2,1)S(1)}, bf16[136,1280]{1,0:T(8,128)(2,1)S(1)}, u32[]{:S(2)}, u32[]{:S(2)}) collective-permute-start(bf16[136,1280]{1,0:T(8,128)(2,1)S(1)} %get-tuple-element.174), channel_id=1, source_target_pairs={{0,4},{8,0},{16,8},{24,16},{28,24},{20,28},{12,20},{4,12},{1,5},{9... | collective-permute-start | bytes 1044488 | tf_op jit(solution)/shard_map/ppermute | solution.py:496
  84.4 2.1 %collective-permute-start.29 = (bf16[128,1280]{1,0:T(8,128)(2,1)S(1)}, bf16[128,1280]{1,0:T(8,128)(2,1)S(1)}, u32[]{:S(2)}, u32[]{:S(2)}) collective-permute-start(bf16[128,1280]{1,0:T(8,128)(2,1)S(1)} %copy-done.9), channel_id=1, source_target_pairs={{0,1},{1,0},{2,3},{3,2},{4,5},{5,4},{6,7},{7,6},{8,9},{9,8},{10,11... | collective-permute-start | bytes 983048 | tf_op jit(solution)/shard_map/ppermute | solution.py:493
  84.9 2.1 %collective-permute-start.31 = (bf16[128,1280]{1,0:T(8,128)(2,1)S(1)}, bf16[128,1280]{1,0:T(8,128)(2,1)S(1)}, u32[]{:S(2)}, u32[]{:S(2)}) collective-permute-start(bf16[128,1280]{1,0:T(8,128)(2,1)S(1)} %collective-permute-done.26.refs_6_), channel_id=1, source_target_pairs={{0,1},{1,0},{2,3},{3,2},{4,5},{5,4},{6,7},{7,6},{8,9},{9,8},{10,11... | collective-permute-start | bytes 983048 | tf_op jit(solution)/shard_map/ppermute | solution.py:493
  94.4 10.2 %collective-permute-start.35 = (bf16[136,1280]{1,0:T(8,128)(2,1)S(1)}, bf16[136,1280]{1,0:T(8,128)(2,1)S(1)}, u32[]{:S(2)}, u32[]{:S(2)}) collective-permute-start(bf16[136,1280]{1,0:T(8,128)(2,1)S(1)} %get-tuple-element.191), channel_id=1, source_target_pairs={{0,8},{8,16},{16,24},{24,28},{28,20},{20,12},{12,4},{4,0},{1,9},{9... | collective-permute-start | bytes 1044488 | tf_op jit(solution)/shard_map/ppermute | solution.py:496
  96.0 9.9 %collective-permute-start.36 = (bf16[136,1280]{1,0:T(8,128)(2,1)S(1)}, bf16[136,1280]{1,0:T(8,128)(2,1)S(1)}, u32[]{:S(2)}, u32[]{:S(2)}) collective-permute-start(bf16[136,1280]{1,0:T(8,128)(2,1)S(1)} %get-tuple-element.192), channel_id=1, source_target_pairs={{0,4},{8,0},{16,8},{24,16},{28,24},{20,28},{12,20},{4,12},{1,5},{9... | collective-permute-start | bytes 1044488 | tf_op jit(solution)/shard_map/ppermute | solution.py:496
  96.5 9.6 %collective-permute-start.32 = (bf16[128,1280]{1,0:T(8,128)(2,1)S(1)}, bf16[128,1280]{1,0:T(8,128)(2,1)S(1)}, u32[]{:S(2)}, u32[]{:S(2)}) collective-permute-start(bf16[128,1280]{1,0:T(8,128)(2,1)S(1)} %get-tuple-element.183), channel_id=1, source_target_pairs={{0,1},{1,0},{2,3},{3,2},{4,5},{5,4},{6,7},{7,6},{8,9},{9,8},{10,11... | collective-permute-start | bytes 983048 | tf_op jit(solution)/shard_map/ppermute | solution.py:493
  98.2 9.8 %collective-permute-start.34 = (bf16[128,1280]{1,0:T(8,128)(2,1)S(1)}, bf16[128,1280]{1,0:T(8,128)(2,1)S(1)}, u32[]{:S(2)}, u32[]{:S(2)}) collective-permute-start(bf16[128,1280]{1,0:T(8,128)(2,1)S(1)} %shard_map.146), channel_id=1, source_target_pairs={{0,2},{1,3},{2,0},{3,1},{4,6},{5,7},{6,4},{7,5},{8,10},{9,11},{10,... | collective-permute-start | bytes 983048 | tf_op jit(solution)/shard_map/ppermute | solution.py:490
  (22 other events, 335.8 us)

commit v4 on v3

--- a/solution.py
+++ b/solution.py
@@ -250,9 +250,10 @@
     )(ids_t, probs_t, grad)
 
 
-def hidden_kernel(halves, tiles, capacity, info_ref, *refs):
+def hidden_kernel(halves, tiles, capacity, steps, info_ref, *refs):
     block_refs = refs[: len(halves)]
-    weight_ref, other_ref, mine_ref, meta_ref, placed_ref = refs[len(halves) :]
+    weight_ref, placed_ref = refs[len(halves)], refs[-1]
+    out_refs = refs[len(halves) + 1 : -1]
     core, tile, row = info_ref[0], info_ref[1], info_ref[2]
     blocks, at = [], 0
     while at < len(halves):
@@ -271,7 +272,7 @@
         return jnp.sum(jnp.where(line == which, value, 0.0), axis=0, keepdims=True)
 
     slot_at = lax.broadcasted_iota(jnp.int32, (capacity, rows), 0).astype(F32)
-    for step in range(2):
+    for step in steps:
         expert = 1 - core if step == 0 else core
         for b, block in enumerate(blocks):
             last = block[-1]
@@ -288,8 +289,8 @@
                 lines += [pick(meta, 1, row) + pick(meta, 2, row)]
                 lines += [pick(meta, 1, row + 1) + pick(meta, 2, row + 1)]
                 lines += [jnp.zeros((4, rows), F32)]
-                meta_ref[8 * b : 8 * b + 8, :] = jnp.concatenate(lines, axis=0)
-        out_ref = other_ref if step == 0 else mine_ref
+                out_refs[-1][8 * b : 8 * b + 8, :] = jnp.concatenate(lines, axis=0)
+        out_ref = out_refs[steps.index(step)]
         for n in range(0, units, 256):
             value = lax.dot_general(
                 placed_ref[step],
@@ -300,7 +301,7 @@
             out_ref[:, n : n + 256] = value.astype(BF16)
 
 
-def hidden_part(info, blocks, down_weight, tiles, capacity):
+def hidden_part(info, blocks, down_weight, tiles, capacity, steps):
     local_count, hidden_units, cols = down_weight.shape
     flat, halves = [], []
     for block in blocks:
@@ -310,13 +311,10 @@
     count = len(blocks)
     shape = (count * capacity, hidden_units)
     return call(
-        functools.partial(hidden_kernel, halves, tiles, capacity),
+        functools.partial(hidden_kernel, halves, tiles, capacity, steps),
         10,
-        [
-            jax.ShapeDtypeStruct(shape, BF16),
-            jax.ShapeDtypeStruct(shape, BF16),
-            jax.ShapeDtypeStruct((8 * count, 128), F32),
-        ],
+        [jax.ShapeDtypeStruct(shape, BF16)] * len(steps)
+        + [jax.ShapeDtypeStruct((8 * count, 128), F32)] * (1 in steps),
         [pltpu.VMEM((2, count * capacity, cols), BF16)],
         1,
     )(info, *flat, down_weight)
@@ -408,17 +406,19 @@
     )(info, *parts, *saved, *weights)
 
 
-def shared_kernel(info_ref, *refs):
+def shared_spans(info_ref, cols):
+    here = info_ref[3]
+    return [
+        pl.ds(pl.multiple_of(jnp.bitwise_xor(here, q) * cols, cols), cols) for q in range(4)
+    ]
+
+
+def shared_slopes_kernel(info_ref, *refs):
     token_refs, grad_refs = refs[0:4], refs[4:8]
-    gate_ref, up_ref, down_ref = refs[8:11]
-    out_refs = refs[11:15]
-    here = info_ref[3]
+    gate_ref, up_ref, down_ref, dgate_ref, dup_ref = refs[8:]
     rows, cols = token_refs[0].shape
     units = gate_ref.shape[1]
-    spans = []
-    for q in range(4):
-        at = pl.multiple_of(jnp.bitwise_xor(here, q) * cols, cols)
-        spans.append(pl.ds(at, cols))
+    spans = shared_spans(info_ref, cols)
     gate_pre = jnp.zeros((rows, units), F32)
     up_pre = jnp.zeros((rows, units), F32)
     hidden_pre = jnp.zeros((rows, units), F32)
@@ -430,23 +430,32 @@
             grad, down_ref[:, spans[q]], LAST, preferred_element_type=F32
         )
     active, slope_term = silu_parts(gate_pre)
-    dgate = (hidden_pre * up_pre * slope_term).astype(BF16)
-    dup = (hidden_pre * active).astype(BF16)
+    dgate_ref[...] = (hidden_pre * up_pre * slope_term).astype(BF16)
+    dup_ref[...] = (hidden_pre * active).astype(BF16)
+
+
+def shared_slopes(info, token_blocks, grad_blocks, shared_gate, shared_up, shared_down):
+    shape = jax.ShapeDtypeStruct((token_blocks[0].shape[0], shared_gate.shape[1]), BF16)
+    return call(shared_slopes_kernel, 8, [shape, shape], (), 1)(
+        info, *token_blocks, *grad_blocks, shared_gate, shared_up, shared_down
+    )
+
+
+def shared_terms_kernel(info_ref, dgate_ref, dup_ref, gate_ref, up_ref, *out_refs):
+    cols = out_refs[0].shape[1]
+    spans = shared_spans(info_ref, cols)
+    dgate, dup = dgate_ref[...], dup_ref[...]
     for q in range(4):
         term = lax.dot_general(dgate, gate_ref[spans[q], :], LAST, preferred_element_type=F32)
         term = term + lax.dot_general(dup, up_ref[spans[q], :], LAST, preferred_element_type=F32)
         out_refs[q][...] = term.astype(BF16)
 
 
-def shared_part_terms(here, token_blocks, grad_blocks, shared_gate, shared_up, shared_down):
-    rows, cols = token_blocks[0].shape
-    return call(
-        shared_kernel,
-        10,
-        [jax.ShapeDtypeStruct((rows, cols), BF16)] * 4,
-        (),
-        1,
-    )(here, *token_blocks, *grad_blocks, shared_gate, shared_up, shared_down)
+def shared_terms(info, dgate, dup, shared_gate, shared_up, cols):
+    shape = jax.ShapeDtypeStruct((dgate.shape[0], cols), BF16)
+    return call(shared_terms_kernel, 8, [shape] * 4, (), 1)(
+        info, dgate, dup, shared_gate, shared_up
+    )
 
 
 def ring_place(position):
@@ -495,8 +504,8 @@
     def ring(fore, back):
         return lax.ppermute(fore, "expert", ahead), lax.ppermute(back, "expert", behind)
 
-    def hidden(blocks):
-        return hidden_part(info, blocks, down_weight, tiles, capacity)
+    def hidden(blocks, steps=(0, 1)):
+        return hidden_part(info, blocks, down_weight, tiles, capacity, steps)
 
     def grads(saved, weights, *parts):
         chunk = sum((part[0] for part in parts), ())
@@ -518,82 +527,87 @@
 
     payload, tokens, out_grad, info = tie((payload, tokens, out_grad, info))
     fore, back = ring(payload, payload)
-    fore1, back1 = tie((fore, back))
+    grad_x = swap_x(out_grad)
+    fore1, back1, grad_x = tie((fore, back, grad_x))
 
     fore, back = ring(fore1, back1)
+    tok_x = swap_x(tokens)
     other1, mine1, meta1 = hidden([payload, fore1, back1])
-    fore2, back2, other1, mine1 = tie((fore, back, other1, mine1))
+    fore2, back2, other1, mine1, tok_x = tie((fore, back, other1, mine1, tok_x))
 
     fore, back = ring(fore2, back2)
     (chip1,) = sums((mine1, swap_core(other1)))
     far1 = swap_x(chip1)
     other2, mine2, meta2 = hidden([fore2, back2])
-    fore3, back3, chip1, other2, mine2 = tie((fore, back, chip1, other2, mine2))
+    (chip2,) = sums((mine2, swap_core(other2)))
+    tok_core, grad_core = swap_core(tokens), swap_core(out_grad)
+    fore3, back3, chip1, chip2, tok_core, grad_core = tie(
+        (fore, back, chip1, chip2, tok_core, grad_core)
+    )
 
     top, bottom = ring(*halves_of(fore3, back3))
-    (chip2,) = sums((mine2, swap_core(other2)))
     far2 = swap_x(chip2)
     other3, mine3, meta3 = hidden([fore3, back3])
-    top, bottom, chip2, other3, mine3, far1 = tie((top, bottom, chip2, other3, mine3, far1))
-
-    other4, mine4, meta4 = hidden([(top, bottom)])
-    swapped4, swapped3 = swap_core(other4), swap_core(other3)
-    (full1,) = sums((chip1, far1))
-    pair1 = swap_core(full1)
+    tok_both, grad_both = swap_core(tok_x), swap_core(grad_x)
+    top, bottom, chip2, other3, mine3, far1, far2, tok_both, grad_both = tie(
+        (top, bottom, chip2, other3, mine3, far1, far2, tok_both, grad_both)
+    )
+
+    (other4,) = hidden([(top, bottom)], (0,))
+    swapped4 = swap_core(other4)
+    top, bottom, other4 = tie((top, bottom, other4))
+    mine4, meta4 = hidden([(top, bottom)], (1,))
     (chip4,) = sums((mine4, swapped4))
-    chip4, far2, swapped3, pair1 = tie((chip4, far2, swapped3, pair1))
+    chip4, other3, dgate_in = tie((chip4, other3, tokens))
     far4 = swap_x(chip4)
-    chip3, full2 = sums((mine3, swapped3), (chip2, far2))
+    (chip3,) = sums((mine3, swap_core(other3)))
+    far3 = swap_x(chip3)
+    chip3, chip2 = tie((chip3, chip2))
+    (full2,) = sums((chip2, far2))
     pair2 = swap_core(full2)
-    far4, chip3, full2, pair2 = tie((far4, chip3, full2, pair2))
-    (full4,) = sums((chip4, far4))
-    pair4 = swap_core(full4)
-    far3 = swap_x(chip3)
-    pair4, full4 = tie((pair4, full4))
-    saved = (gate_saved, up_saved)
-    weights = (gate_weight, up_weight)
-    top, bottom = grads(saved, weights, ((4,), full4, pair4, meta4))
-
-    top, bottom, far3, tokens, out_grad = tie((top, bottom, far3, tokens, out_grad))
-    fore, back = ring(top, bottom)
-    tok_x = swap_x(tokens)
-    tok_core, grad_core = swap_core(tokens), swap_core(out_grad)
-    (full3,) = sums((chip3, far3))
-    pair3 = swap_core(full3)
-    near_b3, near_f3, near_b2, near_f2 = grads(
-        saved, weights, ((-3, 3), full3, pair3, meta3), ((-2, 2), full2, pair2, meta2)
-    )
-    fore, back, near_f3, near_b3, near_f2, near_b2, full1, pair1, out_grad = tie(
-        (fore, back, near_f3, near_b3, near_f2, near_b2, full1, pair1, out_grad)
-    )
-
-    fore, back = join(near_f3, fore, near_b3, back)
-    fore, back = ring(fore, back)
-    grad_x = swap_x(out_grad)
-    tok_both = swap_core(tok_x)
-    near0, near_b1, near_f1 = grads(saved, weights, ((0, -1, 1), full1, pair1, meta1))
-    fore, back, near0, near_b1, near_f1, tok_x, tok_both, grad_x = tie(
-        (fore, back, near0, near_b1, near_f1, tok_x, tok_both, grad_x)
-    )
-
-    fore, back = sums((near_f2, fore), (near_b2, back))
-    fore, back = ring(fore, back)
-    grad_both = swap_core(grad_x)
-    terms = shared_part_terms(
+    dgate, dup = shared_slopes(
         info,
-        [tokens, tok_core, tok_x, tok_both],
+        [dgate_in, tok_core, tok_x, tok_both],
         [out_grad, grad_core, grad_x, grad_both],
         shared_gate,
         shared_up,
         shared_down,
     )
-    fore, back, *terms = tie((fore, back, *terms))
-
-    swapped = swap_core(terms[3])
-    near = swap_core(terms[1])
-    fore, back = sums((near_f1, fore), (near_b1, back))
+    far4, full2, pair2, dgate, dup = tie((far4, full2, pair2, dgate, dup))
+    (full4,) = sums((chip4, far4))
+    pair4 = swap_core(full4)
+    saved = (gate_saved, up_saved)
+    weights = (gate_weight, up_weight)
+    top, bottom = grads(saved, weights, ((4,), full4, pair4, meta4))
+
+    top, bottom, pair2, full2, far3, chip1 = tie((top, bottom, pair2, full2, far3, chip1))
+    fore, back = ring(top, bottom)
+    (full3,) = sums((chip3, far3))
+    pair3 = swap_core(full3)
+    (full1,) = sums((chip1, far1))
+    pair1 = swap_core(full1)
+    near_b3, near_f3, near_b2, near_f2 = grads(
+        saved, weights, ((-3, 3), full3, pair3, meta3), ((-2, 2), full2, pair2, meta2)
+    )
+    fore, back, near_f3, near_b3, near_f2, near_b2, full1, pair1 = tie(
+        (fore, back, near_f3, near_b3, near_f2, near_b2, full1, pair1)
+    )
+
+    fore, back = join(near_f3, fore, near_b3, back)
     fore, back = ring(fore, back)
-    (far,) = sums((terms[2], swapped))
+    near0, near_b1, near_f1 = grads(saved, weights, ((0, -1, 1), full1, pair1, meta1))
+    fore, back, near0, near_b1, near_f1, dgate = tie(
+        (fore, back, near0, near_b1, near_f1, dgate)
+    )
+
+    fore, back = sums((near_f2, fore), (near_b2, back))
+    fore, back = ring(fore, back)
+    terms = shared_terms(info, dgate, dup, shared_gate, shared_up, cols)
+    swapped, near = swap_core(terms[3]), swap_core(terms[1])
+    fore, back, swapped, near = tie((fore, back, swapped, near))
+
+    fore, back, far = sums((near_f1, fore), (near_b1, back), (terms[2], swapped))
+    fore, back = ring(fore, back)
     shared_far = swap_x(far)
     total = near0.astype(F32) + fore.astype(F32) + back.astype(F32)
     shared_part = terms[0].astype(F32) + near.astype(F32) + shared_far.astype(F32)

time: 109 us -> 99.8 us (0.916)
  waiting for transfers between devices: 45.2 us -> 32.2 us
  starting transfers between devices: 28.7 us -> 30.9 us
  Pallas kernels: 30.3 us -> 31.7 us
    ppermute x8, waiting for transfers between devices: 16.9 us -> 8.96 us  [ring(): lax.ppermute(fore, 'expert', ahead)]
    ppermute x8, starting transfers between devices: 8.71 us -> 4.02 us  [ring(): lax.ppermute(back, 'expert', behind)]
    ppermute x8, starting transfers between devices: 9.05 us -> 13.5 us  [ring(): lax.ppermute(fore, 'expert', ahead)]
    ppermute x7, waiting for transfers between devices: 11.3 us -> 8.74 us  [swap_x(): return lax.ppermute(a, 'tensor', x_pairs)]
    ppermute x8, waiting for transfers between devices: 11.6 us -> 9.63 us  [ring(): lax.ppermute(back, 'expert', behind)]
    ppermute x14, starting transfers between devices: 1.89 us -> 3.52 us  [swap_core(): return lax.ppermute(a, 'tensor', core_pairs)]
    pallas_call x21 -> x23, Pallas kernels: 30.3 us -> 31.7 us  [run(): pl.pallas_call(kernel, in_specs=[pl.BlockSpec(memory_space=m) for m in me...]
    unnamed x34 -> x32, local copies, waits for them, and re-layouts: 3.17 us -> 3.17 us
  transfers between devices with their start and end apart: 37 -> 37, of which waited for: 22 -> 20; matrix products, arithmetic and copies ran while one was open for 0% -> 0% of each run, Pallas kernels for 26% -> 28%
where the time goes in v4:
time: 99.8 us; the launch traced here: 99.6 us
  waiting for transfers between devices  32.2 us (32%)
  Pallas kernels  31.7 us (32%)
  starting transfers between devices  30.9 us (31%)
  local copies, waits for them, and re-layouts  3.26 us (3%)
  matrix products  1.01 us (1%)
    pallas_call x23, Pallas kernels, run(): pl.pallas_call(kernel, in_specs=[pl.BlockSpec(memory_space=m) for m in me...  31.7 us
    ppermute x8, starting transfers between devices, ring(): lax.ppermute(fore, 'expert', ahead)  13.5 us
    ppermute x7, starting transfers between devices, swap_x(): return lax.ppermute(a, 'tensor', x_pairs)  9.9 us
    ppermute x8, waiting for transfers between devices, ring(): lax.ppermute(back, 'expert', behind)  9.63 us
    ppermute x8, waiting for transfers between devices, ring(): lax.ppermute(fore, 'expert', ahead)  8.96 us
    ppermute x7, waiting for transfers between devices, swap_x(): return lax.ppermute(a, 'tensor', x_pairs)  8.74 us
    ppermute x14, waiting for transfers between devices, swap_core(): return lax.ppermute(a, 'tensor', core_pairs)  4.88 us
    ppermute x8, starting transfers between devices, ring(): lax.ppermute(back, 'expert', behind)  4.02 us
  transfers between devices with their start and end apart: 37, of which 20 were waited for; matrix products, arithmetic and copies ran while one was open for 0% of the time, Pallas kernels for 28%

profile of v4, /device:TPU:0, one launch (start us, length us, event | category | flops | bytes accessed | tf_op | source)
XLA Modules:
  0.0 99.6 jit_solution(14971406890807611615)
XLA Ops:
  0.0 1.8 %shard_map.127.refs_0_ = bf16[136,1280]{1,0:T(8,128)(2,1)} custom-call(s32[6,128]{1,0:T(8,128)} %bitcast.29, f32[16,128]{1,0:T(8,128)} %bitcast.28, bf16[128,1280]{1,0:T(8,128)(2,1)} %refs_4_.2), custom_call_target="tpu_custom_call" | custom-call | flops 1000 | bytes 1000 | tf_op jit(solution)/shard_map/pallas_call | solution.py:143
  1.9 3.1 %collective-permute-start = (bf16[136,1280]{1,0:T(8,128)(2,1)}, bf16[136,1280]{1,0:T(8,128)(2,1)S(1)}, u32[]{:S(2)}, u32[]{:S(2)}) collective-permute-start(bf16[136,1280]{1,0:T(8,128)(2,1)} %shard_map.127.refs_0_), channel_id=1, source_target_pairs={{0,8},{8,16},{16,24},{24,28},{28,20},{20,12},{12,4},{4,0},{1,9},{9... | collective-permute-start | bytes 1044488 | tf_op jit(solution)/shard_map/ppermute | solution.py:505
  5.0 1.9 %collective-permute-start.2 = (bf16[128,1280]{1,0:T(8,128)(2,1)}, bf16[128,1280]{1,0:T(8,128)(2,1)S(1)}, u32[]{:S(2)}, u32[]{:S(2)}) collective-permute-start(bf16[128,1280]{1,0:T(8,128)(2,1)} %refs_4_.2), channel_id=1, source_target_pairs={{0,2},{1,3},{2,0},{3,1},{4,6},{5,7},{6,4},{7,5},{8,10},{9,11},{10,... | collective-permute-start | bytes 983048 | tf_op jit(solution)/shard_map/ppermute | solution.py:499
  6.9 7.4 %collective-permute-done.2.refs_6_ = bf16[128,1280]{1,0:T(8,128)(2,1)S(1)} collective-permute-done((bf16[128,1280]{1,0:T(8,128)(2,1)}, bf16[128,1280]{1,0:T(8,128)(2,1)S(1)}, u32[]{:S(2)}, u32[]{:S(2)}) %collective-permute-start.2) | collective-permute-done | bytes 327712 | tf_op jit(solution)/shard_map/ppermute | solution.py:499
  14.8 1.6 %collective-permute-start.3 = (bf16[136,1280]{1,0:T(8,128)(2,1)S(1)}, bf16[136,1280]{1,0:T(8,128)(2,1)S(1)}, u32[]{:S(2)}, u32[]{:S(2)}) collective-permute-start(bf16[136,1280]{1,0:T(8,128)(2,1)S(1)} %collective-permute-done.refs_1_), channel_id=1, source_target_pairs={{0,8},{8,16},{16,24},{24,28},{28,20},{20,12},{12,4},{4,0},{1,9},{9... | collective-permute-start | bytes 1044488 | tf_op jit(solution)/shard_map/ppermute | solution.py:505
  16.8 1.5 %collective-permute-start.5 = (bf16[128,1280]{1,0:T(8,128)(2,1)}, bf16[128,1280]{1,0:T(8,128)(2,1)S(1)}, u32[]{:S(2)}, u32[]{:S(2)}) collective-permute-start(bf16[128,1280]{1,0:T(8,128)(2,1)} %refs_0_), channel_id=1, source_target_pairs={{0,2},{1,3},{2,0},{3,1},{4,6},{5,7},{6,4},{7,5},{8,10},{9,11},{10,... | collective-permute-start | bytes 983048 | tf_op jit(solution)/shard_map/ppermute | solution.py:499
  18.8 2.1 %copy-done.1 = bf16[2,768,1280]{2,1,0:T(8,128)(2,1)S(1)} copy-done((bf16[2,768,1280]{2,1,0:T(8,128)(2,1)S(1)}, bf16[2,768,1280]{2,1,0:T(8,128)(2,1)}, u32[]{:S(2)}) %copy-start.1) | copy-done | bytes 3932184
  21.9 2.2 %shard_map.128 = (bf16[192,768]{1,0:T(8,128)(2,1)S(1)}, bf16[192,768]{1,0:T(8,128)(2,1)S(1)}, f32[24,128]{1,0:T(8,128)S(1)}) custom-call(s32[12]{0:T(128)S(1)} %stack.51.info_ref, bf16[136,1280]{1,0:T(8,128)(2,1)S(1)} %copy-done.8, bf16[136,1280]{1,0:T(8,128)(2,1)S(1)} %collective-permute-done.refs_1_, bf16[136,1280]{1,0:T(8,128)(2,1)S(1)} %collective-permute-done.1.refs_2_, ...), custom_call_target="tpu_custom_call" | custom-call | flops 1000 | bytes 1000 | tf_op jit(solution)/shard_map/pallas_call | solution.py:143
  24.8 1.6 %collective-permute-start.6 = (bf16[136,1280]{1,0:T(8,128)(2,1)S(1)}, bf16[136,1280]{1,0:T(8,128)(2,1)S(1)}, u32[]{:S(2)}, u32[]{:S(2)}) collective-permute-start(bf16[136,1280]{1,0:T(8,128)(2,1)S(1)} %collective-permute-done.3.refs_0_), channel_id=1, source_target_pairs={{0,8},{8,16},{16,24},{24,28},{28,20},{20,12},{12,4},{4,0},{1,9},{9... | collective-permute-start | bytes 1044488 | tf_op jit(solution)/shard_map/ppermute | solution.py:505
  26.8 1.9 %shard_map.130 = (bf16[128,768]{1,0:T(8,128)(2,1)S(1)}, bf16[128,768]{1,0:T(8,128)(2,1)S(1)}, f32[16,128]{1,0:T(8,128)S(1)}) custom-call(s32[12]{0:T(128)S(1)} %stack.51.info_ref, bf16[136,1280]{1,0:T(8,128)(2,1)S(1)} %collective-permute-done.3.refs_0_, bf16[136,1280]{1,0:T(8,128)(2,1)S(1)} %collective-permute-done.4.refs_1_, bf16[2,768,1280]{2,1,0:T(8,128)(2,1)S(1)} %copy-done.2), custom_call_target="tpu_custom_call" | custom-call | flops 1000 | bytes 1000 | tf_op jit(solution)/shard_map/pallas_call | solution.py:143
  30.4 1.5 %collective-permute-start.14 = (bf16[192,768]{1,0:T(8,128)(2,1)S(1)}, bf16[192,768]{1,0:T(8,128)(2,1)S(1)}, u32[]{:S(2)}, u32[]{:S(2)}) collective-permute-start(bf16[192,768]{1,0:T(8,128)(2,1)S(1)} %shard_map.129.refs_0_), channel_id=1, source_target_pairs={{0,2},{1,3},{2,0},{3,1},{4,6},{5,7},{6,4},{7,5},{8,10},{9,11},{10,... | collective-permute-start | bytes 884744 | tf_op jit(solution)/shard_map/ppermute | solution.py:499
  32.0 3.3 %collective-permute-done.6.fore_ref.refs_0_ = bf16[136,1280]{1,0:T(8,128)(2,1)S(1)} collective-permute-done((bf16[136,1280]{1,0:T(8,128)(2,1)S(1)}, bf16[136,1280]{1,0:T(8,128)(2,1)S(1)}, u32[]{:S(2)}, u32[]{:S(2)}) %collective-permute-start.6) | collective-permute-done | bytes 348192 | tf_op jit(solution)/shard_map/ppermute | solution.py:505
  35.3 1.3 %collective-permute-done.7.back_ref.refs_1_ = bf16[136,1280]{1,0:T(8,128)(2,1)S(1)} collective-permute-done((bf16[136,1280]{1,0:T(8,128)(2,1)S(1)}, bf16[136,1280]{1,0:T(8,128)(2,1)S(1)}, u32[]{:S(2)}, u32[]{:S(2)}) %collective-permute-start.7) | collective-permute-done | bytes 348192 | tf_op jit(solution)/shard_map/ppermute | solution.py:505
  36.6 1.5 %collective-permute-start.15 = (bf16[128,768]{1,0:T(8,128)(2,1)S(1)}, bf16[128,768]{1,0:T(8,128)(2,1)S(1)}, u32[]{:S(2)}, u32[]{:S(2)}) collective-permute-start(bf16[128,768]{1,0:T(8,128)(2,1)S(1)} %shard_map.131.refs_0_), channel_id=1, source_target_pairs={{0,2},{1,3},{2,0},{3,1},{4,6},{5,7},{6,4},{7,5},{8,10},{9,11},{10,... | collective-permute-start | bytes 589832 | tf_op jit(solution)/shard_map/ppermute | solution.py:499
  38.7 1.6 %collective-permute-start.12 = (bf16[64,1280]{1,0:T(8,128)(2,1)S(1)}, bf16[64,1280]{1,0:T(8,128)(2,1)S(1)}, u32[]{:S(2)}, u32[]{:S(2)}) collective-permute-start(bf16[64,1280]{1,0:T(8,128)(2,1)S(1)} %get-tuple-element.119), channel_id=1, source_target_pairs={{0,8},{8,16},{16,24},{24,28},{28,20},{20,12},{12,4},{4,0},{1,9},{9... | collective-permute-start | bytes 491528 | tf_op jit(solution)/shard_map/ppermute | solution.py:505
  40.2 1.9 %shard_map.133 = (bf16[128,768]{1,0:T(8,128)(2,1)S(1)}, bf16[128,768]{1,0:T(8,128)(2,1)S(1)}, f32[16,128]{1,0:T(8,128)S(1)}) custom-call(s32[12]{0:T(128)S(1)} %stack.51.info_ref, bf16[136,1280]{1,0:T(8,128)(2,1)S(1)} %collective-permute-done.6.fore_ref.refs_0_, bf16[136,1280]{1,0:T(8,128)(2,1)S(1)} %collective-permute-done.7.back_ref.refs_1_, ...), custom_call_target="tpu_custom_call" | custom-call | flops 1000 | bytes 1000 | tf_op jit(solution)/shard_map/pallas_call | solution.py:143
  42.2 1.8 %collective-permute-done.12.refs_0_ = bf16[64,1280]{1,0:T(8,128)(2,1)S(1)} collective-permute-done((bf16[64,1280]{1,0:T(8,128)(2,1)S(1)}, bf16[64,1280]{1,0:T(8,128)(2,1)S(1)}, u32[]{:S(2)}, u32[]{:S(2)}) %collective-permute-start.12) | collective-permute-done | bytes 163872 | tf_op jit(solution)/shard_map/ppermute | solution.py:505
  44.0 1.3 %shard_map.134 = bf16[64,768]{1,0:T(8,128)(2,1)S(1)} custom-call(s32[12]{0:T(128)S(1)} %stack.51.info_ref, bf16[64,1280]{1,0:T(8,128)(2,1)S(1)} %collective-permute-done.12.refs_0_, bf16[72,1280]{1,0:T(8,128)(2,1)S(1)} %collective-permute-done.13.refs_1_, bf16[2,768,1280]{2,1,0:T(8,128)(2,1)S(1)} %copy-done.2), custom_call_target="tpu_custom_call" | custom-call | flops 1000 | bytes 1000 | tf_op jit(solution)/shard_map/pallas_call | solution.py:143
  45.5 1.3 %shard_map.135 = (bf16[64,768]{1,0:T(8,128)(2,1)S(1)}, f32[8,128]{1,0:T(8,128)S(1)}) custom-call(s32[12]{0:T(128)S(1)} %stack.51.info_ref, bf16[64,1280]{1,0:T(8,128)(2,1)S(1)} %collective-permute-done.12.refs_0_, bf16[72,1280]{1,0:T(8,128)(2,1)S(1)} %collective-permute-done.13.refs_1_, bf16[2,768,1280]{2,1,0:T(8,128)(2,1)S(1)} %copy-done.2), custom_call_target="tpu_custom_call" | custom-call | flops 1000 | bytes 1000 | tf_op jit(solution)/shard_map/pallas_call | solution.py:143
  49.1 1.4 %collective-permute-start.19 = (bf16[64,768]{1,0:T(8,128)(2,1)S(1)}, bf16[64,768]{1,0:T(8,128)(2,1)S(1)}, u32[]{:S(2)}, u32[]{:S(2)}) collective-permute-start(bf16[64,768]{1,0:T(8,128)(2,1)S(1)} %shard_map.136.refs_0_), channel_id=1, source_target_pairs={{0,2},{1,3},{2,0},{3,1},{4,6},{5,7},{6,4},{7,5},{8,10},{9,11},{10,... | collective-permute-start | bytes 294920 | tf_op jit(solution)/shard_map/ppermute | solution.py:499
  51.2 3.8 %shard_map.139 = (bf16[128,512]{1,0:T(8,128)(2,1)S(1)}, bf16[128,512]{1,0:T(8,128)(2,1)S(1)}) custom-call(s32[12]{0:T(128)S(1)} %stack.51.info_ref, bf16[128,1280]{1,0:T(8,128)(2,1)S(1)} %copy-done.10, bf16[128,1280]{1,0:T(8,128)(2,1)S(1)} %collective-permute-done.10.refs_1_, bf16[128,1280]{1,0:T(8,128)(2,1)S(1)} %collective-permute-done.5.refs_2_, ...), custom_call_target="tpu_custom_call" | custom-call | flops 1000 | bytes 1000 | tf_op jit(solution)/shard_map/pallas_call | solution.py:143
  56.4 3.7 %shard_map.141 = (bf16[64,1280]{1,0:T(8,128)(2,1)S(1)}, bf16[72,1280]{1,0:T(8,128)(2,1)S(1)}) custom-call(s32[12]{0:T(128)S(1)} %stack.51.info_ref, bf16[64,768]{1,0:T(8,128)(2,1)S(1)} %shard_map.140.refs_0_, bf16[64,768]{1,0:T(8,128)(2,1)S(1)} %collective-permute-done.22.refs_1_, f32[8,128]{1,0:T(8,128)S(1)} %get-tuple-element.146.refs_2_, ...), custom_call_target="tpu_custom_call" | custom-call | flops 1000 | bytes 1000 | tf_op jit(solution)/shard_map/pallas_call | solution.py:143
  62.9 4.6 %shard_map.143 = (bf16[136,1280]{1,0:T(8,128)(2,1)S(1)}, bf16[136,1280]{1,0:T(8,128)(2,1)S(1)}, bf16[136,1280]{1,0:T(8,128)(2,1)S(1)}, bf16[136,1280]{1,0:T(8,128)(2,1)S(1)}) custom-call(s32[12]{0:T(128)S(1)} %stack.51.info_ref, bf16[128,768]{1,0:T(8,128)(2,1)S(1)} %shard_map.142.refs_0_, bf16[128,768]{1,0:T(8,128)(2,1)S(1)} %collective-permute-done.26.refs_1_, ...), custom_call_target="tpu_custom_call" | custom-call | flops 1000 | bytes 1000 | tf_op jit(solution)/shard_map/pallas_call | solution.py:143
  67.9 1.4 %collective-permute-start.28 = (bf16[136,1280]{1,0:T(8,128)(2,1)S(1)}, bf16[136,1280]{1,0:T(8,128)(2,1)S(1)}, u32[]{:S(2)}, u32[]{:S(2)}) collective-permute-start(bf16[136,1280]{1,0:T(8,128)(2,1)S(1)} %get-tuple-element.170), channel_id=1, source_target_pairs={{0,8},{8,16},{16,24},{24,28},{28,20},{20,12},{12,4},{4,0},{1,9},{9... | collective-permute-start | bytes 1044488 | tf_op jit(solution)/shard_map/ppermute | solution.py:505
  70.0 4.2 %shard_map.146 = (bf16[136,1280]{1,0:T(8,128)(2,1)S(1)}, bf16[136,1280]{1,0:T(8,128)(2,1)S(1)}, bf16[136,1280]{1,0:T(8,128)(2,1)S(1)}) custom-call(s32[12]{0:T(128)S(1)} %stack.51.info_ref, bf16[192,768]{1,0:T(8,128)(2,1)S(1)} %shard_map.144.refs_0_, bf16[192,768]{1,0:T(8,128)(2,1)S(1)} %collective-permute-done.27.refs_1_, ...), custom_call_target="tpu_custom_call" | custom-call | flops 1000 | bytes 1000 | tf_op jit(solution)/shard_map/pallas_call | solution.py:143
  74.1 3.2 %collective-permute-done.28.refs_1_ = bf16[136,1280]{1,0:T(8,128)(2,1)S(1)} collective-permute-done((bf16[136,1280]{1,0:T(8,128)(2,1)S(1)}, bf16[136,1280]{1,0:T(8,128)(2,1)S(1)}, u32[]{:S(2)}, u32[]{:S(2)}) %collective-permute-start.28) | collective-permute-done | bytes 348192 | tf_op jit(solution)/shard_map/ppermute | solution.py:505
  77.3 1.3 %collective-permute-done.29.refs_3_ = bf16[136,1280]{1,0:T(8,128)(2,1)S(1)} collective-permute-done((bf16[136,1280]{1,0:T(8,128)(2,1)S(1)}, bf16[136,1280]{1,0:T(8,128)(2,1)S(1)}, u32[]{:S(2)}, u32[]{:S(2)}) %collective-permute-start.29) | collective-permute-done | bytes 348192 | tf_op jit(solution)/shard_map/ppermute | solution.py:505
  78.8 1.6 %collective-permute-start.30 = (bf16[136,1280]{1,0:T(8,128)(2,1)S(1)}, bf16[136,1280]{1,0:T(8,128)(2,1)S(1)}, u32[]{:S(2)}, u32[]{:S(2)}) collective-permute-start(bf16[136,1280]{1,0:T(8,128)(2,1)S(1)} %get-tuple-element.186), channel_id=1, source_target_pairs={{0,8},{8,16},{16,24},{24,28},{28,20},{20,12},{12,4},{4,0},{1,9},{9... | collective-permute-start | bytes 1044488 | tf_op jit(solution)/shard_map/ppermute | solution.py:505
  80.9 4.0 %shard_map.147 = (bf16[128,1280]{1,0:T(8,128)(2,1)S(1)}, bf16[128,1280]{1,0:T(8,128)(2,1)S(1)}, bf16[128,1280]{1,0:T(8,128)(2,1)S(1)}, bf16[128,1280]{1,0:T(8,128)(2,1)S(1)}) custom-call(s32[12]{0:T(128)S(1)} %stack.51.info_ref, bf16[128,512]{1,0:T(8,128)(2,1)S(1)} %get-tuple-element.179.dgate_ref, bf16[128,512]{1,0:T(8,128)(2,1)S(1)} %get-tuple-element.180.dup_ref, ...), custom_call_target="tpu_custom_call" | custom-call | flops 1000 | bytes 1000 | tf_op jit(solution)/shard_map/pallas_call | solution.py:143
  89.3 1.5 %collective-permute-start.35 = (bf16[136,1280]{1,0:T(8,128)(2,1)S(1)}, bf16[136,1280]{1,0:T(8,128)(2,1)S(1)}, u32[]{:S(2)}, u32[]{:S(2)}) collective-permute-start(bf16[136,1280]{1,0:T(8,128)(2,1)S(1)} %get-tuple-element.199), channel_id=1, source_target_pairs={{0,8},{8,16},{16,24},{24,28},{28,20},{20,12},{12,4},{4,0},{1,9},{9... | collective-permute-start | bytes 1044488 | tf_op jit(solution)/shard_map/ppermute | solution.py:505
  90.8 1.5 %collective-permute-start.34 = (bf16[128,1280]{1,0:T(8,128)(2,1)S(1)}, bf16[128,1280]{1,0:T(8,128)(2,1)S(1)}, u32[]{:S(2)}, u32[]{:S(2)}) collective-permute-start(bf16[128,1280]{1,0:T(8,128)(2,1)S(1)} %get-tuple-element.197), channel_id=1, source_target_pairs={{0,2},{1,3},{2,0},{3,1},{4,6},{5,7},{6,4},{7,5},{8,10},{9,11},{10,... | collective-permute-start | bytes 983048 | tf_op jit(solution)/shard_map/ppermute | solution.py:499
  92.3 5.3 %collective-permute-done.36 = bf16[136,1280]{1,0:T(8,128)(2,1)S(1)} collective-permute-done((bf16[136,1280]{1,0:T(8,128)(2,1)S(1)}, bf16[136,1280]{1,0:T(8,128)(2,1)S(1)}, u32[]{:S(2)}, u32[]{:S(2)}) %collective-permute-start.36) | collective-permute-done | bytes 348192 | tf_op jit(solution)/shard_map/ppermute | solution.py:505
  (104 shorter events, 21.1 us)
Async XLA Ops:
  1.9 12.5 %collective-permute-start = (bf16[136,1280]{1,0:T(8,128)(2,1)}, bf16[136,1280]{1,0:T(8,128)(2,1)S(1)}, u32[]{:S(2)}, u32[]{:S(2)}) collective-permute-start(bf16[136,1280]{1,0:T(8,128)(2,1)} %shard_map.127.refs_0_), channel_id=1, source_target_pairs={{0,8},{8,16},{16,24},{24,28},{28,20},{20,12},{12,4},{4,0},{1,9},{9... | collective-permute-start | bytes 1044488 | tf_op jit(solution)/shard_map/ppermute | solution.py:505
  5.0 9.8 %collective-permute-start.1 = (bf16[136,1280]{1,0:T(8,128)(2,1)}, bf16[136,1280]{1,0:T(8,128)(2,1)S(1)}, u32[]{:S(2)}, u32[]{:S(2)}) collective-permute-start(bf16[136,1280]{1,0:T(8,128)(2,1)} %shard_map.127.refs_0_), channel_id=1, source_target_pairs={{0,4},{8,0},{16,8},{24,16},{28,24},{20,28},{12,20},{4,12},{1,5},{9... | collective-permute-start | bytes 1044488 | tf_op jit(solution)/shard_map/ppermute | solution.py:505
  5.0 9.4 %collective-permute-start.2 = (bf16[128,1280]{1,0:T(8,128)(2,1)}, bf16[128,1280]{1,0:T(8,128)(2,1)S(1)}, u32[]{:S(2)}, u32[]{:S(2)}) collective-permute-start(bf16[128,1280]{1,0:T(8,128)(2,1)} %refs_4_.2), channel_id=1, source_target_pairs={{0,2},{1,3},{2,0},{3,1},{4,6},{5,7},{6,4},{7,5},{8,10},{9,11},{10,... | collective-permute-start | bytes 983048 | tf_op jit(solution)/shard_map/ppermute | solution.py:499
  14.8 9.9 %collective-permute-start.3 = (bf16[136,1280]{1,0:T(8,128)(2,1)S(1)}, bf16[136,1280]{1,0:T(8,128)(2,1)S(1)}, u32[]{:S(2)}, u32[]{:S(2)}) collective-permute-start(bf16[136,1280]{1,0:T(8,128)(2,1)S(1)} %collective-permute-done.refs_1_), channel_id=1, source_target_pairs={{0,8},{8,16},{16,24},{24,28},{28,20},{20,12},{12,4},{4,0},{1,9},{9... | collective-permute-start | bytes 1044488 | tf_op jit(solution)/shard_map/ppermute | solution.py:505
  16.4 8.4 %collective-permute-start.4 = (bf16[136,1280]{1,0:T(8,128)(2,1)S(1)}, bf16[136,1280]{1,0:T(8,128)(2,1)S(1)}, u32[]{:S(2)}, u32[]{:S(2)}) collective-permute-start(bf16[136,1280]{1,0:T(8,128)(2,1)S(1)} %collective-permute-done.1.refs_2_), channel_id=1, source_target_pairs={{0,4},{8,0},{16,8},{24,16},{28,24},{20,28},{12,20},{4,12},{1,5},{9... | collective-permute-start | bytes 1044488 | tf_op jit(solution)/shard_map/ppermute | solution.py:505
  16.8 7.9 %collective-permute-start.5 = (bf16[128,1280]{1,0:T(8,128)(2,1)}, bf16[128,1280]{1,0:T(8,128)(2,1)S(1)}, u32[]{:S(2)}, u32[]{:S(2)}) collective-permute-start(bf16[128,1280]{1,0:T(8,128)(2,1)} %refs_0_), channel_id=1, source_target_pairs={{0,2},{1,3},{2,0},{3,1},{4,6},{5,7},{6,4},{7,5},{8,10},{9,11},{10,... | collective-permute-start | bytes 983048 | tf_op jit(solution)/shard_map/ppermute | solution.py:499
  18.3 8.5 %collective-permute-start.10 = (bf16[128,1280]{1,0:T(8,128)(2,1)}, bf16[128,1280]{1,0:T(8,128)(2,1)S(1)}, u32[]{:S(2)}, u32[]{:S(2)}) collective-permute-start(bf16[128,1280]{1,0:T(8,128)(2,1)} %refs_0_), channel_id=1, source_target_pairs={{0,1},{1,0},{2,3},{3,2},{4,5},{5,4},{6,7},{7,6},{8,9},{9,8},{10,11... | collective-permute-start | bytes 983048 | tf_op jit(solution)/shard_map/ppermute | solution.py:502
  18.3 10.5 %collective-permute-start.11 = (bf16[128,1280]{1,0:T(8,128)(2,1)}, bf16[128,1280]{1,0:T(8,128)(2,1)S(1)}, u32[]{:S(2)}, u32[]{:S(2)}) collective-permute-start(bf16[128,1280]{1,0:T(8,128)(2,1)} %refs_4_.2), channel_id=1, source_target_pairs={{0,1},{1,0},{2,3},{3,2},{4,5},{5,4},{6,7},{7,6},{8,9},{9,8},{10,11... | collective-permute-start | bytes 983048 | tf_op jit(solution)/shard_map/ppermute | solution.py:502
  24.8 4.6 %collective-permute-start.8 = (bf16[192,768]{1,0:T(8,128)(2,1)S(1)}, bf16[192,768]{1,0:T(8,128)(2,1)S(1)}, u32[]{:S(2)}, u32[]{:S(2)}) collective-permute-start(bf16[192,768]{1,0:T(8,128)(2,1)S(1)} %get-tuple-element.114), channel_id=1, source_target_pairs={{0,1},{1,0},{2,3},{3,2},{4,5},{5,4},{6,7},{7,6},{8,9},{9,8},{10,11... | collective-permute-start | bytes 884744 | tf_op jit(solution)/shard_map/ppermute | solution.py:502
  24.8 10.6 %collective-permute-start.6 = (bf16[136,1280]{1,0:T(8,128)(2,1)S(1)}, bf16[136,1280]{1,0:T(8,128)(2,1)S(1)}, u32[]{:S(2)}, u32[]{:S(2)}) collective-permute-start(bf16[136,1280]{1,0:T(8,128)(2,1)S(1)} %collective-permute-done.3.refs_0_), channel_id=1, source_target_pairs={{0,8},{8,16},{16,24},{24,28},{28,20},{20,12},{12,4},{4,0},{1,9},{9... | collective-permute-start | bytes 1044488 | tf_op jit(solution)/shard_map/ppermute | solution.py:505
  26.4 10.3 %collective-permute-start.7 = (bf16[136,1280]{1,0:T(8,128)(2,1)S(1)}, bf16[136,1280]{1,0:T(8,128)(2,1)S(1)}, u32[]{:S(2)}, u32[]{:S(2)}) collective-permute-start(bf16[136,1280]{1,0:T(8,128)(2,1)S(1)} %collective-permute-done.4.refs_1_), channel_id=1, source_target_pairs={{0,4},{8,0},{16,8},{24,16},{28,24},{20,28},{12,20},{4,12},{1,5},{9... | collective-permute-start | bytes 1044488 | tf_op jit(solution)/shard_map/ppermute | solution.py:505
  26.8 11.8 %collective-permute-start.17 = (bf16[128,1280]{1,0:T(8,128)(2,1)S(1)}, bf16[128,1280]{1,0:T(8,128)(2,1)S(1)}, u32[]{:S(2)}, u32[]{:S(2)}) collective-permute-start(bf16[128,1280]{1,0:T(8,128)(2,1)S(1)} %collective-permute-done.2.refs_6_), channel_id=1, source_target_pairs={{0,1},{1,0},{2,3},{3,2},{4,5},{5,4},{6,7},{7,6},{8,9},{9,8},{10,11... | collective-permute-start | bytes 983048 | tf_op jit(solution)/shard_map/ppermute | solution.py:502
  29.4 12.8 %collective-permute-start.16 = (bf16[128,1280]{1,0:T(8,128)(2,1)S(1)}, bf16[128,1280]{1,0:T(8,128)(2,1)S(1)}, u32[]{:S(2)}, u32[]{:S(2)}) collective-permute-start(bf16[128,1280]{1,0:T(8,128)(2,1)S(1)} %collective-permute-done.5.refs_2_), channel_id=1, source_target_pairs={{0,1},{1,0},{2,3},{3,2},{4,5},{5,4},{6,7},{7,6},{8,9},{9,8},{10,11... | collective-permute-start | bytes 983048 | tf_op jit(solution)/shard_map/ppermute | solution.py:502
  30.4 13.6 %collective-permute-start.14 = (bf16[192,768]{1,0:T(8,128)(2,1)S(1)}, bf16[192,768]{1,0:T(8,128)(2,1)S(1)}, u32[]{:S(2)}, u32[]{:S(2)}) collective-permute-start(bf16[192,768]{1,0:T(8,128)(2,1)S(1)} %shard_map.129.refs_0_), channel_id=1, source_target_pairs={{0,2},{1,3},{2,0},{3,1},{4,6},{5,7},{6,4},{7,5},{8,10},{9,11},{10,... | collective-permute-start | bytes 884744 | tf_op jit(solution)/shard_map/ppermute | solution.py:499
  36.6 7.3 %collective-permute-start.15 = (bf16[128,768]{1,0:T(8,128)(2,1)S(1)}, bf16[128,768]{1,0:T(8,128)(2,1)S(1)}, u32[]{:S(2)}, u32[]{:S(2)}) collective-permute-start(bf16[128,768]{1,0:T(8,128)(2,1)S(1)} %shard_map.131.refs_0_), channel_id=1, source_target_pairs={{0,2},{1,3},{2,0},{3,1},{4,6},{5,7},{6,4},{7,5},{8,10},{9,11},{10,... | collective-permute-start | bytes 589832 | tf_op jit(solution)/shard_map/ppermute | solution.py:499
  38.2 5.8 %collective-permute-start.13 = (bf16[72,1280]{1,0:T(8,128)(2,1)S(1)}, bf16[72,1280]{1,0:T(8,128)(2,1)S(1)}, u32[]{:S(2)}, u32[]{:S(2)}) collective-permute-start(bf16[72,1280]{1,0:T(8,128)(2,1)S(1)} %get-tuple-element.120), channel_id=1, source_target_pairs={{0,4},{8,0},{16,8},{24,16},{28,24},{20,28},{12,20},{4,12},{1,5},{9... | collective-permute-start | bytes 552968 | tf_op jit(solution)/shard_map/ppermute | solution.py:505
  38.7 5.3 %collective-permute-start.12 = (bf16[64,1280]{1,0:T(8,128)(2,1)S(1)}, bf16[64,1280]{1,0:T(8,128)(2,1)S(1)}, u32[]{:S(2)}, u32[]{:S(2)}) collective-permute-start(bf16[64,1280]{1,0:T(8,128)(2,1)S(1)} %get-tuple-element.119), channel_id=1, source_target_pairs={{0,8},{8,16},{16,24},{24,28},{28,20},{20,12},{12,4},{4,0},{1,9},{9... | collective-permute-start | bytes 491528 | tf_op jit(solution)/shard_map/ppermute | solution.py:505
  48.6 6.3 %collective-permute-start.21 = (bf16[128,768]{1,0:T(8,128)(2,1)S(1)}, bf16[128,768]{1,0:T(8,128)(2,1)S(1)}, u32[]{:S(2)}, u32[]{:S(2)}) collective-permute-start(bf16[128,768]{1,0:T(8,128)(2,1)S(1)} %shard_map.138.refs_3_), channel_id=1, source_target_pairs={{0,1},{1,0},{2,3},{3,2},{4,5},{5,4},{6,7},{7,6},{8,9},{9,8},{10,11... | collective-permute-start | bytes 589832 | tf_op jit(solution)/shard_map/ppermute | solution.py:502
  49.1 5.9 %collective-permute-start.19 = (bf16[64,768]{1,0:T(8,128)(2,1)S(1)}, bf16[64,768]{1,0:T(8,128)(2,1)S(1)}, u32[]{:S(2)}, u32[]{:S(2)}) collective-permute-start(bf16[64,768]{1,0:T(8,128)(2,1)S(1)} %shard_map.136.refs_0_), channel_id=1, source_target_pairs={{0,2},{1,3},{2,0},{3,1},{4,6},{5,7},{6,4},{7,5},{8,10},{9,11},{10,... | collective-permute-start | bytes 294920 | tf_op jit(solution)/shard_map/ppermute | solution.py:499
  50.5 9.7 %collective-permute-start.23 = (bf16[128,768]{1,0:T(8,128)(2,1)S(1)}, bf16[128,768]{1,0:T(8,128)(2,1)S(1)}, u32[]{:S(2)}, u32[]{:S(2)}) collective-permute-start(bf16[128,768]{1,0:T(8,128)(2,1)S(1)} %shard_map.137.refs_0_), channel_id=1, source_target_pairs={{0,2},{1,3},{2,0},{3,1},{4,6},{5,7},{6,4},{7,5},{8,10},{9,11},{10,... | collective-permute-start | bytes 589832 | tf_op jit(solution)/shard_map/ppermute | solution.py:499
  60.2 7.6 %collective-permute-start.27 = (bf16[192,768]{1,0:T(8,128)(2,1)S(1)}, bf16[192,768]{1,0:T(8,128)(2,1)S(1)}, u32[]{:S(2)}, u32[]{:S(2)}) collective-permute-start(bf16[192,768]{1,0:T(8,128)(2,1)S(1)} %shard_map.144.refs_0_), channel_id=1, source_target_pairs={{0,1},{1,0},{2,3},{3,2},{4,5},{5,4},{6,7},{7,6},{8,9},{9,8},{10,11... | collective-permute-start | bytes 884744 | tf_op jit(solution)/shard_map/ppermute | solution.py:502
  60.5 2.5 %collective-permute-start.26 = (bf16[128,768]{1,0:T(8,128)(2,1)S(1)}, bf16[128,768]{1,0:T(8,128)(2,1)S(1)}, u32[]{:S(2)}, u32[]{:S(2)}) collective-permute-start(bf16[128,768]{1,0:T(8,128)(2,1)S(1)} %shard_map.142.refs_0_), channel_id=1, source_target_pairs={{0,1},{1,0},{2,3},{3,2},{4,5},{5,4},{6,7},{7,6},{8,9},{9,8},{10,11... | collective-permute-start | bytes 589832 | tf_op jit(solution)/shard_map/ppermute | solution.py:502
  60.9 6.9 %collective-permute-start.25 = (bf16[72,1280]{1,0:T(8,128)(2,1)S(1)}, bf16[72,1280]{1,0:T(8,128)(2,1)S(1)}, u32[]{:S(2)}, u32[]{:S(2)}) collective-permute-start(bf16[72,1280]{1,0:T(8,128)(2,1)S(1)} %get-tuple-element.153), channel_id=1, source_target_pairs={{0,4},{8,0},{16,8},{24,16},{28,24},{20,28},{12,20},{4,12},{1,5},{9... | collective-permute-start | bytes 552968 | tf_op jit(solution)/shard_map/ppermute | solution.py:505
  61.8 6.0 %collective-permute-start.24 = (bf16[64,1280]{1,0:T(8,128)(2,1)S(1)}, bf16[64,1280]{1,0:T(8,128)(2,1)S(1)}, u32[]{:S(2)}, u32[]{:S(2)}) collective-permute-start(bf16[64,1280]{1,0:T(8,128)(2,1)S(1)} %get-tuple-element.152), channel_id=1, source_target_pairs={{0,8},{8,16},{16,24},{24,28},{28,20},{20,12},{12,4},{4,0},{1,9},{9... | collective-permute-start | bytes 491528 | tf_op jit(solution)/shard_map/ppermute | solution.py:505
  67.9 9.4 %collective-permute-start.28 = (bf16[136,1280]{1,0:T(8,128)(2,1)S(1)}, bf16[136,1280]{1,0:T(8,128)(2,1)S(1)}, u32[]{:S(2)}, u32[]{:S(2)}) collective-permute-start(bf16[136,1280]{1,0:T(8,128)(2,1)S(1)} %get-tuple-element.170), channel_id=1, source_target_pairs={{0,8},{8,16},{16,24},{24,28},{28,20},{20,12},{12,4},{4,0},{1,9},{9... | collective-permute-start | bytes 1044488 | tf_op jit(solution)/shard_map/ppermute | solution.py:505
  69.3 9.3 %collective-permute-start.29 = (bf16[136,1280]{1,0:T(8,128)(2,1)S(1)}, bf16[136,1280]{1,0:T(8,128)(2,1)S(1)}, u32[]{:S(2)}, u32[]{:S(2)}) collective-permute-start(bf16[136,1280]{1,0:T(8,128)(2,1)S(1)} %get-tuple-element.171), channel_id=1, source_target_pairs={{0,4},{8,0},{16,8},{24,16},{28,24},{20,28},{12,20},{4,12},{1,5},{9... | collective-permute-start | bytes 1044488 | tf_op jit(solution)/shard_map/ppermute | solution.py:505
  78.8 8.4 %collective-permute-start.30 = (bf16[136,1280]{1,0:T(8,128)(2,1)S(1)}, bf16[136,1280]{1,0:T(8,128)(2,1)S(1)}, u32[]{:S(2)}, u32[]{:S(2)}) collective-permute-start(bf16[136,1280]{1,0:T(8,128)(2,1)S(1)} %get-tuple-element.186), channel_id=1, source_target_pairs={{0,8},{8,16},{16,24},{24,28},{28,20},{20,12},{12,4},{4,0},{1,9},{9... | collective-permute-start | bytes 1044488 | tf_op jit(solution)/shard_map/ppermute | solution.py:505
  80.4 8.1 %collective-permute-start.31 = (bf16[136,1280]{1,0:T(8,128)(2,1)S(1)}, bf16[136,1280]{1,0:T(8,128)(2,1)S(1)}, u32[]{:S(2)}, u32[]{:S(2)}) collective-permute-start(bf16[136,1280]{1,0:T(8,128)(2,1)S(1)} %get-tuple-element.187), channel_id=1, source_target_pairs={{0,4},{8,0},{16,8},{24,16},{28,24},{20,28},{12,20},{4,12},{1,5},{9... | collective-permute-start | bytes 1044488 | tf_op jit(solution)/shard_map/ppermute | solution.py:505
  85.0 2.1 %collective-permute-start.33 = (bf16[128,1280]{1,0:T(8,128)(2,1)S(1)}, bf16[128,1280]{1,0:T(8,128)(2,1)S(1)}, u32[]{:S(2)}, u32[]{:S(2)}) collective-permute-start(bf16[128,1280]{1,0:T(8,128)(2,1)S(1)} %get-tuple-element.189), channel_id=1, source_target_pairs={{0,1},{1,0},{2,3},{3,2},{4,5},{5,4},{6,7},{7,6},{8,9},{9,8},{10,11... | collective-permute-start | bytes 983048 | tf_op jit(solution)/shard_map/ppermute | solution.py:502
  88.7 8.8 %collective-permute-start.36 = (bf16[136,1280]{1,0:T(8,128)(2,1)S(1)}, bf16[136,1280]{1,0:T(8,128)(2,1)S(1)}, u32[]{:S(2)}, u32[]{:S(2)}) collective-permute-start(bf16[136,1280]{1,0:T(8,128)(2,1)S(1)} %get-tuple-element.200), channel_id=1, source_target_pairs={{0,4},{8,0},{16,8},{24,16},{28,24},{20,28},{12,20},{4,12},{1,5},{9... | collective-permute-start | bytes 1044488 | tf_op jit(solution)/shard_map/ppermute | solution.py:505
  89.3 8.4 %collective-permute-start.35 = (bf16[136,1280]{1,0:T(8,128)(2,1)S(1)}, bf16[136,1280]{1,0:T(8,128)(2,1)S(1)}, u32[]{:S(2)}, u32[]{:S(2)}) collective-permute-start(bf16[136,1280]{1,0:T(8,128)(2,1)S(1)} %get-tuple-element.199), channel_id=1, source_target_pairs={{0,8},{8,16},{16,24},{24,28},{28,20},{20,12},{12,4},{4,0},{1,9},{9... | collective-permute-start | bytes 1044488 | tf_op jit(solution)/shard_map/ppermute | solution.py:505
  90.8 7.8 %collective-permute-start.34 = (bf16[128,1280]{1,0:T(8,128)(2,1)S(1)}, bf16[128,1280]{1,0:T(8,128)(2,1)S(1)}, u32[]{:S(2)}, u32[]{:S(2)}) collective-permute-start(bf16[128,1280]{1,0:T(8,128)(2,1)S(1)} %get-tuple-element.197), channel_id=1, source_target_pairs={{0,2},{1,3},{2,0},{3,1},{4,6},{5,7},{6,4},{7,5},{8,10},{9,11},{10,... | collective-permute-start | bytes 983048 | tf_op jit(solution)/shard_map/ppermute | solution.py:499
  (21 other events, 245.5 us)

commit v5 on v4

--- a/solution.py
+++ b/solution.py
@@ -203,7 +203,25 @@
     return call(join_kernel, 2, [shape, shape])(near_f, top, near_b, bottom)
 
 
-def payload_kernel(capacity, ids_hbm, probs_hbm, grad_hbm, out_ref, ids_ref, probs_ref, sems):
+def attach_kernel(fore_ref, meta_f_ref, back_ref, meta_b_ref, fore_out, back_out):
+    rows = fore_ref.shape[0]
+    for ref, meta_ref, out_ref in (
+        (fore_ref, meta_f_ref, fore_out),
+        (back_ref, meta_b_ref, back_out),
+    ):
+        out_ref[0:rows, :] = ref[...]
+        out_ref[rows:, :] = meta_ref[...]
+
+
+def attach(fore, meta_f, back, meta_b):
+    rows, cols = fore.shape
+    shape = jax.ShapeDtypeStruct((rows + 8, cols), BF16)
+    return call(attach_kernel, 2, [shape, shape])(fore, meta_f, back, meta_b)
+
+
+def payload_kernel(
+    capacity, ids_hbm, probs_hbm, grad_hbm, out_ref, meta_ref, ids_ref, probs_ref, sems
+):
     expert_total, rows = probs_ref.shape
     cols = grad_hbm.shape[1]
     copies = [
@@ -230,7 +248,9 @@
     parts = [slot, high, probs - high]
     pieces = [a[8 * i : 8 * i + 8] for a in parts for i in range(expert_total // 8)]
     pieces.append(jnp.zeros((8, cols - len(pieces) * rows), F32))
-    out_ref[rows : rows + 8, :] = jnp.concatenate(pieces, axis=1).astype(BF16)
+    meta = jnp.concatenate(pieces, axis=1).astype(BF16)
+    out_ref[rows : rows + 8, :] = meta
+    meta_ref[...] = meta
     copies[2].wait()
 
 
@@ -239,7 +259,10 @@
     return call(
         functools.partial(payload_kernel, capacity),
         60,
-        jax.ShapeDtypeStruct((rows + 8, cols), BF16),
+        [
+            jax.ShapeDtypeStruct((rows + 8, cols), BF16),
+            jax.ShapeDtypeStruct((8, cols), BF16),
+        ],
         [
             pltpu.VMEM(ids_t.shape, jnp.int32),
             pltpu.VMEM(probs_t.shape, F32),
@@ -363,14 +386,14 @@
             combine.append(jnp.concatenate(stacked, axis=0))
             scores.append(score_rows)
             b += 1
-    for n in range(0, cols, 256):
+    for n in range(0, cols, 1280):
         grads = []
         for e in range(2):
             value = lax.dot_general(
-                dgate_ref[e], gate_w_ref[e, n : n + 256, :], LAST, preferred_element_type=F32
+                dgate_ref[e], gate_w_ref[e, n : n + 1280, :], LAST, preferred_element_type=F32
             )
             value = value + lax.dot_general(
-                dup_ref[e], up_w_ref[e, n : n + 256, :], LAST, preferred_element_type=F32
+                dup_ref[e], up_w_ref[e, n : n + 1280, :], LAST, preferred_element_type=F32
             )
             grads.append(value.astype(BF16))
         for b in range(total):
@@ -379,15 +402,15 @@
             value = lax.dot_general(combine[b], pile, FIRST, preferred_element_type=F32)
             if n == 0:
                 lanes = [jnp.where(tile == i, scores[b], 0.0) for i in range(tiles)]
-                lanes = jnp.concatenate(lanes, axis=1)
+                lanes = jnp.concatenate(lanes + [jnp.zeros((8, 1280 - tiles * rows), F32)], axis=1)
             else:
-                lanes = jnp.zeros((8, 256), F32)
+                lanes = jnp.zeros((8, 1280), F32)
             if split:
-                out_refs[2 * b][:, n : n + 256] = value[:TOP_ROWS].astype(BF16)
+                out_refs[2 * b][:, n : n + 1280] = value[:TOP_ROWS].astype(BF16)
                 low = jnp.concatenate([value[TOP_ROWS:], lanes], axis=0)
-                out_refs[2 * b + 1][:, n : n + 256] = low.astype(BF16)
+                out_refs[2 * b + 1][:, n : n + 1280] = low.astype(BF16)
             else:
-                out_refs[b][:, n : n + 256] = jnp.concatenate([value, lanes], axis=0).astype(BF16)
+                out_refs[b][:, n : n + 1280] = jnp.concatenate([value, lanes], axis=0).astype(BF16)
 
 
 def grad_part(info, parts, saved, weights, counts, chunk, split, tiles, capacity):
@@ -413,31 +436,46 @@
     ]
 
 
-def shared_slopes_kernel(info_ref, *refs):
-    token_refs, grad_refs = refs[0:4], refs[4:8]
-    gate_ref, up_ref, down_ref, dgate_ref, dup_ref = refs[8:]
+def shared_inner_kernel(info_ref, *refs):
+    token_refs, (gate_ref, up_ref, active_ref, slope_ref) = refs[0:4], refs[4:]
     rows, cols = token_refs[0].shape
     units = gate_ref.shape[1]
     spans = shared_spans(info_ref, cols)
     gate_pre = jnp.zeros((rows, units), F32)
     up_pre = jnp.zeros((rows, units), F32)
-    hidden_pre = jnp.zeros((rows, units), F32)
     for q in range(4):
-        token, grad = token_refs[q][...], grad_refs[q][...]
+        token = token_refs[q][...]
         gate_pre = gate_pre + jnp.dot(token, gate_ref[spans[q], :], preferred_element_type=F32)
         up_pre = up_pre + jnp.dot(token, up_ref[spans[q], :], preferred_element_type=F32)
+    active, slope_term = silu_parts(gate_pre)
+    active_ref[...] = active
+    slope_ref[...] = up_pre * slope_term
+
+
+def shared_inner(info, token_blocks, shared_gate, shared_up):
+    shape = jax.ShapeDtypeStruct((token_blocks[0].shape[0], shared_gate.shape[1]), F32)
+    return call(shared_inner_kernel, 8, [shape, shape], (), 1)(
+        info, *token_blocks, shared_gate, shared_up
+    )
+
+
+def shared_slopes_kernel(info_ref, *refs):
+    grad_refs, (down_ref, active_ref, slope_ref, dgate_ref, dup_ref) = refs[0:4], refs[4:]
+    rows, cols = grad_refs[0].shape
+    spans = shared_spans(info_ref, cols)
+    hidden_pre = jnp.zeros((rows, down_ref.shape[0]), F32)
+    for q in range(4):
         hidden_pre = hidden_pre + lax.dot_general(
-            grad, down_ref[:, spans[q]], LAST, preferred_element_type=F32
+            grad_refs[q][...], down_ref[:, spans[q]], LAST, preferred_element_type=F32
         )
-    active, slope_term = silu_parts(gate_pre)
-    dgate_ref[...] = (hidden_pre * up_pre * slope_term).astype(BF16)
-    dup_ref[...] = (hidden_pre * active).astype(BF16)
-
-
-def shared_slopes(info, token_blocks, grad_blocks, shared_gate, shared_up, shared_down):
-    shape = jax.ShapeDtypeStruct((token_blocks[0].shape[0], shared_gate.shape[1]), BF16)
+    dgate_ref[...] = (hidden_pre * slope_ref[...]).astype(BF16)
+    dup_ref[...] = (hidden_pre * active_ref[...]).astype(BF16)
+
+
+def shared_slopes(info, grad_blocks, shared_down, active, slope):
+    shape = jax.ShapeDtypeStruct(active.shape, BF16)
     return call(shared_slopes_kernel, 8, [shape, shape], (), 1)(
-        info, *token_blocks, *grad_blocks, shared_gate, shared_up, shared_down
+        info, *grad_blocks, shared_down, active, slope
     )
 
 
@@ -523,12 +561,13 @@
 
     numbers = base + [here] + [ring_place(place + d) for d in range(-3, 5)]
     info = jnp.stack([jnp.asarray(n, jnp.int32) for n in numbers])
-    payload = payload_of(expert_ids.T, router_probs.T, out_grad, capacity)
-
-    payload, tokens, out_grad, info = tie((payload, tokens, out_grad, info))
-    fore, back = ring(payload, payload)
+    payload, meta = payload_of(expert_ids.T, router_probs.T, out_grad, capacity)
+
+    fore, back = ring(out_grad, out_grad)
+    meta_f, meta_b = ring(meta, meta)
     grad_x = swap_x(out_grad)
-    fore1, back1, grad_x = tie((fore, back, grad_x))
+    fore, back, grad_x, meta_f, meta_b, info = tie((fore, back, grad_x, meta_f, meta_b, info))
+    fore1, back1 = attach(fore, meta_f, back, meta_b)
 
     fore, back = ring(fore1, back1)
     tok_x = swap_x(tokens)
@@ -548,56 +587,58 @@
     top, bottom = ring(*halves_of(fore3, back3))
     far2 = swap_x(chip2)
     other3, mine3, meta3 = hidden([fore3, back3])
-    tok_both, grad_both = swap_core(tok_x), swap_core(grad_x)
-    top, bottom, chip2, other3, mine3, far1, far2, tok_both, grad_both = tie(
-        (top, bottom, chip2, other3, mine3, far1, far2, tok_both, grad_both)
+    tok_both = swap_core(tok_x)
+    top, bottom, chip2, other3, mine3, far1, far2, tok_both = tie(
+        (top, bottom, chip2, other3, mine3, far1, far2, tok_both)
     )
 
     (other4,) = hidden([(top, bottom)], (0,))
+    top, bottom, other4, other3 = tie((top, bottom, other4, other3))
     swapped4 = swap_core(other4)
-    top, bottom, other4 = tie((top, bottom, other4))
     mine4, meta4 = hidden([(top, bottom)], (1,))
+    swapped3 = swap_core(other3)
     (chip4,) = sums((mine4, swapped4))
-    chip4, other3, dgate_in = tie((chip4, other3, tokens))
+    chip4, chip1, far1 = tie((chip4, chip1, far1))
     far4 = swap_x(chip4)
-    (chip3,) = sums((mine3, swap_core(other3)))
+    (full1,) = sums((chip1, far1))
+    full1, swapped3, mine3 = tie((full1, swapped3, mine3))
+    (chip3,) = sums((mine3, swapped3))
     far3 = swap_x(chip3)
-    chip3, chip2 = tie((chip3, chip2))
+    chip3, tok_in, full1 = tie((chip3, tokens, full1))
+    pair1 = swap_core(full1)
+    active, slope = shared_inner(
+        info, [tok_in, tok_core, tok_x, tok_both], shared_gate, shared_up
+    )
+    active, slope, chip2, far2 = tie((active, slope, chip2, far2))
     (full2,) = sums((chip2, far2))
     pair2 = swap_core(full2)
-    dgate, dup = shared_slopes(
-        info,
-        [dgate_in, tok_core, tok_x, tok_both],
-        [out_grad, grad_core, grad_x, grad_both],
-        shared_gate,
-        shared_up,
-        shared_down,
-    )
-    far4, full2, pair2, dgate, dup = tie((far4, full2, pair2, dgate, dup))
+    far4, full2, active, pair1 = tie((far4, full2, active, pair1))
     (full4,) = sums((chip4, far4))
     pair4 = swap_core(full4)
     saved = (gate_saved, up_saved)
     weights = (gate_weight, up_weight)
     top, bottom = grads(saved, weights, ((4,), full4, pair4, meta4))
 
-    top, bottom, pair2, full2, far3, chip1 = tie((top, bottom, pair2, full2, far3, chip1))
+    top, bottom, pair2, full2, far3 = tie((top, bottom, pair2, full2, far3))
     fore, back = ring(top, bottom)
     (full3,) = sums((chip3, far3))
     pair3 = swap_core(full3)
-    (full1,) = sums((chip1, far1))
-    pair1 = swap_core(full1)
     near_b3, near_f3, near_b2, near_f2 = grads(
         saved, weights, ((-3, 3), full3, pair3, meta3), ((-2, 2), full2, pair2, meta2)
     )
-    fore, back, near_f3, near_b3, near_f2, near_b2, full1, pair1 = tie(
-        (fore, back, near_f3, near_b3, near_f2, near_b2, full1, pair1)
+    fore, back, near_f3, near_b3, near_f2, near_b2, full1, pair1, grad_in = tie(
+        (fore, back, near_f3, near_b3, near_f2, near_b2, full1, pair1, out_grad)
     )
 
     fore, back = join(near_f3, fore, near_b3, back)
     fore, back = ring(fore, back)
     near0, near_b1, near_f1 = grads(saved, weights, ((0, -1, 1), full1, pair1, meta1))
-    fore, back, near0, near_b1, near_f1, dgate = tie(
-        (fore, back, near0, near_b1, near_f1, dgate)
+    grad_both = swap_core(grad_x)
+    dgate, dup = shared_slopes(
+        info, [grad_in, grad_core, grad_x, grad_both], shared_down, active, slope
+    )
+    fore, back, near0, near_b1, near_f1, dgate, dup = tie(
+        (fore, back, near0, near_b1, near_f1, dgate, dup)
     )
 
     fore, back = sums((near_f2, fore), (near_b2, back))

time: 99.8 us -> 96.4 us (0.966)
  waiting for transfers between devices: 32.2 us -> 29.8 us
  Pallas kernels: 31.7 us -> 30.6 us
    ppermute x7, waiting for transfers between devices: 8.74 us -> 3.62 us  [swap_x(): return lax.ppermute(a, 'tensor', x_pairs)]
    ppermute x8 -> x9, waiting for transfers between devices: 8.96 us -> 11 us  [ring(): lax.ppermute(fore, 'expert', ahead)]
    ppermute x8 -> x9, waiting for transfers between devices: 9.63 us -> 11.4 us  [ring(): lax.ppermute(back, 'expert', behind)]
    ppermute x8 -> x9, starting transfers between devices: 13.5 us -> 15.2 us  [ring(): lax.ppermute(fore, 'expert', ahead)]
    ppermute x14, starting transfers between devices: 3.52 us -> 2.31 us  [swap_core(): return lax.ppermute(a, 'tensor', core_pairs)]
    pallas_call x23 -> x25, Pallas kernels: 31.7 us -> 30.6 us  [run(): pl.pallas_call(kernel, in_specs=[pl.BlockSpec(memory_space=m) for m in me...]
    ppermute x14, waiting for transfers between devices: 4.88 us -> 3.81 us  [swap_core(): return lax.ppermute(a, 'tensor', core_pairs)]
    ppermute x8 -> x9, starting transfers between devices: 4.02 us -> 4.45 us  [ring(): lax.ppermute(back, 'expert', behind)]
  transfers between devices with their start and end apart: 37 -> 39, of which waited for: 20 -> 21; matrix products, arithmetic and copies ran while one was open for 0% -> 0% of each run, Pallas kernels for 28% -> 30%
where the time goes in v5:
time: 96.4 us; the launch traced here: 96.2 us
  starting transfers between devices  31 us (32%)
  Pallas kernels  30.6 us (32%)
  waiting for transfers between devices  29.8 us (31%)
  local copies, waits for them, and re-layouts  3.26 us (3%)
  matrix products  1.01 us (1%)
    pallas_call x25, Pallas kernels, run(): pl.pallas_call(kernel, in_specs=[pl.BlockSpec(memory_space=m) for m in me...  30.6 us
    ppermute x9, starting transfers between devices, ring(): lax.ppermute(fore, 'expert', ahead)  15.2 us
    ppermute x9, waiting for transfers between devices, ring(): lax.ppermute(back, 'expert', behind)  11.4 us
    ppermute x9, waiting for transfers between devices, ring(): lax.ppermute(fore, 'expert', ahead)  11 us
    ppermute x7, starting transfers between devices, swap_x(): return lax.ppermute(a, 'tensor', x_pairs)  9.03 us
    ppermute x9, starting transfers between devices, ring(): lax.ppermute(back, 'expert', behind)  4.45 us
    ppermute x14, waiting for transfers between devices, swap_core(): return lax.ppermute(a, 'tensor', core_pairs)  3.81 us
    ppermute x7, waiting for transfers between devices, swap_x(): return lax.ppermute(a, 'tensor', x_pairs)  3.62 us
  transfers between devices with their start and end apart: 39, of which 21 were waited for; matrix products, arithmetic and copies ran while one was open for 0% of the time, Pallas kernels for 30%

profile of v5, /device:TPU:0, one launch (start us, length us, event | category | flops | bytes accessed | tf_op | source)
XLA Modules:
  0.0 96.2 jit_solution(18439162844591354464)
XLA Ops:
  0.0 3.0 %collective-permute-start = (bf16[128,1280]{1,0:T(8,128)(2,1)}, bf16[128,1280]{1,0:T(8,128)(2,1)S(1)}, u32[]{:S(2)}, u32[]{:S(2)}) collective-permute-start(bf16[128,1280]{1,0:T(8,128)(2,1)} %refs_0_.1), channel_id=1, source_target_pairs={{0,8},{8,16},{16,24},{24,28},{28,20},{20,12},{12,4},{4,0},{1,9},{9... | collective-permute-start | bytes 983048 | tf_op jit(solution)/shard_map/ppermute | solution.py:543
  3.0 1.9 %collective-permute-start.2 = (bf16[128,1280]{1,0:T(8,128)(2,1)}, bf16[128,1280]{1,0:T(8,128)(2,1)S(1)}, u32[]{:S(2)}, u32[]{:S(2)}) collective-permute-start(bf16[128,1280]{1,0:T(8,128)(2,1)} %refs_0_.1), channel_id=1, source_target_pairs={{0,2},{1,3},{2,0},{3,1},{4,6},{5,7},{6,4},{7,5},{8,10},{9,11},{10,... | collective-permute-start | bytes 983048 | tf_op jit(solution)/shard_map/ppermute | solution.py:537
  5.0 1.8 %shard_map.127 = (bf16[136,1280]{1,0:T(8,128)(2,1)}, bf16[8,1280]{1,0:T(8,128)(2,1)}) custom-call(s32[6,128]{1,0:T(8,128)} %bitcast.31, f32[16,128]{1,0:T(8,128)} %bitcast.30, bf16[128,1280]{1,0:T(8,128)(2,1)} %refs_0_.1), custom_call_target="tpu_custom_call" | custom-call | flops 1000 | bytes 1000 | tf_op jit(solution)/shard_map/pallas_call | solution.py:143
  6.8 1.6 %collective-permute-start.3 = (bf16[8,1280]{1,0:T(8,128)(2,1)}, bf16[8,1280]{1,0:T(8,128)(2,1)S(1)}, u32[]{:S(2)}, u32[]{:S(2)}) collective-permute-start(bf16[8,1280]{1,0:T(8,128)(2,1)} %get-tuple-element.117), channel_id=1, source_target_pairs={{0,8},{8,16},{16,24},{24,28},{28,20},{20,12},{12,4},{4,0},{1,9},{9... | collective-permute-start | bytes 61448 | tf_op jit(solution)/shard_map/ppermute | solution.py:543
  8.9 2.4 %collective-permute-done.3.meta_f_ref = bf16[8,1280]{1,0:T(8,128)(2,1)S(1)} collective-permute-done((bf16[8,1280]{1,0:T(8,128)(2,1)}, bf16[8,1280]{1,0:T(8,128)(2,1)S(1)}, u32[]{:S(2)}, u32[]{:S(2)}) %collective-permute-start.3) | collective-permute-done | bytes 20512 | tf_op jit(solution)/shard_map/ppermute | solution.py:543
  11.4 1.5 %collective-permute-done.4.meta_b_ref = bf16[8,1280]{1,0:T(8,128)(2,1)S(1)} collective-permute-done((bf16[8,1280]{1,0:T(8,128)(2,1)}, bf16[8,1280]{1,0:T(8,128)(2,1)S(1)}, u32[]{:S(2)}, u32[]{:S(2)}) %collective-permute-start.4) | collective-permute-done | bytes 20512 | tf_op jit(solution)/shard_map/ppermute | solution.py:543
  12.9 1.6 %collective-permute-start.5 = (bf16[136,1280]{1,0:T(8,128)(2,1)S(1)}, bf16[136,1280]{1,0:T(8,128)(2,1)S(1)}, u32[]{:S(2)}, u32[]{:S(2)}) collective-permute-start(bf16[136,1280]{1,0:T(8,128)(2,1)S(1)} %get-tuple-element.123.refs_1_), channel_id=1, source_target_pairs={{0,8},{8,16},{16,24},{24,28},{28,20},{20,12},{12,4},{4,0},{1,9},{9... | collective-permute-start | bytes 1044488 | tf_op jit(solution)/shard_map/ppermute | solution.py:543
  15.0 1.5 %collective-permute-start.7 = (bf16[128,1280]{1,0:T(8,128)(2,1)}, bf16[128,1280]{1,0:T(8,128)(2,1)S(1)}, u32[]{:S(2)}, u32[]{:S(2)}) collective-permute-start(bf16[128,1280]{1,0:T(8,128)(2,1)} %refs_0_), channel_id=1, source_target_pairs={{0,2},{1,3},{2,0},{3,1},{4,6},{5,7},{6,4},{7,5},{8,10},{9,11},{10,... | collective-permute-start | bytes 983048 | tf_op jit(solution)/shard_map/ppermute | solution.py:537
  16.5 2.1 %copy-done.1 = bf16[2,768,1280]{2,1,0:T(8,128)(2,1)S(1)} copy-done((bf16[2,768,1280]{2,1,0:T(8,128)(2,1)S(1)}, bf16[2,768,1280]{2,1,0:T(8,128)(2,1)}, u32[]{:S(2)}) %copy-start.1) | copy-done | bytes 3932184
  19.6 2.2 %shard_map.129 = (bf16[192,768]{1,0:T(8,128)(2,1)S(1)}, bf16[192,768]{1,0:T(8,128)(2,1)S(1)}, f32[24,128]{1,0:T(8,128)S(1)}) custom-call(s32[12]{0:T(128)S(1)} %stack.51.info_ref, bf16[136,1280]{1,0:T(8,128)(2,1)S(1)} %copy-done.8, bf16[136,1280]{1,0:T(8,128)(2,1)S(1)} %get-tuple-element.123.refs_1_, bf16[136,1280]{1,0:T(8,128)(2,1)S(1)} %get-tuple-element.124.refs_2_, ...), custom_call_target="tpu_custom_call" | custom-call | flops 1000 | bytes 1000 | tf_op jit(solution)/shard_map/pallas_call | solution.py:143
  23.0 1.6 %collective-permute-start.8 = (bf16[136,1280]{1,0:T(8,128)(2,1)S(1)}, bf16[136,1280]{1,0:T(8,128)(2,1)S(1)}, u32[]{:S(2)}, u32[]{:S(2)}) collective-permute-start(bf16[136,1280]{1,0:T(8,128)(2,1)S(1)} %collective-permute-done.5.refs_0_), channel_id=1, source_target_pairs={{0,8},{8,16},{16,24},{24,28},{28,20},{20,12},{12,4},{4,0},{1,9},{9... | collective-permute-start | bytes 1044488 | tf_op jit(solution)/shard_map/ppermute | solution.py:543
  25.0 1.9 %shard_map.131 = (bf16[128,768]{1,0:T(8,128)(2,1)S(1)}, bf16[128,768]{1,0:T(8,128)(2,1)S(1)}, f32[16,128]{1,0:T(8,128)S(1)}) custom-call(s32[12]{0:T(128)S(1)} %stack.51.info_ref, bf16[136,1280]{1,0:T(8,128)(2,1)S(1)} %collective-permute-done.5.refs_0_, bf16[136,1280]{1,0:T(8,128)(2,1)S(1)} %collective-permute-done.6.refs_1_, bf16[2,768,1280]{2,1,0:T(8,128)(2,1)S(1)} %copy-done.2), custom_call_target="tpu_custom_call" | custom-call | flops 1000 | bytes 1000 | tf_op jit(solution)/shard_map/pallas_call | solution.py:143
  28.6 1.5 %collective-permute-start.16 = (bf16[192,768]{1,0:T(8,128)(2,1)S(1)}, bf16[192,768]{1,0:T(8,128)(2,1)S(1)}, u32[]{:S(2)}, u32[]{:S(2)}) collective-permute-start(bf16[192,768]{1,0:T(8,128)(2,1)S(1)} %shard_map.130.refs_0_), channel_id=1, source_target_pairs={{0,2},{1,3},{2,0},{3,1},{4,6},{5,7},{6,4},{7,5},{8,10},{9,11},{10,... | collective-permute-start | bytes 884744 | tf_op jit(solution)/shard_map/ppermute | solution.py:537
  30.2 3.3 %collective-permute-done.8.fore_ref.refs_0_ = bf16[136,1280]{1,0:T(8,128)(2,1)S(1)} collective-permute-done((bf16[136,1280]{1,0:T(8,128)(2,1)S(1)}, bf16[136,1280]{1,0:T(8,128)(2,1)S(1)}, u32[]{:S(2)}, u32[]{:S(2)}) %collective-permute-start.8) | collective-permute-done | bytes 348192 | tf_op jit(solution)/shard_map/ppermute | solution.py:543
  34.8 1.5 %collective-permute-start.17 = (bf16[128,768]{1,0:T(8,128)(2,1)S(1)}, bf16[128,768]{1,0:T(8,128)(2,1)S(1)}, u32[]{:S(2)}, u32[]{:S(2)}) collective-permute-start(bf16[128,768]{1,0:T(8,128)(2,1)S(1)} %shard_map.132.refs_0_), channel_id=1, source_target_pairs={{0,2},{1,3},{2,0},{3,1},{4,6},{5,7},{6,4},{7,5},{8,10},{9,11},{10,... | collective-permute-start | bytes 589832 | tf_op jit(solution)/shard_map/ppermute | solution.py:537
  36.8 1.6 %collective-permute-start.14 = (bf16[64,1280]{1,0:T(8,128)(2,1)S(1)}, bf16[64,1280]{1,0:T(8,128)(2,1)S(1)}, u32[]{:S(2)}, u32[]{:S(2)}) collective-permute-start(bf16[64,1280]{1,0:T(8,128)(2,1)S(1)} %get-tuple-element.136), channel_id=1, source_target_pairs={{0,8},{8,16},{16,24},{24,28},{28,20},{20,12},{12,4},{4,0},{1,9},{9... | collective-permute-start | bytes 491528 | tf_op jit(solution)/shard_map/ppermute | solution.py:543
  38.4 1.9 %shard_map.134 = (bf16[128,768]{1,0:T(8,128)(2,1)S(1)}, bf16[128,768]{1,0:T(8,128)(2,1)S(1)}, f32[16,128]{1,0:T(8,128)S(1)}) custom-call(s32[12]{0:T(128)S(1)} %stack.51.info_ref, bf16[136,1280]{1,0:T(8,128)(2,1)S(1)} %collective-permute-done.8.fore_ref.refs_0_, bf16[136,1280]{1,0:T(8,128)(2,1)S(1)} %collective-permute-done.9.back_ref.refs_1_, ...), custom_call_target="tpu_custom_call" | custom-call | flops 1000 | bytes 1000 | tf_op jit(solution)/shard_map/pallas_call | solution.py:143
  40.4 1.8 %collective-permute-done.14.refs_0_ = bf16[64,1280]{1,0:T(8,128)(2,1)S(1)} collective-permute-done((bf16[64,1280]{1,0:T(8,128)(2,1)S(1)}, bf16[64,1280]{1,0:T(8,128)(2,1)S(1)}, u32[]{:S(2)}, u32[]{:S(2)}) %collective-permute-start.14) | collective-permute-done | bytes 163872 | tf_op jit(solution)/shard_map/ppermute | solution.py:543
  42.2 1.3 %shard_map.135 = bf16[64,768]{1,0:T(8,128)(2,1)S(1)} custom-call(s32[12]{0:T(128)S(1)} %stack.51.info_ref, bf16[64,1280]{1,0:T(8,128)(2,1)S(1)} %collective-permute-done.14.refs_0_, bf16[72,1280]{1,0:T(8,128)(2,1)S(1)} %collective-permute-done.15.refs_1_, bf16[2,768,1280]{2,1,0:T(8,128)(2,1)S(1)} %copy-done.2), custom_call_target="tpu_custom_call" | custom-call | flops 1000 | bytes 1000 | tf_op jit(solution)/shard_map/pallas_call | solution.py:143
  44.2 1.3 %shard_map.136 = (bf16[64,768]{1,0:T(8,128)(2,1)S(1)}, f32[8,128]{1,0:T(8,128)S(1)}) custom-call(s32[12]{0:T(128)S(1)} %stack.51.info_ref, bf16[64,1280]{1,0:T(8,128)(2,1)S(1)} %collective-permute-done.14.refs_0_, bf16[72,1280]{1,0:T(8,128)(2,1)S(1)} %collective-permute-done.15.refs_1_, bf16[2,768,1280]{2,1,0:T(8,128)(2,1)S(1)} %copy-done.2), custom_call_target="tpu_custom_call" | custom-call | flops 1000 | bytes 1000 | tf_op jit(solution)/shard_map/pallas_call | solution.py:143
  45.9 1.4 %collective-permute-start.20 = (bf16[64,768]{1,0:T(8,128)(2,1)S(1)}, bf16[64,768]{1,0:T(8,128)(2,1)S(1)}, u32[]{:S(2)}, u32[]{:S(2)}) collective-permute-start(bf16[64,768]{1,0:T(8,128)(2,1)S(1)} %shard_map.137.refs_0_), channel_id=1, source_target_pairs={{0,2},{1,3},{2,0},{3,1},{4,6},{5,7},{6,4},{7,5},{8,10},{9,11},{10,... | collective-permute-start | bytes 294920 | tf_op jit(solution)/shard_map/ppermute | solution.py:537
  47.3 2.1 %shard_map.140 = (f32[128,512]{1,0:T(8,128)S(1)}, f32[128,512]{1,0:T(8,128)S(1)}) custom-call(s32[12]{0:T(128)S(1)} %stack.51.info_ref, bf16[128,1280]{1,0:T(8,128)(2,1)S(1)} %copy-done.9, bf16[128,1280]{1,0:T(8,128)(2,1)S(1)} %collective-permute-done.12.refs_1_, bf16[128,1280]{1,0:T(8,128)(2,1)S(1)} %collective-permute-done.7.refs_2_, ...), custom_call_target="tpu_custom_call" | custom-call | flops 1000 | bytes 1000 | tf_op jit(solution)/shard_map/pallas_call | solution.py:143
  52.4 3.2 %shard_map.143 = (bf16[64,1280]{1,0:T(8,128)(2,1)S(1)}, bf16[72,1280]{1,0:T(8,128)(2,1)S(1)}) custom-call(s32[12]{0:T(128)S(1)} %stack.51.info_ref, bf16[64,768]{1,0:T(8,128)(2,1)S(1)} %shard_map.142.refs_0_, bf16[64,768]{1,0:T(8,128)(2,1)S(1)} %collective-permute-done.23.refs_1_, f32[8,128]{1,0:T(8,128)S(1)} %get-tuple-element.171.refs_2_, ...), custom_call_target="tpu_custom_call" | custom-call | flops 1000 | bytes 1000 | tf_op jit(solution)/shard_map/pallas_call | solution.py:143
  59.1 3.6 %shard_map.145 = (bf16[136,1280]{1,0:T(8,128)(2,1)S(1)}, bf16[136,1280]{1,0:T(8,128)(2,1)S(1)}, bf16[136,1280]{1,0:T(8,128)(2,1)S(1)}, bf16[136,1280]{1,0:T(8,128)(2,1)S(1)}) custom-call(s32[12]{0:T(128)S(1)} %stack.51.info_ref, bf16[128,768]{1,0:T(8,128)(2,1)S(1)} %shard_map.144.refs_0_, bf16[128,768]{1,0:T(8,128)(2,1)S(1)} %collective-permute-done.28.refs_1_, ...), custom_call_target="tpu_custom_call" | custom-call | flops 1000 | bytes 1000 | tf_op jit(solution)/shard_map/pallas_call | solution.py:143
  62.7 1.6 %collective-permute-done.26.top_ref = bf16[64,1280]{1,0:T(8,128)(2,1)S(1)} collective-permute-done((bf16[64,1280]{1,0:T(8,128)(2,1)S(1)}, bf16[64,1280]{1,0:T(8,128)(2,1)S(1)}, u32[]{:S(2)}, u32[]{:S(2)}) %collective-permute-start.26) | collective-permute-done | bytes 163872 | tf_op jit(solution)/shard_map/ppermute | solution.py:543
  64.3 1.4 %collective-permute-start.29 = (bf16[136,1280]{1,0:T(8,128)(2,1)S(1)}, bf16[136,1280]{1,0:T(8,128)(2,1)S(1)}, u32[]{:S(2)}, u32[]{:S(2)}) collective-permute-start(bf16[136,1280]{1,0:T(8,128)(2,1)S(1)} %get-tuple-element.192), channel_id=1, source_target_pairs={{0,8},{8,16},{16,24},{24,28},{28,20},{20,12},{12,4},{4,0},{1,9},{9... | collective-permute-start | bytes 1044488 | tf_op jit(solution)/shard_map/ppermute | solution.py:543
  66.4 3.7 %shard_map.147 = (bf16[136,1280]{1,0:T(8,128)(2,1)S(1)}, bf16[136,1280]{1,0:T(8,128)(2,1)S(1)}, bf16[136,1280]{1,0:T(8,128)(2,1)S(1)}) custom-call(s32[12]{0:T(128)S(1)} %stack.51.info_ref, bf16[192,768]{1,0:T(8,128)(2,1)S(1)} %shard_map.138.refs_0_, bf16[192,768]{1,0:T(8,128)(2,1)S(1)} %collective-permute-done.22.refs_1_, ...), custom_call_target="tpu_custom_call" | custom-call | flops 1000 | bytes 1000 | tf_op jit(solution)/shard_map/pallas_call | solution.py:143
  70.2 2.4 %shard_map.148 = (bf16[128,512]{1,0:T(8,128)(2,1)S(1)}, bf16[128,512]{1,0:T(8,128)(2,1)S(1)}) custom-call(s32[12]{0:T(128)S(1)} %stack.51.info_ref, bf16[128,1280]{1,0:T(8,128)(2,1)S(1)} %copy-done.7, bf16[128,1280]{1,0:T(8,128)(2,1)S(1)} %collective-permute-done.13.refs_1_, bf16[128,1280]{1,0:T(8,128)(2,1)S(1)} %collective-permute-done.2.refs_2_, ...), custom_call_target="tpu_custom_call" | custom-call | flops 1000 | bytes 1000 | tf_op jit(solution)/shard_map/pallas_call | solution.py:143
  75.4 1.6 %collective-permute-start.32 = (bf16[136,1280]{1,0:T(8,128)(2,1)S(1)}, bf16[136,1280]{1,0:T(8,128)(2,1)S(1)}, u32[]{:S(2)}, u32[]{:S(2)}) collective-permute-start(bf16[136,1280]{1,0:T(8,128)(2,1)S(1)} %get-tuple-element.214), channel_id=1, source_target_pairs={{0,8},{8,16},{16,24},{24,28},{28,20},{20,12},{12,4},{4,0},{1,9},{9... | collective-permute-start | bytes 1044488 | tf_op jit(solution)/shard_map/ppermute | solution.py:543
  77.4 4.0 %shard_map.149 = (bf16[128,1280]{1,0:T(8,128)(2,1)S(1)}, bf16[128,1280]{1,0:T(8,128)(2,1)S(1)}, bf16[128,1280]{1,0:T(8,128)(2,1)S(1)}, bf16[128,1280]{1,0:T(8,128)(2,1)S(1)}) custom-call(s32[12]{0:T(128)S(1)} %stack.51.info_ref, bf16[128,512]{1,0:T(8,128)(2,1)S(1)} %get-tuple-element.207.dgate_ref, bf16[128,512]{1,0:T(8,128)(2,1)S(1)} %get-tuple-element.208.dup_ref, ...), custom_call_target="tpu_custom_call" | custom-call | flops 1000 | bytes 1000 | tf_op jit(solution)/shard_map/pallas_call | solution.py:143
  86.0 1.6 %collective-permute-start.37 = (bf16[136,1280]{1,0:T(8,128)(2,1)S(1)}, bf16[136,1280]{1,0:T(8,128)(2,1)S(1)}, u32[]{:S(2)}, u32[]{:S(2)}) collective-permute-start(bf16[136,1280]{1,0:T(8,128)(2,1)S(1)} %get-tuple-element.227), channel_id=1, source_target_pairs={{0,8},{8,16},{16,24},{24,28},{28,20},{20,12},{12,4},{4,0},{1,9},{9... | collective-permute-start | bytes 1044488 | tf_op jit(solution)/shard_map/ppermute | solution.py:543
  88.1 6.0 %collective-permute-done.38 = bf16[136,1280]{1,0:T(8,128)(2,1)S(1)} collective-permute-done((bf16[136,1280]{1,0:T(8,128)(2,1)S(1)}, bf16[136,1280]{1,0:T(8,128)(2,1)S(1)}, u32[]{:S(2)}, u32[]{:S(2)}) %collective-permute-start.38) | collective-permute-done | bytes 348192 | tf_op jit(solution)/shard_map/ppermute | solution.py:543
  (113 shorter events, 25.5 us)
Async XLA Ops:
  0.0 12.8 %collective-permute-start = (bf16[128,1280]{1,0:T(8,128)(2,1)}, bf16[128,1280]{1,0:T(8,128)(2,1)S(1)}, u32[]{:S(2)}, u32[]{:S(2)}) collective-permute-start(bf16[128,1280]{1,0:T(8,128)(2,1)} %refs_0_.1), channel_id=1, source_target_pairs={{0,8},{8,16},{16,24},{24,28},{28,20},{20,12},{12,4},{4,0},{1,9},{9... | collective-permute-start | bytes 983048 | tf_op jit(solution)/shard_map/ppermute | solution.py:543
  3.0 9.8 %collective-permute-start.1 = (bf16[128,1280]{1,0:T(8,128)(2,1)}, bf16[128,1280]{1,0:T(8,128)(2,1)S(1)}, u32[]{:S(2)}, u32[]{:S(2)}) collective-permute-start(bf16[128,1280]{1,0:T(8,128)(2,1)} %refs_0_.1), channel_id=1, source_target_pairs={{0,4},{8,0},{16,8},{24,16},{28,24},{20,28},{12,20},{4,12},{1,5},{9... | collective-permute-start | bytes 983048 | tf_op jit(solution)/shard_map/ppermute | solution.py:543
  3.0 9.8 %collective-permute-start.2 = (bf16[128,1280]{1,0:T(8,128)(2,1)}, bf16[128,1280]{1,0:T(8,128)(2,1)S(1)}, u32[]{:S(2)}, u32[]{:S(2)}) collective-permute-start(bf16[128,1280]{1,0:T(8,128)(2,1)} %refs_0_.1), channel_id=1, source_target_pairs={{0,2},{1,3},{2,0},{3,1},{4,6},{5,7},{6,4},{7,5},{8,10},{9,11},{10,... | collective-permute-start | bytes 983048 | tf_op jit(solution)/shard_map/ppermute | solution.py:537
  6.8 4.6 %collective-permute-start.3 = (bf16[8,1280]{1,0:T(8,128)(2,1)}, bf16[8,1280]{1,0:T(8,128)(2,1)S(1)}, u32[]{:S(2)}, u32[]{:S(2)}) collective-permute-start(bf16[8,1280]{1,0:T(8,128)(2,1)} %get-tuple-element.117), channel_id=1, source_target_pairs={{0,8},{8,16},{16,24},{24,28},{28,20},{20,12},{12,4},{4,0},{1,9},{9... | collective-permute-start | bytes 61448 | tf_op jit(solution)/shard_map/ppermute | solution.py:543
  8.4 4.5 %collective-permute-start.4 = (bf16[8,1280]{1,0:T(8,128)(2,1)}, bf16[8,1280]{1,0:T(8,128)(2,1)S(1)}, u32[]{:S(2)}, u32[]{:S(2)}) collective-permute-start(bf16[8,1280]{1,0:T(8,128)(2,1)} %get-tuple-element.117), channel_id=1, source_target_pairs={{0,4},{8,0},{16,8},{24,16},{28,24},{20,28},{12,20},{4,12},{1,5},{9... | collective-permute-start | bytes 61448 | tf_op jit(solution)/shard_map/ppermute | solution.py:543
  12.9 10.0 %collective-permute-start.5 = (bf16[136,1280]{1,0:T(8,128)(2,1)S(1)}, bf16[136,1280]{1,0:T(8,128)(2,1)S(1)}, u32[]{:S(2)}, u32[]{:S(2)}) collective-permute-start(bf16[136,1280]{1,0:T(8,128)(2,1)S(1)} %get-tuple-element.123.refs_1_), channel_id=1, source_target_pairs={{0,8},{8,16},{16,24},{24,28},{28,20},{20,12},{12,4},{4,0},{1,9},{9... | collective-permute-start | bytes 1044488 | tf_op jit(solution)/shard_map/ppermute | solution.py:543
  14.5 8.4 %collective-permute-start.6 = (bf16[136,1280]{1,0:T(8,128)(2,1)S(1)}, bf16[136,1280]{1,0:T(8,128)(2,1)S(1)}, u32[]{:S(2)}, u32[]{:S(2)}) collective-permute-start(bf16[136,1280]{1,0:T(8,128)(2,1)S(1)} %get-tuple-element.124.refs_2_), channel_id=1, source_target_pairs={{0,4},{8,0},{16,8},{24,16},{28,24},{20,28},{12,20},{4,12},{1,5},{9... | collective-permute-start | bytes 1044488 | tf_op jit(solution)/shard_map/ppermute | solution.py:543
  15.0 7.9 %collective-permute-start.7 = (bf16[128,1280]{1,0:T(8,128)(2,1)}, bf16[128,1280]{1,0:T(8,128)(2,1)S(1)}, u32[]{:S(2)}, u32[]{:S(2)}) collective-permute-start(bf16[128,1280]{1,0:T(8,128)(2,1)} %refs_0_), channel_id=1, source_target_pairs={{0,2},{1,3},{2,0},{3,1},{4,6},{5,7},{6,4},{7,5},{8,10},{9,11},{10,... | collective-permute-start | bytes 983048 | tf_op jit(solution)/shard_map/ppermute | solution.py:537
  16.5 10.5 %collective-permute-start.12 = (bf16[128,1280]{1,0:T(8,128)(2,1)}, bf16[128,1280]{1,0:T(8,128)(2,1)S(1)}, u32[]{:S(2)}, u32[]{:S(2)}) collective-permute-start(bf16[128,1280]{1,0:T(8,128)(2,1)} %refs_0_), channel_id=1, source_target_pairs={{0,1},{1,0},{2,3},{3,2},{4,5},{5,4},{6,7},{7,6},{8,9},{9,8},{10,11... | collective-permute-start | bytes 983048 | tf_op jit(solution)/shard_map/ppermute | solution.py:540
  23.0 4.6 %collective-permute-start.10 = (bf16[192,768]{1,0:T(8,128)(2,1)S(1)}, bf16[192,768]{1,0:T(8,128)(2,1)S(1)}, u32[]{:S(2)}, u32[]{:S(2)}) collective-permute-start(bf16[192,768]{1,0:T(8,128)(2,1)S(1)} %get-tuple-element.131), channel_id=1, source_target_pairs={{0,1},{1,0},{2,3},{3,2},{4,5},{5,4},{6,7},{7,6},{8,9},{9,8},{10,11... | collective-permute-start | bytes 884744 | tf_op jit(solution)/shard_map/ppermute | solution.py:540
  23.0 10.6 %collective-permute-start.8 = (bf16[136,1280]{1,0:T(8,128)(2,1)S(1)}, bf16[136,1280]{1,0:T(8,128)(2,1)S(1)}, u32[]{:S(2)}, u32[]{:S(2)}) collective-permute-start(bf16[136,1280]{1,0:T(8,128)(2,1)S(1)} %collective-permute-done.5.refs_0_), channel_id=1, source_target_pairs={{0,8},{8,16},{16,24},{24,28},{28,20},{20,12},{12,4},{4,0},{1,9},{9... | collective-permute-start | bytes 1044488 | tf_op jit(solution)/shard_map/ppermute | solution.py:543
  24.6 10.3 %collective-permute-start.9 = (bf16[136,1280]{1,0:T(8,128)(2,1)S(1)}, bf16[136,1280]{1,0:T(8,128)(2,1)S(1)}, u32[]{:S(2)}, u32[]{:S(2)}) collective-permute-start(bf16[136,1280]{1,0:T(8,128)(2,1)S(1)} %collective-permute-done.6.refs_1_), channel_id=1, source_target_pairs={{0,4},{8,0},{16,8},{24,16},{28,24},{20,28},{12,20},{4,12},{1,5},{9... | collective-permute-start | bytes 1044488 | tf_op jit(solution)/shard_map/ppermute | solution.py:543
  25.0 5.2 %collective-permute-start.13 = (bf16[128,1280]{1,0:T(8,128)(2,1)S(1)}, bf16[128,1280]{1,0:T(8,128)(2,1)S(1)}, u32[]{:S(2)}, u32[]{:S(2)}) collective-permute-start(bf16[128,1280]{1,0:T(8,128)(2,1)S(1)} %copy-done.7), channel_id=1, source_target_pairs={{0,1},{1,0},{2,3},{3,2},{4,5},{5,4},{6,7},{7,6},{8,9},{9,8},{10,11... | collective-permute-start | bytes 983048 | tf_op jit(solution)/shard_map/ppermute | solution.py:540
  27.5 12.8 %collective-permute-start.18 = (bf16[128,1280]{1,0:T(8,128)(2,1)S(1)}, bf16[128,1280]{1,0:T(8,128)(2,1)S(1)}, u32[]{:S(2)}, u32[]{:S(2)}) collective-permute-start(bf16[128,1280]{1,0:T(8,128)(2,1)S(1)} %collective-permute-done.7.refs_2_), channel_id=1, source_target_pairs={{0,1},{1,0},{2,3},{3,2},{4,5},{5,4},{6,7},{7,6},{8,9},{9,8},{10,11... | collective-permute-start | bytes 983048 | tf_op jit(solution)/shard_map/ppermute | solution.py:540
  28.6 13.6 %collective-permute-start.16 = (bf16[192,768]{1,0:T(8,128)(2,1)S(1)}, bf16[192,768]{1,0:T(8,128)(2,1)S(1)}, u32[]{:S(2)}, u32[]{:S(2)}) collective-permute-start(bf16[192,768]{1,0:T(8,128)(2,1)S(1)} %shard_map.130.refs_0_), channel_id=1, source_target_pairs={{0,2},{1,3},{2,0},{3,1},{4,6},{5,7},{6,4},{7,5},{8,10},{9,11},{10,... | collective-permute-start | bytes 884744 | tf_op jit(solution)/shard_map/ppermute | solution.py:537
  34.8 7.3 %collective-permute-start.17 = (bf16[128,768]{1,0:T(8,128)(2,1)S(1)}, bf16[128,768]{1,0:T(8,128)(2,1)S(1)}, u32[]{:S(2)}, u32[]{:S(2)}) collective-permute-start(bf16[128,768]{1,0:T(8,128)(2,1)S(1)} %shard_map.132.refs_0_), channel_id=1, source_target_pairs={{0,2},{1,3},{2,0},{3,1},{4,6},{5,7},{6,4},{7,5},{8,10},{9,11},{10,... | collective-permute-start | bytes 589832 | tf_op jit(solution)/shard_map/ppermute | solution.py:537
  36.3 5.8 %collective-permute-start.15 = (bf16[72,1280]{1,0:T(8,128)(2,1)S(1)}, bf16[72,1280]{1,0:T(8,128)(2,1)S(1)}, u32[]{:S(2)}, u32[]{:S(2)}) collective-permute-start(bf16[72,1280]{1,0:T(8,128)(2,1)S(1)} %get-tuple-element.137), channel_id=1, source_target_pairs={{0,4},{8,0},{16,8},{24,16},{28,24},{20,28},{12,20},{4,12},{1,5},{9... | collective-permute-start | bytes 552968 | tf_op jit(solution)/shard_map/ppermute | solution.py:543
  36.8 5.3 %collective-permute-start.14 = (bf16[64,1280]{1,0:T(8,128)(2,1)S(1)}, bf16[64,1280]{1,0:T(8,128)(2,1)S(1)}, u32[]{:S(2)}, u32[]{:S(2)}) collective-permute-start(bf16[64,1280]{1,0:T(8,128)(2,1)S(1)} %get-tuple-element.136), channel_id=1, source_target_pairs={{0,8},{8,16},{16,24},{24,28},{28,20},{20,12},{12,4},{4,0},{1,9},{9... | collective-permute-start | bytes 491528 | tf_op jit(solution)/shard_map/ppermute | solution.py:543
  45.7 5.3 %collective-permute-start.22 = (bf16[192,768]{1,0:T(8,128)(2,1)S(1)}, bf16[192,768]{1,0:T(8,128)(2,1)S(1)}, u32[]{:S(2)}, u32[]{:S(2)}) collective-permute-start(bf16[192,768]{1,0:T(8,128)(2,1)S(1)} %shard_map.138.refs_0_), channel_id=1, source_target_pairs={{0,1},{1,0},{2,3},{3,2},{4,5},{5,4},{6,7},{7,6},{8,9},{9,8},{10,11... | collective-permute-start | bytes 884744 | tf_op jit(solution)/shard_map/ppermute | solution.py:540
  45.9 5.1 %collective-permute-start.20 = (bf16[64,768]{1,0:T(8,128)(2,1)S(1)}, bf16[64,768]{1,0:T(8,128)(2,1)S(1)}, u32[]{:S(2)}, u32[]{:S(2)}) collective-permute-start(bf16[64,768]{1,0:T(8,128)(2,1)S(1)} %shard_map.137.refs_0_), channel_id=1, source_target_pairs={{0,2},{1,3},{2,0},{3,1},{4,6},{5,7},{6,4},{7,5},{8,10},{9,11},{10,... | collective-permute-start | bytes 294920 | tf_op jit(solution)/shard_map/ppermute | solution.py:537
  49.5 6.2 %collective-permute-start.24 = (bf16[128,768]{1,0:T(8,128)(2,1)S(1)}, bf16[128,768]{1,0:T(8,128)(2,1)S(1)}, u32[]{:S(2)}, u32[]{:S(2)}) collective-permute-start(bf16[128,768]{1,0:T(8,128)(2,1)S(1)} %shard_map.141.refs_3_), channel_id=1, source_target_pairs={{0,1},{1,0},{2,3},{3,2},{4,5},{5,4},{6,7},{7,6},{8,9},{9,8},{10,11... | collective-permute-start | bytes 589832 | tf_op jit(solution)/shard_map/ppermute | solution.py:540
  49.7 7.2 %collective-permute-start.25 = (bf16[128,768]{1,0:T(8,128)(2,1)S(1)}, bf16[128,768]{1,0:T(8,128)(2,1)S(1)}, u32[]{:S(2)}, u32[]{:S(2)}) collective-permute-start(bf16[128,768]{1,0:T(8,128)(2,1)S(1)} %shard_map.139.refs_0_), channel_id=1, source_target_pairs={{0,2},{1,3},{2,0},{3,1},{4,6},{5,7},{6,4},{7,5},{8,10},{9,11},{10,... | collective-permute-start | bytes 589832 | tf_op jit(solution)/shard_map/ppermute | solution.py:537
  57.0 7.3 %collective-permute-start.27 = (bf16[72,1280]{1,0:T(8,128)(2,1)S(1)}, bf16[72,1280]{1,0:T(8,128)(2,1)S(1)}, u32[]{:S(2)}, u32[]{:S(2)}) collective-permute-start(bf16[72,1280]{1,0:T(8,128)(2,1)S(1)} %get-tuple-element.176), channel_id=1, source_target_pairs={{0,4},{8,0},{16,8},{24,16},{28,24},{20,28},{12,20},{4,12},{1,5},{9... | collective-permute-start | bytes 552968 | tf_op jit(solution)/shard_map/ppermute | solution.py:543
  58.0 6.3 %collective-permute-start.26 = (bf16[64,1280]{1,0:T(8,128)(2,1)S(1)}, bf16[64,1280]{1,0:T(8,128)(2,1)S(1)}, u32[]{:S(2)}, u32[]{:S(2)}) collective-permute-start(bf16[64,1280]{1,0:T(8,128)(2,1)S(1)} %get-tuple-element.175), channel_id=1, source_target_pairs={{0,8},{8,16},{16,24},{24,28},{28,20},{20,12},{12,4},{4,0},{1,9},{9... | collective-permute-start | bytes 491528 | tf_op jit(solution)/shard_map/ppermute | solution.py:543
  64.3 9.6 %collective-permute-start.29 = (bf16[136,1280]{1,0:T(8,128)(2,1)S(1)}, bf16[136,1280]{1,0:T(8,128)(2,1)S(1)}, u32[]{:S(2)}, u32[]{:S(2)}) collective-permute-start(bf16[136,1280]{1,0:T(8,128)(2,1)S(1)} %get-tuple-element.192), channel_id=1, source_target_pairs={{0,8},{8,16},{16,24},{24,28},{28,20},{20,12},{12,4},{4,0},{1,9},{9... | collective-permute-start | bytes 1044488 | tf_op jit(solution)/shard_map/ppermute | solution.py:543
  65.8 9.4 %collective-permute-start.30 = (bf16[136,1280]{1,0:T(8,128)(2,1)S(1)}, bf16[136,1280]{1,0:T(8,128)(2,1)S(1)}, u32[]{:S(2)}, u32[]{:S(2)}) collective-permute-start(bf16[136,1280]{1,0:T(8,128)(2,1)S(1)} %get-tuple-element.193), channel_id=1, source_target_pairs={{0,4},{8,0},{16,8},{24,16},{28,24},{20,28},{12,20},{4,12},{1,5},{9... | collective-permute-start | bytes 1044488 | tf_op jit(solution)/shard_map/ppermute | solution.py:543
  66.4 3.7 %collective-permute-start.31 = (bf16[128,1280]{1,0:T(8,128)(2,1)S(1)}, bf16[128,1280]{1,0:T(8,128)(2,1)S(1)}, u32[]{:S(2)}, u32[]{:S(2)}) collective-permute-start(bf16[128,1280]{1,0:T(8,128)(2,1)S(1)} %collective-permute-done.2.refs_2_), channel_id=1, source_target_pairs={{0,1},{1,0},{2,3},{3,2},{4,5},{5,4},{6,7},{7,6},{8,9},{9,8},{10,11... | collective-permute-start | bytes 983048 | tf_op jit(solution)/shard_map/ppermute | solution.py:540
  75.4 8.6 %collective-permute-start.32 = (bf16[136,1280]{1,0:T(8,128)(2,1)S(1)}, bf16[136,1280]{1,0:T(8,128)(2,1)S(1)}, u32[]{:S(2)}, u32[]{:S(2)}) collective-permute-start(bf16[136,1280]{1,0:T(8,128)(2,1)S(1)} %get-tuple-element.214), channel_id=1, source_target_pairs={{0,8},{8,16},{16,24},{24,28},{28,20},{20,12},{12,4},{4,0},{1,9},{9... | collective-permute-start | bytes 1044488 | tf_op jit(solution)/shard_map/ppermute | solution.py:543
  77.0 8.2 %collective-permute-start.33 = (bf16[136,1280]{1,0:T(8,128)(2,1)S(1)}, bf16[136,1280]{1,0:T(8,128)(2,1)S(1)}, u32[]{:S(2)}, u32[]{:S(2)}) collective-permute-start(bf16[136,1280]{1,0:T(8,128)(2,1)S(1)} %get-tuple-element.215), channel_id=1, source_target_pairs={{0,4},{8,0},{16,8},{24,16},{28,24},{20,28},{12,20},{4,12},{1,5},{9... | collective-permute-start | bytes 1044488 | tf_op jit(solution)/shard_map/ppermute | solution.py:543
  85.5 8.6 %collective-permute-start.38 = (bf16[136,1280]{1,0:T(8,128)(2,1)S(1)}, bf16[136,1280]{1,0:T(8,128)(2,1)S(1)}, u32[]{:S(2)}, u32[]{:S(2)}) collective-permute-start(bf16[136,1280]{1,0:T(8,128)(2,1)S(1)} %get-tuple-element.228), channel_id=1, source_target_pairs={{0,4},{8,0},{16,8},{24,16},{28,24},{20,28},{12,20},{4,12},{1,5},{9... | collective-permute-start | bytes 1044488 | tf_op jit(solution)/shard_map/ppermute | solution.py:543
  86.0 8.4 %collective-permute-start.37 = (bf16[136,1280]{1,0:T(8,128)(2,1)S(1)}, bf16[136,1280]{1,0:T(8,128)(2,1)S(1)}, u32[]{:S(2)}, u32[]{:S(2)}) collective-permute-start(bf16[136,1280]{1,0:T(8,128)(2,1)S(1)} %get-tuple-element.227), channel_id=1, source_target_pairs={{0,8},{8,16},{16,24},{24,28},{28,20},{20,12},{12,4},{4,0},{1,9},{9... | collective-permute-start | bytes 1044488 | tf_op jit(solution)/shard_map/ppermute | solution.py:543
  87.5 7.6 %collective-permute-start.36 = (bf16[128,1280]{1,0:T(8,128)(2,1)S(1)}, bf16[128,1280]{1,0:T(8,128)(2,1)S(1)}, u32[]{:S(2)}, u32[]{:S(2)}) collective-permute-start(bf16[128,1280]{1,0:T(8,128)(2,1)S(1)} %get-tuple-element.225), channel_id=1, source_target_pairs={{0,2},{1,3},{2,0},{3,1},{4,6},{5,7},{6,4},{7,5},{8,10},{9,11},{10,... | collective-permute-start | bytes 983048 | tf_op jit(solution)/shard_map/ppermute | solution.py:537
  (24 other events, 227.2 us)

commit v6 on v5

--- a/solution.py
+++ b/solution.py
@@ -479,21 +479,20 @@
     )
 
 
-def shared_terms_kernel(info_ref, dgate_ref, dup_ref, gate_ref, up_ref, *out_refs):
+def shared_terms_kernel(which, info_ref, dgate_ref, dup_ref, gate_ref, up_ref, *out_refs):
     cols = out_refs[0].shape[1]
     spans = shared_spans(info_ref, cols)
     dgate, dup = dgate_ref[...], dup_ref[...]
-    for q in range(4):
+    for out_ref, q in zip(out_refs, which):
         term = lax.dot_general(dgate, gate_ref[spans[q], :], LAST, preferred_element_type=F32)
         term = term + lax.dot_general(dup, up_ref[spans[q], :], LAST, preferred_element_type=F32)
-        out_refs[q][...] = term.astype(BF16)
-
-
-def shared_terms(info, dgate, dup, shared_gate, shared_up, cols):
+        out_ref[...] = term.astype(BF16)
+
+
+def shared_terms(info, dgate, dup, shared_gate, shared_up, cols, which):
     shape = jax.ShapeDtypeStruct((dgate.shape[0], cols), BF16)
-    return call(shared_terms_kernel, 8, [shape] * 4, (), 1)(
-        info, dgate, dup, shared_gate, shared_up
-    )
+    kernel = functools.partial(shared_terms_kernel, which)
+    return call(kernel, 8, [shape] * len(which), (), 1)(info, dgate, dup, shared_gate, shared_up)
 
 
 def ring_place(position):
@@ -576,82 +575,88 @@
 
     fore, back = ring(fore2, back2)
     (chip1,) = sums((mine1, swap_core(other1)))
-    far1 = swap_x(chip1)
     other2, mine2, meta2 = hidden([fore2, back2])
     (chip2,) = sums((mine2, swap_core(other2)))
-    tok_core, grad_core = swap_core(tokens), swap_core(out_grad)
-    fore3, back3, chip1, chip2, tok_core, grad_core = tie(
-        (fore, back, chip1, chip2, tok_core, grad_core)
-    )
+    fore3, back3, chip1, chip2 = tie((fore, back, chip1, chip2))
 
     top, bottom = ring(*halves_of(fore3, back3))
     far2 = swap_x(chip2)
     other3, mine3, meta3 = hidden([fore3, back3])
     tok_both = swap_core(tok_x)
-    top, bottom, chip2, other3, mine3, far1, far2, tok_both = tie(
-        (top, bottom, chip2, other3, mine3, far1, far2, tok_both)
+    tok_core = swap_core(tokens)
+    top, bottom, chip2, other3, mine3, tok_core, tok_both, out_grad = tie(
+        (top, bottom, chip2, other3, mine3, tok_core, tok_both, out_grad)
     )
 
     (other4,) = hidden([(top, bottom)], (0,))
-    top, bottom, other4, other3 = tie((top, bottom, other4, other3))
+    top, bottom, other4, other3, far2 = tie((top, bottom, other4, other3, far2))
     swapped4 = swap_core(other4)
     mine4, meta4 = hidden([(top, bottom)], (1,))
     swapped3 = swap_core(other3)
     (chip4,) = sums((mine4, swapped4))
-    chip4, chip1, far1 = tie((chip4, chip1, far1))
+    chip4, swapped3, mine3, tok_in = tie((chip4, swapped3, mine3, tokens))
     far4 = swap_x(chip4)
-    (full1,) = sums((chip1, far1))
-    full1, swapped3, mine3 = tie((full1, swapped3, mine3))
     (chip3,) = sums((mine3, swapped3))
     far3 = swap_x(chip3)
-    chip3, tok_in, full1 = tie((chip3, tokens, full1))
-    pair1 = swap_core(full1)
+    chip3, tok_in = tie((chip3, tok_in))
     active, slope = shared_inner(
         info, [tok_in, tok_core, tok_x, tok_both], shared_gate, shared_up
     )
     active, slope, chip2, far2 = tie((active, slope, chip2, far2))
     (full2,) = sums((chip2, far2))
     pair2 = swap_core(full2)
-    far4, full2, active, pair1 = tie((far4, full2, active, pair1))
+    far4, full2, active = tie((far4, full2, active))
     (full4,) = sums((chip4, far4))
     pair4 = swap_core(full4)
     saved = (gate_saved, up_saved)
     weights = (gate_weight, up_weight)
     top, bottom = grads(saved, weights, ((4,), full4, pair4, meta4))
 
-    top, bottom, pair2, full2, far3 = tie((top, bottom, pair2, full2, far3))
+    top, bottom, pair2, full2, far3, out_grad, chip1 = tie(
+        (top, bottom, pair2, full2, far3, out_grad, chip1)
+    )
     fore, back = ring(top, bottom)
+    grad_core = swap_core(out_grad)
+    far1 = swap_x(chip1)
     (full3,) = sums((chip3, far3))
     pair3 = swap_core(full3)
     near_b3, near_f3, near_b2, near_f2 = grads(
         saved, weights, ((-3, 3), full3, pair3, meta3), ((-2, 2), full2, pair2, meta2)
     )
-    fore, back, near_f3, near_b3, near_f2, near_b2, full1, pair1, grad_in = tie(
-        (fore, back, near_f3, near_b3, near_f2, near_b2, full1, pair1, out_grad)
+    fore, back, near_f3, near_b3, near_f2, near_b2, grad_core, grad_in = tie(
+        (fore, back, near_f3, near_b3, near_f2, near_b2, grad_core, out_grad)
     )
 
     fore, back = join(near_f3, fore, near_b3, back)
     fore, back = ring(fore, back)
-    near0, near_b1, near_f1 = grads(saved, weights, ((0, -1, 1), full1, pair1, meta1))
     grad_both = swap_core(grad_x)
+    grad_in, far1 = tie((grad_in, far1))
     dgate, dup = shared_slopes(
         info, [grad_in, grad_core, grad_x, grad_both], shared_down, active, slope
     )
-    fore, back, near0, near_b1, near_f1, dgate, dup = tie(
-        (fore, back, near0, near_b1, near_f1, dgate, dup)
-    )
-
-    fore, back = sums((near_f2, fore), (near_b2, back))
-    fore, back = ring(fore, back)
-    terms = shared_terms(info, dgate, dup, shared_gate, shared_up, cols)
-    swapped, near = swap_core(terms[3]), swap_core(terms[1])
-    fore, back, swapped, near = tie((fore, back, swapped, near))
-
-    fore, back, far = sums((near_f1, fore), (near_b1, back), (terms[2], swapped))
+    term3, term2 = shared_terms(info, dgate, dup, shared_gate, shared_up, cols, (3, 2))
+    swapped = swap_core(term3)
+    term3, dgate, dup = tie((term3, dgate, dup))
+    term1, term0 = shared_terms(info, dgate, dup, shared_gate, shared_up, cols, (1, 0))
+    fore, back, term1, term0, swapped, chip1, far1 = tie(
+        (fore, back, term1, term0, swapped, chip1, far1)
+    )
+
+    fore, back, far = sums((near_f2, fore), (near_b2, back), (term2, swapped))
     fore, back = ring(fore, back)
     shared_far = swap_x(far)
+    near = swap_core(term1)
+    (full1,) = sums((chip1, far1))
+    pair1 = swap_core(full1)
+    near0, near_b1, near_f1 = grads(saved, weights, ((0, -1, 1), full1, pair1, meta1))
+    fore, back, near, near0, near_b1, near_f1 = tie(
+        (fore, back, near, near0, near_b1, near_f1)
+    )
+
+    fore, back = sums((near_f1, fore), (near_b1, back))
+    fore, back = ring(fore, back)
     total = near0.astype(F32) + fore.astype(F32) + back.astype(F32)
-    shared_part = terms[0].astype(F32) + near.astype(F32) + shared_far.astype(F32)
+    shared_part = term0.astype(F32) + near.astype(F32) + shared_far.astype(F32)
     prob_grad = jnp.concatenate(
         [total[rows:, i * rows : (i + 1) * rows] for i in range(tiles)], axis=0
     ).T

time: 96.4 us -> 94.8 us (0.983)
  waiting for transfers between devices: 29.8 us -> 27.1 us
    ppermute x7, waiting for transfers between devices: 3.62 us -> 2.2 us  [swap_x(): return lax.ppermute(a, 'tensor', x_pairs)]
    pallas_call x25 -> x26, Pallas kernels: 30.6 us -> 31.2 us  [run(): pl.pallas_call(kernel, in_specs=[pl.BlockSpec(memory_space=m) for m in me...]
  transfers between devices with their start and end apart: 39 -> 39, of which waited for: 21 -> 19; matrix products, arithmetic and copies ran while one was open for 0% -> 0% of each run, Pallas kernels for 30% -> 32%
where the time goes in v6:
time: 94.8 us; the launch traced here: 94.6 us
  starting transfers between devices  31.4 us (33%)
  Pallas kernels  31.2 us (33%)
  waiting for transfers between devices  27.1 us (29%)
  local copies, waits for them, and re-layouts  3.25 us (3%)
  matrix products  1.02 us (1%)
    pallas_call x26, Pallas kernels, run(): pl.pallas_call(kernel, in_specs=[pl.BlockSpec(memory_space=m) for m in me...  31.2 us
    ppermute x9, starting transfers between devices, ring(): lax.ppermute(fore, 'expert', ahead)  15 us
    ppermute x9, waiting for transfers between devices, ring(): lax.ppermute(back, 'expert', behind)  10.7 us
    ppermute x9, waiting for transfers between devices, ring(): lax.ppermute(fore, 'expert', ahead)  10.4 us
    ppermute x7, starting transfers between devices, swap_x(): return lax.ppermute(a, 'tensor', x_pairs)  9.11 us
    ppermute x9, starting transfers between devices, ring(): lax.ppermute(back, 'expert', behind)  4.56 us
    ppermute x14, waiting for transfers between devices, swap_core(): return lax.ppermute(a, 'tensor', core_pairs)  3.79 us
    unnamed x34, local copies, waits for them, and re-layouts  3.16 us
  transfers between devices with their start and end apart: 39, of which 19 were waited for; matrix products, arithmetic and copies ran while one was open for 0% of the time, Pallas kernels for 32%

profile of v6, /device:TPU:0, one launch (start us, length us, event | category | flops | bytes accessed | tf_op | source)
XLA Modules:
  0.0 94.6 jit_solution(849668166179262062)
XLA Ops:
  0.0 3.0 %collective-permute-start = (bf16[128,1280]{1,0:T(8,128)(2,1)}, bf16[128,1280]{1,0:T(8,128)(2,1)S(1)}, u32[]{:S(2)}, u32[]{:S(2)}) collective-permute-start(bf16[128,1280]{1,0:T(8,128)(2,1)} %refs_0_.1), channel_id=1, source_target_pairs={{0,8},{8,16},{16,24},{24,28},{28,20},{20,12},{12,4},{4,0},{1,9},{9... | collective-permute-start | bytes 983048 | tf_op jit(solution)/shard_map/ppermute | solution.py:542
  3.0 1.9 %collective-permute-start.2 = (bf16[128,1280]{1,0:T(8,128)(2,1)}, bf16[128,1280]{1,0:T(8,128)(2,1)S(1)}, u32[]{:S(2)}, u32[]{:S(2)}) collective-permute-start(bf16[128,1280]{1,0:T(8,128)(2,1)} %refs_0_.1), channel_id=1, source_target_pairs={{0,2},{1,3},{2,0},{3,1},{4,6},{5,7},{6,4},{7,5},{8,10},{9,11},{10,... | collective-permute-start | bytes 983048 | tf_op jit(solution)/shard_map/ppermute | solution.py:536
  5.0 1.8 %shard_map.127 = (bf16[136,1280]{1,0:T(8,128)(2,1)}, bf16[8,1280]{1,0:T(8,128)(2,1)}) custom-call(s32[6,128]{1,0:T(8,128)} %bitcast.31, f32[16,128]{1,0:T(8,128)} %bitcast.30, bf16[128,1280]{1,0:T(8,128)(2,1)} %refs_0_.1), custom_call_target="tpu_custom_call" | custom-call | flops 1000 | bytes 1000 | tf_op jit(solution)/shard_map/pallas_call | solution.py:143
  6.8 1.6 %collective-permute-start.3 = (bf16[8,1280]{1,0:T(8,128)(2,1)}, bf16[8,1280]{1,0:T(8,128)(2,1)S(1)}, u32[]{:S(2)}, u32[]{:S(2)}) collective-permute-start(bf16[8,1280]{1,0:T(8,128)(2,1)} %get-tuple-element.119), channel_id=1, source_target_pairs={{0,8},{8,16},{16,24},{24,28},{28,20},{20,12},{12,4},{4,0},{1,9},{9... | collective-permute-start | bytes 61448 | tf_op jit(solution)/shard_map/ppermute | solution.py:542
  8.9 2.4 %collective-permute-done.3.meta_f_ref = bf16[8,1280]{1,0:T(8,128)(2,1)S(1)} collective-permute-done((bf16[8,1280]{1,0:T(8,128)(2,1)}, bf16[8,1280]{1,0:T(8,128)(2,1)S(1)}, u32[]{:S(2)}, u32[]{:S(2)}) %collective-permute-start.3) | collective-permute-done | bytes 20512 | tf_op jit(solution)/shard_map/ppermute | solution.py:542
  11.3 1.5 %collective-permute-done.4.meta_b_ref = bf16[8,1280]{1,0:T(8,128)(2,1)S(1)} collective-permute-done((bf16[8,1280]{1,0:T(8,128)(2,1)}, bf16[8,1280]{1,0:T(8,128)(2,1)S(1)}, u32[]{:S(2)}, u32[]{:S(2)}) %collective-permute-start.4) | collective-permute-done | bytes 20512 | tf_op jit(solution)/shard_map/ppermute | solution.py:542
  12.9 1.6 %collective-permute-start.5 = (bf16[136,1280]{1,0:T(8,128)(2,1)S(1)}, bf16[136,1280]{1,0:T(8,128)(2,1)S(1)}, u32[]{:S(2)}, u32[]{:S(2)}) collective-permute-start(bf16[136,1280]{1,0:T(8,128)(2,1)S(1)} %get-tuple-element.125.refs_1_), channel_id=1, source_target_pairs={{0,8},{8,16},{16,24},{24,28},{28,20},{20,12},{12,4},{4,0},{1,9},{9... | collective-permute-start | bytes 1044488 | tf_op jit(solution)/shard_map/ppermute | solution.py:542
  15.0 1.5 %collective-permute-start.7 = (bf16[128,1280]{1,0:T(8,128)(2,1)}, bf16[128,1280]{1,0:T(8,128)(2,1)S(1)}, u32[]{:S(2)}, u32[]{:S(2)}) collective-permute-start(bf16[128,1280]{1,0:T(8,128)(2,1)} %refs_0_), channel_id=1, source_target_pairs={{0,2},{1,3},{2,0},{3,1},{4,6},{5,7},{6,4},{7,5},{8,10},{9,11},{10,... | collective-permute-start | bytes 983048 | tf_op jit(solution)/shard_map/ppermute | solution.py:536
  16.5 2.1 %copy-done.1 = bf16[2,768,1280]{2,1,0:T(8,128)(2,1)S(1)} copy-done((bf16[2,768,1280]{2,1,0:T(8,128)(2,1)S(1)}, bf16[2,768,1280]{2,1,0:T(8,128)(2,1)}, u32[]{:S(2)}) %copy-start.1) | copy-done | bytes 3932184
  19.6 2.2 %shard_map.129 = (bf16[192,768]{1,0:T(8,128)(2,1)S(1)}, bf16[192,768]{1,0:T(8,128)(2,1)S(1)}, f32[24,128]{1,0:T(8,128)S(1)}) custom-call(s32[12]{0:T(128)S(1)} %stack.51.info_ref, bf16[136,1280]{1,0:T(8,128)(2,1)S(1)} %copy-done.8, bf16[136,1280]{1,0:T(8,128)(2,1)S(1)} %get-tuple-element.125.refs_1_, bf16[136,1280]{1,0:T(8,128)(2,1)S(1)} %get-tuple-element.126.refs_2_, ...), custom_call_target="tpu_custom_call" | custom-call | flops 1000 | bytes 1000 | tf_op jit(solution)/shard_map/pallas_call | solution.py:143
  23.0 1.6 %collective-permute-start.8 = (bf16[136,1280]{1,0:T(8,128)(2,1)S(1)}, bf16[136,1280]{1,0:T(8,128)(2,1)S(1)}, u32[]{:S(2)}, u32[]{:S(2)}) collective-permute-start(bf16[136,1280]{1,0:T(8,128)(2,1)S(1)} %collective-permute-done.5.refs_0_), channel_id=1, source_target_pairs={{0,8},{8,16},{16,24},{24,28},{28,20},{20,12},{12,4},{4,0},{1,9},{9... | collective-permute-start | bytes 1044488 | tf_op jit(solution)/shard_map/ppermute | solution.py:542
  25.0 1.9 %shard_map.131 = (bf16[128,768]{1,0:T(8,128)(2,1)S(1)}, bf16[128,768]{1,0:T(8,128)(2,1)S(1)}, f32[16,128]{1,0:T(8,128)S(1)}) custom-call(s32[12]{0:T(128)S(1)} %stack.51.info_ref, bf16[136,1280]{1,0:T(8,128)(2,1)S(1)} %collective-permute-done.5.refs_0_, bf16[136,1280]{1,0:T(8,128)(2,1)S(1)} %collective-permute-done.6.refs_1_, bf16[2,768,1280]{2,1,0:T(8,128)(2,1)S(1)} %copy-done.2), custom_call_target="tpu_custom_call" | custom-call | flops 1000 | bytes 1000 | tf_op jit(solution)/shard_map/pallas_call | solution.py:143
  28.9 1.5 %collective-permute-done.8.fore_ref.refs_0_ = bf16[136,1280]{1,0:T(8,128)(2,1)S(1)} collective-permute-done((bf16[136,1280]{1,0:T(8,128)(2,1)S(1)}, bf16[136,1280]{1,0:T(8,128)(2,1)S(1)}, u32[]{:S(2)}, u32[]{:S(2)}) %collective-permute-start.8) | collective-permute-done | bytes 348192 | tf_op jit(solution)/shard_map/ppermute | solution.py:542
  31.8 1.5 %collective-permute-start.16 = (bf16[128,768]{1,0:T(8,128)(2,1)S(1)}, bf16[128,768]{1,0:T(8,128)(2,1)S(1)}, u32[]{:S(2)}, u32[]{:S(2)}) collective-permute-start(bf16[128,768]{1,0:T(8,128)(2,1)S(1)} %shard_map.132.refs_0_), channel_id=1, source_target_pairs={{0,2},{1,3},{2,0},{3,1},{4,6},{5,7},{6,4},{7,5},{8,10},{9,11},{10,... | collective-permute-start | bytes 589832 | tf_op jit(solution)/shard_map/ppermute | solution.py:536
  33.9 1.6 %collective-permute-start.12 = (bf16[64,1280]{1,0:T(8,128)(2,1)S(1)}, bf16[64,1280]{1,0:T(8,128)(2,1)S(1)}, u32[]{:S(2)}, u32[]{:S(2)}) collective-permute-start(bf16[64,1280]{1,0:T(8,128)(2,1)S(1)} %get-tuple-element.138), channel_id=1, source_target_pairs={{0,8},{8,16},{16,24},{24,28},{28,20},{20,12},{12,4},{4,0},{1,9},{9... | collective-permute-start | bytes 491528 | tf_op jit(solution)/shard_map/ppermute | solution.py:542
  35.4 1.9 %shard_map.134 = (bf16[128,768]{1,0:T(8,128)(2,1)S(1)}, bf16[128,768]{1,0:T(8,128)(2,1)S(1)}, f32[16,128]{1,0:T(8,128)S(1)}) custom-call(s32[12]{0:T(128)S(1)} %stack.51.info_ref, bf16[136,1280]{1,0:T(8,128)(2,1)S(1)} %collective-permute-done.8.fore_ref.refs_0_, bf16[136,1280]{1,0:T(8,128)(2,1)S(1)} %collective-permute-done.9.back_ref.refs_1_, ...), custom_call_target="tpu_custom_call" | custom-call | flops 1000 | bytes 1000 | tf_op jit(solution)/shard_map/pallas_call | solution.py:143
  37.4 1.8 %collective-permute-done.12.refs_0_ = bf16[64,1280]{1,0:T(8,128)(2,1)S(1)} collective-permute-done((bf16[64,1280]{1,0:T(8,128)(2,1)S(1)}, bf16[64,1280]{1,0:T(8,128)(2,1)S(1)}, u32[]{:S(2)}, u32[]{:S(2)}) %collective-permute-start.12) | collective-permute-done | bytes 163872 | tf_op jit(solution)/shard_map/ppermute | solution.py:542
  43.3 2.1 %shard_map.139 = (f32[128,512]{1,0:T(8,128)S(1)}, f32[128,512]{1,0:T(8,128)S(1)}) custom-call(s32[12]{0:T(128)S(1)} %stack.51.info_ref, bf16[128,1280]{1,0:T(8,128)(2,1)S(1)} %copy-done.9, bf16[128,1280]{1,0:T(8,128)(2,1)S(1)} %collective-permute-done.14.refs_1_, bf16[128,1280]{1,0:T(8,128)(2,1)S(1)} %collective-permute-done.7.refs_2_, ...), custom_call_target="tpu_custom_call" | custom-call | flops 1000 | bytes 1000 | tf_op jit(solution)/shard_map/pallas_call | solution.py:143
  45.5 1.5 %collective-permute-start.22 = (bf16[128,768]{1,0:T(8,128)(2,1)S(1)}, bf16[128,768]{1,0:T(8,128)(2,1)S(1)}, u32[]{:S(2)}, u32[]{:S(2)}) collective-permute-start(bf16[128,768]{1,0:T(8,128)(2,1)S(1)} %shard_map.138.refs_0_), channel_id=1, source_target_pairs={{0,2},{1,3},{2,0},{3,1},{4,6},{5,7},{6,4},{7,5},{8,10},{9,11},{10,... | collective-permute-start | bytes 589832 | tf_op jit(solution)/shard_map/ppermute | solution.py:536
  48.8 3.2 %shard_map.142 = (bf16[64,1280]{1,0:T(8,128)(2,1)S(1)}, bf16[72,1280]{1,0:T(8,128)(2,1)S(1)}) custom-call(s32[12]{0:T(128)S(1)} %stack.51.info_ref, bf16[64,768]{1,0:T(8,128)(2,1)S(1)} %shard_map.141.refs_0_, bf16[64,768]{1,0:T(8,128)(2,1)S(1)} %collective-permute-done.20.refs_1_, f32[8,128]{1,0:T(8,128)S(1)} %get-tuple-element.168.refs_2_, ...), custom_call_target="tpu_custom_call" | custom-call | flops 1000 | bytes 1000 | tf_op jit(solution)/shard_map/pallas_call | solution.py:143
  53.5 1.5 %collective-permute-start.29 = (bf16[192,768]{1,0:T(8,128)(2,1)S(1)}, bf16[192,768]{1,0:T(8,128)(2,1)S(1)}, u32[]{:S(2)}, u32[]{:S(2)}) collective-permute-start(bf16[192,768]{1,0:T(8,128)(2,1)S(1)} %shard_map.130.refs_0_), channel_id=1, source_target_pairs={{0,2},{1,3},{2,0},{3,1},{4,6},{5,7},{6,4},{7,5},{8,10},{9,11},{10,... | collective-permute-start | bytes 884744 | tf_op jit(solution)/shard_map/ppermute | solution.py:536
  57.0 3.6 %shard_map.144 = (bf16[136,1280]{1,0:T(8,128)(2,1)S(1)}, bf16[136,1280]{1,0:T(8,128)(2,1)S(1)}, bf16[136,1280]{1,0:T(8,128)(2,1)S(1)}, bf16[136,1280]{1,0:T(8,128)(2,1)S(1)}) custom-call(s32[12]{0:T(128)S(1)} %stack.51.info_ref, bf16[128,768]{1,0:T(8,128)(2,1)S(1)} %shard_map.143.refs_0_, bf16[128,768]{1,0:T(8,128)(2,1)S(1)} %collective-permute-done.25.refs_1_, ...), custom_call_target="tpu_custom_call" | custom-call | flops 1000 | bytes 1000 | tf_op jit(solution)/shard_map/pallas_call | solution.py:143
  62.0 1.4 %collective-permute-start.27 = (bf16[136,1280]{1,0:T(8,128)(2,1)S(1)}, bf16[136,1280]{1,0:T(8,128)(2,1)S(1)}, u32[]{:S(2)}, u32[]{:S(2)}) collective-permute-start(bf16[136,1280]{1,0:T(8,128)(2,1)S(1)} %get-tuple-element.191), channel_id=1, source_target_pairs={{0,8},{8,16},{16,24},{24,28},{28,20},{20,12},{12,4},{4,0},{1,9},{9... | collective-permute-start | bytes 1044488 | tf_op jit(solution)/shard_map/ppermute | solution.py:542
  64.1 2.4 %shard_map.146 = (bf16[128,512]{1,0:T(8,128)(2,1)S(1)}, bf16[128,512]{1,0:T(8,128)(2,1)S(1)}) custom-call(s32[12]{0:T(128)S(1)} %stack.51.info_ref, bf16[128,1280]{1,0:T(8,128)(2,1)S(1)} %copy-done.7, bf16[128,1280]{1,0:T(8,128)(2,1)S(1)} %collective-permute-done.26.refs_1_, bf16[128,1280]{1,0:T(8,128)(2,1)S(1)} %collective-permute-done.2.refs_2_, ...), custom_call_target="tpu_custom_call" | custom-call | flops 1000 | bytes 1000 | tf_op jit(solution)/shard_map/pallas_call | solution.py:143
  66.5 2.4 %shard_map.147 = (bf16[128,1280]{1,0:T(8,128)(2,1)S(1)}, bf16[128,1280]{1,0:T(8,128)(2,1)S(1)}) custom-call(s32[12]{0:T(128)S(1)} %stack.51.info_ref, bf16[128,512]{1,0:T(8,128)(2,1)S(1)} %get-tuple-element.203.dgate_ref, bf16[128,512]{1,0:T(8,128)(2,1)S(1)} %get-tuple-element.204.dup_ref, bf16[5120,512]{1,0:T(8,128)(2,1)S(1)} %bitcast.25, ...), custom_call_target="tpu_custom_call" | custom-call | flops 1000 | bytes 1000 | tf_op jit(solution)/shard_map/pallas_call | solution.py:143
  68.9 2.3 %shard_map.148 = (bf16[128,1280]{1,0:T(8,128)(2,1)S(1)}, bf16[128,1280]{1,0:T(8,128)(2,1)S(1)}) custom-call(s32[12]{0:T(128)S(1)} %stack.51.info_ref, bf16[128,512]{1,0:T(8,128)(2,1)S(1)} %get-tuple-element.203.dgate_ref, bf16[128,512]{1,0:T(8,128)(2,1)S(1)} %get-tuple-element.204.dup_ref, bf16[5120,512]{1,0:T(8,128)(2,1)S(1)} %bitcast.25, ...), custom_call_target="tpu_custom_call" | custom-call | flops 1000 | bytes 1000 | tf_op jit(solution)/shard_map/pallas_call | solution.py:143
  72.8 1.6 %collective-permute-start.32 = (bf16[136,1280]{1,0:T(8,128)(2,1)S(1)}, bf16[136,1280]{1,0:T(8,128)(2,1)S(1)}, u32[]{:S(2)}, u32[]{:S(2)}) collective-permute-start(bf16[136,1280]{1,0:T(8,128)(2,1)S(1)} %get-tuple-element.215), channel_id=1, source_target_pairs={{0,8},{8,16},{16,24},{24,28},{28,20},{20,12},{12,4},{4,0},{1,9},{9... | collective-permute-start | bytes 1044488 | tf_op jit(solution)/shard_map/ppermute | solution.py:542
  75.5 1.4 %collective-permute-done.35.refs_1_ = bf16[192,768]{1,0:T(8,128)(2,1)S(1)} collective-permute-done((bf16[192,768]{1,0:T(8,128)(2,1)S(1)}, bf16[192,768]{1,0:T(8,128)(2,1)S(1)}, u32[]{:S(2)}, u32[]{:S(2)}) %collective-permute-start.35) | collective-permute-done | bytes 294944 | tf_op jit(solution)/shard_map/ppermute | solution.py:539
  76.9 3.7 %shard_map.151 = (bf16[136,1280]{1,0:T(8,128)(2,1)S(1)}, bf16[136,1280]{1,0:T(8,128)(2,1)S(1)}, bf16[136,1280]{1,0:T(8,128)(2,1)S(1)}) custom-call(s32[12]{0:T(128)S(1)} %stack.51.info_ref, bf16[192,768]{1,0:T(8,128)(2,1)S(1)} %shard_map.150.refs_0_, bf16[192,768]{1,0:T(8,128)(2,1)S(1)} %collective-permute-done.35.refs_1_, ...), custom_call_target="tpu_custom_call" | custom-call | flops 1000 | bytes 1000 | tf_op jit(solution)/shard_map/pallas_call | solution.py:143
  80.7 1.5 %collective-permute-done.32.refs_1_ = bf16[136,1280]{1,0:T(8,128)(2,1)S(1)} collective-permute-done((bf16[136,1280]{1,0:T(8,128)(2,1)S(1)}, bf16[136,1280]{1,0:T(8,128)(2,1)S(1)}, u32[]{:S(2)}, u32[]{:S(2)}) %collective-permute-start.32) | collective-permute-done | bytes 348192 | tf_op jit(solution)/shard_map/ppermute | solution.py:542
  86.1 5.4 %collective-permute-done.38 = bf16[136,1280]{1,0:T(8,128)(2,1)S(1)} collective-permute-done((bf16[136,1280]{1,0:T(8,128)(2,1)S(1)}, bf16[136,1280]{1,0:T(8,128)(2,1)S(1)}, u32[]{:S(2)}, u32[]{:S(2)}) %collective-permute-start.38) | collective-permute-done | bytes 348192 | tf_op jit(solution)/shard_map/ppermute | solution.py:542
  91.5 1.9 %collective-permute-done.37 = bf16[136,1280]{1,0:T(8,128)(2,1)S(1)} collective-permute-done((bf16[136,1280]{1,0:T(8,128)(2,1)S(1)}, bf16[136,1280]{1,0:T(8,128)(2,1)S(1)}, u32[]{:S(2)}, u32[]{:S(2)}) %collective-permute-start.37) | collective-permute-done | bytes 348192 | tf_op jit(solution)/shard_map/ppermute | solution.py:542
  (114 shorter events, 26.6 us)
Async XLA Ops:
  0.0 12.8 %collective-permute-start = (bf16[128,1280]{1,0:T(8,128)(2,1)}, bf16[128,1280]{1,0:T(8,128)(2,1)S(1)}, u32[]{:S(2)}, u32[]{:S(2)}) collective-permute-start(bf16[128,1280]{1,0:T(8,128)(2,1)} %refs_0_.1), channel_id=1, source_target_pairs={{0,8},{8,16},{16,24},{24,28},{28,20},{20,12},{12,4},{4,0},{1,9},{9... | collective-permute-start | bytes 983048 | tf_op jit(solution)/shard_map/ppermute | solution.py:542
  3.0 9.8 %collective-permute-start.1 = (bf16[128,1280]{1,0:T(8,128)(2,1)}, bf16[128,1280]{1,0:T(8,128)(2,1)S(1)}, u32[]{:S(2)}, u32[]{:S(2)}) collective-permute-start(bf16[128,1280]{1,0:T(8,128)(2,1)} %refs_0_.1), channel_id=1, source_target_pairs={{0,4},{8,0},{16,8},{24,16},{28,24},{20,28},{12,20},{4,12},{1,5},{9... | collective-permute-start | bytes 983048 | tf_op jit(solution)/shard_map/ppermute | solution.py:542
  3.0 9.8 %collective-permute-start.2 = (bf16[128,1280]{1,0:T(8,128)(2,1)}, bf16[128,1280]{1,0:T(8,128)(2,1)S(1)}, u32[]{:S(2)}, u32[]{:S(2)}) collective-permute-start(bf16[128,1280]{1,0:T(8,128)(2,1)} %refs_0_.1), channel_id=1, source_target_pairs={{0,2},{1,3},{2,0},{3,1},{4,6},{5,7},{6,4},{7,5},{8,10},{9,11},{10,... | collective-permute-start | bytes 983048 | tf_op jit(solution)/shard_map/ppermute | solution.py:536
  6.8 4.6 %collective-permute-start.3 = (bf16[8,1280]{1,0:T(8,128)(2,1)}, bf16[8,1280]{1,0:T(8,128)(2,1)S(1)}, u32[]{:S(2)}, u32[]{:S(2)}) collective-permute-start(bf16[8,1280]{1,0:T(8,128)(2,1)} %get-tuple-element.119), channel_id=1, source_target_pairs={{0,8},{8,16},{16,24},{24,28},{28,20},{20,12},{12,4},{4,0},{1,9},{9... | collective-permute-start | bytes 61448 | tf_op jit(solution)/shard_map/ppermute | solution.py:542
  8.4 4.5 %collective-permute-start.4 = (bf16[8,1280]{1,0:T(8,128)(2,1)}, bf16[8,1280]{1,0:T(8,128)(2,1)S(1)}, u32[]{:S(2)}, u32[]{:S(2)}) collective-permute-start(bf16[8,1280]{1,0:T(8,128)(2,1)} %get-tuple-element.119), channel_id=1, source_target_pairs={{0,4},{8,0},{16,8},{24,16},{28,24},{20,28},{12,20},{4,12},{1,5},{9... | collective-permute-start | bytes 61448 | tf_op jit(solution)/shard_map/ppermute | solution.py:542
  12.9 10.0 %collective-permute-start.5 = (bf16[136,1280]{1,0:T(8,128)(2,1)S(1)}, bf16[136,1280]{1,0:T(8,128)(2,1)S(1)}, u32[]{:S(2)}, u32[]{:S(2)}) collective-permute-start(bf16[136,1280]{1,0:T(8,128)(2,1)S(1)} %get-tuple-element.125.refs_1_), channel_id=1, source_target_pairs={{0,8},{8,16},{16,24},{24,28},{28,20},{20,12},{12,4},{4,0},{1,9},{9... | collective-permute-start | bytes 1044488 | tf_op jit(solution)/shard_map/ppermute | solution.py:542
  14.5 8.4 %collective-permute-start.6 = (bf16[136,1280]{1,0:T(8,128)(2,1)S(1)}, bf16[136,1280]{1,0:T(8,128)(2,1)S(1)}, u32[]{:S(2)}, u32[]{:S(2)}) collective-permute-start(bf16[136,1280]{1,0:T(8,128)(2,1)S(1)} %get-tuple-element.126.refs_2_), channel_id=1, source_target_pairs={{0,4},{8,0},{16,8},{24,16},{28,24},{20,28},{12,20},{4,12},{1,5},{9... | collective-permute-start | bytes 1044488 | tf_op jit(solution)/shard_map/ppermute | solution.py:542
  15.0 7.9 %collective-permute-start.7 = (bf16[128,1280]{1,0:T(8,128)(2,1)}, bf16[128,1280]{1,0:T(8,128)(2,1)S(1)}, u32[]{:S(2)}, u32[]{:S(2)}) collective-permute-start(bf16[128,1280]{1,0:T(8,128)(2,1)} %refs_0_), channel_id=1, source_target_pairs={{0,2},{1,3},{2,0},{3,1},{4,6},{5,7},{6,4},{7,5},{8,10},{9,11},{10,... | collective-permute-start | bytes 983048 | tf_op jit(solution)/shard_map/ppermute | solution.py:536
  23.0 7.5 %collective-permute-start.8 = (bf16[136,1280]{1,0:T(8,128)(2,1)S(1)}, bf16[136,1280]{1,0:T(8,128)(2,1)S(1)}, u32[]{:S(2)}, u32[]{:S(2)}) collective-permute-start(bf16[136,1280]{1,0:T(8,128)(2,1)S(1)} %collective-permute-done.5.refs_0_), channel_id=1, source_target_pairs={{0,8},{8,16},{16,24},{24,28},{28,20},{20,12},{12,4},{4,0},{1,9},{9... | collective-permute-start | bytes 1044488 | tf_op jit(solution)/shard_map/ppermute | solution.py:542
  24.5 7.3 %collective-permute-start.9 = (bf16[136,1280]{1,0:T(8,128)(2,1)S(1)}, bf16[136,1280]{1,0:T(8,128)(2,1)S(1)}, u32[]{:S(2)}, u32[]{:S(2)}) collective-permute-start(bf16[136,1280]{1,0:T(8,128)(2,1)S(1)} %collective-permute-done.6.refs_1_), channel_id=1, source_target_pairs={{0,4},{8,0},{16,8},{24,16},{28,24},{20,28},{12,20},{4,12},{1,5},{9... | collective-permute-start | bytes 1044488 | tf_op jit(solution)/shard_map/ppermute | solution.py:542
  27.5 9.9 %collective-permute-start.14 = (bf16[128,1280]{1,0:T(8,128)(2,1)S(1)}, bf16[128,1280]{1,0:T(8,128)(2,1)S(1)}, u32[]{:S(2)}, u32[]{:S(2)}) collective-permute-start(bf16[128,1280]{1,0:T(8,128)(2,1)S(1)} %copy-done.9), channel_id=1, source_target_pairs={{0,1},{1,0},{2,3},{3,2},{4,5},{5,4},{6,7},{7,6},{8,9},{9,8},{10,11... | collective-permute-start | bytes 983048 | tf_op jit(solution)/shard_map/ppermute | solution.py:539
  28.5 8.9 %collective-permute-start.15 = (bf16[128,1280]{1,0:T(8,128)(2,1)S(1)}, bf16[128,1280]{1,0:T(8,128)(2,1)S(1)}, u32[]{:S(2)}, u32[]{:S(2)}) collective-permute-start(bf16[128,1280]{1,0:T(8,128)(2,1)S(1)} %collective-permute-done.7.refs_2_), channel_id=1, source_target_pairs={{0,1},{1,0},{2,3},{3,2},{4,5},{5,4},{6,7},{7,6},{8,9},{9,8},{10,11... | collective-permute-start | bytes 983048 | tf_op jit(solution)/shard_map/ppermute | solution.py:539
  31.8 8.7 %collective-permute-start.16 = (bf16[128,768]{1,0:T(8,128)(2,1)S(1)}, bf16[128,768]{1,0:T(8,128)(2,1)S(1)}, u32[]{:S(2)}, u32[]{:S(2)}) collective-permute-start(bf16[128,768]{1,0:T(8,128)(2,1)S(1)} %shard_map.132.refs_0_), channel_id=1, source_target_pairs={{0,2},{1,3},{2,0},{3,1},{4,6},{5,7},{6,4},{7,5},{8,10},{9,11},{10,... | collective-permute-start | bytes 589832 | tf_op jit(solution)/shard_map/ppermute | solution.py:536
  33.4 5.8 %collective-permute-start.13 = (bf16[72,1280]{1,0:T(8,128)(2,1)S(1)}, bf16[72,1280]{1,0:T(8,128)(2,1)S(1)}, u32[]{:S(2)}, u32[]{:S(2)}) collective-permute-start(bf16[72,1280]{1,0:T(8,128)(2,1)S(1)} %get-tuple-element.139), channel_id=1, source_target_pairs={{0,4},{8,0},{16,8},{24,16},{28,24},{20,28},{12,20},{4,12},{1,5},{9... | collective-permute-start | bytes 552968 | tf_op jit(solution)/shard_map/ppermute | solution.py:542
  33.9 5.3 %collective-permute-start.12 = (bf16[64,1280]{1,0:T(8,128)(2,1)S(1)}, bf16[64,1280]{1,0:T(8,128)(2,1)S(1)}, u32[]{:S(2)}, u32[]{:S(2)}) collective-permute-start(bf16[64,1280]{1,0:T(8,128)(2,1)S(1)} %get-tuple-element.138), channel_id=1, source_target_pairs={{0,8},{8,16},{16,24},{24,28},{28,20},{20,12},{12,4},{4,0},{1,9},{9... | collective-permute-start | bytes 491528 | tf_op jit(solution)/shard_map/ppermute | solution.py:542
  42.5 4.8 %collective-permute-start.19 = (bf16[64,768]{1,0:T(8,128)(2,1)S(1)}, bf16[64,768]{1,0:T(8,128)(2,1)S(1)}, u32[]{:S(2)}, u32[]{:S(2)}) collective-permute-start(bf16[64,768]{1,0:T(8,128)(2,1)S(1)} %shard_map.137.refs_0_), channel_id=1, source_target_pairs={{0,2},{1,3},{2,0},{3,1},{4,6},{5,7},{6,4},{7,5},{8,10},{9,11},{10,... | collective-permute-start | bytes 294920 | tf_op jit(solution)/shard_map/ppermute | solution.py:536
  45.4 6.6 %collective-permute-start.21 = (bf16[128,768]{1,0:T(8,128)(2,1)S(1)}, bf16[128,768]{1,0:T(8,128)(2,1)S(1)}, u32[]{:S(2)}, u32[]{:S(2)}) collective-permute-start(bf16[128,768]{1,0:T(8,128)(2,1)S(1)} %shard_map.140.refs_3_), channel_id=1, source_target_pairs={{0,1},{1,0},{2,3},{3,2},{4,5},{5,4},{6,7},{7,6},{8,9},{9,8},{10,11... | collective-permute-start | bytes 589832 | tf_op jit(solution)/shard_map/ppermute | solution.py:539
  45.5 7.3 %collective-permute-start.22 = (bf16[128,768]{1,0:T(8,128)(2,1)S(1)}, bf16[128,768]{1,0:T(8,128)(2,1)S(1)}, u32[]{:S(2)}, u32[]{:S(2)}) collective-permute-start(bf16[128,768]{1,0:T(8,128)(2,1)S(1)} %shard_map.138.refs_0_), channel_id=1, source_target_pairs={{0,2},{1,3},{2,0},{3,1},{4,6},{5,7},{6,4},{7,5},{8,10},{9,11},{10,... | collective-permute-start | bytes 589832 | tf_op jit(solution)/shard_map/ppermute | solution.py:536
  52.9 3.0 %collective-permute-start.25 = (bf16[128,768]{1,0:T(8,128)(2,1)S(1)}, bf16[128,768]{1,0:T(8,128)(2,1)S(1)}, u32[]{:S(2)}, u32[]{:S(2)}) collective-permute-start(bf16[128,768]{1,0:T(8,128)(2,1)S(1)} %shard_map.143.refs_0_), channel_id=1, source_target_pairs={{0,1},{1,0},{2,3},{3,2},{4,5},{5,4},{6,7},{7,6},{8,9},{9,8},{10,11... | collective-permute-start | bytes 589832 | tf_op jit(solution)/shard_map/ppermute | solution.py:539
  52.9 8.9 %collective-permute-start.26 = (bf16[128,1280]{1,0:T(8,128)(2,1)S(1)}, bf16[128,1280]{1,0:T(8,128)(2,1)S(1)}, u32[]{:S(2)}, u32[]{:S(2)}) collective-permute-start(bf16[128,1280]{1,0:T(8,128)(2,1)S(1)} %copy-done.7), channel_id=1, source_target_pairs={{0,1},{1,0},{2,3},{3,2},{4,5},{5,4},{6,7},{7,6},{8,9},{9,8},{10,11... | collective-permute-start | bytes 983048 | tf_op jit(solution)/shard_map/ppermute | solution.py:539
  53.4 10.6 %collective-permute-start.30 = (bf16[128,1280]{1,0:T(8,128)(2,1)S(1)}, bf16[128,1280]{1,0:T(8,128)(2,1)S(1)}, u32[]{:S(2)}, u32[]{:S(2)}) collective-permute-start(bf16[128,1280]{1,0:T(8,128)(2,1)S(1)} %collective-permute-done.2.refs_2_), channel_id=1, source_target_pairs={{0,1},{1,0},{2,3},{3,2},{4,5},{5,4},{6,7},{7,6},{8,9},{9,8},{10,11... | collective-permute-start | bytes 983048 | tf_op jit(solution)/shard_map/ppermute | solution.py:539
  53.5 10.6 %collective-permute-start.29 = (bf16[192,768]{1,0:T(8,128)(2,1)S(1)}, bf16[192,768]{1,0:T(8,128)(2,1)S(1)}, u32[]{:S(2)}, u32[]{:S(2)}) collective-permute-start(bf16[192,768]{1,0:T(8,128)(2,1)S(1)} %shard_map.130.refs_0_), channel_id=1, source_target_pairs={{0,2},{1,3},{2,0},{3,1},{4,6},{5,7},{6,4},{7,5},{8,10},{9,11},{10,... | collective-permute-start | bytes 884744 | tf_op jit(solution)/shard_map/ppermute | solution.py:536
  55.0 6.9 %collective-permute-start.24 = (bf16[72,1280]{1,0:T(8,128)(2,1)S(1)}, bf16[72,1280]{1,0:T(8,128)(2,1)S(1)}, u32[]{:S(2)}, u32[]{:S(2)}) collective-permute-start(bf16[72,1280]{1,0:T(8,128)(2,1)S(1)} %get-tuple-element.175), channel_id=1, source_target_pairs={{0,4},{8,0},{16,8},{24,16},{28,24},{20,28},{12,20},{4,12},{1,5},{9... | collective-permute-start | bytes 552968 | tf_op jit(solution)/shard_map/ppermute | solution.py:542
  55.9 6.0 %collective-permute-start.23 = (bf16[64,1280]{1,0:T(8,128)(2,1)S(1)}, bf16[64,1280]{1,0:T(8,128)(2,1)S(1)}, u32[]{:S(2)}, u32[]{:S(2)}) collective-permute-start(bf16[64,1280]{1,0:T(8,128)(2,1)S(1)} %get-tuple-element.174), channel_id=1, source_target_pairs={{0,8},{8,16},{16,24},{24,28},{28,20},{20,12},{12,4},{4,0},{1,9},{9... | collective-permute-start | bytes 491528 | tf_op jit(solution)/shard_map/ppermute | solution.py:542
  62.0 9.3 %collective-permute-start.27 = (bf16[136,1280]{1,0:T(8,128)(2,1)S(1)}, bf16[136,1280]{1,0:T(8,128)(2,1)S(1)}, u32[]{:S(2)}, u32[]{:S(2)}) collective-permute-start(bf16[136,1280]{1,0:T(8,128)(2,1)S(1)} %get-tuple-element.191), channel_id=1, source_target_pairs={{0,8},{8,16},{16,24},{24,28},{28,20},{20,12},{12,4},{4,0},{1,9},{9... | collective-permute-start | bytes 1044488 | tf_op jit(solution)/shard_map/ppermute | solution.py:542
  63.4 9.1 %collective-permute-start.28 = (bf16[136,1280]{1,0:T(8,128)(2,1)S(1)}, bf16[136,1280]{1,0:T(8,128)(2,1)S(1)}, u32[]{:S(2)}, u32[]{:S(2)}) collective-permute-start(bf16[136,1280]{1,0:T(8,128)(2,1)S(1)} %get-tuple-element.192), channel_id=1, source_target_pairs={{0,4},{8,0},{16,8},{24,16},{28,24},{20,28},{12,20},{4,12},{1,5},{9... | collective-permute-start | bytes 1044488 | tf_op jit(solution)/shard_map/ppermute | solution.py:542
  72.8 9.4 %collective-permute-start.32 = (bf16[136,1280]{1,0:T(8,128)(2,1)S(1)}, bf16[136,1280]{1,0:T(8,128)(2,1)S(1)}, u32[]{:S(2)}, u32[]{:S(2)}) collective-permute-start(bf16[136,1280]{1,0:T(8,128)(2,1)S(1)} %get-tuple-element.215), channel_id=1, source_target_pairs={{0,8},{8,16},{16,24},{24,28},{28,20},{20,12},{12,4},{4,0},{1,9},{9... | collective-permute-start | bytes 1044488 | tf_op jit(solution)/shard_map/ppermute | solution.py:542
  74.4 8.9 %collective-permute-start.33 = (bf16[136,1280]{1,0:T(8,128)(2,1)S(1)}, bf16[136,1280]{1,0:T(8,128)(2,1)S(1)}, u32[]{:S(2)}, u32[]{:S(2)}) collective-permute-start(bf16[136,1280]{1,0:T(8,128)(2,1)S(1)} %get-tuple-element.216), channel_id=1, source_target_pairs={{0,4},{8,0},{16,8},{24,16},{28,24},{20,28},{12,20},{4,12},{1,5},{9... | collective-permute-start | bytes 1044488 | tf_op jit(solution)/shard_map/ppermute | solution.py:542
  74.9 5.8 %collective-permute-start.34 = (bf16[128,1280]{1,0:T(8,128)(2,1)S(1)}, bf16[128,1280]{1,0:T(8,128)(2,1)S(1)}, u32[]{:S(2)}, u32[]{:S(2)}) collective-permute-start(bf16[128,1280]{1,0:T(8,128)(2,1)S(1)} %get-tuple-element.217), channel_id=1, source_target_pairs={{0,1},{1,0},{2,3},{3,2},{4,5},{5,4},{6,7},{7,6},{8,9},{9,8},{10,11... | collective-permute-start | bytes 983048 | tf_op jit(solution)/shard_map/ppermute | solution.py:539
  83.4 8.0 %collective-permute-start.38 = (bf16[136,1280]{1,0:T(8,128)(2,1)S(1)}, bf16[136,1280]{1,0:T(8,128)(2,1)S(1)}, u32[]{:S(2)}, u32[]{:S(2)}) collective-permute-start(bf16[136,1280]{1,0:T(8,128)(2,1)S(1)} %get-tuple-element.232), channel_id=1, source_target_pairs={{0,4},{8,0},{16,8},{24,16},{28,24},{20,28},{12,20},{4,12},{1,5},{9... | collective-permute-start | bytes 1044488 | tf_op jit(solution)/shard_map/ppermute | solution.py:542
  84.1 9.3 %collective-permute-start.37 = (bf16[136,1280]{1,0:T(8,128)(2,1)S(1)}, bf16[136,1280]{1,0:T(8,128)(2,1)S(1)}, u32[]{:S(2)}, u32[]{:S(2)}) collective-permute-start(bf16[136,1280]{1,0:T(8,128)(2,1)S(1)} %get-tuple-element.231), channel_id=1, source_target_pairs={{0,8},{8,16},{16,24},{24,28},{28,20},{20,12},{12,4},{4,0},{1,9},{9... | collective-permute-start | bytes 1044488 | tf_op jit(solution)/shard_map/ppermute | solution.py:542
  85.5 8.0 %collective-permute-start.36 = (bf16[128,1280]{1,0:T(8,128)(2,1)S(1)}, bf16[128,1280]{1,0:T(8,128)(2,1)S(1)}, u32[]{:S(2)}, u32[]{:S(2)}) collective-permute-start(bf16[128,1280]{1,0:T(8,128)(2,1)S(1)} %get-tuple-element.225), channel_id=1, source_target_pairs={{0,2},{1,3},{2,0},{3,1},{4,6},{5,7},{6,4},{7,5},{8,10},{9,11},{10,... | collective-permute-start | bytes 983048 | tf_op jit(solution)/shard_map/ppermute | solution.py:536
  (24 other events, 205.5 us)

commit v7 on v6

--- a/solution.py
+++ b/solution.py
@@ -571,10 +571,11 @@
     fore, back = ring(fore1, back1)
     tok_x = swap_x(tokens)
     other1, mine1, meta1 = hidden([payload, fore1, back1])
-    fore2, back2, other1, mine1, tok_x = tie((fore, back, other1, mine1, tok_x))
+    fore2, back2, other1, mine1 = tie((fore, back, other1, mine1))
 
     fore, back = ring(fore2, back2)
     (chip1,) = sums((mine1, swap_core(other1)))
+    fore2, tok_x = tie((fore2, tok_x))
     other2, mine2, meta2 = hidden([fore2, back2])
     (chip2,) = sums((mine2, swap_core(other2)))
     fore3, back3, chip1, chip2 = tie((fore, back, chip1, chip2))

time: 94.8 us -> 94.1 us (level)
    ppermute x9, waiting for transfers between devices: 10.4 us -> 8.34 us  [ring(): lax.ppermute(fore, 'expert', ahead)]
    ppermute x9, waiting for transfers between devices: 10.7 us -> 12.6 us  [ring(): lax.ppermute(back, 'expert', behind)]
  transfers between devices with their start and end apart: 39 -> 39, of which waited for: 19 -> 21; matrix products, arithmetic and copies ran while one was open for 0% -> 0% of each run, Pallas kernels for 32% -> 33%
where the time goes in v7:
time: 94.1 us; the launch traced here: 93.9 us
  starting transfers between devices  31.4 us (33%)
  Pallas kernels  31.2 us (33%)
  waiting for transfers between devices  26.4 us (28%)
  local copies, waits for them, and re-layouts  3.25 us (3%)
  matrix products  1.02 us (1%)
    pallas_call x26, Pallas kernels, run(): pl.pallas_call(kernel, in_specs=[pl.BlockSpec(memory_space=m) for m in me...  31.2 us
    ppermute x9, starting transfers between devices, ring(): lax.ppermute(fore, 'expert', ahead)  15.8 us
    ppermute x9, waiting for transfers between devices, ring(): lax.ppermute(back, 'expert', behind)  12.6 us
    ppermute x7, starting transfers between devices, swap_x(): return lax.ppermute(a, 'tensor', x_pairs)  9.11 us
    ppermute x9, waiting for transfers between devices, ring(): lax.ppermute(fore, 'expert', ahead)  8.34 us
    ppermute x14, waiting for transfers between devices, swap_core(): return lax.ppermute(a, 'tensor', core_pairs)  3.79 us
    ppermute x9, starting transfers between devices, ring(): lax.ppermute(back, 'expert', behind)  3.76 us
    unnamed x34, local copies, waits for them, and re-layouts  3.16 us
  transfers between devices with their start and end apart: 39, of which 21 were waited for; matrix products, arithmetic and copies ran while one was open for 0% of the time, Pallas kernels for 33%

profile of v7, /device:TPU:0, one launch (start us, length us, event | category | flops | bytes accessed | tf_op | source)
XLA Modules:
  0.0 93.9 jit_solution(12289984559796478449)
XLA Ops:
  0.0 3.0 %collective-permute-start = (bf16[128,1280]{1,0:T(8,128)(2,1)}, bf16[128,1280]{1,0:T(8,128)(2,1)S(1)}, u32[]{:S(2)}, u32[]{:S(2)}) collective-permute-start(bf16[128,1280]{1,0:T(8,128)(2,1)} %refs_0_.1), channel_id=1, source_target_pairs={{0,8},{8,16},{16,24},{24,28},{28,20},{20,12},{12,4},{4,0},{1,9},{9... | collective-permute-start | bytes 983048 | tf_op jit(solution)/shard_map/ppermute | solution.py:542
  3.0 1.9 %collective-permute-start.2 = (bf16[128,1280]{1,0:T(8,128)(2,1)}, bf16[128,1280]{1,0:T(8,128)(2,1)S(1)}, u32[]{:S(2)}, u32[]{:S(2)}) collective-permute-start(bf16[128,1280]{1,0:T(8,128)(2,1)} %refs_0_.1), channel_id=1, source_target_pairs={{0,2},{1,3},{2,0},{3,1},{4,6},{5,7},{6,4},{7,5},{8,10},{9,11},{10,... | collective-permute-start | bytes 983048 | tf_op jit(solution)/shard_map/ppermute | solution.py:536
  5.0 1.8 %shard_map.127 = (bf16[136,1280]{1,0:T(8,128)(2,1)}, bf16[8,1280]{1,0:T(8,128)(2,1)}) custom-call(s32[6,128]{1,0:T(8,128)} %bitcast.31, f32[16,128]{1,0:T(8,128)} %bitcast.30, bf16[128,1280]{1,0:T(8,128)(2,1)} %refs_0_.1), custom_call_target="tpu_custom_call" | custom-call | flops 1000 | bytes 1000 | tf_op jit(solution)/shard_map/pallas_call | solution.py:143
  6.8 1.6 %collective-permute-start.3 = (bf16[8,1280]{1,0:T(8,128)(2,1)}, bf16[8,1280]{1,0:T(8,128)(2,1)S(1)}, u32[]{:S(2)}, u32[]{:S(2)}) collective-permute-start(bf16[8,1280]{1,0:T(8,128)(2,1)} %get-tuple-element.120), channel_id=1, source_target_pairs={{0,8},{8,16},{16,24},{24,28},{28,20},{20,12},{12,4},{4,0},{1,9},{9... | collective-permute-start | bytes 61448 | tf_op jit(solution)/shard_map/ppermute | solution.py:542
  8.9 2.4 %collective-permute-done.3.meta_f_ref = bf16[8,1280]{1,0:T(8,128)(2,1)S(1)} collective-permute-done((bf16[8,1280]{1,0:T(8,128)(2,1)}, bf16[8,1280]{1,0:T(8,128)(2,1)S(1)}, u32[]{:S(2)}, u32[]{:S(2)}) %collective-permute-start.3) | collective-permute-done | bytes 20512 | tf_op jit(solution)/shard_map/ppermute | solution.py:542
  11.3 1.5 %collective-permute-done.4.meta_b_ref = bf16[8,1280]{1,0:T(8,128)(2,1)S(1)} collective-permute-done((bf16[8,1280]{1,0:T(8,128)(2,1)}, bf16[8,1280]{1,0:T(8,128)(2,1)S(1)}, u32[]{:S(2)}, u32[]{:S(2)}) %collective-permute-start.4) | collective-permute-done | bytes 20512 | tf_op jit(solution)/shard_map/ppermute | solution.py:542
  12.9 1.6 %collective-permute-start.5 = (bf16[136,1280]{1,0:T(8,128)(2,1)S(1)}, bf16[136,1280]{1,0:T(8,128)(2,1)S(1)}, u32[]{:S(2)}, u32[]{:S(2)}) collective-permute-start(bf16[136,1280]{1,0:T(8,128)(2,1)S(1)} %get-tuple-element.126.refs_1_), channel_id=1, source_target_pairs={{0,8},{8,16},{16,24},{24,28},{28,20},{20,12},{12,4},{4,0},{1,9},{9... | collective-permute-start | bytes 1044488 | tf_op jit(solution)/shard_map/ppermute | solution.py:542
  15.0 1.5 %collective-permute-start.10 = (bf16[128,1280]{1,0:T(8,128)(2,1)}, bf16[128,1280]{1,0:T(8,128)(2,1)S(1)}, u32[]{:S(2)}, u32[]{:S(2)}) collective-permute-start(bf16[128,1280]{1,0:T(8,128)(2,1)} %refs_0_), channel_id=1, source_target_pairs={{0,2},{1,3},{2,0},{3,1},{4,6},{5,7},{6,4},{7,5},{8,10},{9,11},{10,... | collective-permute-start | bytes 983048 | tf_op jit(solution)/shard_map/ppermute | solution.py:536
  16.5 2.1 %copy-done.1 = bf16[2,768,1280]{2,1,0:T(8,128)(2,1)S(1)} copy-done((bf16[2,768,1280]{2,1,0:T(8,128)(2,1)S(1)}, bf16[2,768,1280]{2,1,0:T(8,128)(2,1)}, u32[]{:S(2)}) %copy-start.1) | copy-done | bytes 3932184
  19.6 2.2 %shard_map.129 = (bf16[192,768]{1,0:T(8,128)(2,1)S(1)}, bf16[192,768]{1,0:T(8,128)(2,1)S(1)}, f32[24,128]{1,0:T(8,128)S(1)}) custom-call(s32[12]{0:T(128)S(1)} %stack.51.info_ref, bf16[136,1280]{1,0:T(8,128)(2,1)S(1)} %copy-done.8, bf16[136,1280]{1,0:T(8,128)(2,1)S(1)} %get-tuple-element.126.refs_1_, bf16[136,1280]{1,0:T(8,128)(2,1)S(1)} %get-tuple-element.127.refs_2_, ...), custom_call_target="tpu_custom_call" | custom-call | flops 1000 | bytes 1000 | tf_op jit(solution)/shard_map/pallas_call | solution.py:143
  23.0 1.6 %collective-permute-start.7 = (bf16[136,1280]{1,0:T(8,128)(2,1)S(1)}, bf16[136,1280]{1,0:T(8,128)(2,1)S(1)}, u32[]{:S(2)}, u32[]{:S(2)}) collective-permute-start(bf16[136,1280]{1,0:T(8,128)(2,1)S(1)} %collective-permute-done.5.refs_0_), channel_id=1, source_target_pairs={{0,8},{8,16},{16,24},{24,28},{28,20},{20,12},{12,4},{4,0},{1,9},{9... | collective-permute-start | bytes 1044488 | tf_op jit(solution)/shard_map/ppermute | solution.py:542
  25.0 1.9 %shard_map.131 = (bf16[128,768]{1,0:T(8,128)(2,1)S(1)}, bf16[128,768]{1,0:T(8,128)(2,1)S(1)}, f32[16,128]{1,0:T(8,128)S(1)}) custom-call(s32[12]{0:T(128)S(1)} %stack.51.info_ref, bf16[136,1280]{1,0:T(8,128)(2,1)S(1)} %collective-permute-done.5.refs_0_, bf16[136,1280]{1,0:T(8,128)(2,1)S(1)} %collective-permute-done.6.refs_1_, bf16[2,768,1280]{2,1,0:T(8,128)(2,1)S(1)} %copy-done.2), custom_call_target="tpu_custom_call" | custom-call | flops 1000 | bytes 1000 | tf_op jit(solution)/shard_map/pallas_call | solution.py:143
  29.0 1.5 %collective-permute-done.7.fore_ref.refs_0_ = bf16[136,1280]{1,0:T(8,128)(2,1)S(1)} collective-permute-done((bf16[136,1280]{1,0:T(8,128)(2,1)S(1)}, bf16[136,1280]{1,0:T(8,128)(2,1)S(1)}, u32[]{:S(2)}, u32[]{:S(2)}) %collective-permute-start.7) | collective-permute-done | bytes 348192 | tf_op jit(solution)/shard_map/ppermute | solution.py:542
  31.8 1.5 %collective-permute-start.16 = (bf16[128,768]{1,0:T(8,128)(2,1)S(1)}, bf16[128,768]{1,0:T(8,128)(2,1)S(1)}, u32[]{:S(2)}, u32[]{:S(2)}) collective-permute-start(bf16[128,768]{1,0:T(8,128)(2,1)S(1)} %shard_map.132.refs_0_), channel_id=1, source_target_pairs={{0,2},{1,3},{2,0},{3,1},{4,6},{5,7},{6,4},{7,5},{8,10},{9,11},{10,... | collective-permute-start | bytes 589832 | tf_op jit(solution)/shard_map/ppermute | solution.py:536
  33.9 1.6 %collective-permute-start.12 = (bf16[64,1280]{1,0:T(8,128)(2,1)S(1)}, bf16[64,1280]{1,0:T(8,128)(2,1)S(1)}, u32[]{:S(2)}, u32[]{:S(2)}) collective-permute-start(bf16[64,1280]{1,0:T(8,128)(2,1)S(1)} %get-tuple-element.140), channel_id=1, source_target_pairs={{0,8},{8,16},{16,24},{24,28},{28,20},{20,12},{12,4},{4,0},{1,9},{9... | collective-permute-start | bytes 491528 | tf_op jit(solution)/shard_map/ppermute | solution.py:542
  35.4 1.9 %shard_map.134 = (bf16[128,768]{1,0:T(8,128)(2,1)S(1)}, bf16[128,768]{1,0:T(8,128)(2,1)S(1)}, f32[16,128]{1,0:T(8,128)S(1)}) custom-call(s32[12]{0:T(128)S(1)} %stack.51.info_ref, bf16[136,1280]{1,0:T(8,128)(2,1)S(1)} %collective-permute-done.7.fore_ref.refs_0_, bf16[136,1280]{1,0:T(8,128)(2,1)S(1)} %collective-permute-done.8.back_ref.refs_1_, ...), custom_call_target="tpu_custom_call" | custom-call | flops 1000 | bytes 1000 | tf_op jit(solution)/shard_map/pallas_call | solution.py:143
  37.4 1.8 %collective-permute-done.12.refs_0_ = bf16[64,1280]{1,0:T(8,128)(2,1)S(1)} collective-permute-done((bf16[64,1280]{1,0:T(8,128)(2,1)S(1)}, bf16[64,1280]{1,0:T(8,128)(2,1)S(1)}, u32[]{:S(2)}, u32[]{:S(2)}) %collective-permute-start.12) | collective-permute-done | bytes 163872 | tf_op jit(solution)/shard_map/ppermute | solution.py:542
  43.3 2.1 %shard_map.139 = (f32[128,512]{1,0:T(8,128)S(1)}, f32[128,512]{1,0:T(8,128)S(1)}) custom-call(s32[12]{0:T(128)S(1)} %stack.51.info_ref, bf16[128,1280]{1,0:T(8,128)(2,1)S(1)} %copy-done.9, bf16[128,1280]{1,0:T(8,128)(2,1)S(1)} %collective-permute-done.14.refs_1_, bf16[128,1280]{1,0:T(8,128)(2,1)S(1)} %collective-permute-done.10.refs_2_, ...), custom_call_target="tpu_custom_call" | custom-call | flops 1000 | bytes 1000 | tf_op jit(solution)/shard_map/pallas_call | solution.py:143
  45.5 1.5 %collective-permute-start.22 = (bf16[128,768]{1,0:T(8,128)(2,1)S(1)}, bf16[128,768]{1,0:T(8,128)(2,1)S(1)}, u32[]{:S(2)}, u32[]{:S(2)}) collective-permute-start(bf16[128,768]{1,0:T(8,128)(2,1)S(1)} %shard_map.138.refs_0_), channel_id=1, source_target_pairs={{0,2},{1,3},{2,0},{3,1},{4,6},{5,7},{6,4},{7,5},{8,10},{9,11},{10,... | collective-permute-start | bytes 589832 | tf_op jit(solution)/shard_map/ppermute | solution.py:536
  48.8 3.2 %shard_map.142 = (bf16[64,1280]{1,0:T(8,128)(2,1)S(1)}, bf16[72,1280]{1,0:T(8,128)(2,1)S(1)}) custom-call(s32[12]{0:T(128)S(1)} %stack.51.info_ref, bf16[64,768]{1,0:T(8,128)(2,1)S(1)} %shard_map.141.refs_0_, bf16[64,768]{1,0:T(8,128)(2,1)S(1)} %collective-permute-done.20.refs_1_, f32[8,128]{1,0:T(8,128)S(1)} %get-tuple-element.170.refs_2_, ...), custom_call_target="tpu_custom_call" | custom-call | flops 1000 | bytes 1000 | tf_op jit(solution)/shard_map/pallas_call | solution.py:143
  53.5 1.5 %collective-permute-start.29 = (bf16[192,768]{1,0:T(8,128)(2,1)S(1)}, bf16[192,768]{1,0:T(8,128)(2,1)S(1)}, u32[]{:S(2)}, u32[]{:S(2)}) collective-permute-start(bf16[192,768]{1,0:T(8,128)(2,1)S(1)} %shard_map.130.refs_0_), channel_id=1, source_target_pairs={{0,2},{1,3},{2,0},{3,1},{4,6},{5,7},{6,4},{7,5},{8,10},{9,11},{10,... | collective-permute-start | bytes 884744 | tf_op jit(solution)/shard_map/ppermute | solution.py:536
  55.5 1.6 %collective-permute-start.23 = (bf16[64,1280]{1,0:T(8,128)(2,1)S(1)}, bf16[64,1280]{1,0:T(8,128)(2,1)S(1)}, u32[]{:S(2)}, u32[]{:S(2)}) collective-permute-start(bf16[64,1280]{1,0:T(8,128)(2,1)S(1)} %get-tuple-element.176), channel_id=1, source_target_pairs={{0,8},{8,16},{16,24},{24,28},{28,20},{20,12},{12,4},{4,0},{1,9},{9... | collective-permute-start | bytes 491528 | tf_op jit(solution)/shard_map/ppermute | solution.py:542
  57.0 3.6 %shard_map.144 = (bf16[136,1280]{1,0:T(8,128)(2,1)S(1)}, bf16[136,1280]{1,0:T(8,128)(2,1)S(1)}, bf16[136,1280]{1,0:T(8,128)(2,1)S(1)}, bf16[136,1280]{1,0:T(8,128)(2,1)S(1)}) custom-call(s32[12]{0:T(128)S(1)} %stack.51.info_ref, bf16[128,768]{1,0:T(8,128)(2,1)S(1)} %shard_map.143.refs_0_, bf16[128,768]{1,0:T(8,128)(2,1)S(1)} %collective-permute-done.25.refs_1_, ...), custom_call_target="tpu_custom_call" | custom-call | flops 1000 | bytes 1000 | tf_op jit(solution)/shard_map/pallas_call | solution.py:143
  61.8 1.6 %collective-permute-start.27 = (bf16[136,1280]{1,0:T(8,128)(2,1)S(1)}, bf16[136,1280]{1,0:T(8,128)(2,1)S(1)}, u32[]{:S(2)}, u32[]{:S(2)}) collective-permute-start(bf16[136,1280]{1,0:T(8,128)(2,1)S(1)} %get-tuple-element.193), channel_id=1, source_target_pairs={{0,8},{8,16},{16,24},{24,28},{28,20},{20,12},{12,4},{4,0},{1,9},{9... | collective-permute-start | bytes 1044488 | tf_op jit(solution)/shard_map/ppermute | solution.py:542
  63.9 2.4 %shard_map.146 = (bf16[128,512]{1,0:T(8,128)(2,1)S(1)}, bf16[128,512]{1,0:T(8,128)(2,1)S(1)}) custom-call(s32[12]{0:T(128)S(1)} %stack.51.info_ref, bf16[128,1280]{1,0:T(8,128)(2,1)S(1)} %copy-done.7, bf16[128,1280]{1,0:T(8,128)(2,1)S(1)} %collective-permute-done.26.refs_1_, bf16[128,1280]{1,0:T(8,128)(2,1)S(1)} %collective-permute-done.2.refs_2_, ...), custom_call_target="tpu_custom_call" | custom-call | flops 1000 | bytes 1000 | tf_op jit(solution)/shard_map/pallas_call | solution.py:143
  66.3 2.4 %shard_map.147 = (bf16[128,1280]{1,0:T(8,128)(2,1)S(1)}, bf16[128,1280]{1,0:T(8,128)(2,1)S(1)}) custom-call(s32[12]{0:T(128)S(1)} %stack.51.info_ref, bf16[128,512]{1,0:T(8,128)(2,1)S(1)} %get-tuple-element.205.dgate_ref, bf16[128,512]{1,0:T(8,128)(2,1)S(1)} %get-tuple-element.206.dup_ref, bf16[5120,512]{1,0:T(8,128)(2,1)S(1)} %bitcast.25, ...), custom_call_target="tpu_custom_call" | custom-call | flops 1000 | bytes 1000 | tf_op jit(solution)/shard_map/pallas_call | solution.py:143
  68.8 2.3 %shard_map.148 = (bf16[128,1280]{1,0:T(8,128)(2,1)S(1)}, bf16[128,1280]{1,0:T(8,128)(2,1)S(1)}) custom-call(s32[12]{0:T(128)S(1)} %stack.51.info_ref, bf16[128,512]{1,0:T(8,128)(2,1)S(1)} %get-tuple-element.205.dgate_ref, bf16[128,512]{1,0:T(8,128)(2,1)S(1)} %get-tuple-element.206.dup_ref, bf16[5120,512]{1,0:T(8,128)(2,1)S(1)} %bitcast.25, ...), custom_call_target="tpu_custom_call" | custom-call | flops 1000 | bytes 1000 | tf_op jit(solution)/shard_map/pallas_call | solution.py:143
  72.8 1.6 %collective-permute-start.32 = (bf16[136,1280]{1,0:T(8,128)(2,1)S(1)}, bf16[136,1280]{1,0:T(8,128)(2,1)S(1)}, u32[]{:S(2)}, u32[]{:S(2)}) collective-permute-start(bf16[136,1280]{1,0:T(8,128)(2,1)S(1)} %get-tuple-element.217), channel_id=1, source_target_pairs={{0,8},{8,16},{16,24},{24,28},{28,20},{20,12},{12,4},{4,0},{1,9},{9... | collective-permute-start | bytes 1044488 | tf_op jit(solution)/shard_map/ppermute | solution.py:542
  75.5 1.4 %collective-permute-done.35.refs_1_ = bf16[192,768]{1,0:T(8,128)(2,1)S(1)} collective-permute-done((bf16[192,768]{1,0:T(8,128)(2,1)S(1)}, bf16[192,768]{1,0:T(8,128)(2,1)S(1)}, u32[]{:S(2)}, u32[]{:S(2)}) %collective-permute-start.35) | collective-permute-done | bytes 294944 | tf_op jit(solution)/shard_map/ppermute | solution.py:539
  76.9 3.7 %shard_map.151 = (bf16[136,1280]{1,0:T(8,128)(2,1)S(1)}, bf16[136,1280]{1,0:T(8,128)(2,1)S(1)}, bf16[136,1280]{1,0:T(8,128)(2,1)S(1)}) custom-call(s32[12]{0:T(128)S(1)} %stack.51.info_ref, bf16[192,768]{1,0:T(8,128)(2,1)S(1)} %shard_map.150.refs_0_, bf16[192,768]{1,0:T(8,128)(2,1)S(1)} %collective-permute-done.35.refs_1_, ...), custom_call_target="tpu_custom_call" | custom-call | flops 1000 | bytes 1000 | tf_op jit(solution)/shard_map/pallas_call | solution.py:143
  84.0 1.6 %collective-permute-start.37 = (bf16[136,1280]{1,0:T(8,128)(2,1)S(1)}, bf16[136,1280]{1,0:T(8,128)(2,1)S(1)}, u32[]{:S(2)}, u32[]{:S(2)}) collective-permute-start(bf16[136,1280]{1,0:T(8,128)(2,1)S(1)} %get-tuple-element.233), channel_id=1, source_target_pairs={{0,8},{8,16},{16,24},{24,28},{28,20},{20,12},{12,4},{4,0},{1,9},{9... | collective-permute-start | bytes 1044488 | tf_op jit(solution)/shard_map/ppermute | solution.py:542
  86.1 5.7 %collective-permute-done.38 = bf16[136,1280]{1,0:T(8,128)(2,1)S(1)} collective-permute-done((bf16[136,1280]{1,0:T(8,128)(2,1)S(1)}, bf16[136,1280]{1,0:T(8,128)(2,1)S(1)}, u32[]{:S(2)}, u32[]{:S(2)}) %collective-permute-start.38) | collective-permute-done | bytes 348192 | tf_op jit(solution)/shard_map/ppermute | solution.py:542
  (114 shorter events, 25.7 us)
Async XLA Ops:
  0.0 12.8 %collective-permute-start = (bf16[128,1280]{1,0:T(8,128)(2,1)}, bf16[128,1280]{1,0:T(8,128)(2,1)S(1)}, u32[]{:S(2)}, u32[]{:S(2)}) collective-permute-start(bf16[128,1280]{1,0:T(8,128)(2,1)} %refs_0_.1), channel_id=1, source_target_pairs={{0,8},{8,16},{16,24},{24,28},{28,20},{20,12},{12,4},{4,0},{1,9},{9... | collective-permute-start | bytes 983048 | tf_op jit(solution)/shard_map/ppermute | solution.py:542
  3.0 9.8 %collective-permute-start.1 = (bf16[128,1280]{1,0:T(8,128)(2,1)}, bf16[128,1280]{1,0:T(8,128)(2,1)S(1)}, u32[]{:S(2)}, u32[]{:S(2)}) collective-permute-start(bf16[128,1280]{1,0:T(8,128)(2,1)} %refs_0_.1), channel_id=1, source_target_pairs={{0,4},{8,0},{16,8},{24,16},{28,24},{20,28},{12,20},{4,12},{1,5},{9... | collective-permute-start | bytes 983048 | tf_op jit(solution)/shard_map/ppermute | solution.py:542
  3.0 9.8 %collective-permute-start.2 = (bf16[128,1280]{1,0:T(8,128)(2,1)}, bf16[128,1280]{1,0:T(8,128)(2,1)S(1)}, u32[]{:S(2)}, u32[]{:S(2)}) collective-permute-start(bf16[128,1280]{1,0:T(8,128)(2,1)} %refs_0_.1), channel_id=1, source_target_pairs={{0,2},{1,3},{2,0},{3,1},{4,6},{5,7},{6,4},{7,5},{8,10},{9,11},{10,... | collective-permute-start | bytes 983048 | tf_op jit(solution)/shard_map/ppermute | solution.py:536
  6.8 4.6 %collective-permute-start.3 = (bf16[8,1280]{1,0:T(8,128)(2,1)}, bf16[8,1280]{1,0:T(8,128)(2,1)S(1)}, u32[]{:S(2)}, u32[]{:S(2)}) collective-permute-start(bf16[8,1280]{1,0:T(8,128)(2,1)} %get-tuple-element.120), channel_id=1, source_target_pairs={{0,8},{8,16},{16,24},{24,28},{28,20},{20,12},{12,4},{4,0},{1,9},{9... | collective-permute-start | bytes 61448 | tf_op jit(solution)/shard_map/ppermute | solution.py:542
  8.4 4.5 %collective-permute-start.4 = (bf16[8,1280]{1,0:T(8,128)(2,1)}, bf16[8,1280]{1,0:T(8,128)(2,1)S(1)}, u32[]{:S(2)}, u32[]{:S(2)}) collective-permute-start(bf16[8,1280]{1,0:T(8,128)(2,1)} %get-tuple-element.120), channel_id=1, source_target_pairs={{0,4},{8,0},{16,8},{24,16},{28,24},{20,28},{12,20},{4,12},{1,5},{9... | collective-permute-start | bytes 61448 | tf_op jit(solution)/shard_map/ppermute | solution.py:542
  12.9 8.9 %collective-permute-start.5 = (bf16[136,1280]{1,0:T(8,128)(2,1)S(1)}, bf16[136,1280]{1,0:T(8,128)(2,1)S(1)}, u32[]{:S(2)}, u32[]{:S(2)}) collective-permute-start(bf16[136,1280]{1,0:T(8,128)(2,1)S(1)} %get-tuple-element.126.refs_1_), channel_id=1, source_target_pairs={{0,8},{8,16},{16,24},{24,28},{28,20},{20,12},{12,4},{4,0},{1,9},{9... | collective-permute-start | bytes 1044488 | tf_op jit(solution)/shard_map/ppermute | solution.py:542
  14.5 8.4 %collective-permute-start.6 = (bf16[136,1280]{1,0:T(8,128)(2,1)S(1)}, bf16[136,1280]{1,0:T(8,128)(2,1)S(1)}, u32[]{:S(2)}, u32[]{:S(2)}) collective-permute-start(bf16[136,1280]{1,0:T(8,128)(2,1)S(1)} %get-tuple-element.127.refs_2_), channel_id=1, source_target_pairs={{0,4},{8,0},{16,8},{24,16},{28,24},{20,28},{12,20},{4,12},{1,5},{9... | collective-permute-start | bytes 1044488 | tf_op jit(solution)/shard_map/ppermute | solution.py:542
  15.0 10.0 %collective-permute-start.10 = (bf16[128,1280]{1,0:T(8,128)(2,1)}, bf16[128,1280]{1,0:T(8,128)(2,1)S(1)}, u32[]{:S(2)}, u32[]{:S(2)}) collective-permute-start(bf16[128,1280]{1,0:T(8,128)(2,1)} %refs_0_), channel_id=1, source_target_pairs={{0,2},{1,3},{2,0},{3,1},{4,6},{5,7},{6,4},{7,5},{8,10},{9,11},{10,... | collective-permute-start | bytes 983048 | tf_op jit(solution)/shard_map/ppermute | solution.py:536
  23.0 7.5 %collective-permute-start.7 = (bf16[136,1280]{1,0:T(8,128)(2,1)S(1)}, bf16[136,1280]{1,0:T(8,128)(2,1)S(1)}, u32[]{:S(2)}, u32[]{:S(2)}) collective-permute-start(bf16[136,1280]{1,0:T(8,128)(2,1)S(1)} %collective-permute-done.5.refs_0_), channel_id=1, source_target_pairs={{0,8},{8,16},{16,24},{24,28},{28,20},{20,12},{12,4},{4,0},{1,9},{9... | collective-permute-start | bytes 1044488 | tf_op jit(solution)/shard_map/ppermute | solution.py:542
  24.5 7.3 %collective-permute-start.8 = (bf16[136,1280]{1,0:T(8,128)(2,1)S(1)}, bf16[136,1280]{1,0:T(8,128)(2,1)S(1)}, u32[]{:S(2)}, u32[]{:S(2)}) collective-permute-start(bf16[136,1280]{1,0:T(8,128)(2,1)S(1)} %collective-permute-done.6.refs_1_), channel_id=1, source_target_pairs={{0,4},{8,0},{16,8},{24,16},{28,24},{20,28},{12,20},{4,12},{1,5},{9... | collective-permute-start | bytes 1044488 | tf_op jit(solution)/shard_map/ppermute | solution.py:542
  27.5 9.9 %collective-permute-start.14 = (bf16[128,1280]{1,0:T(8,128)(2,1)S(1)}, bf16[128,1280]{1,0:T(8,128)(2,1)S(1)}, u32[]{:S(2)}, u32[]{:S(2)}) collective-permute-start(bf16[128,1280]{1,0:T(8,128)(2,1)S(1)} %copy-done.9), channel_id=1, source_target_pairs={{0,1},{1,0},{2,3},{3,2},{4,5},{5,4},{6,7},{7,6},{8,9},{9,8},{10,11... | collective-permute-start | bytes 983048 | tf_op jit(solution)/shard_map/ppermute | solution.py:539
  28.5 8.9 %collective-permute-start.15 = (bf16[128,1280]{1,0:T(8,128)(2,1)S(1)}, bf16[128,1280]{1,0:T(8,128)(2,1)S(1)}, u32[]{:S(2)}, u32[]{:S(2)}) collective-permute-start(bf16[128,1280]{1,0:T(8,128)(2,1)S(1)} %collective-permute-done.10.refs_2_), channel_id=1, source_target_pairs={{0,1},{1,0},{2,3},{3,2},{4,5},{5,4},{6,7},{7,6},{8,9},{9,8},{10,11... | collective-permute-start | bytes 983048 | tf_op jit(solution)/shard_map/ppermute | solution.py:539
  31.8 8.7 %collective-permute-start.16 = (bf16[128,768]{1,0:T(8,128)(2,1)S(1)}, bf16[128,768]{1,0:T(8,128)(2,1)S(1)}, u32[]{:S(2)}, u32[]{:S(2)}) collective-permute-start(bf16[128,768]{1,0:T(8,128)(2,1)S(1)} %shard_map.132.refs_0_), channel_id=1, source_target_pairs={{0,2},{1,3},{2,0},{3,1},{4,6},{5,7},{6,4},{7,5},{8,10},{9,11},{10,... | collective-permute-start | bytes 589832 | tf_op jit(solution)/shard_map/ppermute | solution.py:536
  33.4 5.8 %collective-permute-start.13 = (bf16[72,1280]{1,0:T(8,128)(2,1)S(1)}, bf16[72,1280]{1,0:T(8,128)(2,1)S(1)}, u32[]{:S(2)}, u32[]{:S(2)}) collective-permute-start(bf16[72,1280]{1,0:T(8,128)(2,1)S(1)} %get-tuple-element.141), channel_id=1, source_target_pairs={{0,4},{8,0},{16,8},{24,16},{28,24},{20,28},{12,20},{4,12},{1,5},{9... | collective-permute-start | bytes 552968 | tf_op jit(solution)/shard_map/ppermute | solution.py:542
  33.9 5.3 %collective-permute-start.12 = (bf16[64,1280]{1,0:T(8,128)(2,1)S(1)}, bf16[64,1280]{1,0:T(8,128)(2,1)S(1)}, u32[]{:S(2)}, u32[]{:S(2)}) collective-permute-start(bf16[64,1280]{1,0:T(8,128)(2,1)S(1)} %get-tuple-element.140), channel_id=1, source_target_pairs={{0,8},{8,16},{16,24},{24,28},{28,20},{20,12},{12,4},{4,0},{1,9},{9... | collective-permute-start | bytes 491528 | tf_op jit(solution)/shard_map/ppermute | solution.py:542
  42.5 4.8 %collective-permute-start.19 = (bf16[64,768]{1,0:T(8,128)(2,1)S(1)}, bf16[64,768]{1,0:T(8,128)(2,1)S(1)}, u32[]{:S(2)}, u32[]{:S(2)}) collective-permute-start(bf16[64,768]{1,0:T(8,128)(2,1)S(1)} %shard_map.137.refs_0_), channel_id=1, source_target_pairs={{0,2},{1,3},{2,0},{3,1},{4,6},{5,7},{6,4},{7,5},{8,10},{9,11},{10,... | collective-permute-start | bytes 294920 | tf_op jit(solution)/shard_map/ppermute | solution.py:536
  45.4 6.6 %collective-permute-start.21 = (bf16[128,768]{1,0:T(8,128)(2,1)S(1)}, bf16[128,768]{1,0:T(8,128)(2,1)S(1)}, u32[]{:S(2)}, u32[]{:S(2)}) collective-permute-start(bf16[128,768]{1,0:T(8,128)(2,1)S(1)} %shard_map.140.refs_3_), channel_id=1, source_target_pairs={{0,1},{1,0},{2,3},{3,2},{4,5},{5,4},{6,7},{7,6},{8,9},{9,8},{10,11... | collective-permute-start | bytes 589832 | tf_op jit(solution)/shard_map/ppermute | solution.py:539
  45.5 7.3 %collective-permute-start.22 = (bf16[128,768]{1,0:T(8,128)(2,1)S(1)}, bf16[128,768]{1,0:T(8,128)(2,1)S(1)}, u32[]{:S(2)}, u32[]{:S(2)}) collective-permute-start(bf16[128,768]{1,0:T(8,128)(2,1)S(1)} %shard_map.138.refs_0_), channel_id=1, source_target_pairs={{0,2},{1,3},{2,0},{3,1},{4,6},{5,7},{6,4},{7,5},{8,10},{9,11},{10,... | collective-permute-start | bytes 589832 | tf_op jit(solution)/shard_map/ppermute | solution.py:536
  52.9 2.6 %collective-permute-start.25 = (bf16[128,768]{1,0:T(8,128)(2,1)S(1)}, bf16[128,768]{1,0:T(8,128)(2,1)S(1)}, u32[]{:S(2)}, u32[]{:S(2)}) collective-permute-start(bf16[128,768]{1,0:T(8,128)(2,1)S(1)} %shard_map.143.refs_0_), channel_id=1, source_target_pairs={{0,1},{1,0},{2,3},{3,2},{4,5},{5,4},{6,7},{7,6},{8,9},{9,8},{10,11... | collective-permute-start | bytes 589832 | tf_op jit(solution)/shard_map/ppermute | solution.py:539
  52.9 8.8 %collective-permute-start.26 = (bf16[128,1280]{1,0:T(8,128)(2,1)S(1)}, bf16[128,1280]{1,0:T(8,128)(2,1)S(1)}, u32[]{:S(2)}, u32[]{:S(2)}) collective-permute-start(bf16[128,1280]{1,0:T(8,128)(2,1)S(1)} %copy-done.7), channel_id=1, source_target_pairs={{0,1},{1,0},{2,3},{3,2},{4,5},{5,4},{6,7},{7,6},{8,9},{9,8},{10,11... | collective-permute-start | bytes 983048 | tf_op jit(solution)/shard_map/ppermute | solution.py:539
  53.4 10.5 %collective-permute-start.30 = (bf16[128,1280]{1,0:T(8,128)(2,1)S(1)}, bf16[128,1280]{1,0:T(8,128)(2,1)S(1)}, u32[]{:S(2)}, u32[]{:S(2)}) collective-permute-start(bf16[128,1280]{1,0:T(8,128)(2,1)S(1)} %collective-permute-done.2.refs_2_), channel_id=1, source_target_pairs={{0,1},{1,0},{2,3},{3,2},{4,5},{5,4},{6,7},{7,6},{8,9},{9,8},{10,11... | collective-permute-start | bytes 983048 | tf_op jit(solution)/shard_map/ppermute | solution.py:539
  53.5 10.4 %collective-permute-start.29 = (bf16[192,768]{1,0:T(8,128)(2,1)S(1)}, bf16[192,768]{1,0:T(8,128)(2,1)S(1)}, u32[]{:S(2)}, u32[]{:S(2)}) collective-permute-start(bf16[192,768]{1,0:T(8,128)(2,1)S(1)} %shard_map.130.refs_0_), channel_id=1, source_target_pairs={{0,2},{1,3},{2,0},{3,1},{4,6},{5,7},{6,4},{7,5},{8,10},{9,11},{10,... | collective-permute-start | bytes 884744 | tf_op jit(solution)/shard_map/ppermute | solution.py:536
  55.0 6.7 %collective-permute-start.24 = (bf16[72,1280]{1,0:T(8,128)(2,1)S(1)}, bf16[72,1280]{1,0:T(8,128)(2,1)S(1)}, u32[]{:S(2)}, u32[]{:S(2)}) collective-permute-start(bf16[72,1280]{1,0:T(8,128)(2,1)S(1)} %get-tuple-element.177), channel_id=1, source_target_pairs={{0,4},{8,0},{16,8},{24,16},{28,24},{20,28},{12,20},{4,12},{1,5},{9... | collective-permute-start | bytes 552968 | tf_op jit(solution)/shard_map/ppermute | solution.py:542
  55.5 6.0 %collective-permute-start.23 = (bf16[64,1280]{1,0:T(8,128)(2,1)S(1)}, bf16[64,1280]{1,0:T(8,128)(2,1)S(1)}, u32[]{:S(2)}, u32[]{:S(2)}) collective-permute-start(bf16[64,1280]{1,0:T(8,128)(2,1)S(1)} %get-tuple-element.176), channel_id=1, source_target_pairs={{0,8},{8,16},{16,24},{24,28},{28,20},{20,12},{12,4},{4,0},{1,9},{9... | collective-permute-start | bytes 491528 | tf_op jit(solution)/shard_map/ppermute | solution.py:542
  61.8 9.4 %collective-permute-start.27 = (bf16[136,1280]{1,0:T(8,128)(2,1)S(1)}, bf16[136,1280]{1,0:T(8,128)(2,1)S(1)}, u32[]{:S(2)}, u32[]{:S(2)}) collective-permute-start(bf16[136,1280]{1,0:T(8,128)(2,1)S(1)} %get-tuple-element.193), channel_id=1, source_target_pairs={{0,8},{8,16},{16,24},{24,28},{28,20},{20,12},{12,4},{4,0},{1,9},{9... | collective-permute-start | bytes 1044488 | tf_op jit(solution)/shard_map/ppermute | solution.py:542
  63.4 9.1 %collective-permute-start.28 = (bf16[136,1280]{1,0:T(8,128)(2,1)S(1)}, bf16[136,1280]{1,0:T(8,128)(2,1)S(1)}, u32[]{:S(2)}, u32[]{:S(2)}) collective-permute-start(bf16[136,1280]{1,0:T(8,128)(2,1)S(1)} %get-tuple-element.194), channel_id=1, source_target_pairs={{0,4},{8,0},{16,8},{24,16},{28,24},{20,28},{12,20},{4,12},{1,5},{9... | collective-permute-start | bytes 1044488 | tf_op jit(solution)/shard_map/ppermute | solution.py:542
  72.8 9.2 %collective-permute-start.32 = (bf16[136,1280]{1,0:T(8,128)(2,1)S(1)}, bf16[136,1280]{1,0:T(8,128)(2,1)S(1)}, u32[]{:S(2)}, u32[]{:S(2)}) collective-permute-start(bf16[136,1280]{1,0:T(8,128)(2,1)S(1)} %get-tuple-element.217), channel_id=1, source_target_pairs={{0,8},{8,16},{16,24},{24,28},{28,20},{20,12},{12,4},{4,0},{1,9},{9... | collective-permute-start | bytes 1044488 | tf_op jit(solution)/shard_map/ppermute | solution.py:542
  74.4 8.9 %collective-permute-start.33 = (bf16[136,1280]{1,0:T(8,128)(2,1)S(1)}, bf16[136,1280]{1,0:T(8,128)(2,1)S(1)}, u32[]{:S(2)}, u32[]{:S(2)}) collective-permute-start(bf16[136,1280]{1,0:T(8,128)(2,1)S(1)} %get-tuple-element.218), channel_id=1, source_target_pairs={{0,4},{8,0},{16,8},{24,16},{28,24},{20,28},{12,20},{4,12},{1,5},{9... | collective-permute-start | bytes 1044488 | tf_op jit(solution)/shard_map/ppermute | solution.py:542
  74.9 5.8 %collective-permute-start.34 = (bf16[128,1280]{1,0:T(8,128)(2,1)S(1)}, bf16[128,1280]{1,0:T(8,128)(2,1)S(1)}, u32[]{:S(2)}, u32[]{:S(2)}) collective-permute-start(bf16[128,1280]{1,0:T(8,128)(2,1)S(1)} %get-tuple-element.219), channel_id=1, source_target_pairs={{0,1},{1,0},{2,3},{3,2},{4,5},{5,4},{6,7},{7,6},{8,9},{9,8},{10,11... | collective-permute-start | bytes 983048 | tf_op jit(solution)/shard_map/ppermute | solution.py:539
  83.5 8.4 %collective-permute-start.38 = (bf16[136,1280]{1,0:T(8,128)(2,1)S(1)}, bf16[136,1280]{1,0:T(8,128)(2,1)S(1)}, u32[]{:S(2)}, u32[]{:S(2)}) collective-permute-start(bf16[136,1280]{1,0:T(8,128)(2,1)S(1)} %get-tuple-element.234), channel_id=1, source_target_pairs={{0,4},{8,0},{16,8},{24,16},{28,24},{20,28},{12,20},{4,12},{1,5},{9... | collective-permute-start | bytes 1044488 | tf_op jit(solution)/shard_map/ppermute | solution.py:542
  84.0 8.2 %collective-permute-start.37 = (bf16[136,1280]{1,0:T(8,128)(2,1)S(1)}, bf16[136,1280]{1,0:T(8,128)(2,1)S(1)}, u32[]{:S(2)}, u32[]{:S(2)}) collective-permute-start(bf16[136,1280]{1,0:T(8,128)(2,1)S(1)} %get-tuple-element.233), channel_id=1, source_target_pairs={{0,8},{8,16},{16,24},{24,28},{28,20},{20,12},{12,4},{4,0},{1,9},{9... | collective-permute-start | bytes 1044488 | tf_op jit(solution)/shard_map/ppermute | solution.py:542
  85.5 7.4 %collective-permute-start.36 = (bf16[128,1280]{1,0:T(8,128)(2,1)S(1)}, bf16[128,1280]{1,0:T(8,128)(2,1)S(1)}, u32[]{:S(2)}, u32[]{:S(2)}) collective-permute-start(bf16[128,1280]{1,0:T(8,128)(2,1)S(1)} %get-tuple-element.227), channel_id=1, source_target_pairs={{0,2},{1,3},{2,0},{3,1},{4,6},{5,7},{6,4},{7,5},{8,10},{9,11},{10,... | collective-permute-start | bytes 983048 | tf_op jit(solution)/shard_map/ppermute | solution.py:536
  (24 other events, 203.3 us)

commit v8 on v7

--- a/solution.py
+++ b/solution.py
@@ -585,12 +585,14 @@
     other3, mine3, meta3 = hidden([fore3, back3])
     tok_both = swap_core(tok_x)
     tok_core = swap_core(tokens)
-    top, bottom, chip2, other3, mine3, tok_core, tok_both, out_grad = tie(
-        (top, bottom, chip2, other3, mine3, tok_core, tok_both, out_grad)
+    top, bottom, chip2, other3, mine3, out_grad = tie(
+        (top, bottom, chip2, other3, mine3, out_grad)
     )
 
     (other4,) = hidden([(top, bottom)], (0,))
-    top, bottom, other4, other3, far2 = tie((top, bottom, other4, other3, far2))
+    top, bottom, other4, other3, far2, tok_core, tok_both = tie(
+        (top, bottom, other4, other3, far2, tok_core, tok_both)
+    )
     swapped4 = swap_core(other4)
     mine4, meta4 = hidden([(top, bottom)], (1,))
     swapped3 = swap_core(other3)

time: 94.1 us -> 94.2 us (level)
  no operation moved by 1% of the time
where the time goes in v8:
time: 94.2 us; the launch traced here: 94 us
  starting transfers between devices  31.4 us (33%)
  Pallas kernels  31.2 us (33%)
  waiting for transfers between devices  26.5 us (28%)
  local copies, waits for them, and re-layouts  3.25 us (3%)
  matrix products  1.02 us (1%)
    pallas_call x26, Pallas kernels, run(): pl.pallas_call(kernel, in_specs=[pl.BlockSpec(memory_space=m) for m in me...  31.2 us
    ppermute x9, starting transfers between devices, ring(): lax.ppermute(fore, 'expert', ahead)  15.8 us
    ppermute x9, waiting for transfers between devices, ring(): lax.ppermute(back, 'expert', behind)  12.6 us
    ppermute x7, starting transfers between devices, swap_x(): return lax.ppermute(a, 'tensor', x_pairs)  9.11 us
    ppermute x9, waiting for transfers between devices, ring(): lax.ppermute(fore, 'expert', ahead)  8.35 us
    ppermute x14, waiting for transfers between devices, swap_core(): return lax.ppermute(a, 'tensor', core_pairs)  3.79 us
    ppermute x9, starting transfers between devices, ring(): lax.ppermute(back, 'expert', behind)  3.76 us
    unnamed x34, local copies, waits for them, and re-layouts  3.16 us
  transfers between devices with their start and end apart: 39, of which 21 were waited for; matrix products, arithmetic and copies ran while one was open for 0% of the time, Pallas kernels for 33%

profile of v8, /device:TPU:0, one launch (start us, length us, event | category | flops | bytes accessed | tf_op | source)
XLA Modules:
  0.0 94.0 jit_solution(17405014218907988240)
XLA Ops:
  0.0 3.0 %collective-permute-start = (bf16[128,1280]{1,0:T(8,128)(2,1)}, bf16[128,1280]{1,0:T(8,128)(2,1)S(1)}, u32[]{:S(2)}, u32[]{:S(2)}) collective-permute-start(bf16[128,1280]{1,0:T(8,128)(2,1)} %refs_0_.1), channel_id=1, source_target_pairs={{0,8},{8,16},{16,24},{24,28},{28,20},{20,12},{12,4},{4,0},{1,9},{9... | collective-permute-start | bytes 983048 | tf_op jit(solution)/shard_map/ppermute | solution.py:542
  3.0 1.9 %collective-permute-start.2 = (bf16[128,1280]{1,0:T(8,128)(2,1)}, bf16[128,1280]{1,0:T(8,128)(2,1)S(1)}, u32[]{:S(2)}, u32[]{:S(2)}) collective-permute-start(bf16[128,1280]{1,0:T(8,128)(2,1)} %refs_0_.1), channel_id=1, source_target_pairs={{0,2},{1,3},{2,0},{3,1},{4,6},{5,7},{6,4},{7,5},{8,10},{9,11},{10,... | collective-permute-start | bytes 983048 | tf_op jit(solution)/shard_map/ppermute | solution.py:536
  5.0 1.8 %shard_map.127 = (bf16[136,1280]{1,0:T(8,128)(2,1)}, bf16[8,1280]{1,0:T(8,128)(2,1)}) custom-call(s32[6,128]{1,0:T(8,128)} %bitcast.31, f32[16,128]{1,0:T(8,128)} %bitcast.30, bf16[128,1280]{1,0:T(8,128)(2,1)} %refs_0_.1), custom_call_target="tpu_custom_call" | custom-call | flops 1000 | bytes 1000 | tf_op jit(solution)/shard_map/pallas_call | solution.py:143
  6.8 1.6 %collective-permute-start.3 = (bf16[8,1280]{1,0:T(8,128)(2,1)}, bf16[8,1280]{1,0:T(8,128)(2,1)S(1)}, u32[]{:S(2)}, u32[]{:S(2)}) collective-permute-start(bf16[8,1280]{1,0:T(8,128)(2,1)} %get-tuple-element.120), channel_id=1, source_target_pairs={{0,8},{8,16},{16,24},{24,28},{28,20},{20,12},{12,4},{4,0},{1,9},{9... | collective-permute-start | bytes 61448 | tf_op jit(solution)/shard_map/ppermute | solution.py:542
  8.9 2.4 %collective-permute-done.3.meta_f_ref = bf16[8,1280]{1,0:T(8,128)(2,1)S(1)} collective-permute-done((bf16[8,1280]{1,0:T(8,128)(2,1)}, bf16[8,1280]{1,0:T(8,128)(2,1)S(1)}, u32[]{:S(2)}, u32[]{:S(2)}) %collective-permute-start.3) | collective-permute-done | bytes 20512 | tf_op jit(solution)/shard_map/ppermute | solution.py:542
  11.3 1.5 %collective-permute-done.4.meta_b_ref = bf16[8,1280]{1,0:T(8,128)(2,1)S(1)} collective-permute-done((bf16[8,1280]{1,0:T(8,128)(2,1)}, bf16[8,1280]{1,0:T(8,128)(2,1)S(1)}, u32[]{:S(2)}, u32[]{:S(2)}) %collective-permute-start.4) | collective-permute-done | bytes 20512 | tf_op jit(solution)/shard_map/ppermute | solution.py:542
  12.9 1.6 %collective-permute-start.5 = (bf16[136,1280]{1,0:T(8,128)(2,1)S(1)}, bf16[136,1280]{1,0:T(8,128)(2,1)S(1)}, u32[]{:S(2)}, u32[]{:S(2)}) collective-permute-start(bf16[136,1280]{1,0:T(8,128)(2,1)S(1)} %get-tuple-element.126.refs_1_), channel_id=1, source_target_pairs={{0,8},{8,16},{16,24},{24,28},{28,20},{20,12},{12,4},{4,0},{1,9},{9... | collective-permute-start | bytes 1044488 | tf_op jit(solution)/shard_map/ppermute | solution.py:542
  15.0 1.5 %collective-permute-start.10 = (bf16[128,1280]{1,0:T(8,128)(2,1)}, bf16[128,1280]{1,0:T(8,128)(2,1)S(1)}, u32[]{:S(2)}, u32[]{:S(2)}) collective-permute-start(bf16[128,1280]{1,0:T(8,128)(2,1)} %refs_0_), channel_id=1, source_target_pairs={{0,2},{1,3},{2,0},{3,1},{4,6},{5,7},{6,4},{7,5},{8,10},{9,11},{10,... | collective-permute-start | bytes 983048 | tf_op jit(solution)/shard_map/ppermute | solution.py:536
  16.5 2.1 %copy-done.1 = bf16[2,768,1280]{2,1,0:T(8,128)(2,1)S(1)} copy-done((bf16[2,768,1280]{2,1,0:T(8,128)(2,1)S(1)}, bf16[2,768,1280]{2,1,0:T(8,128)(2,1)}, u32[]{:S(2)}) %copy-start.1) | copy-done | bytes 3932184
  19.6 2.2 %shard_map.129 = (bf16[192,768]{1,0:T(8,128)(2,1)S(1)}, bf16[192,768]{1,0:T(8,128)(2,1)S(1)}, f32[24,128]{1,0:T(8,128)S(1)}) custom-call(s32[12]{0:T(128)S(1)} %stack.51.info_ref, bf16[136,1280]{1,0:T(8,128)(2,1)S(1)} %copy-done.8, bf16[136,1280]{1,0:T(8,128)(2,1)S(1)} %get-tuple-element.126.refs_1_, bf16[136,1280]{1,0:T(8,128)(2,1)S(1)} %get-tuple-element.127.refs_2_, ...), custom_call_target="tpu_custom_call" | custom-call | flops 1000 | bytes 1000 | tf_op jit(solution)/shard_map/pallas_call | solution.py:143
  23.0 1.6 %collective-permute-start.7 = (bf16[136,1280]{1,0:T(8,128)(2,1)S(1)}, bf16[136,1280]{1,0:T(8,128)(2,1)S(1)}, u32[]{:S(2)}, u32[]{:S(2)}) collective-permute-start(bf16[136,1280]{1,0:T(8,128)(2,1)S(1)} %collective-permute-done.5.refs_0_), channel_id=1, source_target_pairs={{0,8},{8,16},{16,24},{24,28},{28,20},{20,12},{12,4},{4,0},{1,9},{9... | collective-permute-start | bytes 1044488 | tf_op jit(solution)/shard_map/ppermute | solution.py:542
  25.0 1.9 %shard_map.131 = (bf16[128,768]{1,0:T(8,128)(2,1)S(1)}, bf16[128,768]{1,0:T(8,128)(2,1)S(1)}, f32[16,128]{1,0:T(8,128)S(1)}) custom-call(s32[12]{0:T(128)S(1)} %stack.51.info_ref, bf16[136,1280]{1,0:T(8,128)(2,1)S(1)} %collective-permute-done.5.refs_0_, bf16[136,1280]{1,0:T(8,128)(2,1)S(1)} %collective-permute-done.6.refs_1_, bf16[2,768,1280]{2,1,0:T(8,128)(2,1)S(1)} %copy-done.2), custom_call_target="tpu_custom_call" | custom-call | flops 1000 | bytes 1000 | tf_op jit(solution)/shard_map/pallas_call | solution.py:143
  29.0 1.5 %collective-permute-done.7.fore_ref.refs_0_ = bf16[136,1280]{1,0:T(8,128)(2,1)S(1)} collective-permute-done((bf16[136,1280]{1,0:T(8,128)(2,1)S(1)}, bf16[136,1280]{1,0:T(8,128)(2,1)S(1)}, u32[]{:S(2)}, u32[]{:S(2)}) %collective-permute-start.7) | collective-permute-done | bytes 348192 | tf_op jit(solution)/shard_map/ppermute | solution.py:542
  31.8 1.5 %collective-permute-start.14 = (bf16[128,768]{1,0:T(8,128)(2,1)S(1)}, bf16[128,768]{1,0:T(8,128)(2,1)S(1)}, u32[]{:S(2)}, u32[]{:S(2)}) collective-permute-start(bf16[128,768]{1,0:T(8,128)(2,1)S(1)} %shard_map.132.refs_0_), channel_id=1, source_target_pairs={{0,2},{1,3},{2,0},{3,1},{4,6},{5,7},{6,4},{7,5},{8,10},{9,11},{10,... | collective-permute-start | bytes 589832 | tf_op jit(solution)/shard_map/ppermute | solution.py:536
  33.9 1.6 %collective-permute-start.12 = (bf16[64,1280]{1,0:T(8,128)(2,1)S(1)}, bf16[64,1280]{1,0:T(8,128)(2,1)S(1)}, u32[]{:S(2)}, u32[]{:S(2)}) collective-permute-start(bf16[64,1280]{1,0:T(8,128)(2,1)S(1)} %get-tuple-element.140), channel_id=1, source_target_pairs={{0,8},{8,16},{16,24},{24,28},{28,20},{20,12},{12,4},{4,0},{1,9},{9... | collective-permute-start | bytes 491528 | tf_op jit(solution)/shard_map/ppermute | solution.py:542
  35.4 1.9 %shard_map.134 = (bf16[128,768]{1,0:T(8,128)(2,1)S(1)}, bf16[128,768]{1,0:T(8,128)(2,1)S(1)}, f32[16,128]{1,0:T(8,128)S(1)}) custom-call(s32[12]{0:T(128)S(1)} %stack.51.info_ref, bf16[136,1280]{1,0:T(8,128)(2,1)S(1)} %collective-permute-done.7.fore_ref.refs_0_, bf16[136,1280]{1,0:T(8,128)(2,1)S(1)} %collective-permute-done.8.back_ref.refs_1_, ...), custom_call_target="tpu_custom_call" | custom-call | flops 1000 | bytes 1000 | tf_op jit(solution)/shard_map/pallas_call | solution.py:143
  37.4 1.8 %collective-permute-done.12.refs_0_ = bf16[64,1280]{1,0:T(8,128)(2,1)S(1)} collective-permute-done((bf16[64,1280]{1,0:T(8,128)(2,1)S(1)}, bf16[64,1280]{1,0:T(8,128)(2,1)S(1)}, u32[]{:S(2)}, u32[]{:S(2)}) %collective-permute-start.12) | collective-permute-done | bytes 163872 | tf_op jit(solution)/shard_map/ppermute | solution.py:542
  43.3 2.1 %shard_map.139 = (f32[128,512]{1,0:T(8,128)S(1)}, f32[128,512]{1,0:T(8,128)S(1)}) custom-call(s32[12]{0:T(128)S(1)} %stack.51.info_ref, bf16[128,1280]{1,0:T(8,128)(2,1)S(1)} %copy-done.9, bf16[128,1280]{1,0:T(8,128)(2,1)S(1)} %collective-permute-done.15.refs_1_, bf16[128,1280]{1,0:T(8,128)(2,1)S(1)} %collective-permute-done.10.refs_2_, ...), custom_call_target="tpu_custom_call" | custom-call | flops 1000 | bytes 1000 | tf_op jit(solution)/shard_map/pallas_call | solution.py:143
  45.5 1.6 %collective-permute-start.22 = (bf16[128,768]{1,0:T(8,128)(2,1)S(1)}, bf16[128,768]{1,0:T(8,128)(2,1)S(1)}, u32[]{:S(2)}, u32[]{:S(2)}) collective-permute-start(bf16[128,768]{1,0:T(8,128)(2,1)S(1)} %shard_map.138.refs_0_), channel_id=1, source_target_pairs={{0,2},{1,3},{2,0},{3,1},{4,6},{5,7},{6,4},{7,5},{8,10},{9,11},{10,... | collective-permute-start | bytes 589832 | tf_op jit(solution)/shard_map/ppermute | solution.py:536
  48.8 3.2 %shard_map.142 = (bf16[64,1280]{1,0:T(8,128)(2,1)S(1)}, bf16[72,1280]{1,0:T(8,128)(2,1)S(1)}) custom-call(s32[12]{0:T(128)S(1)} %stack.51.info_ref, bf16[64,768]{1,0:T(8,128)(2,1)S(1)} %shard_map.141.refs_0_, bf16[64,768]{1,0:T(8,128)(2,1)S(1)} %collective-permute-done.20.refs_1_, f32[8,128]{1,0:T(8,128)S(1)} %get-tuple-element.170.refs_2_, ...), custom_call_target="tpu_custom_call" | custom-call | flops 1000 | bytes 1000 | tf_op jit(solution)/shard_map/pallas_call | solution.py:143
  53.6 1.5 %collective-permute-start.29 = (bf16[192,768]{1,0:T(8,128)(2,1)S(1)}, bf16[192,768]{1,0:T(8,128)(2,1)S(1)}, u32[]{:S(2)}, u32[]{:S(2)}) collective-permute-start(bf16[192,768]{1,0:T(8,128)(2,1)S(1)} %shard_map.130.refs_0_), channel_id=1, source_target_pairs={{0,2},{1,3},{2,0},{3,1},{4,6},{5,7},{6,4},{7,5},{8,10},{9,11},{10,... | collective-permute-start | bytes 884744 | tf_op jit(solution)/shard_map/ppermute | solution.py:536
  55.5 1.6 %collective-permute-start.23 = (bf16[64,1280]{1,0:T(8,128)(2,1)S(1)}, bf16[64,1280]{1,0:T(8,128)(2,1)S(1)}, u32[]{:S(2)}, u32[]{:S(2)}) collective-permute-start(bf16[64,1280]{1,0:T(8,128)(2,1)S(1)} %get-tuple-element.176), channel_id=1, source_target_pairs={{0,8},{8,16},{16,24},{24,28},{28,20},{20,12},{12,4},{4,0},{1,9},{9... | collective-permute-start | bytes 491528 | tf_op jit(solution)/shard_map/ppermute | solution.py:542
  57.1 3.6 %shard_map.144 = (bf16[136,1280]{1,0:T(8,128)(2,1)S(1)}, bf16[136,1280]{1,0:T(8,128)(2,1)S(1)}, bf16[136,1280]{1,0:T(8,128)(2,1)S(1)}, bf16[136,1280]{1,0:T(8,128)(2,1)S(1)}) custom-call(s32[12]{0:T(128)S(1)} %stack.51.info_ref, bf16[128,768]{1,0:T(8,128)(2,1)S(1)} %shard_map.143.refs_0_, bf16[128,768]{1,0:T(8,128)(2,1)S(1)} %collective-permute-done.25.refs_1_, ...), custom_call_target="tpu_custom_call" | custom-call | flops 1000 | bytes 1000 | tf_op jit(solution)/shard_map/pallas_call | solution.py:143
  61.8 1.6 %collective-permute-start.27 = (bf16[136,1280]{1,0:T(8,128)(2,1)S(1)}, bf16[136,1280]{1,0:T(8,128)(2,1)S(1)}, u32[]{:S(2)}, u32[]{:S(2)}) collective-permute-start(bf16[136,1280]{1,0:T(8,128)(2,1)S(1)} %get-tuple-element.193), channel_id=1, source_target_pairs={{0,8},{8,16},{16,24},{24,28},{28,20},{20,12},{12,4},{4,0},{1,9},{9... | collective-permute-start | bytes 1044488 | tf_op jit(solution)/shard_map/ppermute | solution.py:542
  64.0 2.4 %shard_map.146 = (bf16[128,512]{1,0:T(8,128)(2,1)S(1)}, bf16[128,512]{1,0:T(8,128)(2,1)S(1)}) custom-call(s32[12]{0:T(128)S(1)} %stack.51.info_ref, bf16[128,1280]{1,0:T(8,128)(2,1)S(1)} %copy-done.7, bf16[128,1280]{1,0:T(8,128)(2,1)S(1)} %collective-permute-done.26.refs_1_, bf16[128,1280]{1,0:T(8,128)(2,1)S(1)} %collective-permute-done.2.refs_2_, ...), custom_call_target="tpu_custom_call" | custom-call | flops 1000 | bytes 1000 | tf_op jit(solution)/shard_map/pallas_call | solution.py:143
  66.3 2.4 %shard_map.147 = (bf16[128,1280]{1,0:T(8,128)(2,1)S(1)}, bf16[128,1280]{1,0:T(8,128)(2,1)S(1)}) custom-call(s32[12]{0:T(128)S(1)} %stack.51.info_ref, bf16[128,512]{1,0:T(8,128)(2,1)S(1)} %get-tuple-element.205.dgate_ref, bf16[128,512]{1,0:T(8,128)(2,1)S(1)} %get-tuple-element.206.dup_ref, bf16[5120,512]{1,0:T(8,128)(2,1)S(1)} %bitcast.25, ...), custom_call_target="tpu_custom_call" | custom-call | flops 1000 | bytes 1000 | tf_op jit(solution)/shard_map/pallas_call | solution.py:143
  68.8 2.3 %shard_map.148 = (bf16[128,1280]{1,0:T(8,128)(2,1)S(1)}, bf16[128,1280]{1,0:T(8,128)(2,1)S(1)}) custom-call(s32[12]{0:T(128)S(1)} %stack.51.info_ref, bf16[128,512]{1,0:T(8,128)(2,1)S(1)} %get-tuple-element.205.dgate_ref, bf16[128,512]{1,0:T(8,128)(2,1)S(1)} %get-tuple-element.206.dup_ref, bf16[5120,512]{1,0:T(8,128)(2,1)S(1)} %bitcast.25, ...), custom_call_target="tpu_custom_call" | custom-call | flops 1000 | bytes 1000 | tf_op jit(solution)/shard_map/pallas_call | solution.py:143
  72.8 1.6 %collective-permute-start.32 = (bf16[136,1280]{1,0:T(8,128)(2,1)S(1)}, bf16[136,1280]{1,0:T(8,128)(2,1)S(1)}, u32[]{:S(2)}, u32[]{:S(2)}) collective-permute-start(bf16[136,1280]{1,0:T(8,128)(2,1)S(1)} %get-tuple-element.217), channel_id=1, source_target_pairs={{0,8},{8,16},{16,24},{24,28},{28,20},{20,12},{12,4},{4,0},{1,9},{9... | collective-permute-start | bytes 1044488 | tf_op jit(solution)/shard_map/ppermute | solution.py:542
  75.6 1.4 %collective-permute-done.35.refs_1_ = bf16[192,768]{1,0:T(8,128)(2,1)S(1)} collective-permute-done((bf16[192,768]{1,0:T(8,128)(2,1)S(1)}, bf16[192,768]{1,0:T(8,128)(2,1)S(1)}, u32[]{:S(2)}, u32[]{:S(2)}) %collective-permute-start.35) | collective-permute-done | bytes 294944 | tf_op jit(solution)/shard_map/ppermute | solution.py:539
  77.0 3.7 %shard_map.151 = (bf16[136,1280]{1,0:T(8,128)(2,1)S(1)}, bf16[136,1280]{1,0:T(8,128)(2,1)S(1)}, bf16[136,1280]{1,0:T(8,128)(2,1)S(1)}) custom-call(s32[12]{0:T(128)S(1)} %stack.51.info_ref, bf16[192,768]{1,0:T(8,128)(2,1)S(1)} %shard_map.150.refs_0_, bf16[192,768]{1,0:T(8,128)(2,1)S(1)} %collective-permute-done.35.refs_1_, ...), custom_call_target="tpu_custom_call" | custom-call | flops 1000 | bytes 1000 | tf_op jit(solution)/shard_map/pallas_call | solution.py:143
  84.0 1.6 %collective-permute-start.37 = (bf16[136,1280]{1,0:T(8,128)(2,1)S(1)}, bf16[136,1280]{1,0:T(8,128)(2,1)S(1)}, u32[]{:S(2)}, u32[]{:S(2)}) collective-permute-start(bf16[136,1280]{1,0:T(8,128)(2,1)S(1)} %get-tuple-element.233), channel_id=1, source_target_pairs={{0,8},{8,16},{16,24},{24,28},{28,20},{20,12},{12,4},{4,0},{1,9},{9... | collective-permute-start | bytes 1044488 | tf_op jit(solution)/shard_map/ppermute | solution.py:542
  86.1 5.7 %collective-permute-done.38 = bf16[136,1280]{1,0:T(8,128)(2,1)S(1)} collective-permute-done((bf16[136,1280]{1,0:T(8,128)(2,1)S(1)}, bf16[136,1280]{1,0:T(8,128)(2,1)S(1)}, u32[]{:S(2)}, u32[]{:S(2)}) %collective-permute-start.38) | collective-permute-done | bytes 348192 | tf_op jit(solution)/shard_map/ppermute | solution.py:542
  (114 shorter events, 25.7 us)
Async XLA Ops:
  0.0 12.8 %collective-permute-start = (bf16[128,1280]{1,0:T(8,128)(2,1)}, bf16[128,1280]{1,0:T(8,128)(2,1)S(1)}, u32[]{:S(2)}, u32[]{:S(2)}) collective-permute-start(bf16[128,1280]{1,0:T(8,128)(2,1)} %refs_0_.1), channel_id=1, source_target_pairs={{0,8},{8,16},{16,24},{24,28},{28,20},{20,12},{12,4},{4,0},{1,9},{9... | collective-permute-start | bytes 983048 | tf_op jit(solution)/shard_map/ppermute | solution.py:542
  3.0 9.8 %collective-permute-start.1 = (bf16[128,1280]{1,0:T(8,128)(2,1)}, bf16[128,1280]{1,0:T(8,128)(2,1)S(1)}, u32[]{:S(2)}, u32[]{:S(2)}) collective-permute-start(bf16[128,1280]{1,0:T(8,128)(2,1)} %refs_0_.1), channel_id=1, source_target_pairs={{0,4},{8,0},{16,8},{24,16},{28,24},{20,28},{12,20},{4,12},{1,5},{9... | collective-permute-start | bytes 983048 | tf_op jit(solution)/shard_map/ppermute | solution.py:542
  3.0 9.8 %collective-permute-start.2 = (bf16[128,1280]{1,0:T(8,128)(2,1)}, bf16[128,1280]{1,0:T(8,128)(2,1)S(1)}, u32[]{:S(2)}, u32[]{:S(2)}) collective-permute-start(bf16[128,1280]{1,0:T(8,128)(2,1)} %refs_0_.1), channel_id=1, source_target_pairs={{0,2},{1,3},{2,0},{3,1},{4,6},{5,7},{6,4},{7,5},{8,10},{9,11},{10,... | collective-permute-start | bytes 983048 | tf_op jit(solution)/shard_map/ppermute | solution.py:536
  6.8 4.6 %collective-permute-start.3 = (bf16[8,1280]{1,0:T(8,128)(2,1)}, bf16[8,1280]{1,0:T(8,128)(2,1)S(1)}, u32[]{:S(2)}, u32[]{:S(2)}) collective-permute-start(bf16[8,1280]{1,0:T(8,128)(2,1)} %get-tuple-element.120), channel_id=1, source_target_pairs={{0,8},{8,16},{16,24},{24,28},{28,20},{20,12},{12,4},{4,0},{1,9},{9... | collective-permute-start | bytes 61448 | tf_op jit(solution)/shard_map/ppermute | solution.py:542
  8.4 4.5 %collective-permute-start.4 = (bf16[8,1280]{1,0:T(8,128)(2,1)}, bf16[8,1280]{1,0:T(8,128)(2,1)S(1)}, u32[]{:S(2)}, u32[]{:S(2)}) collective-permute-start(bf16[8,1280]{1,0:T(8,128)(2,1)} %get-tuple-element.120), channel_id=1, source_target_pairs={{0,4},{8,0},{16,8},{24,16},{28,24},{20,28},{12,20},{4,12},{1,5},{9... | collective-permute-start | bytes 61448 | tf_op jit(solution)/shard_map/ppermute | solution.py:542
  12.9 8.9 %collective-permute-start.5 = (bf16[136,1280]{1,0:T(8,128)(2,1)S(1)}, bf16[136,1280]{1,0:T(8,128)(2,1)S(1)}, u32[]{:S(2)}, u32[]{:S(2)}) collective-permute-start(bf16[136,1280]{1,0:T(8,128)(2,1)S(1)} %get-tuple-element.126.refs_1_), channel_id=1, source_target_pairs={{0,8},{8,16},{16,24},{24,28},{28,20},{20,12},{12,4},{4,0},{1,9},{9... | collective-permute-start | bytes 1044488 | tf_op jit(solution)/shard_map/ppermute | solution.py:542
  14.5 8.4 %collective-permute-start.6 = (bf16[136,1280]{1,0:T(8,128)(2,1)S(1)}, bf16[136,1280]{1,0:T(8,128)(2,1)S(1)}, u32[]{:S(2)}, u32[]{:S(2)}) collective-permute-start(bf16[136,1280]{1,0:T(8,128)(2,1)S(1)} %get-tuple-element.127.refs_2_), channel_id=1, source_target_pairs={{0,4},{8,0},{16,8},{24,16},{28,24},{20,28},{12,20},{4,12},{1,5},{9... | collective-permute-start | bytes 1044488 | tf_op jit(solution)/shard_map/ppermute | solution.py:542
  15.0 10.0 %collective-permute-start.10 = (bf16[128,1280]{1,0:T(8,128)(2,1)}, bf16[128,1280]{1,0:T(8,128)(2,1)S(1)}, u32[]{:S(2)}, u32[]{:S(2)}) collective-permute-start(bf16[128,1280]{1,0:T(8,128)(2,1)} %refs_0_), channel_id=1, source_target_pairs={{0,2},{1,3},{2,0},{3,1},{4,6},{5,7},{6,4},{7,5},{8,10},{9,11},{10,... | collective-permute-start | bytes 983048 | tf_op jit(solution)/shard_map/ppermute | solution.py:536
  23.0 7.5 %collective-permute-start.7 = (bf16[136,1280]{1,0:T(8,128)(2,1)S(1)}, bf16[136,1280]{1,0:T(8,128)(2,1)S(1)}, u32[]{:S(2)}, u32[]{:S(2)}) collective-permute-start(bf16[136,1280]{1,0:T(8,128)(2,1)S(1)} %collective-permute-done.5.refs_0_), channel_id=1, source_target_pairs={{0,8},{8,16},{16,24},{24,28},{28,20},{20,12},{12,4},{4,0},{1,9},{9... | collective-permute-start | bytes 1044488 | tf_op jit(solution)/shard_map/ppermute | solution.py:542
  24.5 7.3 %collective-permute-start.8 = (bf16[136,1280]{1,0:T(8,128)(2,1)S(1)}, bf16[136,1280]{1,0:T(8,128)(2,1)S(1)}, u32[]{:S(2)}, u32[]{:S(2)}) collective-permute-start(bf16[136,1280]{1,0:T(8,128)(2,1)S(1)} %collective-permute-done.6.refs_1_), channel_id=1, source_target_pairs={{0,4},{8,0},{16,8},{24,16},{28,24},{20,28},{12,20},{4,12},{1,5},{9... | collective-permute-start | bytes 1044488 | tf_op jit(solution)/shard_map/ppermute | solution.py:542
  27.5 13.0 %collective-permute-start.15 = (bf16[128,1280]{1,0:T(8,128)(2,1)S(1)}, bf16[128,1280]{1,0:T(8,128)(2,1)S(1)}, u32[]{:S(2)}, u32[]{:S(2)}) collective-permute-start(bf16[128,1280]{1,0:T(8,128)(2,1)S(1)} %copy-done.9), channel_id=1, source_target_pairs={{0,1},{1,0},{2,3},{3,2},{4,5},{5,4},{6,7},{7,6},{8,9},{9,8},{10,11... | collective-permute-start | bytes 983048 | tf_op jit(solution)/shard_map/ppermute | solution.py:539
  28.5 12.1 %collective-permute-start.16 = (bf16[128,1280]{1,0:T(8,128)(2,1)S(1)}, bf16[128,1280]{1,0:T(8,128)(2,1)S(1)}, u32[]{:S(2)}, u32[]{:S(2)}) collective-permute-start(bf16[128,1280]{1,0:T(8,128)(2,1)S(1)} %collective-permute-done.10.refs_2_), channel_id=1, source_target_pairs={{0,1},{1,0},{2,3},{3,2},{4,5},{5,4},{6,7},{7,6},{8,9},{9,8},{10,11... | collective-permute-start | bytes 983048 | tf_op jit(solution)/shard_map/ppermute | solution.py:539
  31.8 8.7 %collective-permute-start.14 = (bf16[128,768]{1,0:T(8,128)(2,1)S(1)}, bf16[128,768]{1,0:T(8,128)(2,1)S(1)}, u32[]{:S(2)}, u32[]{:S(2)}) collective-permute-start(bf16[128,768]{1,0:T(8,128)(2,1)S(1)} %shard_map.132.refs_0_), channel_id=1, source_target_pairs={{0,2},{1,3},{2,0},{3,1},{4,6},{5,7},{6,4},{7,5},{8,10},{9,11},{10,... | collective-permute-start | bytes 589832 | tf_op jit(solution)/shard_map/ppermute | solution.py:536
  33.4 5.8 %collective-permute-start.13 = (bf16[72,1280]{1,0:T(8,128)(2,1)S(1)}, bf16[72,1280]{1,0:T(8,128)(2,1)S(1)}, u32[]{:S(2)}, u32[]{:S(2)}) collective-permute-start(bf16[72,1280]{1,0:T(8,128)(2,1)S(1)} %get-tuple-element.141), channel_id=1, source_target_pairs={{0,4},{8,0},{16,8},{24,16},{28,24},{20,28},{12,20},{4,12},{1,5},{9... | collective-permute-start | bytes 552968 | tf_op jit(solution)/shard_map/ppermute | solution.py:542
  33.9 5.3 %collective-permute-start.12 = (bf16[64,1280]{1,0:T(8,128)(2,1)S(1)}, bf16[64,1280]{1,0:T(8,128)(2,1)S(1)}, u32[]{:S(2)}, u32[]{:S(2)}) collective-permute-start(bf16[64,1280]{1,0:T(8,128)(2,1)S(1)} %get-tuple-element.140), channel_id=1, source_target_pairs={{0,8},{8,16},{16,24},{24,28},{28,20},{20,12},{12,4},{4,0},{1,9},{9... | collective-permute-start | bytes 491528 | tf_op jit(solution)/shard_map/ppermute | solution.py:542
  42.5 4.9 %collective-permute-start.19 = (bf16[64,768]{1,0:T(8,128)(2,1)S(1)}, bf16[64,768]{1,0:T(8,128)(2,1)S(1)}, u32[]{:S(2)}, u32[]{:S(2)}) collective-permute-start(bf16[64,768]{1,0:T(8,128)(2,1)S(1)} %shard_map.137.refs_0_), channel_id=1, source_target_pairs={{0,2},{1,3},{2,0},{3,1},{4,6},{5,7},{6,4},{7,5},{8,10},{9,11},{10,... | collective-permute-start | bytes 294920 | tf_op jit(solution)/shard_map/ppermute | solution.py:536
  45.4 6.6 %collective-permute-start.21 = (bf16[128,768]{1,0:T(8,128)(2,1)S(1)}, bf16[128,768]{1,0:T(8,128)(2,1)S(1)}, u32[]{:S(2)}, u32[]{:S(2)}) collective-permute-start(bf16[128,768]{1,0:T(8,128)(2,1)S(1)} %shard_map.140.refs_3_), channel_id=1, source_target_pairs={{0,1},{1,0},{2,3},{3,2},{4,5},{5,4},{6,7},{7,6},{8,9},{9,8},{10,11... | collective-permute-start | bytes 589832 | tf_op jit(solution)/shard_map/ppermute | solution.py:539
  45.5 7.3 %collective-permute-start.22 = (bf16[128,768]{1,0:T(8,128)(2,1)S(1)}, bf16[128,768]{1,0:T(8,128)(2,1)S(1)}, u32[]{:S(2)}, u32[]{:S(2)}) collective-permute-start(bf16[128,768]{1,0:T(8,128)(2,1)S(1)} %shard_map.138.refs_0_), channel_id=1, source_target_pairs={{0,2},{1,3},{2,0},{3,1},{4,6},{5,7},{6,4},{7,5},{8,10},{9,11},{10,... | collective-permute-start | bytes 589832 | tf_op jit(solution)/shard_map/ppermute | solution.py:536
  52.9 2.6 %collective-permute-start.25 = (bf16[128,768]{1,0:T(8,128)(2,1)S(1)}, bf16[128,768]{1,0:T(8,128)(2,1)S(1)}, u32[]{:S(2)}, u32[]{:S(2)}) collective-permute-start(bf16[128,768]{1,0:T(8,128)(2,1)S(1)} %shard_map.143.refs_0_), channel_id=1, source_target_pairs={{0,1},{1,0},{2,3},{3,2},{4,5},{5,4},{6,7},{7,6},{8,9},{9,8},{10,11... | collective-permute-start | bytes 589832 | tf_op jit(solution)/shard_map/ppermute | solution.py:539
  53.0 8.8 %collective-permute-start.26 = (bf16[128,1280]{1,0:T(8,128)(2,1)S(1)}, bf16[128,1280]{1,0:T(8,128)(2,1)S(1)}, u32[]{:S(2)}, u32[]{:S(2)}) collective-permute-start(bf16[128,1280]{1,0:T(8,128)(2,1)S(1)} %copy-done.7), channel_id=1, source_target_pairs={{0,1},{1,0},{2,3},{3,2},{4,5},{5,4},{6,7},{7,6},{8,9},{9,8},{10,11... | collective-permute-start | bytes 983048 | tf_op jit(solution)/shard_map/ppermute | solution.py:539
  53.5 10.5 %collective-permute-start.30 = (bf16[128,1280]{1,0:T(8,128)(2,1)S(1)}, bf16[128,1280]{1,0:T(8,128)(2,1)S(1)}, u32[]{:S(2)}, u32[]{:S(2)}) collective-permute-start(bf16[128,1280]{1,0:T(8,128)(2,1)S(1)} %collective-permute-done.2.refs_2_), channel_id=1, source_target_pairs={{0,1},{1,0},{2,3},{3,2},{4,5},{5,4},{6,7},{7,6},{8,9},{9,8},{10,11... | collective-permute-start | bytes 983048 | tf_op jit(solution)/shard_map/ppermute | solution.py:539
  53.6 10.4 %collective-permute-start.29 = (bf16[192,768]{1,0:T(8,128)(2,1)S(1)}, bf16[192,768]{1,0:T(8,128)(2,1)S(1)}, u32[]{:S(2)}, u32[]{:S(2)}) collective-permute-start(bf16[192,768]{1,0:T(8,128)(2,1)S(1)} %shard_map.130.refs_0_), channel_id=1, source_target_pairs={{0,2},{1,3},{2,0},{3,1},{4,6},{5,7},{6,4},{7,5},{8,10},{9,11},{10,... | collective-permute-start | bytes 884744 | tf_op jit(solution)/shard_map/ppermute | solution.py:536
  55.0 6.7 %collective-permute-start.24 = (bf16[72,1280]{1,0:T(8,128)(2,1)S(1)}, bf16[72,1280]{1,0:T(8,128)(2,1)S(1)}, u32[]{:S(2)}, u32[]{:S(2)}) collective-permute-start(bf16[72,1280]{1,0:T(8,128)(2,1)S(1)} %get-tuple-element.177), channel_id=1, source_target_pairs={{0,4},{8,0},{16,8},{24,16},{28,24},{20,28},{12,20},{4,12},{1,5},{9... | collective-permute-start | bytes 552968 | tf_op jit(solution)/shard_map/ppermute | solution.py:542
  55.5 6.0 %collective-permute-start.23 = (bf16[64,1280]{1,0:T(8,128)(2,1)S(1)}, bf16[64,1280]{1,0:T(8,128)(2,1)S(1)}, u32[]{:S(2)}, u32[]{:S(2)}) collective-permute-start(bf16[64,1280]{1,0:T(8,128)(2,1)S(1)} %get-tuple-element.176), channel_id=1, source_target_pairs={{0,8},{8,16},{16,24},{24,28},{28,20},{20,12},{12,4},{4,0},{1,9},{9... | collective-permute-start | bytes 491528 | tf_op jit(solution)/shard_map/ppermute | solution.py:542
  61.8 9.4 %collective-permute-start.27 = (bf16[136,1280]{1,0:T(8,128)(2,1)S(1)}, bf16[136,1280]{1,0:T(8,128)(2,1)S(1)}, u32[]{:S(2)}, u32[]{:S(2)}) collective-permute-start(bf16[136,1280]{1,0:T(8,128)(2,1)S(1)} %get-tuple-element.193), channel_id=1, source_target_pairs={{0,8},{8,16},{16,24},{24,28},{28,20},{20,12},{12,4},{4,0},{1,9},{9... | collective-permute-start | bytes 1044488 | tf_op jit(solution)/shard_map/ppermute | solution.py:542
  63.5 9.1 %collective-permute-start.28 = (bf16[136,1280]{1,0:T(8,128)(2,1)S(1)}, bf16[136,1280]{1,0:T(8,128)(2,1)S(1)}, u32[]{:S(2)}, u32[]{:S(2)}) collective-permute-start(bf16[136,1280]{1,0:T(8,128)(2,1)S(1)} %get-tuple-element.194), channel_id=1, source_target_pairs={{0,4},{8,0},{16,8},{24,16},{28,24},{20,28},{12,20},{4,12},{1,5},{9... | collective-permute-start | bytes 1044488 | tf_op jit(solution)/shard_map/ppermute | solution.py:542
  72.8 9.2 %collective-permute-start.32 = (bf16[136,1280]{1,0:T(8,128)(2,1)S(1)}, bf16[136,1280]{1,0:T(8,128)(2,1)S(1)}, u32[]{:S(2)}, u32[]{:S(2)}) collective-permute-start(bf16[136,1280]{1,0:T(8,128)(2,1)S(1)} %get-tuple-element.217), channel_id=1, source_target_pairs={{0,8},{8,16},{16,24},{24,28},{28,20},{20,12},{12,4},{4,0},{1,9},{9... | collective-permute-start | bytes 1044488 | tf_op jit(solution)/shard_map/ppermute | solution.py:542
  74.4 8.9 %collective-permute-start.33 = (bf16[136,1280]{1,0:T(8,128)(2,1)S(1)}, bf16[136,1280]{1,0:T(8,128)(2,1)S(1)}, u32[]{:S(2)}, u32[]{:S(2)}) collective-permute-start(bf16[136,1280]{1,0:T(8,128)(2,1)S(1)} %get-tuple-element.218), channel_id=1, source_target_pairs={{0,4},{8,0},{16,8},{24,16},{28,24},{20,28},{12,20},{4,12},{1,5},{9... | collective-permute-start | bytes 1044488 | tf_op jit(solution)/shard_map/ppermute | solution.py:542
  74.9 5.8 %collective-permute-start.34 = (bf16[128,1280]{1,0:T(8,128)(2,1)S(1)}, bf16[128,1280]{1,0:T(8,128)(2,1)S(1)}, u32[]{:S(2)}, u32[]{:S(2)}) collective-permute-start(bf16[128,1280]{1,0:T(8,128)(2,1)S(1)} %get-tuple-element.219), channel_id=1, source_target_pairs={{0,1},{1,0},{2,3},{3,2},{4,5},{5,4},{6,7},{7,6},{8,9},{9,8},{10,11... | collective-permute-start | bytes 983048 | tf_op jit(solution)/shard_map/ppermute | solution.py:539
  83.5 8.4 %collective-permute-start.38 = (bf16[136,1280]{1,0:T(8,128)(2,1)S(1)}, bf16[136,1280]{1,0:T(8,128)(2,1)S(1)}, u32[]{:S(2)}, u32[]{:S(2)}) collective-permute-start(bf16[136,1280]{1,0:T(8,128)(2,1)S(1)} %get-tuple-element.234), channel_id=1, source_target_pairs={{0,4},{8,0},{16,8},{24,16},{28,24},{20,28},{12,20},{4,12},{1,5},{9... | collective-permute-start | bytes 1044488 | tf_op jit(solution)/shard_map/ppermute | solution.py:542
  84.0 8.2 %collective-permute-start.37 = (bf16[136,1280]{1,0:T(8,128)(2,1)S(1)}, bf16[136,1280]{1,0:T(8,128)(2,1)S(1)}, u32[]{:S(2)}, u32[]{:S(2)}) collective-permute-start(bf16[136,1280]{1,0:T(8,128)(2,1)S(1)} %get-tuple-element.233), channel_id=1, source_target_pairs={{0,8},{8,16},{16,24},{24,28},{28,20},{20,12},{12,4},{4,0},{1,9},{9... | collective-permute-start | bytes 1044488 | tf_op jit(solution)/shard_map/ppermute | solution.py:542
  85.6 7.4 %collective-permute-start.36 = (bf16[128,1280]{1,0:T(8,128)(2,1)S(1)}, bf16[128,1280]{1,0:T(8,128)(2,1)S(1)}, u32[]{:S(2)}, u32[]{:S(2)}) collective-permute-start(bf16[128,1280]{1,0:T(8,128)(2,1)S(1)} %get-tuple-element.227), channel_id=1, source_target_pairs={{0,2},{1,3},{2,0},{3,1},{4,6},{5,7},{6,4},{7,5},{8,10},{9,11},{10,... | collective-permute-start | bytes 983048 | tf_op jit(solution)/shard_map/ppermute | solution.py:536
  (24 other events, 203.4 us)
